TPU v7x, 512 devices: a whole 4x8x8 slice. The times are simulated.
512 devices in a mesh: dp: 8 (over x, core), blk: 64 (over y, z).
Axes of the slice: x: 4, y: 8, z: 8, core: 2. Of those that a mesh axis runs over, the one named last changes fastest.
Arguments:
- inputs: bfloat16 [1536, 8192], P('dp', 'blk'), may hold values from -6 to 6
- upstream: bfloat16 [1536, 8192], P('dp', 'blk'), may hold values from -6 to 6
- w_in: bfloat16 [256, 16, 128, 128], P('blk'), may hold values from -0.125 to 0.125
- cols_in: int32 [256, 16], P('blk'), may hold values from 0 to 63, as said below
- w_out: bfloat16 [256, 16, 128, 128], P('blk'), may hold values from -0.0625 to 0.0625
- cols_out: int32 [256, 16], P('blk'), may hold values from 0 to 63, as said below
Outputs:
- grad_inputs: bfloat16 [1536, 8192], P('dp', 'blk')
- grad_w_in: bfloat16 [256, 16, 128, 128], P('blk', 'dp')
- grad_w_out: bfloat16 [256, 16, 128, 128], P('blk', 'dp')
Inputs may be any that keep to these rules, and one draw needn't show every extreme that they name: `cols_in`: each block row lists 16 distinct feature blocks. `cols_out`: each block row lists 16 distinct feature blocks.
All inputs are finite; a program needn't handle non-finite values.
Results may differ from a plain program's by a relative error of at most 0.017.
Values may be sent and summed in bfloat16 or wider, within the bound.
No kernel may reach another device: no remote copies, remote signals or barrier semaphores. Data moves between devices by JAX's collectives and lax.ppermute only.
A program may use at most 128 MiB of HBM per device.

v0:
```python
import jax
import jax.numpy as jnp
from jax import lax
from jax.sharding import PartitionSpec as P


def gelu_tanh(values):
    return jax.nn.gelu(values, approximate=True)


def per_device(inputs, upstream, w_in, cols_in, w_out, cols_out):
    tok_count = inputs.shape[0]
    width_block = w_in.shape[2]
    row_count = w_in.shape[0]
    per_row = w_in.shape[1]
    whole_in = lax.all_gather(inputs, "blk", axis=1, tiled=True)
    col_blocks = whole_in.shape[1] // width_block
    in_blocks = whole_in.reshape(tok_count, col_blocks, width_block)[:, cols_in]
    hidden = jnp.einsum("trki,rkih->trh", in_blocks, w_in, preferred_element_type=jnp.float32)
    activated = gelu_tanh(hidden).astype(jnp.bfloat16)
    whole_up = lax.all_gather(upstream, "blk", axis=1, tiled=True)
    up_blocks = whole_up.reshape(tok_count, col_blocks, width_block)[:, cols_out]
    grad_act = jnp.einsum("trko,rkho->trh", up_blocks, w_out, preferred_element_type=jnp.float32)
    unused, pull_back = jax.vjp(gelu_tanh, hidden)
    grad_hidden = pull_back(grad_act)[0].astype(jnp.bfloat16)
    terms = jnp.einsum("trh,rkih->trki", grad_hidden, w_in, preferred_element_type=jnp.float32)
    terms = terms.reshape(tok_count, row_count * per_row, width_block)
    picks = (
        cols_in.reshape(-1)[:, None] == jnp.arange(col_blocks, dtype=jnp.int32)[None, :]
    ).astype(jnp.float32)
    placed = jnp.einsum("tjb,jc->tcb", terms, picks, precision=lax.Precision.HIGHEST)
    received = lax.all_to_all(placed, "blk", split_axis=1, concat_axis=1, tiled=True)
    grad_inputs = jnp.sum(received, axis=1).astype(jnp.bfloat16)
    part_out = jnp.einsum(
        "trh,trko->rkho", activated, up_blocks, preferred_element_type=jnp.float32
    )
    part_in = jnp.einsum(
        "trki,trh->rkih", in_blocks, grad_hidden, preferred_element_type=jnp.float32
    )
    summed_in, summed_out = (
        lax.psum_scatter(
            part_in.astype(jnp.bfloat16), "dp", scatter_dimension=1, tiled=True
        ).astype(jnp.float32),
        lax.psum_scatter(
            part_out.astype(jnp.bfloat16), "dp", scatter_dimension=1, tiled=True
        ).astype(jnp.float32),
    )
    return (grad_inputs, summed_in.astype(jnp.bfloat16), summed_out.astype(jnp.bfloat16))


def solution(mesh):
    return jax.shard_map(
        per_device,
        mesh=mesh,
        in_specs=(
            P("dp", "blk"),
            P("dp", "blk"),
            P("blk", None, None, None),
            P("blk", None),
            P("blk", None, None, None),
            P("blk", None),
        ),
        out_specs=(P("dp", "blk"), P("blk", "dp", None, None), P("blk", "dp", None, None)),
        check_vma=False,
    )
```

profile of v0, /device:TPU:40, one launch (start us, length us, event | category | flops | bytes accessed | tf_op | source)
XLA Modules:
  0.0 443.6 jit_solution(5249329966461871973)
XLA Ops:
  8.0 0.7 all-gather.3.cloned.1.call-update
  8.7 0.8 eq.15
  9.4 0.7 compare_select_fusion.1
  11.0 90.0 %all-gather.5.cloned.1.call-done = bf16[192,8192]{1,0:T(8,128)(2,1)} async-done(((bf16[192,128]{1,0:T(8,128)(2,1)}), bf16[192,8192]{1,0:T(8,128)(2,1)}) %all-gather.5.cloned.1.call-update) | async-done | bytes 3145744 | tf_op jit(solution)/shard_map/all_gather | solution.py:16
  101.0 4.5 %copy_bitcast_fusion = bf16[192,64,128]{2,0,1:T(8,128)(2,1)} fusion(bf16[192,8192]{1,0:T(8,128)(2,1)} %all-gather.5.cloned.1.call-done), kind=kLoop, calls=%fused_computation.4 | loop fusion | bytes 6291456 | tf_op jit(solution)/shard_map/reshape | solution.py:18
  105.5 4.5 %gather_fusion.1 = bf16[64,192,128]{2,1,0:T(8,128)(2,1)} fusion(bf16[192,64,128]{2,0,1:T(8,128)(2,1)} %copy_bitcast_fusion, s32[1024]{0:T(1024)S(1)} %pad_clamp_fusion), kind=kCustom, calls=%fused_computation.1 | custom fusion | bytes 6291712 | tf_op jit(solution)/shard_map/gather | solution.py:18
  109.9 77.5 %all-gather.3.cloned.1.call-done = bf16[192,8192]{1,0:T(8,128)(2,1)} async-done(((bf16[192,128]{1,0:T(8,128)(2,1)}), bf16[192,8192]{1,0:T(8,128)(2,1)}) %all-gather.3.cloned.1.call-update) | async-done | bytes 3145744 | tf_op jit(solution)/shard_map/all_gather | solution.py:21
  187.4 4.5 %copy_bitcast_fusion.1 = bf16[192,64,128]{2,0,1:T(8,128)(2,1)} fusion(bf16[192,8192]{1,0:T(8,128)(2,1)} %all-gather.3.cloned.1.call-done), kind=kLoop, calls=%fused_computation.5 | loop fusion | bytes 6291456 | tf_op jit(solution)/shard_map/reshape | solution.py:22
  191.9 4.5 %gather_fusion = bf16[64,192,128]{2,1,0:T(8,128)(2,1)} fusion(bf16[192,64,128]{2,0,1:T(8,128)(2,1)} %copy_bitcast_fusion.1, s32[1024]{0:T(1024)S(1)} %pad_clamp_fusion.1), kind=kCustom, calls=%fused_computation | custom fusion | bytes 6291712 | tf_op jit(solution)/shard_map/gather | solution.py:22
  196.4 3.0 convolution_bitcast_fusion
  199.9 1.0 fusion.12
  200.9 1.0 fusion.24
  201.9 7.3 %fusion.2 = f32[192,64,128]{2,1,0:T(8,128)S(1)} fusion(f32[192,64,128]{2,0,1:T(8,128)S(1)} %bitcast.75, s32[64]{0:T(128)S(1)} %eq.15), kind=kOutput, calls=%fused_computation.6 | convolution fusion | flops 1207963648 | bytes 12583168 | tf_op jit(solution)/shard_map/tjb,jc->tcb/dot_general | solution.py:31
  209.2 6.5 %copy.22 = f32[192,64,128]{2,0,1:T(8,128)} copy(f32[192,64,128]{2,1,0:T(8,128)S(1)} %fusion.2) | data formatting | bytes 12582912 | tf_op jit(solution)/shard_map/tjb,jc->tcb/transpose | solution.py:31
  215.7 10.0 %all-to-all-start = ((f32[192,64,128]{2,0,1:T(8,128)}), f32[192,64,128]{2,0,1:T(8,128)}, u32[]{:S(2)}, u32[]{:S(2)}) async-start(f32[192,64,128]{2,0,1:T(8,128)} %copy.22), calls=%async_computation | async-start | bytes 12582912 | tf_op jit(solution)/shard_map/all_to_all | solution.py:32
  225.8 5.0 %convolution_convert_fusion = bf16[4,16,128,128]{3,2,1,0:T(8,128)(2,1)} fusion(bf16[192,4,16,128]{3,0,2,1:T(8,128)(2,1)} %bitcast.74, bf16[192,4,128,1]{2,0,3,1:T(8,128)(2,1)S(1)} %fusion.12), kind=kOutput, calls=%fused_computation.8 | convolution fusion | flops 403701760 | bytes 5439488 | tf_op jit(solution)/shard_map/trki,trh->rkih/dot_general | solution.py:37
  230.8 3.0 convert_bitcast_fusion
  233.9 1.3 dynamic-slice
  235.8 84.1 %all-reduce.5.cloned.1.call-done = (bf16[4,16,128,128]{3,2,1,0:T(8,128)(2,1)}, bf16[4,16,128,128]{2,3,1,0:T(8,128)(2,1)}) async-done(((bf16[4,16,128,128]{3,2,1,0:T(8,128)(2,1)}, bf16[4,16,128,128]{2,3,1,0:T(8,128)(2,1)}), (bf16[4,16,128,128]{3,2,1,0:T(8,128)(2,1)}, bf16[4,16,128,128]{2,3,1,0:T(8,128)(2,1)})) %all-reduce.5.cloned.1.call-update) | async-done | bytes 4194320
  319.9 1.0 constant_dynamic-slice_fusion
  320.9 0.9 copy.23
  321.7 1.7 constant_dynamic-slice_fusion.1
  323.4 109.9 %all-to-all-done = f32[192,64,128]{2,0,1:T(8,128)} async-done(((f32[192,64,128]{2,0,1:T(8,128)}), f32[192,64,128]{2,0,1:T(8,128)}, u32[]{:S(2)}, u32[]{:S(2)}) %all-to-all-start) | async-done | bytes 6291488 | tf_op jit(solution)/shard_map/all_to_all | solution.py:32
  433.3 3.7 reduce_sum.9
  (18 shorter events, 2.2 us)
Async XLA Ops:
  7.2 189.2 %copy-start = (bf16[4,16,128,128]{3,2,1,0:T(8,128)(2,1)S(1)}, bf16[4,16,128,128]{3,2,1,0:T(8,128)(2,1)}, u32[]{:S(2)}) copy-start(bf16[4,16,128,128]{3,2,1,0:T(8,128)(2,1)} %param.8) | copy-start | bytes 6291460
  7.2 93.8 %all-gather.5.cloned.1.call-start = ((), (), s32[]{:S(2)}) async-start(), calls=%async_computation.2 | async-start | bytes 3194880 | tf_op jit(solution)/shard_map/all_gather | solution.py:16
  7.9 179.5 %all-gather.3.cloned.1.call-start = ((), (), s32[]{:S(2)}) async-start(), calls=%async_computation.1 | async-start | bytes 3194880 | tf_op jit(solution)/shard_map/all_gather | solution.py:21
  196.4 3.0 copy-start.1
  196.4 3.5 copy-start.3
  215.7 217.6 %all-to-all-start = ((f32[192,64,128]{2,0,1:T(8,128)}), f32[192,64,128]{2,0,1:T(8,128)}, u32[]{:S(2)}, u32[]{:S(2)}) async-start(f32[192,64,128]{2,0,1:T(8,128)} %copy.22), calls=%async_computation | async-start | bytes 12582912 | tf_op jit(solution)/shard_map/all_to_all | solution.py:32
  225.7 94.2 %all-reduce.5.cloned.1.call-start = ((), (), s32[]{:S(2)}) async-start(), calls=%async_computation.3 | async-start | bytes 8388608
  225.8 5.1 %copy-start.2 = (bf16[64,192,128]{2,1,0:T(8,128)(2,1)S(1)}, bf16[64,192,128]{2,1,0:T(8,128)(2,1)}, u32[]{:S(2)}) copy-start(bf16[64,192,128]{2,1,0:T(8,128)(2,1)} %gather_fusion) | copy-start | bytes 9437188
Sparse Core Ops, SparseCore 0:
  11.0 89.9 all-gather.4
  103.9 83.4 all-gather.2
  234.0 85.8 all-reduce.4
where the time goes:
time: 444 us
  waiting for transfers between devices  363 us (82%)
  local copies, waits for them, and re-layouts  30.6 us (7%)
  matrix products  20.4 us (5%)
  between operations  14.5 us (3%)
  starting transfers between devices  10.2 us (2%)
  other arithmetic  5.1 us (1%)
    all_to_all x1, waiting for transfers between devices, per_device(): lax.all_to_all(placed, 'blk', split_axis=1, concat_axis=1, tiled=True)  110 us
    all_gather x1, waiting for transfers between devices, per_device(): whole_in = lax.all_gather(inputs, 'blk', axis=1, tiled=True)  90 us
    unnamed x4, waiting for transfers between devices  85.5 us
    all_gather x1, waiting for transfers between devices, per_device(): whole_up = lax.all_gather(upstream, 'blk', axis=1, tiled=True)  77.5 us
    all_to_all x1, starting transfers between devices, per_device(): lax.all_to_all(placed, 'blk', split_axis=1, concat_axis=1, tiled=True)  10 us
  transfers between devices with their start and end apart: 4, of which 4 were waited for; matrix products, arithmetic and copies ran while one was open for 5% of the time, Pallas kernels for 0%

commit v1 on v0

v1 whole, which is shorter than its diff:
```python
import functools

import jax
import jax.numpy as jnp
from jax import lax
from jax.experimental import pallas as pl
from jax.experimental.pallas import tpu as pltpu
from jax.sharding import Mesh, PartitionSpec as P

BF16 = jnp.bfloat16
F32 = jnp.float32
GELU_SCALE = 0.7978845608028654
GELU_CUBE = 0.044715


def dot_nn(a, b):
    return lax.dot_general(a, b, (((1,), (0,)), ((), ())), preferred_element_type=F32)


def dot_nt(a, b):
    return lax.dot_general(a, b, (((1,), (1,)), ((), ())), preferred_element_type=F32)


def dot_tn(a, b):
    return lax.dot_general(a, b, (((0,), (0,)), ((), ())), preferred_element_type=F32)


def act_kernel(cols_in, cols_out, xy, w_in, w_out, placed, act, grad, total):
    rows, per_row, width, _ = w_in.shape
    total[...] = jnp.zeros_like(total)
    for r in range(rows):
        x_row = jnp.concatenate([xy[cols_in[r, k], 0] for k in range(per_row)], axis=1)
        hidden = dot_nn(x_row, w_in[r].reshape(per_row * width, width))
        y_row = jnp.concatenate([xy[cols_out[r, k], 1] for k in range(per_row)], axis=1)
        w_row = jnp.concatenate([w_out[r, k] for k in range(per_row)], axis=1)
        grad_act = dot_nt(y_row, w_row)
        square = hidden * hidden
        tanh = jnp.tanh(GELU_SCALE * hidden * (1.0 + GELU_CUBE * square))
        half = 0.5 * (1.0 + tanh)
        act[r] = (hidden * half).astype(BF16)
        slope = half + 0.5 * hidden * (1.0 - tanh * tanh) * (
            GELU_SCALE * (1.0 + 3.0 * GELU_CUBE * square)
        )
        grad_hidden = (grad_act * slope).astype(BF16)
        grad[r] = grad_hidden
        for k in range(per_row):
            c = cols_in[r, k]
            total[c] = total[c] + dot_nt(grad_hidden, w_in[r, k])
    placed[...] = total[...].astype(BF16)


def weight_kernel(cols_in, cols_out, xy, act, grad, parts):
    cores, xs, _, rows, each, width, _ = parts.shape
    per_row = cores * xs * each
    for r in range(rows):
        act_t = act[r].T
        grad_r = grad[r]
        for k in range(per_row):
            x_at, rest = divmod(k, cores * each)
            c_at, j = divmod(rest, each)
            parts[c_at, x_at, 0, r, j] = dot_tn(xy[cols_in[r, k], 0], grad_r).astype(BF16)
            parts[c_at, x_at, 1, r, j] = dot_nn(act_t, xy[cols_out[r, k], 1]).astype(BF16)


def per_device(sizes, inputs, upstream, w_in, cols_in, w_out, cols_out):
    nx, nc, ny, nz = sizes
    tok, width = inputs.shape
    rows, per_row = cols_in.shape
    each = per_row // (nx * nc)
    blocks = ny * nz
    smem = pl.BlockSpec(memory_space=pltpu.SMEM)
    vmem = pl.BlockSpec(memory_space=pltpu.VMEM)
    params = pltpu.CompilerParams(vmem_limit_bytes=48 * 1024 * 1024)

    xy = lax.all_gather(jnp.stack([inputs, upstream]), ("y", "z"), axis=0, tiled=False)
    placed, act, grad = pl.pallas_call(
        act_kernel,
        out_shape=(
            jax.ShapeDtypeStruct((blocks, tok, width), BF16),
            jax.ShapeDtypeStruct((rows, tok, width), BF16),
            jax.ShapeDtypeStruct((rows, tok, width), BF16),
        ),
        in_specs=[smem, smem, vmem, vmem, vmem],
        out_specs=(vmem, vmem, vmem),
        scratch_shapes=[pltpu.VMEM((blocks, tok, width), F32)],
        compiler_params=params,
        name="act",
    )(cols_in, cols_out, xy, w_in, w_out)

    over_y = lax.psum_scatter(
        placed.reshape(ny, nz * tok, width), "y", scatter_dimension=0, tiled=False
    )

    parts = pl.pallas_call(
        weight_kernel,
        out_shape=jax.ShapeDtypeStruct((nc, nx, 2, rows, each, width, width), BF16),
        in_specs=[smem, smem, vmem, vmem, vmem],
        out_specs=vmem,
        compiler_params=params,
        name="weights",
    )(cols_in, cols_out, xy, act, grad)
    swapped = lax.all_to_all(parts, "c", split_axis=0, concat_axis=0, tiled=True)
    paired = jnp.sum(swapped.astype(F32), axis=0).astype(BF16)
    spread = lax.all_to_all(paired, "x", split_axis=0, concat_axis=0, tiled=True)
    summed = jnp.sum(spread.astype(F32), axis=0).astype(BF16)

    over_y, summed = lax.optimization_barrier((over_y, summed))
    over_y = over_y.reshape(nz, tok, width)
    received = lax.all_to_all(over_y, "z", split_axis=0, concat_axis=0, tiled=True)
    grad_inputs = jnp.sum(received.astype(F32), axis=0).astype(BF16)
    return grad_inputs, summed[0], summed[1]


def solution(mesh):
    n_dp, n_blk = mesh.devices.shape
    sizes = (n_dp // 2, 2, 8, n_blk // 8)
    fine = Mesh(mesh.devices.reshape(sizes), ("x", "c", "y", "z"))
    dp, blk = ("x", "c"), ("y", "z")
    return jax.shard_map(
        functools.partial(per_device, sizes),
        mesh=fine,
        in_specs=(
            P(dp, blk),
            P(dp, blk),
            P(blk, None, None, None),
            P(blk, None),
            P(blk, None, None, None),
            P(blk, None),
        ),
        out_specs=(P(dp, blk), P(blk, dp, None, None), P(blk, dp, None, None)),
        check_vma=False,
    )
```

time: 444 us -> 197 us (0.44)
  the two profiles are of different devices: /device:TPU:40 before, /device:TPU:6 now
where the time goes in v1:
time: 197 us; the launch traced here: 195 us
  waiting for transfers between devices  111 us (56%)
  blocking collectives  37.4 us (19%)
  Pallas kernels  14.2 us (7%)
  between operations  14.1 us (7%)
  other arithmetic  7.64 us (4%)
  local copies, waits for them, and re-layouts  6.04 us (3%)
  starting transfers between devices  4.94 us (3%)
    all_gather x1, waiting for transfers between devices, per_device(): lax.all_gather(jnp.stack([inputs, upstream]), ('y', 'z'), axis=0, tiled=F...  98.3 us
    all_to_all x1, blocking collectives, per_device(): lax.all_to_all(paired, 'x', split_axis=0, concat_axis=0, tiled=True)  29.3 us
    all_to_all x1, waiting for transfers between devices, per_device(): lax.all_to_all(over_y, 'z', split_axis=0, concat_axis=0, tiled=True)  12.7 us
    pallas_call x1, Pallas kernels, per_device(): pl.pallas_call(act_kernel, out_shape=(jax.ShapeDtypeStruct((blocks, tok,...  8.97 us
    all_to_all x1, blocking collectives, per_device(): lax.all_to_all(parts, 'c', split_axis=0, concat_axis=0, tiled=True)  8.15 us
    pallas_call x1, Pallas kernels, per_device(): pl.pallas_call(weight_kernel, out_shape=jax.ShapeDtypeStruct((nc, nx, 2,...  5.25 us
    unnamed x12, local copies, waits for them, and re-layouts  5.21 us
    all_to_all x1, starting transfers between devices, per_device(): lax.all_to_all(over_y, 'z', split_axis=0, concat_axis=0, tiled=True)  4.86 us
  transfers between devices with their start and end apart: 3, of which 2 were waited for; matrix products, arithmetic and copies ran while one was open for 3% of the time, Pallas kernels for 3%

profile of v1, /device:TPU:6, one launch (start us, length us, event | category | flops | bytes accessed | tf_op | source)
XLA Modules:
  0.0 195.4 jit_solution(13496853282681351200)
XLA Ops:
  7.2 0.0 all-gather.3.cloned.1.call-start
  7.2 1.5 pad_maximum_fusion
  8.7 0.0 all-gather.3.cloned.1.call-update
  8.7 0.0 reduce-scatter.2.cloned.1.call-start
  8.8 98.3 %all-gather.3.cloned.1.call-done = bf16[128,192,128]{2,1,0:T(8,128)(2,1)} async-done(((bf16[2,192,128]{2,1,0:T(8,128)(2,1)}), bf16[128,192,128]{2,1,0:T(8,128)(2,1)}) %all-gather.3.cloned.1.call-update) | async-done | bytes 6291472 | tf_op jit(solution)/shard_map/all_gather | solution.py:75
  107.1 0.0 copy-start
  107.1 1.6 copy-done
  108.7 1.6 copy-done.1
  110.3 0.7 copy-done.2
  110.9 0.7 copy-done.4
  111.6 9.0 %act.1 = (bf16[64,192,128]{2,1,0:T(8,128)(2,1)}, bf16[4,192,128]{2,1,0:T(8,128)(2,1)S(1)}, bf16[4,192,128]{2,1,0:T(8,128)(2,1)S(1)}) custom-call(s32[4,16]{1,0:T(4,128)S(1)} %copy-done.2, s32[4,16]{1,0:T(4,128)S(1)} %copy-done.4, bf16[64,2,192,128]{3,2,1,0:T(8,128)(2,1)} %bitcast.10, bf16[4,16,128,128]{3,2,1,0:T(8,128)(2,1)S(1)} %copy-done, ...), custom_call_target="tpu_custom_call" | custom-call | tf_op jit(solution)/shard_map/act/pallas_call | solution.py:76
  120.6 0.0 reduce-scatter.2.cloned.1.call-update
  120.6 0.7 copy-done.3
  121.3 0.0 copy-done.5
  121.3 5.3 %weights.1 = bf16[2,4,2,4,2,128,128]{6,5,4,3,2,1,0:T(8,128)(2,1)S(1)} custom-call(s32[4,16]{1,0:T(4,128)S(1)} %copy-done.3, s32[4,16]{1,0:T(4,128)S(1)} %copy-done.5, bf16[64,2,192,128]{3,2,1,0:T(8,128)(2,1)} %bitcast.11, bf16[4,192,128]{2,1,0:T(8,128)(2,1)S(1)} %get-tuple-element.9.act, bf16[4,192,128]{2,1,0:T(8,128)(2,1)S(1)} %get-tuple-element.10.grad), custom_call_target="tpu_custom_call" | custom-call | tf_op jit(solution)/shard_map/weights/pallas_call | solution.py:94
  126.5 8.1 %all_to_all.15 = bf16[2,4,2,4,2,128,128]{6,5,4,3,2,1,0:T(8,128)(2,1)} all-to-all(bf16[2,4,2,4,2,128,128]{6,5,4,3,2,1,0:T(8,128)(2,1)S(1)} %weights.1), channel_id=1, replica_groups=mesh['x'=4,'c'=2,'y'=8,'z'=8] {'c'}, dimensions={0} | all-to-all | bytes 8388608 | tf_op jit(solution)/shard_map/all_to_all | solution.py:102
  134.7 3.5 %reduce_sum.36 = bf16[4,2,4,2,128,128]{5,4,3,2,1,0:T(8,128)(2,1)S(1)} reduce(bf16[2,4,2,4,2,128,128]{6,5,4,3,2,1,0:T(8,128)(2,1)} %all_to_all.15, bf16[]{:T(256)} %constant.4.clone.1), dimensions={0}, to_apply=%region_1.0 | reduce | flops 1048576 | bytes 6291458 | tf_op jit(solution)/shard_map/reduce_sum | solution.py:103
  138.2 29.3 %all_to_all.16 = bf16[4,2,4,2,128,128]{5,4,3,2,1,0:T(8,128)(2,1)} all-to-all(bf16[4,2,4,2,128,128]{5,4,3,2,1,0:T(8,128)(2,1)S(1)} %reduce_sum.36), channel_id=1, replica_groups=mesh['x'=4,'c'=2,'y'=8,'z'=8] {'x'}, dimensions={0} | all-to-all | bytes 4194304 | tf_op jit(solution)/shard_map/all_to_all | solution.py:104
  167.5 2.0 %reduce_sum.37 = bf16[2,4,2,128,128]{4,3,2,1,0:T(8,128)(2,1)S(1)} reduce(bf16[4,2,4,2,128,128]{5,4,3,2,1,0:T(8,128)(2,1)} %all_to_all.16, bf16[]{:T(256)} %constant.4.clone.1), dimensions={0}, to_apply=%region_2.0 | reduce | flops 786432 | bytes 2621442 | tf_op jit(solution)/shard_map/reduce_sum | solution.py:105
  169.5 0.0 reduce-scatter.2.cloned.1.call-done
  169.5 4.9 %all-to-all-start.2 = ((bf16[8,192,128]{2,1,0:T(8,128)(2,1)}), bf16[8,192,128]{2,1,0:T(8,128)(2,1)S(1)}, u32[]{:S(2)}, u32[]{:S(2)}) async-start(bf16[8,192,128]{2,1,0:T(8,128)(2,1)} %bitcast.13), calls=%async_computation.3 | async-start | bytes 786432 | tf_op jit(solution)/shard_map/all_to_all | solution.py:109
  174.4 0.8 slice_bitcast_fusion
  175.2 12.7 %all-to-all-done.2 = bf16[8,192,128]{2,1,0:T(8,128)(2,1)S(1)} async-done(((bf16[8,192,128]{2,1,0:T(8,128)(2,1)}), bf16[8,192,128]{2,1,0:T(8,128)(2,1)S(1)}, u32[]{:S(2)}, u32[]{:S(2)}) %all-to-all-start.2) | async-done | bytes 393248 | tf_op jit(solution)/shard_map/all_to_all | solution.py:109
  187.9 0.7 reduce_sum.38
  (5 shorter events, 0.0 us)
Async XLA Ops:
  7.2 99.9 %all-gather.3.cloned.1.call-start = ((), (), s32[]{:S(2)}) async-start(), calls=%async_computation.5 | async-start | bytes 6389760 | tf_op jit(solution)/shard_map/all_gather | solution.py:75
  8.7 160.8 %reduce-scatter.2.cloned.1.call-start = ((), (), s32[]{:S(2)}) async-start(), calls=%async_computation.4 | async-start | bytes 3538944 | tf_op jit(solution)/shard_map/reduce_scatter | solution.py:90
  107.1 1.6 copy-start
  108.7 1.6 copy-start.1
  110.2 0.7 copy-start.2
  110.9 0.7 copy-start.4
  120.6 0.7 copy-start.3
  120.6 0.7 copy-start.5
  169.5 18.4 %all-to-all-start.2 = ((bf16[8,192,128]{2,1,0:T(8,128)(2,1)}), bf16[8,192,128]{2,1,0:T(8,128)(2,1)S(1)}, u32[]{:S(2)}, u32[]{:S(2)}) async-start(bf16[8,192,128]{2,1,0:T(8,128)(2,1)} %bitcast.13), calls=%async_computation.3 | async-start | bytes 786432 | tf_op jit(solution)/shard_map/all_to_all | solution.py:109
Sparse Core Ops, SparseCore 0:
  11.6 95.3 all-gather.2
  120.7 45.7 reduce-scatter.1

commit v2 on v1

v2 whole, which is shorter than its diff:
```python
import functools

import jax
import jax.numpy as jnp
from jax import lax
from jax.experimental import pallas as pl
from jax.experimental.pallas import tpu as pltpu
from jax.sharding import Mesh, PartitionSpec as P

BF16 = jnp.bfloat16
F32 = jnp.float32
GELU_SCALE = 0.7978845608028654
GELU_CUBE = 0.044715
VMEM_LIMIT = 32 * 1024 * 1024
SLABS = 8


def dot_nn(a, b):
    return lax.dot_general(a, b, (((1,), (0,)), ((), ())), preferred_element_type=F32)


def dot_nt(a, b):
    return lax.dot_general(a, b, (((1,), (1,)), ((), ())), preferred_element_type=F32)


def dot_tn(a, b):
    return lax.dot_general(a, b, (((0,), (0,)), ((), ())), preferred_element_type=F32)


def start_loads(xy, x, y, sem):
    slab = xy.shape[0] // SLABS
    both = []
    for which, into in ((0, x), (1, y)):
        ats = [pl.ds(s * slab, slab) for s in range(SLABS)]
        both.append(
            [
                pltpu.make_async_copy(xy.at[at, which], into.at[at], sem.at[which * SLABS + s])
                for s, at in enumerate(ats)
            ]
        )
        for copy in both[-1]:
            copy.start()
    return both


def act_kernel(
    where, xy, w_in, w_out, placed, act, grad, x, y, wi, wo, total, rounded, slope, in_sem, w_sem, out_sem
):
    rows, per_row, width, _ = w_in.shape
    blocks = total.shape[0]
    load_in = pltpu.make_async_copy(w_in, wi, w_sem.at[0])
    load_out = pltpu.make_async_copy(w_out, wo, w_sem.at[1])
    load_in.start()
    load_x, load_y = start_loads(xy, x, y, in_sem)
    load_out.start()
    total[...] = jnp.zeros_like(total)
    load_in.wait()
    for copy in load_x:
        copy.wait()
    for r in range(rows):
        x_row = jnp.concatenate([x[where[0, r * per_row + k]] for k in range(per_row)], axis=1)
        hidden = dot_nn(x_row, wi[r].reshape(per_row * width, width))
        square = hidden * hidden
        tanh = jnp.tanh(GELU_SCALE * hidden * (1.0 + GELU_CUBE * square))
        half = 0.5 * (1.0 + tanh)
        act[r] = (hidden * half).astype(BF16)
        slope[r] = half + 0.5 * hidden * (1.0 - tanh * tanh) * (
            GELU_SCALE * (1.0 + 3.0 * GELU_CUBE * square)
        )
    for copy in load_y:
        copy.wait()
    load_out.wait()
    for r in range(rows):
        y_row = jnp.concatenate([y[where[1, r * per_row + k]] for k in range(per_row)], axis=1)
        w_row = jnp.concatenate([wo[r, k] for k in range(per_row)], axis=1)
        grad_hidden = (dot_nt(y_row, w_row) * slope[r]).astype(BF16)
        grad[r] = grad_hidden
        terms = dot_nt(grad_hidden, wi[r].reshape(per_row * width, width))
        for k in range(per_row):
            c = where[0, r * per_row + k]
            total[c] = total[c] + terms[:, k * width : (k + 1) * width]
    stores = []
    slab = blocks // SLABS
    for s in range(SLABS):
        at = pl.ds(s * slab, slab)
        rounded[at] = total[at].astype(BF16)
        stores.append(pltpu.make_async_copy(rounded.at[at], placed.at[at], out_sem.at[s]))
        stores[-1].start()
    for copy in stores:
        copy.wait()


def weight_kernel(where, xy, act, grad, own, other, x, y, in_sem):
    load_x, load_y = start_loads(xy, x, y, in_sem)
    for copy in load_x + load_y:
        copy.wait()
    xs, _, rows, each, width, _ = own.shape
    per_row = xs * 2 * each
    core = where[2, 0]
    for r in range(rows):
        act_t = act[r].T
        grad_r = grad[r]
        for x_at in range(xs):
            for half, out in ((core, own), (1 - core, other)):
                for j in range(each):
                    at = r * per_row + (x_at * 2 + half) * each + j
                    out[x_at, 0, r, j] = dot_tn(x[where[0, at]], grad_r).astype(BF16)
                    out[x_at, 1, r, j] = dot_nn(act_t, y[where[1, at]]).astype(BF16)


def per_device(sizes, inputs, upstream, w_in, cols_in, w_out, cols_out):
    nx, nc, ny, nz = sizes
    tok, width = inputs.shape
    rows, per_row = cols_in.shape
    each = per_row // (nx * nc)
    blocks = ny * nz
    smem = pl.BlockSpec(memory_space=pltpu.SMEM)
    vmem = pl.BlockSpec(memory_space=pltpu.VMEM)
    hbm = pl.BlockSpec(memory_space=pltpu.HBM)
    params = pltpu.CompilerParams(vmem_limit_bytes=VMEM_LIMIT)

    where = jnp.stack(
        [
            cols_in.reshape(-1),
            cols_out.reshape(-1),
            jnp.full((rows * per_row,), lax.axis_index("c"), jnp.int32),
        ]
    )
    xy = lax.all_gather(jnp.stack([inputs, upstream]), ("y", "z"), axis=0, tiled=False)
    xy, w_in, w_out = (pltpu.with_memory_space_constraint(v, pltpu.HBM) for v in (xy, w_in, w_out))
    placed, act, grad = pl.pallas_call(
        act_kernel,
        out_shape=(
            jax.ShapeDtypeStruct((blocks, tok, width), BF16),
            jax.ShapeDtypeStruct((rows, tok, width), BF16),
            jax.ShapeDtypeStruct((rows, tok, width), BF16),
        ),
        in_specs=[smem, hbm, hbm, hbm],
        out_specs=(hbm, vmem, vmem),
        scratch_shapes=[
            pltpu.VMEM((blocks, tok, width), BF16),
            pltpu.VMEM((blocks, tok, width), BF16),
            pltpu.VMEM(w_in.shape, BF16),
            pltpu.VMEM(w_out.shape, BF16),
            pltpu.VMEM((blocks, tok, width), F32),
            pltpu.VMEM((blocks, tok, width), BF16),
            pltpu.VMEM((rows, tok, width), F32),
            pltpu.SemaphoreType.DMA((2 * SLABS,)),
            pltpu.SemaphoreType.DMA((2,)),
            pltpu.SemaphoreType.DMA((SLABS,)),
        ],
        compiler_params=params,
        name="act",
    )(where, xy, w_in, w_out)

    over_y = lax.psum_scatter(
        placed.reshape(ny, nz * tok, width), "y", scatter_dimension=0, tiled=False
    )

    half = jax.ShapeDtypeStruct((nx, 2, rows, each, width, width), BF16)
    own, other = pl.pallas_call(
        weight_kernel,
        out_shape=(half, half),
        in_specs=[smem, hbm, vmem, vmem],
        out_specs=(vmem, vmem),
        scratch_shapes=[
            pltpu.VMEM((blocks, tok, width), BF16),
            pltpu.VMEM((blocks, tok, width), BF16),
            pltpu.SemaphoreType.DMA((2 * SLABS,)),
        ],
        compiler_params=params,
        name="weights",
    )(where, xy, act, grad)
    swapped = lax.ppermute(other, "c", [(0, 1), (1, 0)])
    paired = (own.astype(F32) + swapped.astype(F32)).astype(BF16)
    spread = lax.all_to_all(paired, "x", split_axis=0, concat_axis=0, tiled=True)

    over_y, spread = lax.optimization_barrier((over_y, spread))
    over_y = over_y.reshape(nz, tok, width)
    received = lax.all_to_all(over_y, "z", split_axis=0, concat_axis=0, tiled=True)
    summed = jnp.sum(spread.astype(F32), axis=0).astype(BF16)
    grad_inputs = jnp.sum(received.astype(F32), axis=0).astype(BF16)
    return grad_inputs, summed[0], summed[1]


def solution(mesh):
    n_dp, n_blk = mesh.devices.shape
    sizes = (n_dp // 2, 2, 8, n_blk // 8)
    fine = Mesh(mesh.devices.reshape(sizes), ("x", "c", "y", "z"))
    dp, blk = ("x", "c"), ("y", "z")
    return jax.shard_map(
        functools.partial(per_device, sizes),
        mesh=fine,
        in_specs=(
            P(dp, blk),
            P(dp, blk),
            P(blk, None, None, None),
            P(blk, None),
            P(blk, None, None, None),
            P(blk, None),
        ),
        out_specs=(P(dp, blk), P(blk, dp, None, None), P(blk, dp, None, None)),
        check_vma=False,
    )
```

time: 197 us -> 190 us (0.964)
  blocking collectives: 37.4 us -> 29.2 us
  starting transfers between devices: 4.94 us -> 9.35 us
  other arithmetic: 7.64 us -> 3.47 us
  waiting for transfers between devices: 111 us -> 115 us
  local copies, waits for them, and re-layouts: 6.04 us -> 2.43 us
    all_to_all x1 -> x0, blocking collectives: 8.15 us -> none  [per_device(): lax.all_to_all(parts, 'c', split_axis=0, concat_axis=0, tiled=True)]
    unnamed x12 -> x0, local copies, waits for them, and re-layouts: 5.21 us -> none
    ppermute x0 -> x1, waiting for transfers between devices: none -> 4.13 us  [per_device(): swapped = lax.ppermute(other, 'c', [(0, 1), (1, 0)])]
    reduce_scatter x1, waiting for transfers between devices: 0.02 us -> 3.95 us  [per_device(): lax.psum_scatter(placed.reshape(ny, nz * tok, width), 'y', scatter_dimens...]
    reduce_sum x1 -> x0, other arithmetic: 3.48 us -> none  [per_device(): paired = jnp.sum(swapped.astype(F32), axis=0).astype(BF16)]
    all_to_all x1, starting transfers between devices: 4.86 us -> 7.35 us  [per_device(): lax.all_to_all(over_y, 'z', split_axis=0, concat_axis=0, tiled=True)]
    all_to_all x1, waiting for transfers between devices: 12.7 us -> 10.7 us  [per_device(): lax.all_to_all(over_y, 'z', split_axis=0, concat_axis=0, tiled=True)]
  transfers between devices with their start and end apart: 3 -> 4, of which waited for: 2 -> 4; matrix products, arithmetic and copies ran while one was open for 3% -> 2% of each run, Pallas kernels for 3% -> 3%
where the time goes in v2:
time: 190 us; the launch traced here: 189 us
  waiting for transfers between devices  115 us (61%)
  blocking collectives  29.2 us (15%)
  Pallas kernels  15 us (8%)
  between operations  14.1 us (7%)
  starting transfers between devices  9.35 us (5%)
  other arithmetic  3.47 us (2%)
  local copies, waits for them, and re-layouts  2.43 us (1%)
    all_gather x1, waiting for transfers between devices, per_device(): lax.all_gather(jnp.stack([inputs, upstream]), ('y', 'z'), axis=0, tiled=F...  96.6 us
    all_to_all x1, blocking collectives, per_device(): lax.all_to_all(paired, 'x', split_axis=0, concat_axis=0, tiled=True)  29.2 us
    all_to_all x1, waiting for transfers between devices, per_device(): lax.all_to_all(over_y, 'z', split_axis=0, concat_axis=0, tiled=True)  10.7 us
    pallas_call x1, Pallas kernels, per_device(): pl.pallas_call(act_kernel, out_shape=(jax.ShapeDtypeStruct((blocks, tok,...  9.12 us
    all_to_all x1, starting transfers between devices, per_device(): lax.all_to_all(over_y, 'z', split_axis=0, concat_axis=0, tiled=True)  7.35 us
    pallas_call x1, Pallas kernels, per_device(): pl.pallas_call(weight_kernel, out_shape=(half, half), in_specs=[smem, hbm...  5.92 us
    ppermute x1, waiting for transfers between devices, per_device(): swapped = lax.ppermute(other, 'c', [(0, 1), (1, 0)])  4.13 us
    reduce_scatter x1, waiting for transfers between devices, per_device(): lax.psum_scatter(placed.reshape(ny, nz * tok, width), 'y', scatter_dimens...  3.95 us
  transfers between devices with their start and end apart: 4, of which 4 were waited for; matrix products, arithmetic and copies ran while one was open for 2% of the time, Pallas kernels for 3%

profile of v2, /device:TPU:6, one launch (start us, length us, event | category | flops | bytes accessed | tf_op | source)
XLA Modules:
  0.0 189.0 jit_solution(2986775736135361241)
XLA Ops:
  7.2 0.0 all-gather.3.cloned.1.call-start
  7.2 1.5 pad_maximum_fusion
  8.7 0.0 all-gather.3.cloned.1.call-update
  8.7 0.0 reduce-scatter.2.cloned.1.call-start
  8.8 0.8 stack_reshape.7
  9.5 0.8 stack_reshape.6
  10.3 0.1 pad.4.clone
  10.4 0.1 add_add_fusion.where
  10.4 96.6 %all-gather.3.cloned.1.call-done = bf16[128,192,128]{2,1,0:T(8,128)(2,1)} async-done(((bf16[2,192,128]{2,1,0:T(8,128)(2,1)}), bf16[128,192,128]{2,1,0:T(8,128)(2,1)}) %all-gather.3.cloned.1.call-update) | async-done | bytes 6291472 | tf_op jit(solution)/shard_map/all_gather | solution.py:129
  107.1 9.1 %act.1 = (bf16[64,192,128]{2,1,0:T(8,128)(2,1)}, bf16[4,192,128]{2,1,0:T(8,128)(2,1)S(1)}, bf16[4,192,128]{2,1,0:T(8,128)(2,1)S(1)}) custom-call(s32[3,64]{1,0:T(4,128)S(1)} %add_add_fusion.where, bf16[64,2,192,128]{3,2,1,0:T(8,128)(2,1)} %bitcast.11, bf16[4,16,128,128]{3,2,1,0:T(8,128)(2,1)} %w_in.1, bf16[4,16,128,128]{3,2,1,0:T(8,128)(2,1)} %w_out.1), custom_call_target="tpu_custom_call" | custom-call | tf_op jit(solution)/shard_map/act/pallas_call | solution.py:131
  116.2 0.0 reduce-scatter.2.cloned.1.call-update
  116.2 5.9 %weights.1 = (bf16[4,2,4,2,128,128]{5,4,3,2,1,0:T(8,128)(2,1)S(1)}, bf16[4,2,4,2,128,128]{5,4,3,2,1,0:T(8,128)(2,1)S(1)}) custom-call(s32[3,64]{1,0:T(4,128)S(1)} %add_add_fusion.where, bf16[64,2,192,128]{3,2,1,0:T(8,128)(2,1)} %bitcast.12, bf16[4,192,128]{2,1,0:T(8,128)(2,1)S(1)} %get-tuple-element.11.act, bf16[4,192,128]{2,1,0:T(8,128)(2,1)S(1)} %get-tuple-element.12.grad), custom_call_target="tpu_custom_call" | custom-call | tf_op jit(solution)/shard_map/weights/pallas_call | solution.py:161
  122.1 1.9 %collective-permute-start = (bf16[4,2,4,2,128,128]{5,4,3,2,1,0:T(8,128)(2,1)S(1)}, bf16[4,2,4,2,128,128]{5,4,3,2,1,0:T(8,128)(2,1)S(1)}, u32[]{:S(2)}, u32[]{:S(2)}) collective-permute-start(bf16[4,2,4,2,128,128]{5,4,3,2,1,0:T(8,128)(2,1)S(1)} %get-tuple-element.14), channel_id=1, source_target_pairs={{0,64},{64,0},{1,65},{65,1},{2,66},{66,2},{3,67},{67,3},{4,68},{68... | collective-permute-start | bytes 6291464 | tf_op jit(solution)/shard_map/ppermute | solution.py:174
  124.1 4.1 %collective-permute-done = bf16[4,2,4,2,128,128]{5,4,3,2,1,0:T(8,128)(2,1)S(1)} collective-permute-done((bf16[4,2,4,2,128,128]{5,4,3,2,1,0:T(8,128)(2,1)S(1)}, bf16[4,2,4,2,128,128]{5,4,3,2,1,0:T(8,128)(2,1)S(1)}, u32[]{:S(2)}, u32[]{:S(2)}) %collective-permute-start) | collective-permute-done | bytes 2097184 | tf_op jit(solution)/shard_map/ppermute | solution.py:174
  128.2 0.8 add_convert_fusion
  129.0 29.2 %all_to_all.10 = bf16[4,2,4,2,128,128]{5,4,3,2,1,0:T(8,128)(2,1)S(1)} all-to-all(bf16[4,2,4,2,128,128]{5,4,3,2,1,0:T(8,128)(2,1)S(1)} %add_convert_fusion), channel_id=1, replica_groups=mesh['x'=4,'c'=2,'y'=8,'z'=8] {'x'}, dimensions={0} | all-to-all | bytes 4194304 | tf_op jit(solution)/shard_map/all_to_all | solution.py:176
  158.2 4.0 %reduce-scatter.2.cloned.1.call-done = bf16[1,1536,128]{2,1,0:T(8,128)(2,1)} async-done(((bf16[8,1536,128]{2,1,0:T(8,128)(2,1)}), bf16[1,1536,128]{2,1,0:T(8,128)(2,1)}) %reduce-scatter.2.cloned.1.call-update) | async-done | bytes 393232 | tf_op jit(solution)/shard_map/reduce_scatter | solution.py:156
  162.1 7.3 %all-to-all-start.1 = ((bf16[8,192,128]{2,1,0:T(8,128)(2,1)}), bf16[8,192,128]{2,1,0:T(8,128)(2,1)S(1)}, u32[]{:S(2)}, u32[]{:S(2)}) async-start(bf16[8,192,128]{2,1,0:T(8,128)(2,1)} %bitcast.13), calls=%async_computation.2 | async-start | bytes 786432 | tf_op jit(solution)/shard_map/all_to_all | solution.py:180
  169.5 0.4 reduce_sum.25
  169.9 0.8 slice_bitcast_fusion
  170.7 10.7 %all-to-all-done.1 = bf16[8,192,128]{2,1,0:T(8,128)(2,1)S(1)} async-done(((bf16[8,192,128]{2,1,0:T(8,128)(2,1)}), bf16[8,192,128]{2,1,0:T(8,128)(2,1)S(1)}, u32[]{:S(2)}, u32[]{:S(2)}) %all-to-all-start.1) | async-done | bytes 393248 | tf_op jit(solution)/shard_map/all_to_all | solution.py:180
  181.4 0.7 reduce_sum.24
Async XLA Ops:
  7.2 99.9 %all-gather.3.cloned.1.call-start = ((), (), s32[]{:S(2)}) async-start(), calls=%async_computation.4 | async-start | bytes 6389760 | tf_op jit(solution)/shard_map/all_gather | solution.py:129
  8.7 153.4 %reduce-scatter.2.cloned.1.call-start = ((), (), s32[]{:S(2)}) async-start(), calls=%async_computation.3 | async-start | bytes 3538944 | tf_op jit(solution)/shard_map/reduce_scatter | solution.py:156
  122.1 6.1 %collective-permute-start = (bf16[4,2,4,2,128,128]{5,4,3,2,1,0:T(8,128)(2,1)S(1)}, bf16[4,2,4,2,128,128]{5,4,3,2,1,0:T(8,128)(2,1)S(1)}, u32[]{:S(2)}, u32[]{:S(2)}) collective-permute-start(bf16[4,2,4,2,128,128]{5,4,3,2,1,0:T(8,128)(2,1)S(1)} %get-tuple-element.14), channel_id=1, source_target_pairs={{0,64},{64,0},{1,65},{65,1},{2,66},{66,2},{3,67},{67,3},{4,68},{68... | collective-permute-start | bytes 6291464 | tf_op jit(solution)/shard_map/ppermute | solution.py:174
  162.1 19.3 %all-to-all-start.1 = ((bf16[8,192,128]{2,1,0:T(8,128)(2,1)}), bf16[8,192,128]{2,1,0:T(8,128)(2,1)S(1)}, u32[]{:S(2)}, u32[]{:S(2)}) async-start(bf16[8,192,128]{2,1,0:T(8,128)(2,1)} %bitcast.13), calls=%async_computation.2 | async-start | bytes 786432 | tf_op jit(solution)/shard_map/all_to_all | solution.py:180
Sparse Core Ops, SparseCore 0:
  11.6 95.3 all-gather.2
  116.3 45.7 reduce-scatter.1

commit v3 on v2

v3 whole, which is shorter than its diff:
```python
import functools

import jax
import jax.numpy as jnp
from jax import lax
from jax.experimental import pallas as pl
from jax.experimental.pallas import tpu as pltpu
from jax.sharding import Mesh, PartitionSpec as P

BF16 = jnp.bfloat16
F32 = jnp.float32
GELU_SCALE = 0.7978845608028654
GELU_CUBE = 0.044715
VMEM_LIMIT = 52 * 1024 * 1024
SLABS = 8
CYZ = ("c", "y", "z")


def dot_nn(a, b):
    return lax.dot_general(a, b, (((1,), (0,)), ((), ())), preferred_element_type=F32)


def dot_nt(a, b):
    return lax.dot_general(a, b, (((1,), (1,)), ((), ())), preferred_element_type=F32)


def dot_tn(a, b):
    return lax.dot_general(a, b, (((0,), (0,)), ((), ())), preferred_element_type=F32)


def start_loads(where, units, x, y, sem, side):
    places = x.shape[0] // side
    both = []
    for which, into in ((0, x), (1, y)):
        both.append([])
        for n, (ref, steps, first) in enumerate(units):
            place = lax.rem(where[2, 1] + (steps + places), places)
            at = pl.ds(place * side + first, ref.shape[0])
            both[-1].append(
                pltpu.make_async_copy(ref.at[:, which], into.at[at], sem.at[which * len(units) + n])
            )
            both[-1][-1].start()
    return both


def act_kernel(plan, where, *refs):
    side, steps = plan
    units = [(ref, *step) for ref, step in zip(refs, steps)]
    (
        w_in, w_out, placed, act, grad,
        x, y, wi, wo, total, rounded, slope, in_sem, w_sem, out_sem,
    ) = refs[len(steps) :]
    rows, per_row, width, _ = w_in.shape
    blocks = total.shape[0]
    load_in = pltpu.make_async_copy(w_in, wi, w_sem.at[0])
    load_out = pltpu.make_async_copy(w_out, wo, w_sem.at[1])
    load_in.start()
    load_x, load_y = start_loads(where, units, x, y, in_sem, side)
    load_out.start()
    total[...] = jnp.zeros_like(total)
    load_in.wait()
    for copy in load_x:
        copy.wait()
    for r in range(rows):
        x_row = jnp.concatenate([x[where[0, r * per_row + k]] for k in range(per_row)], axis=1)
        hidden = dot_nn(x_row, wi[r].reshape(per_row * width, width))
        square = hidden * hidden
        tanh = jnp.tanh(GELU_SCALE * hidden * (1.0 + GELU_CUBE * square))
        half = 0.5 * (1.0 + tanh)
        act[r] = (hidden * half).astype(BF16)
        slope[r] = half + 0.5 * hidden * (1.0 - tanh * tanh) * (
            GELU_SCALE * (1.0 + 3.0 * GELU_CUBE * square)
        )
    for copy in load_y:
        copy.wait()
    load_out.wait()
    for r in range(rows):
        y_row = jnp.concatenate([y[where[1, r * per_row + k]] for k in range(per_row)], axis=1)
        w_row = jnp.concatenate([wo[r, k] for k in range(per_row)], axis=1)
        grad_hidden = (dot_nt(y_row, w_row) * slope[r]).astype(BF16)
        grad[r] = grad_hidden
        terms = dot_nt(grad_hidden, wi[r].reshape(per_row * width, width))
        for k in range(per_row):
            c = where[0, r * per_row + k]
            total[c] = total[c] + terms[:, k * width : (k + 1) * width]
    stores = []
    slab = blocks // SLABS
    for s in range(SLABS):
        at = pl.ds(s * slab, slab)
        rounded[at] = total[at].astype(BF16)
        stores.append(pltpu.make_async_copy(rounded.at[at], placed.at[at], out_sem.at[s]))
        stores[-1].start()
    for copy in stores:
        copy.wait()


def weight_kernel(plan, where, *refs):
    side, steps = plan
    units = [(ref, *step) for ref, step in zip(refs, steps)]
    act, grad, own, other, x, y, in_sem = refs[len(steps) :]
    load_x, load_y = start_loads(where, units, x, y, in_sem, side)
    for copy in load_x + load_y:
        copy.wait()
    xs, _, rows, each, width, _ = own.shape
    per_row = xs * 2 * each
    core = where[2, 0]
    for r in range(rows):
        act_t = act[r].T
        grad_r = grad[r]
        for away in range(xs):
            x_at = lax.rem(where[2, 2] + away, xs)
            for half, out in ((core, own), (1 - core, other)):
                for j in range(each):
                    at = r * per_row + (x_at * 2 + half) * each + j
                    out[away, 0, r, j] = dot_tn(x[where[0, at]], grad_r).astype(BF16)
                    out[away, 1, r, j] = dot_nn(act_t, y[where[1, at]]).astype(BF16)


def lines_and_rings(ny, nz):
    along_z = [[y * nz + z for z in range(nz)] for y in range(ny)]
    along_y = [[y * nz + z for y in range(ny)] for z in range(nz)]
    second = [[[ny * nz + p for p in group] for group in groups] for groups in (along_z, along_y)]
    return along_z + second[1], along_y + second[0]


def per_device(sizes, inputs, upstream, w_in, cols_in, w_out, cols_out):
    nx, nc, ny, nz = sizes
    side = nz
    tok, width = inputs.shape
    rows, per_row = cols_in.shape
    each = per_row // (nx * nc)
    blocks = ny * nz
    lines, rings = lines_and_rings(ny, nz)
    smem = pl.BlockSpec(memory_space=pltpu.SMEM)
    vmem = pl.BlockSpec(memory_space=pltpu.VMEM)
    anywhere = pl.BlockSpec(memory_space=pl.ANY)
    params = pltpu.CompilerParams(vmem_limit_bytes=VMEM_LIMIT)

    def in_hbm(values):
        return pltpu.with_memory_space_constraint(values, pltpu.HBM)

    def swap(values, groups):
        return lax.all_to_all(
            values, CYZ, split_axis=0, concat_axis=0, tiled=True, axis_index_groups=groups
        )

    def turn(values, by):
        pairs = [(g[i], g[(i + by) % side]) for g in rings for i in range(side)]
        return lax.ppermute(values, CYZ, pairs)

    mine = jnp.stack([inputs, upstream])
    unit = swap(jnp.broadcast_to(mine, (side, *mine.shape)), lines)
    units, steps = [unit], [(0, 0)]
    ahead = back = unit
    for s in range(1, side // 2):
        ahead, back = turn(ahead, 1), turn(back, -1)
        units += [ahead, back]
        steps += [(-s, 0), (s, 0)]
    units += [turn(ahead[: side // 2], 1), turn(back[side // 2 :], -1)]
    steps += [(side // 2, 0), (side // 2, side // 2)]
    units = [in_hbm(u) for u in units]
    plan = (side, tuple(steps))

    core, y_at, z_at = (lax.axis_index(a) for a in CYZ)
    cols = jnp.stack([cols_in.reshape(-1), cols_out.reshape(-1)])
    cols = jnp.where(core == 0, cols, cols % nz * ny + cols // nz)
    place = jnp.where(core == 0, y_at, z_at)
    here = jnp.stack([core, place, lax.axis_index("x")]).astype(jnp.int32)
    here = jnp.pad(here, (0, rows * per_row - 3)).reshape(1, -1)
    where = jnp.concatenate([cols, here])

    gathered = [pltpu.VMEM((blocks, tok, width), BF16)] * 2
    placed, act, grad = pl.pallas_call(
        functools.partial(act_kernel, plan),
        out_shape=(
            jax.ShapeDtypeStruct((blocks, tok, width), BF16),
            jax.ShapeDtypeStruct((rows, tok, width), BF16),
            jax.ShapeDtypeStruct((rows, tok, width), BF16),
        ),
        in_specs=[smem] + [anywhere] * (len(units) + 2),
        out_specs=(anywhere, vmem, vmem),
        scratch_shapes=gathered
        + [
            pltpu.VMEM(w_in.shape, BF16),
            pltpu.VMEM(w_out.shape, BF16),
            pltpu.VMEM((blocks, tok, width), F32),
            pltpu.VMEM((blocks, tok, width), BF16),
            pltpu.VMEM((rows, tok, width), F32),
            pltpu.SemaphoreType.DMA((2 * len(units),)),
            pltpu.SemaphoreType.DMA((2,)),
            pltpu.SemaphoreType.DMA((SLABS,)),
        ],
        compiler_params=params,
        name="act",
    )(where, *units, in_hbm(w_in), in_hbm(w_out))

    on_ring = swap(placed.reshape(side, blocks // side, tok, width), rings)

    half = jax.ShapeDtypeStruct((nx, 2, rows, each, width, width), BF16)
    own, other = pl.pallas_call(
        functools.partial(weight_kernel, plan),
        out_shape=(half, half),
        in_specs=[smem] + [anywhere] * len(units) + [vmem, vmem],
        out_specs=(vmem, vmem),
        scratch_shapes=gathered + [pltpu.SemaphoreType.DMA((2 * len(units),))],
        compiler_params=params,
        name="weights",
    )(where, *units, act, grad)
    swapped = lax.ppermute(other, "c", [(0, 1), (1, 0)])
    paired = [(own[d].astype(F32) + swapped[d].astype(F32)).astype(BF16) for d in range(nx)]
    spread = [
        lax.ppermute(paired[d], "x", [(i, (i + d) % nx) for i in range(nx)]) for d in range(1, nx)
    ]
    summed = sum((v.astype(F32) for v in spread), paired[0].astype(F32)).astype(BF16)

    on_line = jnp.sum(on_ring.astype(F32), axis=0).astype(BF16)
    received = swap(on_line, lines)
    grad_inputs = jnp.sum(received.astype(F32), axis=0).astype(BF16)
    return grad_inputs, summed[0], summed[1]


def solution(mesh):
    n_dp, n_blk = mesh.devices.shape
    sizes = (n_dp // 2, 2, 8, n_blk // 8)
    fine = Mesh(mesh.devices.reshape(sizes), ("x", "c", "y", "z"))
    dp, blk = ("x", "c"), ("y", "z")
    return jax.shard_map(
        functools.partial(per_device, sizes),
        mesh=fine,
        in_specs=(
            P(dp, blk),
            P(dp, blk),
            P(blk, None, None, None),
            P(blk, None),
            P(blk, None, None, None),
            P(blk, None),
        ),
        out_specs=(P(dp, blk), P(blk, dp, None, None), P(blk, dp, None, None)),
        check_vma=False,
    )
```

time: 190 us -> 164 us (0.86)
  waiting for transfers between devices: 115 us -> 56.5 us
  starting transfers between devices: 9.35 us -> 51.4 us
  between operations: 14.1 us -> 0.89 us
  other arithmetic: 3.47 us -> 8.7 us
  blocking collectives: 29.2 us -> 26.2 us
  Pallas kernels: 15 us -> 17.2 us
    all_gather x1 -> x0, waiting for transfers between devices: 96.6 us -> none  [per_device(): lax.all_gather(jnp.stack([inputs, upstream]), ('y', 'z'), axis=0, tiled=F...]
    ppermute x0 -> x11, starting transfers between devices: none -> 38.2 us  [the longest x8 28.4 us: turn(): return lax.ppermute(values, CYZ, pairs)]
    ppermute x0 -> x11, waiting for transfers between devices: none -> 31.9 us  [the longest x8 29.3 us: turn(): return lax.ppermute(values, CYZ, pairs)]
    all_to_all x1 -> x2, waiting for transfers between devices: 10.7 us -> 20.2 us  [swap(): lax.all_to_all(values, CYZ, split_axis=0, concat_axis=0, tiled=True, axis...]
    convert_element_type x1 -> x2, other arithmetic: 0.82 us -> 5.71 us  [the longest x1 3.61 us: per_device(): (own[d].astype(F32) + swapped[d].astype(F32)).astype(BF16)]
    all_to_all x1 -> x2, starting transfers between devices: 7.35 us -> 11.3 us  [swap(): lax.all_to_all(values, CYZ, split_axis=0, concat_axis=0, tiled=True, axis...]
    reduce_scatter x1 -> x0, waiting for transfers between devices: 3.95 us -> none  [per_device(): lax.psum_scatter(placed.reshape(ny, nz * tok, width), 'y', scatter_dimens...]
    all_to_all x1, blocking collectives: 29.2 us -> 26.2 us  [swap(): lax.all_to_all(values, CYZ, split_axis=0, concat_axis=0, tiled=True, axis...]
  transfers between devices with their start and end apart: 4 -> 14, of which waited for: 4 -> 10; matrix products, arithmetic and copies ran while one was open for 2% -> 5% of each run, Pallas kernels for 3% -> 5%
where the time goes in v3:
time: 164 us; the launch traced here: 163 us
  waiting for transfers between devices  56.5 us (34%)
  starting transfers between devices  51.4 us (31%)
  blocking collectives  26.2 us (16%)
  Pallas kernels  17.2 us (10%)
  other arithmetic  8.7 us (5%)
  local copies, waits for them, and re-layouts  1.98 us (1%)
    ppermute x8, waiting for transfers between devices, turn(): return lax.ppermute(values, CYZ, pairs)  29.3 us
    ppermute x8, starting transfers between devices, turn(): return lax.ppermute(values, CYZ, pairs)  28.4 us
    all_to_all x1, blocking collectives, swap(): lax.all_to_all(values, CYZ, split_axis=0, concat_axis=0, tiled=True, axis...  26.2 us
    all_to_all x2, waiting for transfers between devices, swap(): lax.all_to_all(values, CYZ, split_axis=0, concat_axis=0, tiled=True, axis...  20.2 us
    all_to_all x2, starting transfers between devices, swap(): lax.all_to_all(values, CYZ, split_axis=0, concat_axis=0, tiled=True, axis...  11.3 us
    ppermute x3, starting transfers between devices, per_device(): lax.ppermute(paired[d], 'x', [(i, (i + d) % nx) for i in range(nx)])  9.76 us
    pallas_call x1, Pallas kernels, per_device(): pl.pallas_call(functools.partial(act_kernel, plan), out_shape=(jax.ShapeD...  9.32 us
    pallas_call x1, Pallas kernels, per_device(): pl.pallas_call(functools.partial(weight_kernel, plan), out_shape=(half, h...  7.85 us
  transfers between devices with their start and end apart: 14, of which 10 were waited for; matrix products, arithmetic and copies ran while one was open for 5% of the time, Pallas kernels for 5%

profile of v3, /device:TPU:6, one launch (start us, length us, event | category | flops | bytes accessed | tf_op | source)
XLA Modules:
  0.0 162.9 jit_solution(2363073875634434213)
XLA Ops:
  1.7 26.2 %all_to_all.15.refs_0_ = bf16[8,2,192,128]{3,2,1,0:T(8,128)(2,1)S(1)} all-to-all(bf16[8,2,192,128]{3,2,1,0:T(8,128)(2,1)S(1)} %broadcast_in_dim.3), channel_id=1, replica_groups={{0,1,2,3,4,5,6,7},{8,9,10,11,12,13,14,15},{16,17,18,19,20,21,22,23},{24..., dimensions={0} | all-to-all | bytes 1572864 | tf_op jit(solution)/shard_map/all_to_all | solution.py:143
  27.9 3.5 %collective-permute-start = (bf16[8,2,192,128]{3,2,1,0:T(8,128)(2,1)S(1)}, bf16[8,2,192,128]{3,2,1,0:T(8,128)(2,1)S(1)}, u32[]{:S(2)}, u32[]{:S(2)}) collective-permute-start(bf16[8,2,192,128]{3,2,1,0:T(8,128)(2,1)S(1)} %all_to_all.15.refs_0_), channel_id=1, source_target_pairs={{0,8},{8,16},{16,24},{24,32},{32,40},{40,48},{48,56},{56,0},{1,9},... | collective-permute-start | bytes 2359304 | tf_op jit(solution)/shard_map/ppermute | solution.py:149
  31.3 3.8 %collective-permute-start.1 = (bf16[8,2,192,128]{3,2,1,0:T(8,128)(2,1)S(1)}, bf16[8,2,192,128]{3,2,1,0:T(8,128)(2,1)S(1)}, u32[]{:S(2)}, u32[]{:S(2)}) collective-permute-start(bf16[8,2,192,128]{3,2,1,0:T(8,128)(2,1)S(1)} %all_to_all.15.refs_0_), channel_id=1, source_target_pairs={{0,56},{8,0},{16,8},{24,16},{32,24},{40,32},{48,40},{56,48},{1,57}... | collective-permute-start | bytes 2359304 | tf_op jit(solution)/shard_map/ppermute | solution.py:149
  35.2 8.0 %collective-permute-done.refs_1_ = bf16[8,2,192,128]{3,2,1,0:T(8,128)(2,1)S(1)} collective-permute-done((bf16[8,2,192,128]{3,2,1,0:T(8,128)(2,1)S(1)}, bf16[8,2,192,128]{3,2,1,0:T(8,128)(2,1)S(1)}, u32[]{:S(2)}, u32[]{:S(2)}) %collective-permute-start) | collective-permute-done | bytes 786464 | tf_op jit(solution)/shard_map/ppermute | solution.py:149
  43.2 2.0 %collective-permute-start.2 = (bf16[8,2,192,128]{3,2,1,0:T(8,128)(2,1)S(1)}, bf16[8,2,192,128]{3,2,1,0:T(8,128)(2,1)}, u32[]{:S(2)}, u32[]{:S(2)}) collective-permute-start(bf16[8,2,192,128]{3,2,1,0:T(8,128)(2,1)S(1)} %collective-permute-done.refs_1_), channel_id=1, source_target_pairs={{0,8},{8,16},{16,24},{24,32},{32,40},{40,48},{48,56},{56,0},{1,9},... | collective-permute-start | bytes 2359304 | tf_op jit(solution)/shard_map/ppermute | solution.py:149
  45.2 5.0 %collective-permute-start.3 = (bf16[8,2,192,128]{3,2,1,0:T(8,128)(2,1)S(1)}, bf16[8,2,192,128]{3,2,1,0:T(8,128)(2,1)}, u32[]{:S(2)}, u32[]{:S(2)}) collective-permute-start(bf16[8,2,192,128]{3,2,1,0:T(8,128)(2,1)S(1)} %collective-permute-done.1.refs_2_), channel_id=1, source_target_pairs={{0,56},{8,0},{16,8},{24,16},{32,24},{40,32},{48,40},{56,48},{1,57}... | collective-permute-start | bytes 2359304 | tf_op jit(solution)/shard_map/ppermute | solution.py:149
  50.3 8.1 %collective-permute-done.2.refs_3_ = bf16[8,2,192,128]{3,2,1,0:T(8,128)(2,1)} collective-permute-done((bf16[8,2,192,128]{3,2,1,0:T(8,128)(2,1)S(1)}, bf16[8,2,192,128]{3,2,1,0:T(8,128)(2,1)}, u32[]{:S(2)}, u32[]{:S(2)}) %collective-permute-start.2) | collective-permute-done | bytes 786464 | tf_op jit(solution)/shard_map/ppermute | solution.py:149
  60.3 5.1 %collective-permute-start.5 = (bf16[8,2,192,128]{3,2,1,0:T(8,128)(2,1)}, bf16[8,2,192,128]{3,2,1,0:T(8,128)(2,1)S(1)}, u32[]{:S(2)}, u32[]{:S(2)}) collective-permute-start(bf16[8,2,192,128]{3,2,1,0:T(8,128)(2,1)} %collective-permute-done.3.refs_4_), channel_id=1, source_target_pairs={{0,56},{8,0},{16,8},{24,16},{32,24},{40,32},{48,40},{56,48},{1,57}... | collective-permute-start | bytes 2359304 | tf_op jit(solution)/shard_map/ppermute | solution.py:149
  65.7 8.0 %collective-permute-done.4.refs_5_ = bf16[8,2,192,128]{3,2,1,0:T(8,128)(2,1)S(1)} collective-permute-done((bf16[8,2,192,128]{3,2,1,0:T(8,128)(2,1)}, bf16[8,2,192,128]{3,2,1,0:T(8,128)(2,1)S(1)}, u32[]{:S(2)}, u32[]{:S(2)}) %collective-permute-start.4) | collective-permute-done | bytes 786464 | tf_op jit(solution)/shard_map/ppermute | solution.py:149
  75.7 5.1 %collective-permute-start.7 = (bf16[4,2,192,128]{3,2,1,0:T(8,128)(2,1)S(1)}, bf16[4,2,192,128]{3,2,1,0:T(8,128)(2,1)S(1)}, u32[]{:S(2)}, u32[]{:S(2)}) collective-permute-start(bf16[4,2,192,128]{3,2,1,0:T(8,128)(2,1)S(1)} %slice.49), channel_id=1, source_target_pairs={{0,56},{8,0},{16,8},{24,16},{32,24},{40,32},{48,40},{56,48},{1,57}... | collective-permute-start | bytes 1179656 | tf_op jit(solution)/shard_map/ppermute | solution.py:149
  81.0 3.6 %collective-permute-done.6.refs_7_ = bf16[4,2,192,128]{3,2,1,0:T(8,128)(2,1)S(1)} collective-permute-done((bf16[4,2,192,128]{3,2,1,0:T(8,128)(2,1)S(1)}, bf16[4,2,192,128]{3,2,1,0:T(8,128)(2,1)S(1)}, u32[]{:S(2)}, u32[]{:S(2)}) %collective-permute-start.6) | collective-permute-done | bytes 393248 | tf_op jit(solution)/shard_map/ppermute | solution.py:149
  86.9 9.3 %act.1 = (bf16[64,192,128]{2,1,0:T(8,128)(2,1)}, bf16[4,192,128]{2,1,0:T(8,128)(2,1)S(1)}, bf16[4,192,128]{2,1,0:T(8,128)(2,1)S(1)}) custom-call(s32[3,64]{1,0:T(4,128)S(1)} %pad_add_fusion.where, bf16[8,2,192,128]{3,2,1,0:T(8,128)(2,1)} %copy-done, bf16[8,2,192,128]{3,2,1,0:T(8,128)(2,1)} %copy-done.3, bf16[8,2,192,128]{3,2,1,0:T(8,128)(2,1)} %copy-done.4, ...), custom_call_target="tpu_custom_call" | custom-call | tf_op jit(solution)/shard_map/act/pallas_call | solution.py:173
  96.2 7.9 %all-to-all-start.1 = ((bf16[8,8,192,128]{3,2,1,0:T(8,128)(2,1)}), bf16[8,8,192,128]{3,2,1,0:T(8,128)(2,1)S(1)}, u32[]{:S(2)}, u32[]{:S(2)}) async-start(bf16[8,8,192,128]{3,2,1,0:T(8,128)(2,1)} %bitcast.23), calls=%async_computation.1 | async-start | bytes 6291456 | tf_op jit(solution)/shard_map/all_to_all | solution.py:143
  104.1 7.9 %weights.1 = (bf16[4,2,4,2,128,128]{5,4,3,2,1,0:T(8,128)(2,1)}, bf16[4,2,4,2,128,128]{5,4,3,2,1,0:T(8,128)(2,1)}) custom-call(s32[3,64]{1,0:T(4,128)S(1)} %pad_add_fusion.where, bf16[8,2,192,128]{3,2,1,0:T(8,128)(2,1)} %copy-done, bf16[8,2,192,128]{3,2,1,0:T(8,128)(2,1)} %copy-done.3, bf16[8,2,192,128]{3,2,1,0:T(8,128)(2,1)} %copy-done.4, ...), custom_call_target="tpu_custom_call" | custom-call | tf_op jit(solution)/shard_map/weights/pallas_call | solution.py:200
  113.9 4.3 %collective-permute-done.8 = bf16[4,2,4,2,128,128]{5,4,3,2,1,0:T(8,128)(2,1)S(1)} collective-permute-done((bf16[4,2,4,2,128,128]{5,4,3,2,1,0:T(8,128)(2,1)}, bf16[4,2,4,2,128,128]{5,4,3,2,1,0:T(8,128)(2,1)S(1)}, u32[]{:S(2)}, u32[]{:S(2)}) %collective-permute-start.8) | collective-permute-done | bytes 2097184 | tf_op jit(solution)/shard_map/ppermute | solution.py:209
  118.2 3.6 %fusion.4 = (bf16[2,4,2,128,128]{4,3,2,1,0:T(8,128)(2,1)}, bf16[2,4,2,128,128]{4,3,2,1,0:T(8,128)(2,1)}, bf16[2,4,2,128,128]{4,3,2,1,0:T(8,128)(2,1)}) fusion(bf16[4,2,4,2,128,128]{5,4,3,2,1,0:T(8,128)(2,1)S(1)} %collective-permute-done.8, bf16[4,2,4,2,128,128]{5,4,3,2,1,0:T(8,128)(2,1)} %get-tuple-element.11), kind=kLoop, calls=%fused_computation.9 | loop fusion | flops 3145728 | bytes 4718592 | tf_op jit(solution)/shard_map/convert_element_type | solution.py:210
  121.8 2.7 %collective-permute-start.11 = (bf16[2,4,2,128,128]{4,3,2,1,0:T(8,128)(2,1)}, bf16[2,4,2,128,128]{4,3,2,1,0:T(8,128)(2,1)}, u32[]{:S(2)}, u32[]{:S(2)}) collective-permute-start(bf16[2,4,2,128,128]{4,3,2,1,0:T(8,128)(2,1)} %get-tuple-element.14), channel_id=1, source_target_pairs={{0,384},{128,0},{256,128},{384,256},{1,385},{129,1},{257,129},{385... | collective-permute-start | bytes 1572872 | tf_op jit(solution)/shard_map/ppermute | solution.py:212
  124.6 3.0 %collective-permute-start.10 = (bf16[2,4,2,128,128]{4,3,2,1,0:T(8,128)(2,1)}, bf16[2,4,2,128,128]{4,3,2,1,0:T(8,128)(2,1)}, u32[]{:S(2)}, u32[]{:S(2)}) collective-permute-start(bf16[2,4,2,128,128]{4,3,2,1,0:T(8,128)(2,1)} %get-tuple-element.15), channel_id=1, source_target_pairs={{0,256},{128,384},{256,0},{384,128},{1,257},{129,385},{257,1},{385... | collective-permute-start | bytes 1572872 | tf_op jit(solution)/shard_map/ppermute | solution.py:212
  127.6 4.0 %collective-permute-start.9 = (bf16[2,4,2,128,128]{4,3,2,1,0:T(8,128)(2,1)}, bf16[2,4,2,128,128]{4,3,2,1,0:T(8,128)(2,1)}, u32[]{:S(2)}, u32[]{:S(2)}) collective-permute-start(bf16[2,4,2,128,128]{4,3,2,1,0:T(8,128)(2,1)} %get-tuple-element.13), channel_id=1, source_target_pairs={{0,128},{128,256},{256,384},{384,0},{1,129},{129,257},{257,385},{3... | collective-permute-start | bytes 1572872 | tf_op jit(solution)/shard_map/ppermute | solution.py:212
  131.6 13.9 %all-to-all-done.1 = bf16[8,8,192,128]{3,2,1,0:T(8,128)(2,1)S(1)} async-done(((bf16[8,8,192,128]{3,2,1,0:T(8,128)(2,1)}), bf16[8,8,192,128]{3,2,1,0:T(8,128)(2,1)S(1)}, u32[]{:S(2)}, u32[]{:S(2)}) %all-to-all-start.1) | async-done | bytes 3145760 | tf_op jit(solution)/shard_map/all_to_all | solution.py:143
  146.9 3.5 %all-to-all-start.2 = ((bf16[8,192,128]{2,1,0:T(8,128)(2,1)}), bf16[8,192,128]{2,1,0:T(8,128)(2,1)S(1)}, u32[]{:S(2)}, u32[]{:S(2)}) async-start(bf16[8,192,128]{2,1,0:T(8,128)(2,1)} %reduce_sum.24), calls=%async_computation.2 | async-start | bytes 786432 | tf_op jit(solution)/shard_map/all_to_all | solution.py:143
  150.5 2.5 %collective-permute-done.9 = bf16[2,4,2,128,128]{4,3,2,1,0:T(8,128)(2,1)} collective-permute-done((bf16[2,4,2,128,128]{4,3,2,1,0:T(8,128)(2,1)}, bf16[2,4,2,128,128]{4,3,2,1,0:T(8,128)(2,1)}, u32[]{:S(2)}, u32[]{:S(2)}) %collective-permute-start.9) | collective-permute-done | bytes 524320 | tf_op jit(solution)/shard_map/ppermute | solution.py:212
  153.0 2.1 %fusion.2 = bf16[2,4,2,128,128]{4,3,2,1,0:T(8,128)(2,1)S(1)} fusion(bf16[2,4,2,128,128]{4,3,2,1,0:T(8,128)(2,1)} %collective-permute-done.11, bf16[2,4,2,128,128]{4,3,2,1,0:T(8,128)(2,1)} %collective-permute-done.10, bf16[2,4,2,128,128]{4,3,2,1,0:T(8,128)(2,1)} %collective-permute-done.9, bf16[4,2,4,2,128,128]{5,4,3,2,1,0:T(8,128)(2,1)} %copy-done.5, ...), kind=kLoop, calls=%fused_computation.3 | loop fusion | flops 3145728 | bytes 3145728 | tf_op jit(solution)/shard_map/convert_element_type | solution.py:214
  155.9 6.3 %all-to-all-done.2 = bf16[8,192,128]{2,1,0:T(8,128)(2,1)S(1)} async-done(((bf16[8,192,128]{2,1,0:T(8,128)(2,1)}), bf16[8,192,128]{2,1,0:T(8,128)(2,1)S(1)}, u32[]{:S(2)}, u32[]{:S(2)}) %all-to-all-start.2) | async-done | bytes 393248 | tf_op jit(solution)/shard_map/all_to_all | solution.py:143
  (42 shorter events, 12.3 us)
Async XLA Ops:
  0.6 64.8 %copy-start.8 = (s32[4,16]{1,0:T(4,128)S(1)}, s32[4,16]{1,0:T(4,128)}, u32[]{:S(2)}) copy-start(s32[4,16]{1,0:T(4,128)} %param.11) | copy-start | bytes 772
  0.6 64.9 %copy-start.9 = (s32[4,16]{1,0:T(4,128)S(1)}, s32[4,16]{1,0:T(4,128)}, u32[]{:S(2)}) copy-start(s32[4,16]{1,0:T(4,128)} %param.9) | copy-start | bytes 772
  27.9 58.2 %copy-start = (bf16[8,2,192,128]{3,2,1,0:T(8,128)(2,1)}, bf16[8,2,192,128]{3,2,1,0:T(8,128)(2,1)S(1)}, u32[]{:S(2)}) copy-start(bf16[8,2,192,128]{3,2,1,0:T(8,128)(2,1)S(1)} %all_to_all.15.refs_0_) | copy-start | bytes 2359300
  27.9 15.3 %collective-permute-start = (bf16[8,2,192,128]{3,2,1,0:T(8,128)(2,1)S(1)}, bf16[8,2,192,128]{3,2,1,0:T(8,128)(2,1)S(1)}, u32[]{:S(2)}, u32[]{:S(2)}) collective-permute-start(bf16[8,2,192,128]{3,2,1,0:T(8,128)(2,1)S(1)} %all_to_all.15.refs_0_), channel_id=1, source_target_pairs={{0,8},{8,16},{16,24},{24,32},{32,40},{40,48},{48,56},{56,0},{1,9},... | collective-permute-start | bytes 2359304 | tf_op jit(solution)/shard_map/ppermute | solution.py:149
  31.3 13.9 %collective-permute-start.1 = (bf16[8,2,192,128]{3,2,1,0:T(8,128)(2,1)S(1)}, bf16[8,2,192,128]{3,2,1,0:T(8,128)(2,1)S(1)}, u32[]{:S(2)}, u32[]{:S(2)}) collective-permute-start(bf16[8,2,192,128]{3,2,1,0:T(8,128)(2,1)S(1)} %all_to_all.15.refs_0_), channel_id=1, source_target_pairs={{0,56},{8,0},{16,8},{24,16},{32,24},{40,32},{48,40},{56,48},{1,57}... | collective-permute-start | bytes 2359304 | tf_op jit(solution)/shard_map/ppermute | solution.py:149
  43.2 42.9 %copy-start.3 = (bf16[8,2,192,128]{3,2,1,0:T(8,128)(2,1)}, bf16[8,2,192,128]{3,2,1,0:T(8,128)(2,1)S(1)}, u32[]{:S(2)}) copy-start(bf16[8,2,192,128]{3,2,1,0:T(8,128)(2,1)S(1)} %collective-permute-done.refs_1_) | copy-start | bytes 2359300
  43.2 15.2 %collective-permute-start.2 = (bf16[8,2,192,128]{3,2,1,0:T(8,128)(2,1)S(1)}, bf16[8,2,192,128]{3,2,1,0:T(8,128)(2,1)}, u32[]{:S(2)}, u32[]{:S(2)}) collective-permute-start(bf16[8,2,192,128]{3,2,1,0:T(8,128)(2,1)S(1)} %collective-permute-done.refs_1_), channel_id=1, source_target_pairs={{0,8},{8,16},{16,24},{24,32},{32,40},{40,48},{48,56},{56,0},{1,9},... | collective-permute-start | bytes 2359304 | tf_op jit(solution)/shard_map/ppermute | solution.py:149
  45.2 15.1 %copy-start.4 = (bf16[8,2,192,128]{3,2,1,0:T(8,128)(2,1)}, bf16[8,2,192,128]{3,2,1,0:T(8,128)(2,1)S(1)}, u32[]{:S(2)}) copy-start(bf16[8,2,192,128]{3,2,1,0:T(8,128)(2,1)S(1)} %collective-permute-done.1.refs_2_) | copy-start | bytes 2359300
  45.2 15.1 %collective-permute-start.3 = (bf16[8,2,192,128]{3,2,1,0:T(8,128)(2,1)S(1)}, bf16[8,2,192,128]{3,2,1,0:T(8,128)(2,1)}, u32[]{:S(2)}, u32[]{:S(2)}) collective-permute-start(bf16[8,2,192,128]{3,2,1,0:T(8,128)(2,1)S(1)} %collective-permute-done.1.refs_2_), channel_id=1, source_target_pairs={{0,56},{8,0},{16,8},{24,16},{32,24},{40,32},{48,40},{56,48},{1,57}... | collective-permute-start | bytes 2359304 | tf_op jit(solution)/shard_map/ppermute | solution.py:149
  58.4 15.3 %collective-permute-start.4 = (bf16[8,2,192,128]{3,2,1,0:T(8,128)(2,1)}, bf16[8,2,192,128]{3,2,1,0:T(8,128)(2,1)S(1)}, u32[]{:S(2)}, u32[]{:S(2)}) collective-permute-start(bf16[8,2,192,128]{3,2,1,0:T(8,128)(2,1)} %collective-permute-done.2.refs_3_), channel_id=1, source_target_pairs={{0,8},{8,16},{16,24},{24,32},{32,40},{40,48},{48,56},{56,0},{1,9},... | collective-permute-start | bytes 2359304 | tf_op jit(solution)/shard_map/ppermute | solution.py:149
  60.3 15.3 %collective-permute-start.5 = (bf16[8,2,192,128]{3,2,1,0:T(8,128)(2,1)}, bf16[8,2,192,128]{3,2,1,0:T(8,128)(2,1)S(1)}, u32[]{:S(2)}, u32[]{:S(2)}) collective-permute-start(bf16[8,2,192,128]{3,2,1,0:T(8,128)(2,1)} %collective-permute-done.3.refs_4_), channel_id=1, source_target_pairs={{0,56},{8,0},{16,8},{24,16},{32,24},{40,32},{48,40},{56,48},{1,57}... | collective-permute-start | bytes 2359304 | tf_op jit(solution)/shard_map/ppermute | solution.py:149
  73.7 12.4 %copy-start.1 = (bf16[8,2,192,128]{3,2,1,0:T(8,128)(2,1)}, bf16[8,2,192,128]{3,2,1,0:T(8,128)(2,1)S(1)}, u32[]{:S(2)}) copy-start(bf16[8,2,192,128]{3,2,1,0:T(8,128)(2,1)S(1)} %collective-permute-done.4.refs_5_) | copy-start | bytes 2359300
  73.7 10.9 %collective-permute-start.6 = (bf16[4,2,192,128]{3,2,1,0:T(8,128)(2,1)S(1)}, bf16[4,2,192,128]{3,2,1,0:T(8,128)(2,1)S(1)}, u32[]{:S(2)}, u32[]{:S(2)}) collective-permute-start(bf16[4,2,192,128]{3,2,1,0:T(8,128)(2,1)S(1)} %slice.48), channel_id=1, source_target_pairs={{0,8},{8,16},{16,24},{24,32},{32,40},{40,48},{48,56},{56,0},{1,9},... | collective-permute-start | bytes 1179656 | tf_op jit(solution)/shard_map/ppermute | solution.py:149
  75.7 10.5 %copy-start.2 = (bf16[8,2,192,128]{3,2,1,0:T(8,128)(2,1)}, bf16[8,2,192,128]{3,2,1,0:T(8,128)(2,1)S(1)}, u32[]{:S(2)}) copy-start(bf16[8,2,192,128]{3,2,1,0:T(8,128)(2,1)S(1)} %collective-permute-done.5.refs_6_) | copy-start | bytes 2359300
  75.7 10.4 %collective-permute-start.7 = (bf16[4,2,192,128]{3,2,1,0:T(8,128)(2,1)S(1)}, bf16[4,2,192,128]{3,2,1,0:T(8,128)(2,1)S(1)}, u32[]{:S(2)}, u32[]{:S(2)}) collective-permute-start(bf16[4,2,192,128]{3,2,1,0:T(8,128)(2,1)S(1)} %slice.49), channel_id=1, source_target_pairs={{0,56},{8,0},{16,8},{24,16},{32,24},{40,32},{48,40},{56,48},{1,57}... | collective-permute-start | bytes 1179656 | tf_op jit(solution)/shard_map/ppermute | solution.py:149
  84.6 1.5 copy-start.6
  86.1 0.7 copy-start.7
  96.2 49.4 %all-to-all-start.1 = ((bf16[8,8,192,128]{3,2,1,0:T(8,128)(2,1)}), bf16[8,8,192,128]{3,2,1,0:T(8,128)(2,1)S(1)}, u32[]{:S(2)}, u32[]{:S(2)}) async-start(bf16[8,8,192,128]{3,2,1,0:T(8,128)(2,1)} %bitcast.23), calls=%async_computation.1 | async-start | bytes 6291456 | tf_op jit(solution)/shard_map/all_to_all | solution.py:143
  112.0 6.3 %collective-permute-start.8 = (bf16[4,2,4,2,128,128]{5,4,3,2,1,0:T(8,128)(2,1)}, bf16[4,2,4,2,128,128]{5,4,3,2,1,0:T(8,128)(2,1)S(1)}, u32[]{:S(2)}, u32[]{:S(2)}) collective-permute-start(bf16[4,2,4,2,128,128]{5,4,3,2,1,0:T(8,128)(2,1)} %get-tuple-element.12), channel_id=1, source_target_pairs={{0,64},{64,0},{1,65},{65,1},{2,66},{66,2},{3,67},{67,3},{4,68},{68... | collective-permute-start | bytes 6291464 | tf_op jit(solution)/shard_map/ppermute | solution.py:209
  118.2 3.6 %copy-start.5 = (bf16[4,2,4,2,128,128]{5,4,3,2,1,0:T(8,128)(2,1)}, bf16[4,2,4,2,128,128]{5,4,3,2,1,0:T(8,128)(2,1)S(1)}, u32[]{:S(2)}) copy-start(bf16[4,2,4,2,128,128]{5,4,3,2,1,0:T(8,128)(2,1)S(1)} %collective-permute-done.8) | copy-start | bytes 6291460
  121.8 28.6 %collective-permute-start.11 = (bf16[2,4,2,128,128]{4,3,2,1,0:T(8,128)(2,1)}, bf16[2,4,2,128,128]{4,3,2,1,0:T(8,128)(2,1)}, u32[]{:S(2)}, u32[]{:S(2)}) collective-permute-start(bf16[2,4,2,128,128]{4,3,2,1,0:T(8,128)(2,1)} %get-tuple-element.14), channel_id=1, source_target_pairs={{0,384},{128,0},{256,128},{384,256},{1,385},{129,1},{257,129},{385... | collective-permute-start | bytes 1572872 | tf_op jit(solution)/shard_map/ppermute | solution.py:212
  124.6 25.9 %collective-permute-start.10 = (bf16[2,4,2,128,128]{4,3,2,1,0:T(8,128)(2,1)}, bf16[2,4,2,128,128]{4,3,2,1,0:T(8,128)(2,1)}, u32[]{:S(2)}, u32[]{:S(2)}) collective-permute-start(bf16[2,4,2,128,128]{4,3,2,1,0:T(8,128)(2,1)} %get-tuple-element.15), channel_id=1, source_target_pairs={{0,256},{128,384},{256,0},{384,128},{1,257},{129,385},{257,1},{385... | collective-permute-start | bytes 1572872 | tf_op jit(solution)/shard_map/ppermute | solution.py:212
  127.6 25.4 %collective-permute-start.9 = (bf16[2,4,2,128,128]{4,3,2,1,0:T(8,128)(2,1)}, bf16[2,4,2,128,128]{4,3,2,1,0:T(8,128)(2,1)}, u32[]{:S(2)}, u32[]{:S(2)}) collective-permute-start(bf16[2,4,2,128,128]{4,3,2,1,0:T(8,128)(2,1)} %get-tuple-element.13), channel_id=1, source_target_pairs={{0,128},{128,256},{256,384},{384,0},{1,129},{129,257},{257,385},{3... | collective-permute-start | bytes 1572872 | tf_op jit(solution)/shard_map/ppermute | solution.py:212
  146.9 15.3 %all-to-all-start.2 = ((bf16[8,192,128]{2,1,0:T(8,128)(2,1)}), bf16[8,192,128]{2,1,0:T(8,128)(2,1)S(1)}, u32[]{:S(2)}, u32[]{:S(2)}) async-start(bf16[8,192,128]{2,1,0:T(8,128)(2,1)} %reduce_sum.24), calls=%async_computation.2 | async-start | bytes 786432 | tf_op jit(solution)/shard_map/all_to_all | solution.py:143

commit v4 on v3

--- a/solution.py
+++ b/solution.py
@@ -11,7 +11,7 @@
 F32 = jnp.float32
 GELU_SCALE = 0.7978845608028654
 GELU_CUBE = 0.044715
-VMEM_LIMIT = 52 * 1024 * 1024
+VMEM_LIMIT = 36 * 1024 * 1024
 SLABS = 8
 CYZ = ("c", "y", "z")
 
@@ -28,38 +28,28 @@
     return lax.dot_general(a, b, (((0,), (0,)), ((), ())), preferred_element_type=F32)
 
 
-def start_loads(where, units, x, y, sem, side):
-    places = x.shape[0] // side
-    both = []
-    for which, into in ((0, x), (1, y)):
-        both.append([])
-        for n, (ref, steps, first) in enumerate(units):
-            place = lax.rem(where[2, 1] + (steps + places), places)
-            at = pl.ds(place * side + first, ref.shape[0])
-            both[-1].append(
-                pltpu.make_async_copy(ref.at[:, which], into.at[at], sem.at[which * len(units) + n])
-            )
-            both[-1][-1].start()
-    return both
-
-
-def act_kernel(plan, where, *refs):
+def start_loads(where, units, into, sem, side):
+    places = into.shape[0] // side
+    loads = []
+    for n, (ref, steps) in enumerate(units):
+        place = lax.rem(where[2, 1] + (steps + places), places)
+        loads.append(pltpu.make_async_copy(ref, into.at[pl.ds(place * side, side)], sem.at[n]))
+        loads[-1].start()
+    return loads
+
+
+def hidden_kernel(plan, where, *refs):
     side, steps = plan
-    units = [(ref, *step) for ref, step in zip(refs, steps)]
-    (
-        w_in, w_out, placed, act, grad,
-        x, y, wi, wo, total, rounded, slope, in_sem, w_sem, out_sem,
-    ) = refs[len(steps) :]
+    units = list(zip(refs, steps))
+    w_in, w_out, act, slope, wi, wo, x, sem, w_sem = refs[len(steps) :]
     rows, per_row, width, _ = w_in.shape
-    blocks = total.shape[0]
     load_in = pltpu.make_async_copy(w_in, wi, w_sem.at[0])
     load_out = pltpu.make_async_copy(w_out, wo, w_sem.at[1])
     load_in.start()
-    load_x, load_y = start_loads(where, units, x, y, in_sem, side)
+    loads = start_loads(where, units, x, sem, side)
     load_out.start()
-    total[...] = jnp.zeros_like(total)
     load_in.wait()
-    for copy in load_x:
+    for copy in loads:
         copy.wait()
     for r in range(rows):
         x_row = jnp.concatenate([x[where[0, r * per_row + k]] for k in range(per_row)], axis=1)
@@ -71,9 +61,19 @@
         slope[r] = half + 0.5 * hidden * (1.0 - tanh * tanh) * (
             GELU_SCALE * (1.0 + 3.0 * GELU_CUBE * square)
         )
-    for copy in load_y:
-        copy.wait()
     load_out.wait()
+
+
+def back_kernel(plan, where, *refs):
+    side, steps = plan
+    units = list(zip(refs, steps))
+    slope, wi, wo, placed, grad, y, total, rounded, sem, out_sem = refs[len(steps) :]
+    rows, per_row, width, _ = wi.shape
+    blocks = total.shape[0]
+    loads = start_loads(where, units, y, sem, side)
+    total[...] = jnp.zeros_like(total)
+    for copy in loads:
+        copy.wait()
     for r in range(rows):
         y_row = jnp.concatenate([y[where[1, r * per_row + k]] for k in range(per_row)], axis=1)
         w_row = jnp.concatenate([wo[r, k] for k in range(per_row)], axis=1)
@@ -94,12 +94,13 @@
         copy.wait()
 
 
-def weight_kernel(plan, where, *refs):
-    side, steps = plan
-    units = [(ref, *step) for ref, step in zip(refs, steps)]
-    act, grad, own, other, x, y, in_sem = refs[len(steps) :]
-    load_x, load_y = start_loads(where, units, x, y, in_sem, side)
-    for copy in load_x + load_y:
+def weight_kernel(plans, where, *refs):
+    (side, x_steps), (_, y_steps) = plans
+    n_x, n_y = len(x_steps), len(y_steps)
+    act, grad, own, other, x, y, x_sem, y_sem = refs[n_x + n_y :]
+    loads = start_loads(where, list(zip(refs[:n_x], x_steps)), x, x_sem, side)
+    loads += start_loads(where, list(zip(refs[n_x : n_x + n_y], y_steps)), y, y_sem, side)
+    for copy in loads:
         copy.wait()
     xs, _, rows, each, width, _ = own.shape
     per_row = xs * 2 * each
@@ -150,16 +151,23 @@
 
     mine = jnp.stack([inputs, upstream])
     unit = swap(jnp.broadcast_to(mine, (side, *mine.shape)), lines)
-    units, steps = [unit], [(0, 0)]
-    ahead = back = unit
+    x_units, y_units = [unit[:, 0]], [unit[:, 1]]
+    x_steps, y_steps = [0], [0]
+    x_ahead = x_back = x_units[0]
+    y_ahead = y_back = y_units[0]
     for s in range(1, side // 2):
-        ahead, back = turn(ahead, 1), turn(back, -1)
-        units += [ahead, back]
-        steps += [(-s, 0), (s, 0)]
-    units += [turn(ahead[: side // 2], 1), turn(back[side // 2 :], -1)]
-    steps += [(side // 2, 0), (side // 2, side // 2)]
-    units = [in_hbm(u) for u in units]
-    plan = (side, tuple(steps))
+        x_ahead, x_back = turn(x_ahead, 1), turn(x_back, -1)
+        y_back, y_ahead = turn(y_back, -1), turn(y_ahead, 1)
+        x_units += [x_ahead, x_back]
+        y_units += [y_ahead, y_back]
+        x_steps += [-s, s]
+        y_steps += [-s, s]
+    x_units.append(turn(x_ahead, 1))
+    y_units.append(turn(y_back, -1))
+    x_steps.append(-(side // 2))
+    y_steps.append(side // 2)
+    x_units, y_units = [in_hbm(u) for u in x_units], [in_hbm(u) for u in y_units]
+    x_plan, y_plan = (side, tuple(x_steps)), (side, tuple(y_steps))
 
     core, y_at, z_at = (lax.axis_index(a) for a in CYZ)
     cols = jnp.stack([cols_in.reshape(-1), cols_out.reshape(-1)])
@@ -169,43 +177,50 @@
     here = jnp.pad(here, (0, rows * per_row - 3)).reshape(1, -1)
     where = jnp.concatenate([cols, here])
 
-    gathered = [pltpu.VMEM((blocks, tok, width), BF16)] * 2
-    placed, act, grad = pl.pallas_call(
-        functools.partial(act_kernel, plan),
+    gathered = pltpu.VMEM((blocks, tok, width), BF16)
+    loaded = pltpu.SemaphoreType.DMA((side,))
+    values = jax.ShapeDtypeStruct((rows, tok, width), BF16)
+    act, slope, wi, wo = pl.pallas_call(
+        functools.partial(hidden_kernel, x_plan),
         out_shape=(
-            jax.ShapeDtypeStruct((blocks, tok, width), BF16),
-            jax.ShapeDtypeStruct((rows, tok, width), BF16),
-            jax.ShapeDtypeStruct((rows, tok, width), BF16),
-        ),
-        in_specs=[smem] + [anywhere] * (len(units) + 2),
-        out_specs=(anywhere, vmem, vmem),
-        scratch_shapes=gathered
-        + [
+            values,
+            jax.ShapeDtypeStruct((rows, tok, width), F32),
             pltpu.VMEM(w_in.shape, BF16),
             pltpu.VMEM(w_out.shape, BF16),
+        ),
+        in_specs=[smem] + [anywhere] * (len(x_units) + 2),
+        scratch_shapes=[gathered, loaded, pltpu.SemaphoreType.DMA((2,))],
+        compiler_params=params,
+        name="hidden",
+    )(where, *x_units, in_hbm(w_in), in_hbm(w_out))
+    placed, grad = pl.pallas_call(
+        functools.partial(back_kernel, y_plan),
+        out_shape=(jax.ShapeDtypeStruct((blocks, tok, width), BF16), values),
+        in_specs=[smem] + [anywhere] * len(y_units) + [vmem] * 3,
+        out_specs=(anywhere, vmem),
+        scratch_shapes=[
+            gathered,
             pltpu.VMEM((blocks, tok, width), F32),
             pltpu.VMEM((blocks, tok, width), BF16),
-            pltpu.VMEM((rows, tok, width), F32),
-            pltpu.SemaphoreType.DMA((2 * len(units),)),
-            pltpu.SemaphoreType.DMA((2,)),
+            loaded,
             pltpu.SemaphoreType.DMA((SLABS,)),
         ],
         compiler_params=params,
-        name="act",
-    )(where, *units, in_hbm(w_in), in_hbm(w_out))
+        name="back",
+    )(where, *y_units, slope, wi, wo)
 
     on_ring = swap(placed.reshape(side, blocks // side, tok, width), rings)
 
     half = jax.ShapeDtypeStruct((nx, 2, rows, each, width, width), BF16)
     own, other = pl.pallas_call(
-        functools.partial(weight_kernel, plan),
+        functools.partial(weight_kernel, (x_plan, y_plan)),
         out_shape=(half, half),
-        in_specs=[smem] + [anywhere] * len(units) + [vmem, vmem],
+        in_specs=[smem] + [anywhere] * (len(x_units) + len(y_units)) + [vmem, vmem],
         out_specs=(vmem, vmem),
-        scratch_shapes=gathered + [pltpu.SemaphoreType.DMA((2 * len(units),))],
+        scratch_shapes=[gathered, gathered, loaded, loaded],
         compiler_params=params,
         name="weights",
-    )(where, *units, act, grad)
+    )(where, *x_units, *y_units, act, grad)
     swapped = lax.ppermute(other, "c", [(0, 1), (1, 0)])
     paired = [(own[d].astype(F32) + swapped[d].astype(F32)).astype(BF16) for d in range(nx)]
     spread = [

time: 164 us -> 160 us (0.976)
  waiting for transfers between devices: 56.5 us -> 37.8 us
  starting transfers between devices: 51.4 us -> 65.5 us
    ppermute x8 -> x14, waiting for transfers between devices: 29.3 us -> 5.98 us  [turn(): return lax.ppermute(values, CYZ, pairs)]
    ppermute x8 -> x14, starting transfers between devices: 28.4 us -> 46 us  [turn(): return lax.ppermute(values, CYZ, pairs)]
    all_to_all x2, waiting for transfers between devices: 20.2 us -> 27.7 us  [swap(): lax.all_to_all(values, CYZ, split_axis=0, concat_axis=0, tiled=True, axis...]
    all_to_all x2, starting transfers between devices: 11.3 us -> 8.48 us  [swap(): lax.all_to_all(values, CYZ, split_axis=0, concat_axis=0, tiled=True, axis...]
    ppermute x3, waiting for transfers between devices: 2.6 us -> 0.01 us  [per_device(): lax.ppermute(paired[d], 'x', [(i, (i + d) % nx) for i in range(nx)])]
    convert_element_type x1, other arithmetic: 3.61 us -> 1.66 us  [per_device(): (own[d].astype(F32) + swapped[d].astype(F32)).astype(BF16)]
    reduce_sum x1, other arithmetic: 1.36 us -> 3.29 us  [per_device(): on_line = jnp.sum(on_ring.astype(F32), axis=0).astype(BF16)]
    pallas_call x2 -> x3, Pallas kernels: 17.2 us -> 17.2 us  [the longest x1 6.55 us: per_device(): pl.pallas_call(functools.partial(back_kernel, y_plan), out_shape=(jax.Sha...]
  transfers between devices with their start and end apart: 14 -> 20, of which waited for: 10 -> 5; matrix products, arithmetic and copies ran while one was open for 5% -> 5% of each run, Pallas kernels for 5% -> 7%
where the time goes in v4:
time: 160 us; the launch traced here: 159 us
  starting transfers between devices  65.5 us (41%)
  waiting for transfers between devices  37.8 us (24%)
  blocking collectives  26.2 us (16%)
  Pallas kernels  17.2 us (11%)
  other arithmetic  8.52 us (5%)
  local copies, waits for them, and re-layouts  2.93 us (2%)
    ppermute x14, starting transfers between devices, turn(): return lax.ppermute(values, CYZ, pairs)  46 us
    all_to_all x2, waiting for transfers between devices, swap(): lax.all_to_all(values, CYZ, split_axis=0, concat_axis=0, tiled=True, axis...  27.7 us
    all_to_all x1, blocking collectives, swap(): lax.all_to_all(values, CYZ, split_axis=0, concat_axis=0, tiled=True, axis...  26.2 us
    ppermute x3, starting transfers between devices, per_device(): lax.ppermute(paired[d], 'x', [(i, (i + d) % nx) for i in range(nx)])  9.15 us
    all_to_all x2, starting transfers between devices, swap(): lax.all_to_all(values, CYZ, split_axis=0, concat_axis=0, tiled=True, axis...  8.48 us
    pallas_call x1, Pallas kernels, per_device(): pl.pallas_call(functools.partial(back_kernel, y_plan), out_shape=(jax.Sha...  6.55 us
    ppermute x14, waiting for transfers between devices, turn(): return lax.ppermute(values, CYZ, pairs)  5.98 us
    pallas_call x1, Pallas kernels, per_device(): pl.pallas_call(functools.partial(weight_kernel, (x_plan, y_plan)), out_sh...  5.92 us
  transfers between devices with their start and end apart: 20, of which 5 were waited for; matrix products, arithmetic and copies ran while one was open for 5% of the time, Pallas kernels for 7%

profile of v4, /device:TPU:6, one launch (start us, length us, event | category | flops | bytes accessed | tf_op | source)
XLA Modules:
  0.0 159.4 jit_solution(13862760658723827345)
XLA Ops:
  1.7 26.2 %all_to_all.15 = bf16[8,2,192,128]{3,2,1,0:T(8,128)(2,1)S(1)} all-to-all(bf16[8,2,192,128]{3,2,1,0:T(8,128)(2,1)S(1)} %broadcast_in_dim.3), channel_id=1, replica_groups={{0,1,2,3,4,5,6,7},{8,9,10,11,12,13,14,15},{16,17,18,19,20,21,22,23},{24..., dimensions={0} | all-to-all | bytes 1572864 | tf_op jit(solution)/shard_map/all_to_all | solution.py:144
  27.9 3.5 %collective-permute-start.7 = (bf16[8,192,128]{2,1,0:T(8,128)(2,1)S(1)}, bf16[8,192,128]{2,1,0:T(8,128)(2,1)S(1)}, u32[]{:S(2)}, u32[]{:S(2)}) collective-permute-start(bf16[8,192,128]{2,1,0:T(8,128)(2,1)S(1)} %get-tuple-element.22.refs_0_), channel_id=1, source_target_pairs={{0,8},{8,16},{16,24},{24,32},{32,40},{40,48},{48,56},{56,0},{1,9},... | collective-permute-start | bytes 1179656 | tf_op jit(solution)/shard_map/ppermute | solution.py:150
  31.4 3.8 %collective-permute-start.1 = (bf16[8,192,128]{2,1,0:T(8,128)(2,1)S(1)}, bf16[8,192,128]{2,1,0:T(8,128)(2,1)S(1)}, u32[]{:S(2)}, u32[]{:S(2)}) collective-permute-start(bf16[8,192,128]{2,1,0:T(8,128)(2,1)S(1)} %get-tuple-element.23.refs_0_.refs_8_), channel_id=1, source_target_pairs={{0,56},{8,0},{16,8},{24,16},{32,24},{40,32},{48,40},{56,48},{1,57}... | collective-permute-start | bytes 1179656 | tf_op jit(solution)/shard_map/ppermute | solution.py:150
  35.3 3.9 %collective-permute-start.8 = (bf16[8,192,128]{2,1,0:T(8,128)(2,1)S(1)}, bf16[8,192,128]{2,1,0:T(8,128)(2,1)S(1)}, u32[]{:S(2)}, u32[]{:S(2)}) collective-permute-start(bf16[8,192,128]{2,1,0:T(8,128)(2,1)S(1)} %get-tuple-element.22.refs_0_), channel_id=1, source_target_pairs={{0,56},{8,0},{16,8},{24,16},{32,24},{40,32},{48,40},{56,48},{1,57}... | collective-permute-start | bytes 1179656 | tf_op jit(solution)/shard_map/ppermute | solution.py:150
  41.1 2.0 %collective-permute-start.9 = (bf16[8,192,128]{2,1,0:T(8,128)(2,1)S(1)}, bf16[8,192,128]{2,1,0:T(8,128)(2,1)}, u32[]{:S(2)}, u32[]{:S(2)}) collective-permute-start(bf16[8,192,128]{2,1,0:T(8,128)(2,1)S(1)} %collective-permute-done.7.refs_1_), channel_id=1, source_target_pairs={{0,8},{8,16},{16,24},{24,32},{32,40},{40,48},{48,56},{56,0},{1,9},... | collective-permute-start | bytes 1179656 | tf_op jit(solution)/shard_map/ppermute | solution.py:150
  43.2 5.0 %collective-permute-start.3 = (bf16[8,192,128]{2,1,0:T(8,128)(2,1)S(1)}, bf16[8,192,128]{2,1,0:T(8,128)(2,1)S(1)}, u32[]{:S(2)}, u32[]{:S(2)}) collective-permute-start(bf16[8,192,128]{2,1,0:T(8,128)(2,1)S(1)} %collective-permute-done.1.refs_2_.refs_10_), channel_id=1, source_target_pairs={{0,56},{8,0},{16,8},{24,16},{32,24},{40,32},{48,40},{56,48},{1,57}... | collective-permute-start | bytes 1179656 | tf_op jit(solution)/shard_map/ppermute | solution.py:150
  48.2 3.9 %collective-permute-start.10 = (bf16[8,192,128]{2,1,0:T(8,128)(2,1)S(1)}, bf16[8,192,128]{2,1,0:T(8,128)(2,1)}, u32[]{:S(2)}, u32[]{:S(2)}) collective-permute-start(bf16[8,192,128]{2,1,0:T(8,128)(2,1)S(1)} %collective-permute-done.8.refs_2_), channel_id=1, source_target_pairs={{0,56},{8,0},{16,8},{24,16},{32,24},{40,32},{48,40},{56,48},{1,57}... | collective-permute-start | bytes 1179656 | tf_op jit(solution)/shard_map/ppermute | solution.py:150
  56.3 5.1 %collective-permute-start.5 = (bf16[8,192,128]{2,1,0:T(8,128)(2,1)S(1)}, bf16[8,192,128]{2,1,0:T(8,128)(2,1)S(1)}, u32[]{:S(2)}, u32[]{:S(2)}) collective-permute-start(bf16[8,192,128]{2,1,0:T(8,128)(2,1)S(1)} %collective-permute-done.3.refs_4_.refs_12_), channel_id=1, source_target_pairs={{0,56},{8,0},{16,8},{24,16},{32,24},{40,32},{48,40},{56,48},{1,57}... | collective-permute-start | bytes 1179656 | tf_op jit(solution)/shard_map/ppermute | solution.py:150
  61.7 3.7 %collective-permute-start.12 = (bf16[8,192,128]{2,1,0:T(8,128)(2,1)}, bf16[8,192,128]{2,1,0:T(8,128)(2,1)S(1)}, u32[]{:S(2)}, u32[]{:S(2)}) collective-permute-start(bf16[8,192,128]{2,1,0:T(8,128)(2,1)} %collective-permute-done.10.refs_4_), channel_id=1, source_target_pairs={{0,56},{8,0},{16,8},{24,16},{32,24},{40,32},{48,40},{56,48},{1,57}... | collective-permute-start | bytes 1179656 | tf_op jit(solution)/shard_map/ppermute | solution.py:150
  65.4 2.2 %collective-permute-start.4 = (bf16[8,192,128]{2,1,0:T(8,128)(2,1)S(1)}, bf16[8,192,128]{2,1,0:T(8,128)(2,1)S(1)}, u32[]{:S(2)}, u32[]{:S(2)}) collective-permute-start(bf16[8,192,128]{2,1,0:T(8,128)(2,1)S(1)} %collective-permute-done.2.refs_3_.refs_11_), channel_id=1, source_target_pairs={{0,8},{8,16},{16,24},{24,32},{32,40},{40,48},{48,56},{56,0},{1,9},... | collective-permute-start | bytes 1179656 | tf_op jit(solution)/shard_map/ppermute | solution.py:150
  69.5 5.1 %collective-permute-start.6 = (bf16[8,192,128]{2,1,0:T(8,128)(2,1)S(1)}, bf16[8,192,128]{2,1,0:T(8,128)(2,1)S(1)}, u32[]{:S(2)}, u32[]{:S(2)}) collective-permute-start(bf16[8,192,128]{2,1,0:T(8,128)(2,1)S(1)} %collective-permute-done.5.refs_6_.refs_14_), channel_id=1, source_target_pairs={{0,56},{8,0},{16,8},{24,16},{32,24},{40,32},{48,40},{56,48},{1,57}... | collective-permute-start | bytes 1179656 | tf_op jit(solution)/shard_map/ppermute | solution.py:150
  74.8 5.7 %collective-permute-done.13.refs_7_ = bf16[8,192,128]{2,1,0:T(8,128)(2,1)S(1)} collective-permute-done((bf16[8,192,128]{2,1,0:T(8,128)(2,1)}, bf16[8,192,128]{2,1,0:T(8,128)(2,1)S(1)}, u32[]{:S(2)}, u32[]{:S(2)}) %collective-permute-start.13) | collective-permute-done | bytes 393248 | tf_op jit(solution)/shard_map/ppermute | solution.py:150
  81.3 4.7 %hidden.1 = (bf16[4,192,128]{2,1,0:T(8,128)(2,1)S(1)}, f32[4,192,128]{2,1,0:T(8,128)S(1)}, bf16[4,16,128,128]{3,2,1,0:T(8,128)(2,1)S(1)}, bf16[4,16,128,128]{3,2,1,0:T(8,128)(2,1)S(1)}) custom-call(s32[3,64]{1,0:T(4,128)S(1)} %pad_add_fusion.where, bf16[8,192,128]{2,1,0:T(8,128)(2,1)} %copy-done.1, bf16[8,192,128]{2,1,0:T(8,128)(2,1)} %copy-done.10, ...), custom_call_target="tpu_custom_call" | custom-call | tf_op jit(solution)/shard_map/hidden/pallas_call | solution.py:183
  87.0 6.5 %back.1 = (bf16[64,192,128]{2,1,0:T(8,128)(2,1)}, bf16[4,192,128]{2,1,0:T(8,128)(2,1)S(1)}) custom-call(s32[3,64]{1,0:T(4,128)S(1)} %pad_add_fusion.where, bf16[8,192,128]{2,1,0:T(8,128)(2,1)} %copy-done, bf16[8,192,128]{2,1,0:T(8,128)(2,1)} %copy-done.4, bf16[8,192,128]{2,1,0:T(8,128)(2,1)} %copy-done.3, bf16[8,192,128]{2,1,0:T(8,128)(2,1)} %copy-done.6, ...), custom_call_target="tpu_custom_call" | custom-call | tf_op jit(solution)/shard_map/back/pallas_call | solution.py:196
  93.5 5.0 %all-to-all-start.1 = ((bf16[8,8,192,128]{3,2,1,0:T(8,128)(2,1)}), bf16[8,8,192,128]{3,2,1,0:T(8,128)(2,1)}, u32[]{:S(2)}, u32[]{:S(2)}) async-start(bf16[8,8,192,128]{3,2,1,0:T(8,128)(2,1)} %bitcast.8), calls=%async_computation.1 | async-start | bytes 6291456 | tf_op jit(solution)/shard_map/all_to_all | solution.py:144
  98.6 5.9 %weights.1 = (bf16[4,2,4,2,128,128]{5,4,3,2,1,0:T(8,128)(2,1)S(1)}, bf16[4,2,4,2,128,128]{5,4,3,2,1,0:T(8,128)(2,1)S(1)}) custom-call(s32[3,64]{1,0:T(4,128)S(1)} %pad_add_fusion.where, bf16[8,192,128]{2,1,0:T(8,128)(2,1)} %copy-done.1, bf16[8,192,128]{2,1,0:T(8,128)(2,1)} %copy-done.10, bf16[8,192,128]{2,1,0:T(8,128)(2,1)} %copy-done.11, ...), custom_call_target="tpu_custom_call" | custom-call | tf_op jit(solution)/shard_map/weights/pallas_call | solution.py:215
  106.4 4.1 %collective-permute-done.14 = bf16[4,2,4,2,128,128]{5,4,3,2,1,0:T(8,128)(2,1)S(1)} collective-permute-done((bf16[4,2,4,2,128,128]{5,4,3,2,1,0:T(8,128)(2,1)S(1)}, bf16[4,2,4,2,128,128]{5,4,3,2,1,0:T(8,128)(2,1)S(1)}, u32[]{:S(2)}, u32[]{:S(2)}) %collective-permute-start.14) | collective-permute-done | bytes 2097184 | tf_op jit(solution)/shard_map/ppermute | solution.py:224
  112.2 2.4 %collective-permute-start.15 = (bf16[2,4,2,128,128]{4,3,2,1,0:T(8,128)(2,1)}, bf16[2,4,2,128,128]{4,3,2,1,0:T(8,128)(2,1)}, u32[]{:S(2)}, u32[]{:S(2)}) collective-permute-start(bf16[2,4,2,128,128]{4,3,2,1,0:T(8,128)(2,1)} %get-tuple-element.19), channel_id=1, source_target_pairs={{0,128},{128,256},{256,384},{384,0},{1,129},{129,257},{257,385},{3... | collective-permute-start | bytes 1572872 | tf_op jit(solution)/shard_map/ppermute | solution.py:227
  114.6 3.5 %collective-permute-start.17 = (bf16[2,4,2,128,128]{4,3,2,1,0:T(8,128)(2,1)}, bf16[2,4,2,128,128]{4,3,2,1,0:T(8,128)(2,1)}, u32[]{:S(2)}, u32[]{:S(2)}) collective-permute-start(bf16[2,4,2,128,128]{4,3,2,1,0:T(8,128)(2,1)} %get-tuple-element.20), channel_id=1, source_target_pairs={{0,384},{128,0},{256,128},{384,256},{1,385},{129,1},{257,129},{385... | collective-permute-start | bytes 1572872 | tf_op jit(solution)/shard_map/ppermute | solution.py:227
  118.1 3.3 %collective-permute-start.16 = (bf16[2,4,2,128,128]{4,3,2,1,0:T(8,128)(2,1)S(1)}, bf16[2,4,2,128,128]{4,3,2,1,0:T(8,128)(2,1)}, u32[]{:S(2)}, u32[]{:S(2)}) collective-permute-start(bf16[2,4,2,128,128]{4,3,2,1,0:T(8,128)(2,1)S(1)} %get-tuple-element.21), channel_id=1, source_target_pairs={{0,256},{128,384},{256,0},{384,128},{1,257},{129,385},{257,1},{385... | collective-permute-start | bytes 1572872 | tf_op jit(solution)/shard_map/ppermute | solution.py:227
  121.4 18.8 %all-to-all-done.1 = bf16[8,8,192,128]{3,2,1,0:T(8,128)(2,1)} async-done(((bf16[8,8,192,128]{3,2,1,0:T(8,128)(2,1)}), bf16[8,8,192,128]{3,2,1,0:T(8,128)(2,1)}, u32[]{:S(2)}, u32[]{:S(2)}) %all-to-all-start.1) | async-done | bytes 3145760 | tf_op jit(solution)/shard_map/all_to_all | solution.py:144
  140.1 3.3 %reduce_sum.24 = bf16[8,192,128]{2,1,0:T(8,128)(2,1)} reduce(bf16[8,8,192,128]{3,2,1,0:T(8,128)(2,1)} %all-to-all-done.1, bf16[]{:T(256)} %constant.50.clone.1), dimensions={0}, to_apply=%region_0.1 | reduce | flops 1376256 | bytes 3538946 | tf_op jit(solution)/shard_map/reduce_sum | solution.py:231
  143.4 3.5 %all-to-all-start.2 = ((bf16[8,192,128]{2,1,0:T(8,128)(2,1)}), bf16[8,192,128]{2,1,0:T(8,128)(2,1)S(1)}, u32[]{:S(2)}, u32[]{:S(2)}) async-start(bf16[8,192,128]{2,1,0:T(8,128)(2,1)} %reduce_sum.24), calls=%async_computation.2 | async-start | bytes 786432 | tf_op jit(solution)/shard_map/all_to_all | solution.py:144
  149.7 9.0 %all-to-all-done.2 = bf16[8,192,128]{2,1,0:T(8,128)(2,1)S(1)} async-done(((bf16[8,192,128]{2,1,0:T(8,128)(2,1)}), bf16[8,192,128]{2,1,0:T(8,128)(2,1)S(1)}, u32[]{:S(2)}, u32[]{:S(2)}) %all-to-all-start.2) | async-done | bytes 393248 | tf_op jit(solution)/shard_map/all_to_all | solution.py:144
  (66 shorter events, 18.1 us)
Async XLA Ops:
  0.6 60.9 %copy-start.14 = (s32[4,16]{1,0:T(4,128)S(1)}, s32[4,16]{1,0:T(4,128)}, u32[]{:S(2)}) copy-start(s32[4,16]{1,0:T(4,128)} %param.9) | copy-start | bytes 772
  0.6 60.9 %copy-start.15 = (s32[4,16]{1,0:T(4,128)S(1)}, s32[4,16]{1,0:T(4,128)}, u32[]{:S(2)}) copy-start(s32[4,16]{1,0:T(4,128)} %param.11) | copy-start | bytes 772
  27.9 52.6 %copy-start.1 = (bf16[8,192,128]{2,1,0:T(8,128)(2,1)}, bf16[8,192,128]{2,1,0:T(8,128)(2,1)S(1)}, u32[]{:S(2)}) copy-start(bf16[8,192,128]{2,1,0:T(8,128)(2,1)S(1)} %get-tuple-element.22.refs_0_) | copy-start | bytes 1179652
  27.9 58.1 %copy-start = (bf16[8,192,128]{2,1,0:T(8,128)(2,1)}, bf16[8,192,128]{2,1,0:T(8,128)(2,1)S(1)}, u32[]{:S(2)}) copy-start(bf16[8,192,128]{2,1,0:T(8,128)(2,1)S(1)} %get-tuple-element.23.refs_0_.refs_8_) | copy-start | bytes 1179652
  27.9 13.2 %collective-permute-start.7 = (bf16[8,192,128]{2,1,0:T(8,128)(2,1)S(1)}, bf16[8,192,128]{2,1,0:T(8,128)(2,1)S(1)}, u32[]{:S(2)}, u32[]{:S(2)}) collective-permute-start(bf16[8,192,128]{2,1,0:T(8,128)(2,1)S(1)} %get-tuple-element.22.refs_0_), channel_id=1, source_target_pairs={{0,8},{8,16},{16,24},{24,32},{32,40},{40,48},{48,56},{56,0},{1,9},... | collective-permute-start | bytes 1179656 | tf_op jit(solution)/shard_map/ppermute | solution.py:150
  31.4 11.7 %collective-permute-start.1 = (bf16[8,192,128]{2,1,0:T(8,128)(2,1)S(1)}, bf16[8,192,128]{2,1,0:T(8,128)(2,1)S(1)}, u32[]{:S(2)}, u32[]{:S(2)}) collective-permute-start(bf16[8,192,128]{2,1,0:T(8,128)(2,1)S(1)} %get-tuple-element.23.refs_0_.refs_8_), channel_id=1, source_target_pairs={{0,56},{8,0},{16,8},{24,16},{32,24},{40,32},{48,40},{56,48},{1,57}... | collective-permute-start | bytes 1179656 | tf_op jit(solution)/shard_map/ppermute | solution.py:150
  35.3 13.0 %collective-permute-start.8 = (bf16[8,192,128]{2,1,0:T(8,128)(2,1)S(1)}, bf16[8,192,128]{2,1,0:T(8,128)(2,1)S(1)}, u32[]{:S(2)}, u32[]{:S(2)}) collective-permute-start(bf16[8,192,128]{2,1,0:T(8,128)(2,1)S(1)} %get-tuple-element.22.refs_0_), channel_id=1, source_target_pairs={{0,56},{8,0},{16,8},{24,16},{32,24},{40,32},{48,40},{56,48},{1,57}... | collective-permute-start | bytes 1179656 | tf_op jit(solution)/shard_map/ppermute | solution.py:150
  39.2 13.0 %collective-permute-start = (bf16[8,192,128]{2,1,0:T(8,128)(2,1)S(1)}, bf16[8,192,128]{2,1,0:T(8,128)(2,1)S(1)}, u32[]{:S(2)}, u32[]{:S(2)}) collective-permute-start(bf16[8,192,128]{2,1,0:T(8,128)(2,1)S(1)} %get-tuple-element.23.refs_0_.refs_8_), channel_id=1, source_target_pairs={{0,8},{8,16},{16,24},{24,32},{32,40},{40,48},{48,56},{56,0},{1,9},... | collective-permute-start | bytes 1179656 | tf_op jit(solution)/shard_map/ppermute | solution.py:150
  41.1 13.3 %collective-permute-start.9 = (bf16[8,192,128]{2,1,0:T(8,128)(2,1)S(1)}, bf16[8,192,128]{2,1,0:T(8,128)(2,1)}, u32[]{:S(2)}, u32[]{:S(2)}) collective-permute-start(bf16[8,192,128]{2,1,0:T(8,128)(2,1)S(1)} %collective-permute-done.7.refs_1_), channel_id=1, source_target_pairs={{0,8},{8,16},{16,24},{24,32},{32,40},{40,48},{48,56},{56,0},{1,9},... | collective-permute-start | bytes 1179656 | tf_op jit(solution)/shard_map/ppermute | solution.py:150
  43.2 13.1 %collective-permute-start.3 = (bf16[8,192,128]{2,1,0:T(8,128)(2,1)S(1)}, bf16[8,192,128]{2,1,0:T(8,128)(2,1)S(1)}, u32[]{:S(2)}, u32[]{:S(2)}) collective-permute-start(bf16[8,192,128]{2,1,0:T(8,128)(2,1)S(1)} %collective-permute-done.1.refs_2_.refs_10_), channel_id=1, source_target_pairs={{0,56},{8,0},{16,8},{24,16},{32,24},{40,32},{48,40},{56,48},{1,57}... | collective-permute-start | bytes 1179656 | tf_op jit(solution)/shard_map/ppermute | solution.py:150
  48.2 13.4 %collective-permute-start.10 = (bf16[8,192,128]{2,1,0:T(8,128)(2,1)S(1)}, bf16[8,192,128]{2,1,0:T(8,128)(2,1)}, u32[]{:S(2)}, u32[]{:S(2)}) collective-permute-start(bf16[8,192,128]{2,1,0:T(8,128)(2,1)S(1)} %collective-permute-done.8.refs_2_), channel_id=1, source_target_pairs={{0,56},{8,0},{16,8},{24,16},{32,24},{40,32},{48,40},{56,48},{1,57}... | collective-permute-start | bytes 1179656 | tf_op jit(solution)/shard_map/ppermute | solution.py:150
  52.2 13.2 %collective-permute-start.2 = (bf16[8,192,128]{2,1,0:T(8,128)(2,1)S(1)}, bf16[8,192,128]{2,1,0:T(8,128)(2,1)S(1)}, u32[]{:S(2)}, u32[]{:S(2)}) collective-permute-start(bf16[8,192,128]{2,1,0:T(8,128)(2,1)S(1)} %collective-permute-done.refs_1_.refs_9_), channel_id=1, source_target_pairs={{0,8},{8,16},{16,24},{24,32},{32,40},{40,48},{48,56},{56,0},{1,9},... | collective-permute-start | bytes 1179656 | tf_op jit(solution)/shard_map/ppermute | solution.py:150
  54.4 13.2 %collective-permute-start.11 = (bf16[8,192,128]{2,1,0:T(8,128)(2,1)}, bf16[8,192,128]{2,1,0:T(8,128)(2,1)}, u32[]{:S(2)}, u32[]{:S(2)}) collective-permute-start(bf16[8,192,128]{2,1,0:T(8,128)(2,1)} %collective-permute-done.9.refs_3_), channel_id=1, source_target_pairs={{0,8},{8,16},{16,24},{24,32},{32,40},{40,48},{48,56},{56,0},{1,9},... | collective-permute-start | bytes 1179656 | tf_op jit(solution)/shard_map/ppermute | solution.py:150
  56.3 13.2 %collective-permute-start.5 = (bf16[8,192,128]{2,1,0:T(8,128)(2,1)S(1)}, bf16[8,192,128]{2,1,0:T(8,128)(2,1)S(1)}, u32[]{:S(2)}, u32[]{:S(2)}) collective-permute-start(bf16[8,192,128]{2,1,0:T(8,128)(2,1)S(1)} %collective-permute-done.3.refs_4_.refs_12_), channel_id=1, source_target_pairs={{0,56},{8,0},{16,8},{24,16},{32,24},{40,32},{48,40},{56,48},{1,57}... | collective-permute-start | bytes 1179656 | tf_op jit(solution)/shard_map/ppermute | solution.py:150
  61.7 13.1 %collective-permute-start.12 = (bf16[8,192,128]{2,1,0:T(8,128)(2,1)}, bf16[8,192,128]{2,1,0:T(8,128)(2,1)S(1)}, u32[]{:S(2)}, u32[]{:S(2)}) collective-permute-start(bf16[8,192,128]{2,1,0:T(8,128)(2,1)} %collective-permute-done.10.refs_4_), channel_id=1, source_target_pairs={{0,56},{8,0},{16,8},{24,16},{32,24},{40,32},{48,40},{56,48},{1,57}... | collective-permute-start | bytes 1179656 | tf_op jit(solution)/shard_map/ppermute | solution.py:150
  65.4 20.7 %collective-permute-start.4 = (bf16[8,192,128]{2,1,0:T(8,128)(2,1)S(1)}, bf16[8,192,128]{2,1,0:T(8,128)(2,1)S(1)}, u32[]{:S(2)}, u32[]{:S(2)}) collective-permute-start(bf16[8,192,128]{2,1,0:T(8,128)(2,1)S(1)} %collective-permute-done.2.refs_3_.refs_11_), channel_id=1, source_target_pairs={{0,8},{8,16},{16,24},{24,32},{32,40},{40,48},{48,56},{56,0},{1,9},... | collective-permute-start | bytes 1179656 | tf_op jit(solution)/shard_map/ppermute | solution.py:150
  67.6 12.9 %collective-permute-start.13 = (bf16[8,192,128]{2,1,0:T(8,128)(2,1)}, bf16[8,192,128]{2,1,0:T(8,128)(2,1)S(1)}, u32[]{:S(2)}, u32[]{:S(2)}) collective-permute-start(bf16[8,192,128]{2,1,0:T(8,128)(2,1)} %collective-permute-done.11.refs_5_), channel_id=1, source_target_pairs={{0,8},{8,16},{16,24},{24,32},{32,40},{40,48},{48,56},{56,0},{1,9},... | collective-permute-start | bytes 1179656 | tf_op jit(solution)/shard_map/ppermute | solution.py:150
  69.5 16.6 %collective-permute-start.6 = (bf16[8,192,128]{2,1,0:T(8,128)(2,1)S(1)}, bf16[8,192,128]{2,1,0:T(8,128)(2,1)S(1)}, u32[]{:S(2)}, u32[]{:S(2)}) collective-permute-start(bf16[8,192,128]{2,1,0:T(8,128)(2,1)S(1)} %collective-permute-done.5.refs_6_.refs_14_), channel_id=1, source_target_pairs={{0,56},{8,0},{16,8},{24,16},{32,24},{40,32},{48,40},{56,48},{1,57}... | collective-permute-start | bytes 1179656 | tf_op jit(solution)/shard_map/ppermute | solution.py:150
  93.5 46.6 %all-to-all-start.1 = ((bf16[8,8,192,128]{3,2,1,0:T(8,128)(2,1)}), bf16[8,8,192,128]{3,2,1,0:T(8,128)(2,1)}, u32[]{:S(2)}, u32[]{:S(2)}) async-start(bf16[8,8,192,128]{3,2,1,0:T(8,128)(2,1)} %bitcast.8), calls=%async_computation.1 | async-start | bytes 6291456 | tf_op jit(solution)/shard_map/all_to_all | solution.py:144
  104.5 6.1 %collective-permute-start.14 = (bf16[4,2,4,2,128,128]{5,4,3,2,1,0:T(8,128)(2,1)S(1)}, bf16[4,2,4,2,128,128]{5,4,3,2,1,0:T(8,128)(2,1)S(1)}, u32[]{:S(2)}, u32[]{:S(2)}) collective-permute-start(bf16[4,2,4,2,128,128]{5,4,3,2,1,0:T(8,128)(2,1)S(1)} %get-tuple-element.18), channel_id=1, source_target_pairs={{0,64},{64,0},{1,65},{65,1},{2,66},{66,2},{3,67},{67,3},{4,68},{68... | collective-permute-start | bytes 6291464 | tf_op jit(solution)/shard_map/ppermute | solution.py:224
  112.2 34.7 %collective-permute-start.15 = (bf16[2,4,2,128,128]{4,3,2,1,0:T(8,128)(2,1)}, bf16[2,4,2,128,128]{4,3,2,1,0:T(8,128)(2,1)}, u32[]{:S(2)}, u32[]{:S(2)}) collective-permute-start(bf16[2,4,2,128,128]{4,3,2,1,0:T(8,128)(2,1)} %get-tuple-element.19), channel_id=1, source_target_pairs={{0,128},{128,256},{256,384},{384,0},{1,129},{129,257},{257,385},{3... | collective-permute-start | bytes 1572872 | tf_op jit(solution)/shard_map/ppermute | solution.py:227
  114.6 32.3 %collective-permute-start.17 = (bf16[2,4,2,128,128]{4,3,2,1,0:T(8,128)(2,1)}, bf16[2,4,2,128,128]{4,3,2,1,0:T(8,128)(2,1)}, u32[]{:S(2)}, u32[]{:S(2)}) collective-permute-start(bf16[2,4,2,128,128]{4,3,2,1,0:T(8,128)(2,1)} %get-tuple-element.20), channel_id=1, source_target_pairs={{0,384},{128,0},{256,128},{384,256},{1,385},{129,1},{257,129},{385... | collective-permute-start | bytes 1572872 | tf_op jit(solution)/shard_map/ppermute | solution.py:227
  118.1 28.9 %collective-permute-start.16 = (bf16[2,4,2,128,128]{4,3,2,1,0:T(8,128)(2,1)S(1)}, bf16[2,4,2,128,128]{4,3,2,1,0:T(8,128)(2,1)}, u32[]{:S(2)}, u32[]{:S(2)}) collective-permute-start(bf16[2,4,2,128,128]{4,3,2,1,0:T(8,128)(2,1)S(1)} %get-tuple-element.21), channel_id=1, source_target_pairs={{0,256},{128,384},{256,0},{384,128},{1,257},{129,385},{257,1},{385... | collective-permute-start | bytes 1572872 | tf_op jit(solution)/shard_map/ppermute | solution.py:227
  143.4 15.3 %all-to-all-start.2 = ((bf16[8,192,128]{2,1,0:T(8,128)(2,1)}), bf16[8,192,128]{2,1,0:T(8,128)(2,1)S(1)}, u32[]{:S(2)}, u32[]{:S(2)}) async-start(bf16[8,192,128]{2,1,0:T(8,128)(2,1)} %reduce_sum.24), calls=%async_computation.2 | async-start | bytes 786432 | tf_op jit(solution)/shard_map/all_to_all | solution.py:144
  (12 other events, 185.7 us)

commit v5 on v4

--- a/solution.py
+++ b/solution.py
@@ -38,46 +38,68 @@
     return loads
 
 
-def hidden_kernel(plan, where, *refs):
-    side, steps = plan
-    units = list(zip(refs, steps))
-    w_in, w_out, act, slope, wi, wo, x, sem, w_sem = refs[len(steps) :]
+def row_of(blocks, where, line, r, per_row):
+    return jnp.concatenate([blocks[where[line, r * per_row + k]] for k in range(per_row)], axis=1)
+
+
+def early_kernel(plans, where, *refs):
+    (side, x_steps), (_, y_steps) = plans
+    n_x, n_y = len(x_steps), len(y_steps)
+    x_units = list(zip(refs[:n_x], x_steps))
+    y_units = list(zip(refs[n_x : n_x + n_y], y_steps))
+    w_in, w_out, hidden, grad_act, wi, wo, x, y, x_sem, y_sem, w_sem = refs[n_x + n_y :]
     rows, per_row, width, _ = w_in.shape
     load_in = pltpu.make_async_copy(w_in, wi, w_sem.at[0])
     load_out = pltpu.make_async_copy(w_out, wo, w_sem.at[1])
     load_in.start()
-    loads = start_loads(where, units, x, sem, side)
+    x_loads = start_loads(where, x_units, x, x_sem, side)
     load_out.start()
+    y_loads = start_loads(where, y_units, y, y_sem, side)
+    places = x.shape[0] // side
+    opposite = pl.ds(lax.rem(where[2, 1] + places // 2, places) * side, side)
+    x[opposite] = jnp.zeros((side, *x.shape[1:]), BF16)
+    y[opposite] = jnp.zeros((side, *y.shape[1:]), BF16)
     load_in.wait()
-    for copy in loads:
-        copy.wait()
-    for r in range(rows):
-        x_row = jnp.concatenate([x[where[0, r * per_row + k]] for k in range(per_row)], axis=1)
-        hidden = dot_nn(x_row, wi[r].reshape(per_row * width, width))
+    for copy in x_loads:
+        copy.wait()
+    for r in range(rows):
+        x_row = row_of(x, where, 0, r, per_row)
+        hidden[r] = dot_nn(x_row, wi[r].reshape(per_row * width, width))
+    load_out.wait()
+    for copy in y_loads:
+        copy.wait()
+    for r in range(rows):
+        w_row = jnp.concatenate([wo[r, k] for k in range(per_row)], axis=1)
+        grad_act[r] = dot_nt(row_of(y, where, 1, r, per_row), w_row)
+
+
+def back_kernel(where, x_last, y_last, hidden_most, grad_most, wi, wo, *refs):
+    placed, act, grad, x, y, total, rounded, sem, out_sem = refs
+    rows, per_row, width, _ = wi.shape
+    blocks, side = total.shape[0], x_last.shape[0]
+    load_x = pltpu.make_async_copy(x_last, x.at[pl.ds(0, side)], sem.at[0])
+    load_y = pltpu.make_async_copy(y_last, y.at[pl.ds(0, side)], sem.at[1])
+    load_x.start()
+    load_y.start()
+    x[side] = jnp.zeros(x.shape[1:], BF16)
+    y[side] = jnp.zeros(y.shape[1:], BF16)
+    total[...] = jnp.zeros_like(total)
+    load_x.wait()
+    load_y.wait()
+    for r in range(rows):
+        x_row = row_of(x, where, 3, r, per_row)
+        y_row = row_of(y, where, 4, r, per_row)
+        w_row = jnp.concatenate([wo[r, k] for k in range(per_row)], axis=1)
+        hidden = hidden_most[r] + dot_nn(x_row, wi[r].reshape(per_row * width, width))
+        grad_act = grad_most[r] + dot_nt(y_row, w_row)
         square = hidden * hidden
         tanh = jnp.tanh(GELU_SCALE * hidden * (1.0 + GELU_CUBE * square))
         half = 0.5 * (1.0 + tanh)
         act[r] = (hidden * half).astype(BF16)
-        slope[r] = half + 0.5 * hidden * (1.0 - tanh * tanh) * (
+        slope = half + 0.5 * hidden * (1.0 - tanh * tanh) * (
             GELU_SCALE * (1.0 + 3.0 * GELU_CUBE * square)
         )
-    load_out.wait()
-
-
-def back_kernel(plan, where, *refs):
-    side, steps = plan
-    units = list(zip(refs, steps))
-    slope, wi, wo, placed, grad, y, total, rounded, sem, out_sem = refs[len(steps) :]
-    rows, per_row, width, _ = wi.shape
-    blocks = total.shape[0]
-    loads = start_loads(where, units, y, sem, side)
-    total[...] = jnp.zeros_like(total)
-    for copy in loads:
-        copy.wait()
-    for r in range(rows):
-        y_row = jnp.concatenate([y[where[1, r * per_row + k]] for k in range(per_row)], axis=1)
-        w_row = jnp.concatenate([wo[r, k] for k in range(per_row)], axis=1)
-        grad_hidden = (dot_nt(y_row, w_row) * slope[r]).astype(BF16)
+        grad_hidden = (grad_act * slope).astype(BF16)
         grad[r] = grad_hidden
         terms = dot_nt(grad_hidden, wi[r].reshape(per_row * width, width))
         for k in range(per_row):
@@ -115,6 +137,20 @@
                     at = r * per_row + (x_at * 2 + half) * each + j
                     out[away, 0, r, j] = dot_tn(x[where[0, at]], grad_r).astype(BF16)
                     out[away, 1, r, j] = dot_nn(act_t, y[where[1, at]]).astype(BF16)
+
+
+def sum_kernel(parts, out, here, sem):
+    loads = [
+        pltpu.make_async_copy(parts.at[:, n], here.at[n], sem.at[n]) for n in range(here.shape[0])
+    ]
+    for copy in loads:
+        copy.start()
+    for n, copy in enumerate(loads):
+        copy.wait()
+        kept = here[n, 0].astype(F32)
+        for s in range(1, here.shape[1]):
+            kept = kept + here[n, s].astype(F32)
+        out[n] = kept.astype(BF16)
 
 
 def lines_and_rings(ny, nz):
@@ -166,7 +202,7 @@
     y_units.append(turn(y_back, -1))
     x_steps.append(-(side // 2))
     y_steps.append(side // 2)
-    x_units, y_units = [in_hbm(u) for u in x_units], [in_hbm(u) for u in y_units]
+    x_units, y_units = ([in_hbm(u) for u in us[:-1]] + us[-1:] for us in (x_units, y_units))
     x_plan, y_plan = (side, tuple(x_steps)), (side, tuple(y_steps))
 
     core, y_at, z_at = (lax.axis_index(a) for a in CYZ)
@@ -175,39 +211,39 @@
     place = jnp.where(core == 0, y_at, z_at)
     here = jnp.stack([core, place, lax.axis_index("x")]).astype(jnp.int32)
     here = jnp.pad(here, (0, rows * per_row - 3)).reshape(1, -1)
-    where = jnp.concatenate([cols, here])
+    opposite = (place + ny // 2) % ny
+    lasts = jnp.where(cols // side == opposite, cols % side, side)
+    where = jnp.concatenate([cols, here, lasts])
 
     gathered = pltpu.VMEM((blocks, tok, width), BF16)
     loaded = pltpu.SemaphoreType.DMA((side,))
     values = jax.ShapeDtypeStruct((rows, tok, width), BF16)
-    act, slope, wi, wo = pl.pallas_call(
-        functools.partial(hidden_kernel, x_plan),
-        out_shape=(
-            values,
-            jax.ShapeDtypeStruct((rows, tok, width), F32),
-            pltpu.VMEM(w_in.shape, BF16),
-            pltpu.VMEM(w_out.shape, BF16),
-        ),
-        in_specs=[smem] + [anywhere] * (len(x_units) + 2),
-        scratch_shapes=[gathered, loaded, pltpu.SemaphoreType.DMA((2,))],
-        compiler_params=params,
-        name="hidden",
-    )(where, *x_units, in_hbm(w_in), in_hbm(w_out))
-    placed, grad = pl.pallas_call(
-        functools.partial(back_kernel, y_plan),
-        out_shape=(jax.ShapeDtypeStruct((blocks, tok, width), BF16), values),
-        in_specs=[smem] + [anywhere] * len(y_units) + [vmem] * 3,
-        out_specs=(anywhere, vmem),
+    kept = jax.ShapeDtypeStruct((rows, tok, width), F32)
+    hidden_most, grad_most, wi, wo = pl.pallas_call(
+        functools.partial(early_kernel, ((side, x_plan[1][:-1]), (side, y_plan[1][:-1]))),
+        out_shape=(kept, kept, pltpu.VMEM(w_in.shape, BF16), pltpu.VMEM(w_out.shape, BF16)),
+        in_specs=[smem] + [anywhere] * (len(x_units) + len(y_units)),
+        scratch_shapes=[gathered, gathered, loaded, loaded, pltpu.SemaphoreType.DMA((2,))],
+        compiler_params=params,
+        name="early",
+    )(where, *x_units[:-1], *y_units[:-1], in_hbm(w_in), in_hbm(w_out))
+    last = pltpu.VMEM((side + 1, tok, width), BF16)
+    placed, act, grad = pl.pallas_call(
+        back_kernel,
+        out_shape=(jax.ShapeDtypeStruct((blocks, tok, width), BF16), values, values),
+        in_specs=[smem] + [anywhere] * 2 + [vmem] * 4,
+        out_specs=(anywhere, vmem, vmem),
         scratch_shapes=[
-            gathered,
+            last,
+            last,
             pltpu.VMEM((blocks, tok, width), F32),
             pltpu.VMEM((blocks, tok, width), BF16),
-            loaded,
+            pltpu.SemaphoreType.DMA((2,)),
             pltpu.SemaphoreType.DMA((SLABS,)),
         ],
         compiler_params=params,
         name="back",
-    )(where, *y_units, slope, wi, wo)
+    )(where, x_units[-1], y_units[-1], hidden_most, grad_most, wi, wo)
 
     on_ring = swap(placed.reshape(side, blocks // side, tok, width), rings)
 
@@ -228,7 +264,15 @@
     ]
     summed = sum((v.astype(F32) for v in spread), paired[0].astype(F32)).astype(BF16)
 
-    on_line = jnp.sum(on_ring.astype(F32), axis=0).astype(BF16)
+    on_line = pl.pallas_call(
+        sum_kernel,
+        out_shape=jax.ShapeDtypeStruct(on_ring.shape[1:], BF16),
+        in_specs=[anywhere],
+        out_specs=vmem,
+        scratch_shapes=[pltpu.VMEM((blocks // side, side, tok, width), BF16), loaded],
+        compiler_params=params,
+        name="sums",
+    )(in_hbm(on_ring))
     received = swap(on_line, lines)
     grad_inputs = jnp.sum(received.astype(F32), axis=0).astype(BF16)
     return grad_inputs, summed[0], summed[1]

time: 160 us -> 156 us (0.975)
  waiting for transfers between devices: 37.8 us -> 32.1 us
  Pallas kernels: 17.2 us -> 21.3 us
  other arithmetic: 8.52 us -> 4.95 us
    ppermute x14, waiting for transfers between devices: 5.98 us -> 1.21 us  [turn(): return lax.ppermute(values, CYZ, pairs)]
    pallas_call x2 -> x3, Pallas kernels: 11.3 us -> 15.5 us  [the longest x1 6.45 us: per_device(): pl.pallas_call(back_kernel, out_shape=(jax.ShapeDtypeStruct((blocks, tok,...]
    reduce_sum x1 -> x0, other arithmetic: 3.29 us -> none  [per_device(): on_line = jnp.sum(on_ring.astype(F32), axis=0).astype(BF16)]
  transfers between devices with their start and end apart: 20 -> 20, of which waited for: 5 -> 5; matrix products, arithmetic and copies ran while one was open for 5% -> 3% of each run, Pallas kernels for 7% -> 10%
where the time goes in v5:
time: 156 us; the launch traced here: 155 us
  starting transfers between devices  65 us (42%)
  waiting for transfers between devices  32.1 us (21%)
  blocking collectives  26.2 us (17%)
  Pallas kernels  21.3 us (14%)
  other arithmetic  4.95 us (3%)
  local copies, waits for them, and re-layouts  4.06 us (3%)
    ppermute x14, starting transfers between devices, turn(): return lax.ppermute(values, CYZ, pairs)  46 us
    all_to_all x2, waiting for transfers between devices, swap(): lax.all_to_all(values, CYZ, split_axis=0, concat_axis=0, tiled=True, axis...  26.8 us
    all_to_all x1, blocking collectives, swap(): lax.all_to_all(values, CYZ, split_axis=0, concat_axis=0, tiled=True, axis...  26.2 us
    ppermute x3, starting transfers between devices, per_device(): lax.ppermute(paired[d], 'x', [(i, (i + d) % nx) for i in range(nx)])  9.14 us
    all_to_all x2, starting transfers between devices, swap(): lax.all_to_all(values, CYZ, split_axis=0, concat_axis=0, tiled=True, axis...  7.99 us
    pallas_call x1, Pallas kernels, per_device(): pl.pallas_call(back_kernel, out_shape=(jax.ShapeDtypeStruct((blocks, tok,...  6.45 us
    pallas_call x1, Pallas kernels, per_device(): pl.pallas_call(functools.partial(early_kernel, ((side, x_plan[1][:-1]), (...  6.36 us
    pallas_call x1, Pallas kernels, per_device(): pl.pallas_call(functools.partial(weight_kernel, (x_plan, y_plan)), out_sh...  5.77 us
  transfers between devices with their start and end apart: 20, of which 5 were waited for; matrix products, arithmetic and copies ran while one was open for 3% of the time, Pallas kernels for 10%

profile of v5, /device:TPU:6, one launch (start us, length us, event | category | flops | bytes accessed | tf_op | source)
XLA Modules:
  0.0 154.8 jit_solution(10163739915241934076)
XLA Ops:
  1.7 26.2 %all_to_all.15 = bf16[8,2,192,128]{3,2,1,0:T(8,128)(2,1)S(1)} all-to-all(bf16[8,2,192,128]{3,2,1,0:T(8,128)(2,1)S(1)} %broadcast_in_dim.5), channel_id=1, replica_groups={{0,1,2,3,4,5,6,7},{8,9,10,11,12,13,14,15},{16,17,18,19,20,21,22,23},{24..., dimensions={0} | all-to-all | bytes 1572864 | tf_op jit(solution)/shard_map/all_to_all | solution.py:180
  27.9 5.4 %collective-permute-start.4 = (bf16[8,192,128]{2,1,0:T(8,128)(2,1)S(1)}, bf16[8,192,128]{2,1,0:T(8,128)(2,1)S(1)}, u32[]{:S(2)}, u32[]{:S(2)}) collective-permute-start(bf16[8,192,128]{2,1,0:T(8,128)(2,1)S(1)} %get-tuple-element.26.refs_7_.refs_8_), channel_id=1, source_target_pairs={{0,56},{8,0},{16,8},{24,16},{32,24},{40,32},{48,40},{56,48},{1,57}... | collective-permute-start | bytes 1179656 | tf_op jit(solution)/shard_map/ppermute | solution.py:186
  35.3 2.0 %collective-permute-start.11 = (bf16[8,192,128]{2,1,0:T(8,128)(2,1)S(1)}, bf16[8,192,128]{2,1,0:T(8,128)(2,1)S(1)}, u32[]{:S(2)}, u32[]{:S(2)}) collective-permute-start(bf16[8,192,128]{2,1,0:T(8,128)(2,1)S(1)} %get-tuple-element.26.refs_7_.refs_8_), channel_id=1, source_target_pairs={{0,8},{8,16},{16,24},{24,32},{32,40},{40,48},{48,56},{56,0},{1,9},... | collective-permute-start | bytes 1179656 | tf_op jit(solution)/shard_map/ppermute | solution.py:186
  37.3 5.0 %collective-permute-start.8 = (bf16[8,192,128]{2,1,0:T(8,128)(2,1)S(1)}, bf16[8,192,128]{2,1,0:T(8,128)(2,1)S(1)}, u32[]{:S(2)}, u32[]{:S(2)}) collective-permute-start(bf16[8,192,128]{2,1,0:T(8,128)(2,1)S(1)} %get-tuple-element.27.refs_0_), channel_id=1, source_target_pairs={{0,56},{8,0},{16,8},{24,16},{32,24},{40,32},{48,40},{56,48},{1,57}... | collective-permute-start | bytes 1179656 | tf_op jit(solution)/shard_map/ppermute | solution.py:186
  42.3 3.9 %collective-permute-start.5 = (bf16[8,192,128]{2,1,0:T(8,128)(2,1)S(1)}, bf16[8,192,128]{2,1,0:T(8,128)(2,1)S(1)}, u32[]{:S(2)}, u32[]{:S(2)}) collective-permute-start(bf16[8,192,128]{2,1,0:T(8,128)(2,1)S(1)} %collective-permute-done.4.refs_9_.refs_10_), channel_id=1, source_target_pairs={{0,56},{8,0},{16,8},{24,16},{32,24},{40,32},{48,40},{56,48},{1,57}... | collective-permute-start | bytes 1179656 | tf_op jit(solution)/shard_map/ppermute | solution.py:186
  50.4 5.1 %collective-permute-start.9 = (bf16[8,192,128]{2,1,0:T(8,128)(2,1)S(1)}, bf16[8,192,128]{2,1,0:T(8,128)(2,1)}, u32[]{:S(2)}, u32[]{:S(2)}) collective-permute-start(bf16[8,192,128]{2,1,0:T(8,128)(2,1)S(1)} %collective-permute-done.8.refs_2_), channel_id=1, source_target_pairs={{0,56},{8,0},{16,8},{24,16},{32,24},{40,32},{48,40},{56,48},{1,57}... | collective-permute-start | bytes 1179656 | tf_op jit(solution)/shard_map/ppermute | solution.py:186
  55.5 3.8 %collective-permute-start.6 = (bf16[8,192,128]{2,1,0:T(8,128)(2,1)S(1)}, bf16[8,192,128]{2,1,0:T(8,128)(2,1)}, u32[]{:S(2)}, u32[]{:S(2)}) collective-permute-start(bf16[8,192,128]{2,1,0:T(8,128)(2,1)S(1)} %collective-permute-done.5.refs_11_.refs_12_), channel_id=1, source_target_pairs={{0,56},{8,0},{16,8},{24,16},{32,24},{40,32},{48,40},{56,48},{1,57}... | collective-permute-start | bytes 1179656 | tf_op jit(solution)/shard_map/ppermute | solution.py:186
  59.3 2.1 %collective-permute-start.2 = (bf16[8,192,128]{2,1,0:T(8,128)(2,1)S(1)}, bf16[8,192,128]{2,1,0:T(8,128)(2,1)}, u32[]{:S(2)}, u32[]{:S(2)}) collective-permute-start(bf16[8,192,128]{2,1,0:T(8,128)(2,1)S(1)} %collective-permute-done.1.refs_3_), channel_id=1, source_target_pairs={{0,8},{8,16},{16,24},{24,32},{32,40},{40,48},{48,56},{56,0},{1,9},... | collective-permute-start | bytes 1179656 | tf_op jit(solution)/shard_map/ppermute | solution.py:186
  63.5 5.1 %collective-permute-start.10 = (bf16[8,192,128]{2,1,0:T(8,128)(2,1)}, bf16[8,192,128]{2,1,0:T(8,128)(2,1)S(1)}, u32[]{:S(2)}, u32[]{:S(2)}) collective-permute-start(bf16[8,192,128]{2,1,0:T(8,128)(2,1)} %collective-permute-done.9.refs_4_), channel_id=1, source_target_pairs={{0,56},{8,0},{16,8},{24,16},{32,24},{40,32},{48,40},{56,48},{1,57}... | collective-permute-start | bytes 1179656 | tf_op jit(solution)/shard_map/ppermute | solution.py:186
  68.7 3.8 %collective-permute-start.7 = (bf16[8,192,128]{2,1,0:T(8,128)(2,1)}, bf16[8,192,128]{2,1,0:T(8,128)(2,1)S(1)}, u32[]{:S(2)}, u32[]{:S(2)}) collective-permute-start(bf16[8,192,128]{2,1,0:T(8,128)(2,1)} %collective-permute-done.6.refs_13_.refs_14_), channel_id=1, source_target_pairs={{0,56},{8,0},{16,8},{24,16},{32,24},{40,32},{48,40},{56,48},{1,57}... | collective-permute-start | bytes 1179656 | tf_op jit(solution)/shard_map/ppermute | solution.py:186
  72.5 2.1 %collective-permute-start.3 = (bf16[8,192,128]{2,1,0:T(8,128)(2,1)}, bf16[8,192,128]{2,1,0:T(8,128)(2,1)S(1)}, u32[]{:S(2)}, u32[]{:S(2)}) collective-permute-start(bf16[8,192,128]{2,1,0:T(8,128)(2,1)} %collective-permute-done.2.refs_5_), channel_id=1, source_target_pairs={{0,8},{8,16},{16,24},{24,32},{32,40},{40,48},{48,56},{56,0},{1,9},... | collective-permute-start | bytes 1179656 | tf_op jit(solution)/shard_map/ppermute | solution.py:186
  76.2 6.4 %early.1 = (f32[4,192,128]{2,1,0:T(8,128)S(1)}, f32[4,192,128]{2,1,0:T(8,128)S(1)}, bf16[4,16,128,128]{3,2,1,0:T(8,128)(2,1)S(1)}, bf16[4,16,128,128]{3,2,1,0:T(8,128)(2,1)S(1)}) custom-call(s32[5,64]{1,0:T(8,128)S(1)} %pad_add_fusion.where, bf16[8,192,128]{2,1,0:T(8,128)(2,1)} %copy-done.1, bf16[8,192,128]{2,1,0:T(8,128)(2,1)} %copy-done.4, ...), custom_call_target="tpu_custom_call" | custom-call | tf_op jit(solution)/shard_map/early/pallas_call | solution.py:222
  83.6 6.5 %back.1 = (bf16[64,192,128]{2,1,0:T(8,128)(2,1)}, bf16[4,192,128]{2,1,0:T(8,128)(2,1)S(1)}, bf16[4,192,128]{2,1,0:T(8,128)(2,1)S(1)}) custom-call(s32[5,64]{1,0:T(8,128)S(1)} %pad_add_fusion.where, bf16[8,192,128]{2,1,0:T(8,128)(2,1)S(1)} %collective-permute-done.3.x_last.refs_7_, bf16[8,192,128]{2,1,0:T(8,128)(2,1)S(1)} %collective-permute-done.7.y_last.refs_15_, ...), custom_call_target="tpu_custom_call" | custom-call | tf_op jit(solution)/shard_map/back/pallas_call | solution.py:231
  90.0 4.5 %all-to-all-start.1 = ((bf16[8,8,192,128]{3,2,1,0:T(8,128)(2,1)}), bf16[8,8,192,128]{3,2,1,0:T(8,128)(2,1)}, u32[]{:S(2)}, u32[]{:S(2)}) async-start(bf16[8,8,192,128]{3,2,1,0:T(8,128)(2,1)} %bitcast.8), calls=%async_computation.1 | async-start | bytes 6291456 | tf_op jit(solution)/shard_map/all_to_all | solution.py:180
  94.6 5.8 %weights.1 = (bf16[4,2,4,2,128,128]{5,4,3,2,1,0:T(8,128)(2,1)S(1)}, bf16[4,2,4,2,128,128]{5,4,3,2,1,0:T(8,128)(2,1)S(1)}) custom-call(s32[5,64]{1,0:T(8,128)S(1)} %pad_add_fusion.where, bf16[8,192,128]{2,1,0:T(8,128)(2,1)} %copy-done.1, bf16[8,192,128]{2,1,0:T(8,128)(2,1)} %copy-done.4, bf16[8,192,128]{2,1,0:T(8,128)(2,1)} %copy-done.6, ...), custom_call_target="tpu_custom_call" | custom-call | tf_op jit(solution)/shard_map/weights/pallas_call | solution.py:251
  102.3 4.1 %collective-permute-done.14 = bf16[4,2,4,2,128,128]{5,4,3,2,1,0:T(8,128)(2,1)S(1)} collective-permute-done((bf16[4,2,4,2,128,128]{5,4,3,2,1,0:T(8,128)(2,1)S(1)}, bf16[4,2,4,2,128,128]{5,4,3,2,1,0:T(8,128)(2,1)S(1)}, u32[]{:S(2)}, u32[]{:S(2)}) %collective-permute-start.14) | collective-permute-done | bytes 2097184 | tf_op jit(solution)/shard_map/ppermute | solution.py:260
  109.2 2.4 %collective-permute-start.15 = (bf16[2,4,2,128,128]{4,3,2,1,0:T(8,128)(2,1)}, bf16[2,4,2,128,128]{4,3,2,1,0:T(8,128)(2,1)}, u32[]{:S(2)}, u32[]{:S(2)}) collective-permute-start(bf16[2,4,2,128,128]{4,3,2,1,0:T(8,128)(2,1)} %get-tuple-element.23), channel_id=1, source_target_pairs={{0,128},{128,256},{256,384},{384,0},{1,129},{129,257},{257,385},{3... | collective-permute-start | bytes 1572872 | tf_op jit(solution)/shard_map/ppermute | solution.py:263
  111.5 3.5 %collective-permute-start.17 = (bf16[2,4,2,128,128]{4,3,2,1,0:T(8,128)(2,1)S(1)}, bf16[2,4,2,128,128]{4,3,2,1,0:T(8,128)(2,1)}, u32[]{:S(2)}, u32[]{:S(2)}) collective-permute-start(bf16[2,4,2,128,128]{4,3,2,1,0:T(8,128)(2,1)S(1)} %get-tuple-element.24), channel_id=1, source_target_pairs={{0,384},{128,0},{256,128},{384,256},{1,385},{129,1},{257,129},{385... | collective-permute-start | bytes 1572872 | tf_op jit(solution)/shard_map/ppermute | solution.py:263
  115.0 3.3 %collective-permute-start.16 = (bf16[2,4,2,128,128]{4,3,2,1,0:T(8,128)(2,1)S(1)}, bf16[2,4,2,128,128]{4,3,2,1,0:T(8,128)(2,1)}, u32[]{:S(2)}, u32[]{:S(2)}) collective-permute-start(bf16[2,4,2,128,128]{4,3,2,1,0:T(8,128)(2,1)S(1)} %get-tuple-element.25), channel_id=1, source_target_pairs={{0,256},{128,384},{256,0},{384,128},{1,257},{129,385},{257,1},{385... | collective-permute-start | bytes 1572872 | tf_op jit(solution)/shard_map/ppermute | solution.py:263
  118.3 17.8 %all-to-all-done.1.parts = bf16[8,8,192,128]{3,2,1,0:T(8,128)(2,1)} async-done(((bf16[8,8,192,128]{3,2,1,0:T(8,128)(2,1)}), bf16[8,8,192,128]{3,2,1,0:T(8,128)(2,1)}, u32[]{:S(2)}, u32[]{:S(2)}) %all-to-all-start.1) | async-done | bytes 3145760 | tf_op jit(solution)/shard_map/all_to_all | solution.py:180
  136.1 2.7 %sums.1 = bf16[8,192,128]{2,1,0:T(8,128)(2,1)} custom-call(bf16[8,8,192,128]{3,2,1,0:T(8,128)(2,1)} %all-to-all-done.1.parts), custom_call_target="tpu_custom_call" | custom-call | tf_op jit(solution)/shard_map/sums/pallas_call | solution.py:267
  138.9 3.5 %all-to-all-start.2 = ((bf16[8,192,128]{2,1,0:T(8,128)(2,1)}), bf16[8,192,128]{2,1,0:T(8,128)(2,1)S(1)}, u32[]{:S(2)}, u32[]{:S(2)}) async-start(bf16[8,192,128]{2,1,0:T(8,128)(2,1)} %sums.1), calls=%async_computation.2 | async-start | bytes 786432 | tf_op jit(solution)/shard_map/all_to_all | solution.py:180
  142.4 1.9 %fusion.2 = bf16[2,4,2,128,128]{4,3,2,1,0:T(8,128)(2,1)S(1)} fusion(bf16[2,4,2,128,128]{4,3,2,1,0:T(8,128)(2,1)} %collective-permute-done.17, bf16[2,4,2,128,128]{4,3,2,1,0:T(8,128)(2,1)} %collective-permute-done.16, bf16[2,4,2,128,128]{4,3,2,1,0:T(8,128)(2,1)} %collective-permute-done.15, bf16[4,2,4,2,128,128]{5,4,3,2,1,0:T(8,128)(2,1)} %copy-done.2, ...), kind=kLoop, calls=%fused_computation.3 | loop fusion | flops 3145728 | bytes 3145728 | tf_op jit(solution)/shard_map/convert_element_type | solution.py:265
  145.1 9.0 %all-to-all-done.2 = bf16[8,192,128]{2,1,0:T(8,128)(2,1)S(1)} async-done(((bf16[8,192,128]{2,1,0:T(8,128)(2,1)}), bf16[8,192,128]{2,1,0:T(8,128)(2,1)S(1)}, u32[]{:S(2)}, u32[]{:S(2)}) %all-to-all-start.2) | async-done | bytes 393248 | tf_op jit(solution)/shard_map/all_to_all | solution.py:180
  (60 shorter events, 17.9 us)
Async XLA Ops:
  0.6 60.8 %copy-start.11 = (s32[4,16]{1,0:T(4,128)S(1)}, s32[4,16]{1,0:T(4,128)}, u32[]{:S(2)}) copy-start(s32[4,16]{1,0:T(4,128)} %param.9) | copy-start | bytes 772
  0.6 60.9 %copy-start.12 = (s32[4,16]{1,0:T(4,128)S(1)}, s32[4,16]{1,0:T(4,128)}, u32[]{:S(2)}) copy-start(s32[4,16]{1,0:T(4,128)} %param.11) | copy-start | bytes 772
  27.9 46.8 %copy-start = (bf16[8,192,128]{2,1,0:T(8,128)(2,1)}, bf16[8,192,128]{2,1,0:T(8,128)(2,1)S(1)}, u32[]{:S(2)}) copy-start(bf16[8,192,128]{2,1,0:T(8,128)(2,1)S(1)} %get-tuple-element.26.refs_7_.refs_8_) | copy-start | bytes 1179652
  27.9 46.8 %copy-start.1 = (bf16[8,192,128]{2,1,0:T(8,128)(2,1)}, bf16[8,192,128]{2,1,0:T(8,128)(2,1)S(1)}, u32[]{:S(2)}) copy-start(bf16[8,192,128]{2,1,0:T(8,128)(2,1)S(1)} %get-tuple-element.27.refs_0_) | copy-start | bytes 1179652
  27.9 14.4 %collective-permute-start.4 = (bf16[8,192,128]{2,1,0:T(8,128)(2,1)S(1)}, bf16[8,192,128]{2,1,0:T(8,128)(2,1)S(1)}, u32[]{:S(2)}, u32[]{:S(2)}) collective-permute-start(bf16[8,192,128]{2,1,0:T(8,128)(2,1)S(1)} %get-tuple-element.26.refs_7_.refs_8_), channel_id=1, source_target_pairs={{0,56},{8,0},{16,8},{24,16},{32,24},{40,32},{48,40},{56,48},{1,57}... | collective-permute-start | bytes 1179656 | tf_op jit(solution)/shard_map/ppermute | solution.py:186
  33.3 13.0 %collective-permute-start = (bf16[8,192,128]{2,1,0:T(8,128)(2,1)S(1)}, bf16[8,192,128]{2,1,0:T(8,128)(2,1)S(1)}, u32[]{:S(2)}, u32[]{:S(2)}) collective-permute-start(bf16[8,192,128]{2,1,0:T(8,128)(2,1)S(1)} %get-tuple-element.27.refs_0_), channel_id=1, source_target_pairs={{0,8},{8,16},{16,24},{24,32},{32,40},{40,48},{48,56},{56,0},{1,9},... | collective-permute-start | bytes 1179656 | tf_op jit(solution)/shard_map/ppermute | solution.py:186
  35.3 13.2 %collective-permute-start.11 = (bf16[8,192,128]{2,1,0:T(8,128)(2,1)S(1)}, bf16[8,192,128]{2,1,0:T(8,128)(2,1)S(1)}, u32[]{:S(2)}, u32[]{:S(2)}) collective-permute-start(bf16[8,192,128]{2,1,0:T(8,128)(2,1)S(1)} %get-tuple-element.26.refs_7_.refs_8_), channel_id=1, source_target_pairs={{0,8},{8,16},{16,24},{24,32},{32,40},{40,48},{48,56},{56,0},{1,9},... | collective-permute-start | bytes 1179656 | tf_op jit(solution)/shard_map/ppermute | solution.py:186
  37.3 13.1 %collective-permute-start.8 = (bf16[8,192,128]{2,1,0:T(8,128)(2,1)S(1)}, bf16[8,192,128]{2,1,0:T(8,128)(2,1)S(1)}, u32[]{:S(2)}, u32[]{:S(2)}) collective-permute-start(bf16[8,192,128]{2,1,0:T(8,128)(2,1)S(1)} %get-tuple-element.27.refs_0_), channel_id=1, source_target_pairs={{0,56},{8,0},{16,8},{24,16},{32,24},{40,32},{48,40},{56,48},{1,57}... | collective-permute-start | bytes 1179656 | tf_op jit(solution)/shard_map/ppermute | solution.py:186
  42.3 13.2 %collective-permute-start.5 = (bf16[8,192,128]{2,1,0:T(8,128)(2,1)S(1)}, bf16[8,192,128]{2,1,0:T(8,128)(2,1)S(1)}, u32[]{:S(2)}, u32[]{:S(2)}) collective-permute-start(bf16[8,192,128]{2,1,0:T(8,128)(2,1)S(1)} %collective-permute-done.4.refs_9_.refs_10_), channel_id=1, source_target_pairs={{0,56},{8,0},{16,8},{24,16},{32,24},{40,32},{48,40},{56,48},{1,57}... | collective-permute-start | bytes 1179656 | tf_op jit(solution)/shard_map/ppermute | solution.py:186
  46.3 13.0 %collective-permute-start.1 = (bf16[8,192,128]{2,1,0:T(8,128)(2,1)S(1)}, bf16[8,192,128]{2,1,0:T(8,128)(2,1)S(1)}, u32[]{:S(2)}, u32[]{:S(2)}) collective-permute-start(bf16[8,192,128]{2,1,0:T(8,128)(2,1)S(1)} %collective-permute-done.refs_1_), channel_id=1, source_target_pairs={{0,8},{8,16},{16,24},{24,32},{32,40},{40,48},{48,56},{56,0},{1,9},... | collective-permute-start | bytes 1179656 | tf_op jit(solution)/shard_map/ppermute | solution.py:186
  48.4 13.2 %collective-permute-start.12 = (bf16[8,192,128]{2,1,0:T(8,128)(2,1)S(1)}, bf16[8,192,128]{2,1,0:T(8,128)(2,1)}, u32[]{:S(2)}, u32[]{:S(2)}) collective-permute-start(bf16[8,192,128]{2,1,0:T(8,128)(2,1)S(1)} %collective-permute-done.11.refs_8_.refs_9_), channel_id=1, source_target_pairs={{0,8},{8,16},{16,24},{24,32},{32,40},{40,48},{48,56},{56,0},{1,9},... | collective-permute-start | bytes 1179656 | tf_op jit(solution)/shard_map/ppermute | solution.py:186
  50.4 13.2 %collective-permute-start.9 = (bf16[8,192,128]{2,1,0:T(8,128)(2,1)S(1)}, bf16[8,192,128]{2,1,0:T(8,128)(2,1)}, u32[]{:S(2)}, u32[]{:S(2)}) collective-permute-start(bf16[8,192,128]{2,1,0:T(8,128)(2,1)S(1)} %collective-permute-done.8.refs_2_), channel_id=1, source_target_pairs={{0,56},{8,0},{16,8},{24,16},{32,24},{40,32},{48,40},{56,48},{1,57}... | collective-permute-start | bytes 1179656 | tf_op jit(solution)/shard_map/ppermute | solution.py:186
  55.5 13.2 %collective-permute-start.6 = (bf16[8,192,128]{2,1,0:T(8,128)(2,1)S(1)}, bf16[8,192,128]{2,1,0:T(8,128)(2,1)}, u32[]{:S(2)}, u32[]{:S(2)}) collective-permute-start(bf16[8,192,128]{2,1,0:T(8,128)(2,1)S(1)} %collective-permute-done.5.refs_11_.refs_12_), channel_id=1, source_target_pairs={{0,56},{8,0},{16,8},{24,16},{32,24},{40,32},{48,40},{56,48},{1,57}... | collective-permute-start | bytes 1179656 | tf_op jit(solution)/shard_map/ppermute | solution.py:186
  59.3 13.2 %collective-permute-start.2 = (bf16[8,192,128]{2,1,0:T(8,128)(2,1)S(1)}, bf16[8,192,128]{2,1,0:T(8,128)(2,1)}, u32[]{:S(2)}, u32[]{:S(2)}) collective-permute-start(bf16[8,192,128]{2,1,0:T(8,128)(2,1)S(1)} %collective-permute-done.1.refs_3_), channel_id=1, source_target_pairs={{0,8},{8,16},{16,24},{24,32},{32,40},{40,48},{48,56},{56,0},{1,9},... | collective-permute-start | bytes 1179656 | tf_op jit(solution)/shard_map/ppermute | solution.py:186
  61.6 13.1 %collective-permute-start.13 = (bf16[8,192,128]{2,1,0:T(8,128)(2,1)}, bf16[8,192,128]{2,1,0:T(8,128)(2,1)S(1)}, u32[]{:S(2)}, u32[]{:S(2)}) collective-permute-start(bf16[8,192,128]{2,1,0:T(8,128)(2,1)} %collective-permute-done.12.refs_10_.refs_11_), channel_id=1, source_target_pairs={{0,8},{8,16},{16,24},{24,32},{32,40},{40,48},{48,56},{56,0},{1,9},... | collective-permute-start | bytes 1179656 | tf_op jit(solution)/shard_map/ppermute | solution.py:186
  63.5 11.2 %collective-permute-start.10 = (bf16[8,192,128]{2,1,0:T(8,128)(2,1)}, bf16[8,192,128]{2,1,0:T(8,128)(2,1)S(1)}, u32[]{:S(2)}, u32[]{:S(2)}) collective-permute-start(bf16[8,192,128]{2,1,0:T(8,128)(2,1)} %collective-permute-done.9.refs_4_), channel_id=1, source_target_pairs={{0,56},{8,0},{16,8},{24,16},{32,24},{40,32},{48,40},{56,48},{1,57}... | collective-permute-start | bytes 1179656 | tf_op jit(solution)/shard_map/ppermute | solution.py:186
  68.7 13.9 %collective-permute-start.7 = (bf16[8,192,128]{2,1,0:T(8,128)(2,1)}, bf16[8,192,128]{2,1,0:T(8,128)(2,1)S(1)}, u32[]{:S(2)}, u32[]{:S(2)}) collective-permute-start(bf16[8,192,128]{2,1,0:T(8,128)(2,1)} %collective-permute-done.6.refs_13_.refs_14_), channel_id=1, source_target_pairs={{0,56},{8,0},{16,8},{24,16},{32,24},{40,32},{48,40},{56,48},{1,57}... | collective-permute-start | bytes 1179656 | tf_op jit(solution)/shard_map/ppermute | solution.py:186
  72.5 11.1 %collective-permute-start.3 = (bf16[8,192,128]{2,1,0:T(8,128)(2,1)}, bf16[8,192,128]{2,1,0:T(8,128)(2,1)S(1)}, u32[]{:S(2)}, u32[]{:S(2)}) collective-permute-start(bf16[8,192,128]{2,1,0:T(8,128)(2,1)} %collective-permute-done.2.refs_5_), channel_id=1, source_target_pairs={{0,8},{8,16},{16,24},{24,32},{32,40},{40,48},{48,56},{56,0},{1,9},... | collective-permute-start | bytes 1179656 | tf_op jit(solution)/shard_map/ppermute | solution.py:186
  90.0 46.1 %all-to-all-start.1 = ((bf16[8,8,192,128]{3,2,1,0:T(8,128)(2,1)}), bf16[8,8,192,128]{3,2,1,0:T(8,128)(2,1)}, u32[]{:S(2)}, u32[]{:S(2)}) async-start(bf16[8,8,192,128]{3,2,1,0:T(8,128)(2,1)} %bitcast.8), calls=%async_computation.1 | async-start | bytes 6291456 | tf_op jit(solution)/shard_map/all_to_all | solution.py:180
  100.3 6.1 %collective-permute-start.14 = (bf16[4,2,4,2,128,128]{5,4,3,2,1,0:T(8,128)(2,1)S(1)}, bf16[4,2,4,2,128,128]{5,4,3,2,1,0:T(8,128)(2,1)S(1)}, u32[]{:S(2)}, u32[]{:S(2)}) collective-permute-start(bf16[4,2,4,2,128,128]{5,4,3,2,1,0:T(8,128)(2,1)S(1)} %get-tuple-element.20), channel_id=1, source_target_pairs={{0,64},{64,0},{1,65},{65,1},{2,66},{66,2},{3,67},{67,3},{4,68},{68... | collective-permute-start | bytes 6291464 | tf_op jit(solution)/shard_map/ppermute | solution.py:260
  109.2 33.2 %collective-permute-start.15 = (bf16[2,4,2,128,128]{4,3,2,1,0:T(8,128)(2,1)}, bf16[2,4,2,128,128]{4,3,2,1,0:T(8,128)(2,1)}, u32[]{:S(2)}, u32[]{:S(2)}) collective-permute-start(bf16[2,4,2,128,128]{4,3,2,1,0:T(8,128)(2,1)} %get-tuple-element.23), channel_id=1, source_target_pairs={{0,128},{128,256},{256,384},{384,0},{1,129},{129,257},{257,385},{3... | collective-permute-start | bytes 1572872 | tf_op jit(solution)/shard_map/ppermute | solution.py:263
  111.5 30.8 %collective-permute-start.17 = (bf16[2,4,2,128,128]{4,3,2,1,0:T(8,128)(2,1)S(1)}, bf16[2,4,2,128,128]{4,3,2,1,0:T(8,128)(2,1)}, u32[]{:S(2)}, u32[]{:S(2)}) collective-permute-start(bf16[2,4,2,128,128]{4,3,2,1,0:T(8,128)(2,1)S(1)} %get-tuple-element.24), channel_id=1, source_target_pairs={{0,384},{128,0},{256,128},{384,256},{1,385},{129,1},{257,129},{385... | collective-permute-start | bytes 1572872 | tf_op jit(solution)/shard_map/ppermute | solution.py:263
  115.0 27.3 %collective-permute-start.16 = (bf16[2,4,2,128,128]{4,3,2,1,0:T(8,128)(2,1)S(1)}, bf16[2,4,2,128,128]{4,3,2,1,0:T(8,128)(2,1)}, u32[]{:S(2)}, u32[]{:S(2)}) collective-permute-start(bf16[2,4,2,128,128]{4,3,2,1,0:T(8,128)(2,1)S(1)} %get-tuple-element.25), channel_id=1, source_target_pairs={{0,256},{128,384},{256,0},{384,128},{1,257},{129,385},{257,1},{385... | collective-permute-start | bytes 1572872 | tf_op jit(solution)/shard_map/ppermute | solution.py:263
  138.9 15.3 %all-to-all-start.2 = ((bf16[8,192,128]{2,1,0:T(8,128)(2,1)}), bf16[8,192,128]{2,1,0:T(8,128)(2,1)S(1)}, u32[]{:S(2)}, u32[]{:S(2)}) async-start(bf16[8,192,128]{2,1,0:T(8,128)(2,1)} %sums.1), calls=%async_computation.2 | async-start | bytes 786432 | tf_op jit(solution)/shard_map/all_to_all | solution.py:180
  (9 other events, 140.9 us)

commit v6 on v5

--- a/solution.py
+++ b/solution.py
@@ -42,12 +42,24 @@
     return jnp.concatenate([blocks[where[line, r * per_row + k]] for k in range(per_row)], axis=1)
 
 
+def last_kernel(where, w_in, w_out, in_last, out_last):
+    rows, per_row, width, _ = w_in.shape
+    in_last[...] = jnp.zeros_like(in_last)
+    out_last[...] = jnp.zeros_like(out_last)
+    for r in range(rows):
+        at = slice(r * width, (r + 1) * width)
+        for k in range(per_row):
+            in_last[where[3, r * per_row + k], :, at] = w_in[r, k]
+            out_last[where[4, r * per_row + k], :, at] = w_out[r, k].T
+
+
 def early_kernel(plans, where, *refs):
     (side, x_steps), (_, y_steps) = plans
     n_x, n_y = len(x_steps), len(y_steps)
     x_units = list(zip(refs[:n_x], x_steps))
     y_units = list(zip(refs[n_x : n_x + n_y], y_steps))
-    w_in, w_out, hidden, grad_act, wi, wo, x, y, x_sem, y_sem, w_sem = refs[n_x + n_y :]
+    w_in, w_out, in_last, out_last = refs[n_x + n_y : n_x + n_y + 4]
+    hidden, grad_act, wi, li, lo, wo, x, y, x_sem, y_sem, w_sem = refs[n_x + n_y + 4 :]
     rows, per_row, width, _ = w_in.shape
     load_in = pltpu.make_async_copy(w_in, wi, w_sem.at[0])
     load_out = pltpu.make_async_copy(w_out, wo, w_sem.at[1])
@@ -55,6 +67,12 @@
     x_loads = start_loads(where, x_units, x, x_sem, side)
     load_out.start()
     y_loads = start_loads(where, y_units, y, y_sem, side)
+    lasts = [
+        pltpu.make_async_copy(ref.at[pl.ds(0, side)], into, w_sem.at[2 + n])
+        for n, (ref, into) in enumerate(((in_last, li), (out_last, lo)))
+    ]
+    for copy in lasts:
+        copy.start()
     places = x.shape[0] // side
     opposite = pl.ds(lax.rem(where[2, 1] + places // 2, places) * side, side)
     x[opposite] = jnp.zeros((side, *x.shape[1:]), BF16)
@@ -64,44 +82,41 @@
         copy.wait()
     for r in range(rows):
         x_row = row_of(x, where, 0, r, per_row)
-        hidden[r] = dot_nn(x_row, wi[r].reshape(per_row * width, width))
+        at = slice(r * width, (r + 1) * width)
+        hidden[:, at] = dot_nn(x_row, wi[r].reshape(per_row * width, width))
     load_out.wait()
     for copy in y_loads:
         copy.wait()
     for r in range(rows):
         w_row = jnp.concatenate([wo[r, k] for k in range(per_row)], axis=1)
-        grad_act[r] = dot_nt(row_of(y, where, 1, r, per_row), w_row)
-
-
-def back_kernel(where, x_last, y_last, hidden_most, grad_most, wi, wo, *refs):
-    placed, act, grad, x, y, total, rounded, sem, out_sem = refs
+        at = slice(r * width, (r + 1) * width)
+        grad_act[:, at] = dot_nt(row_of(y, where, 1, r, per_row), w_row)
+    for copy in lasts:
+        copy.wait()
+
+
+def back_kernel(where, x_last, y_last, hidden_most, grad_most, wi, li, lo, *refs):
+    placed, act, grad, total, rounded, out_sem = refs
     rows, per_row, width, _ = wi.shape
     blocks, side = total.shape[0], x_last.shape[0]
-    load_x = pltpu.make_async_copy(x_last, x.at[pl.ds(0, side)], sem.at[0])
-    load_y = pltpu.make_async_copy(y_last, y.at[pl.ds(0, side)], sem.at[1])
-    load_x.start()
-    load_y.start()
-    x[side] = jnp.zeros(x.shape[1:], BF16)
-    y[side] = jnp.zeros(y.shape[1:], BF16)
     total[...] = jnp.zeros_like(total)
-    load_x.wait()
-    load_y.wait()
-    for r in range(rows):
-        x_row = row_of(x, where, 3, r, per_row)
-        y_row = row_of(y, where, 4, r, per_row)
-        w_row = jnp.concatenate([wo[r, k] for k in range(per_row)], axis=1)
-        hidden = hidden_most[r] + dot_nn(x_row, wi[r].reshape(per_row * width, width))
-        grad_act = grad_most[r] + dot_nt(y_row, w_row)
-        square = hidden * hidden
-        tanh = jnp.tanh(GELU_SCALE * hidden * (1.0 + GELU_CUBE * square))
-        half = 0.5 * (1.0 + tanh)
-        act[r] = (hidden * half).astype(BF16)
-        slope = half + 0.5 * hidden * (1.0 - tanh * tanh) * (
-            GELU_SCALE * (1.0 + 3.0 * GELU_CUBE * square)
-        )
-        grad_hidden = (grad_act * slope).astype(BF16)
-        grad[r] = grad_hidden
-        terms = dot_nt(grad_hidden, wi[r].reshape(per_row * width, width))
+    x_unit = jnp.concatenate([x_last[n] for n in range(side)], axis=1)
+    y_unit = jnp.concatenate([y_last[n] for n in range(side)], axis=1)
+    hidden = hidden_most[...] + dot_nn(x_unit, li[...].reshape(side * width, rows * width))
+    grad_act = grad_most[...] + dot_nn(y_unit, lo[...].reshape(side * width, rows * width))
+    square = hidden * hidden
+    tanh = jnp.tanh(GELU_SCALE * hidden * (1.0 + GELU_CUBE * square))
+    half = 0.5 * (1.0 + tanh)
+    slope = half + 0.5 * hidden * (1.0 - tanh * tanh) * (
+        GELU_SCALE * (1.0 + 3.0 * GELU_CUBE * square)
+    )
+    activated = (hidden * half).astype(BF16)
+    grad_hidden = (grad_act * slope).astype(BF16)
+    for r in range(rows):
+        at = slice(r * width, (r + 1) * width)
+        act[r] = activated[:, at]
+        grad[r] = grad_hidden[:, at]
+        terms = dot_nt(grad_hidden[:, at], wi[r].reshape(per_row * width, width))
         for k in range(per_row):
             c = where[0, r * per_row + k]
             total[c] = total[c] + terms[:, k * width : (k + 1) * width]
@@ -185,8 +200,28 @@
         pairs = [(g[i], g[(i + by) % side]) for g in rings for i in range(side)]
         return lax.ppermute(values, CYZ, pairs)
 
+    core, y_at, z_at = (lax.axis_index(a) for a in CYZ)
+    cols = jnp.stack([cols_in.reshape(-1), cols_out.reshape(-1)])
+    cols = jnp.where(core == 0, cols, cols % nz * ny + cols // nz)
+    place = jnp.where(core == 0, y_at, z_at)
+    here = jnp.stack([core, place, lax.axis_index("x")]).astype(jnp.int32)
+    here = jnp.pad(here, (0, rows * per_row - 3)).reshape(1, -1)
+    opposite = (place + ny // 2) % ny
+    lasts = jnp.where(cols // side == opposite, cols % side, side)
+    where = jnp.concatenate([cols, here, lasts])
+
     mine = jnp.stack([inputs, upstream])
     unit = swap(jnp.broadcast_to(mine, (side, *mine.shape)), lines)
+    dense = jax.ShapeDtypeStruct((side + 1, width, rows * width), BF16)
+    in_last, out_last = pl.pallas_call(
+        last_kernel,
+        out_shape=(dense, dense),
+        in_specs=[smem, vmem, vmem],
+        out_specs=(vmem, vmem),
+        compiler_params=params,
+        name="last",
+    )(where, w_in, w_out)
+    unit, in_last, out_last = lax.optimization_barrier((unit, in_last, out_last))
     x_units, y_units = [unit[:, 0]], [unit[:, 1]]
     x_steps, y_steps = [0], [0]
     x_ahead = x_back = x_units[0]
@@ -205,45 +240,39 @@
     x_units, y_units = ([in_hbm(u) for u in us[:-1]] + us[-1:] for us in (x_units, y_units))
     x_plan, y_plan = (side, tuple(x_steps)), (side, tuple(y_steps))
 
-    core, y_at, z_at = (lax.axis_index(a) for a in CYZ)
-    cols = jnp.stack([cols_in.reshape(-1), cols_out.reshape(-1)])
-    cols = jnp.where(core == 0, cols, cols % nz * ny + cols // nz)
-    place = jnp.where(core == 0, y_at, z_at)
-    here = jnp.stack([core, place, lax.axis_index("x")]).astype(jnp.int32)
-    here = jnp.pad(here, (0, rows * per_row - 3)).reshape(1, -1)
-    opposite = (place + ny // 2) % ny
-    lasts = jnp.where(cols // side == opposite, cols % side, side)
-    where = jnp.concatenate([cols, here, lasts])
-
     gathered = pltpu.VMEM((blocks, tok, width), BF16)
     loaded = pltpu.SemaphoreType.DMA((side,))
     values = jax.ShapeDtypeStruct((rows, tok, width), BF16)
-    kept = jax.ShapeDtypeStruct((rows, tok, width), F32)
-    hidden_most, grad_most, wi, wo = pl.pallas_call(
+    kept = pltpu.VMEM((tok, rows * width), F32)
+    last = pltpu.VMEM((side, width, rows * width), BF16)
+    hidden_most, grad_most, wi, li, lo = pl.pallas_call(
         functools.partial(early_kernel, ((side, x_plan[1][:-1]), (side, y_plan[1][:-1]))),
-        out_shape=(kept, kept, pltpu.VMEM(w_in.shape, BF16), pltpu.VMEM(w_out.shape, BF16)),
-        in_specs=[smem] + [anywhere] * (len(x_units) + len(y_units)),
-        scratch_shapes=[gathered, gathered, loaded, loaded, pltpu.SemaphoreType.DMA((2,))],
+        out_shape=(kept, kept, pltpu.VMEM(w_in.shape, BF16), last, last),
+        in_specs=[smem] + [anywhere] * (len(x_units) + len(y_units) + 2),
+        scratch_shapes=[
+            pltpu.VMEM(w_out.shape, BF16),
+            gathered,
+            gathered,
+            loaded,
+            loaded,
+            pltpu.SemaphoreType.DMA((4,)),
+        ],
         compiler_params=params,
         name="early",
-    )(where, *x_units[:-1], *y_units[:-1], in_hbm(w_in), in_hbm(w_out))
-    last = pltpu.VMEM((side + 1, tok, width), BF16)
+    )(where, *x_units[:-1], *y_units[:-1], *(in_hbm(v) for v in (w_in, w_out, in_last, out_last)))
     placed, act, grad = pl.pallas_call(
         back_kernel,
         out_shape=(jax.ShapeDtypeStruct((blocks, tok, width), BF16), values, values),
-        in_specs=[smem] + [anywhere] * 2 + [vmem] * 4,
+        in_specs=[smem] + [vmem] * 7,
         out_specs=(anywhere, vmem, vmem),
         scratch_shapes=[
-            last,
-            last,
             pltpu.VMEM((blocks, tok, width), F32),
             pltpu.VMEM((blocks, tok, width), BF16),
-            pltpu.SemaphoreType.DMA((2,)),
             pltpu.SemaphoreType.DMA((SLABS,)),
         ],
         compiler_params=params,
         name="back",
-    )(where, x_units[-1], y_units[-1], hidden_most, grad_most, wi, wo)
+    )(where, x_units[-1], y_units[-1], hidden_most, grad_most, wi, li, lo)
 
     on_ring = swap(placed.reshape(side, blocks // side, tok, width), rings)
 

time: 156 us -> 155 us (level)
  blocking collectives: 26.2 us -> 0 us
  starting transfers between devices: 65 us -> 76 us
  waiting for transfers between devices: 32.1 us -> 42 us
  local copies, waits for them, and re-layouts: 4.06 us -> 8.58 us
    all_to_all x1 -> x0, blocking collectives: 26.2 us -> none  [swap(): lax.all_to_all(values, CYZ, split_axis=0, concat_axis=0, tiled=True, axis...]
    all_to_all x2 -> x3, starting transfers between devices: 7.99 us -> 19 us  [swap(): lax.all_to_all(values, CYZ, split_axis=0, concat_axis=0, tiled=True, axis...]
    all_to_all x2 -> x3, waiting for transfers between devices: 26.8 us -> 37.4 us  [swap(): lax.all_to_all(values, CYZ, split_axis=0, concat_axis=0, tiled=True, axis...]
    unnamed x26 -> x42, local copies, waits for them, and re-layouts: 2.85 us -> 6.49 us
    pallas_call x1, Pallas kernels: 6.45 us -> 4.5 us  [per_device(): pl.pallas_call(back_kernel, out_shape=(jax.ShapeDtypeStruct((blocks, tok,...]
    pallas_call x0 -> x1, Pallas kernels: none -> 1.58 us  [per_device(): pl.pallas_call(last_kernel, out_shape=(dense, dense), in_specs=[smem, vme...]
  transfers between devices with their start and end apart: 20 -> 21, of which waited for: 5 -> 6; matrix products, arithmetic and copies ran while one was open for 3% -> 3% of each run, Pallas kernels for 10% -> 11%
where the time goes in v6:
time: 155 us; the launch traced here: 154 us
  starting transfers between devices  76 us (49%)
  waiting for transfers between devices  42 us (27%)
  Pallas kernels  21.5 us (14%)
  local copies, waits for them, and re-layouts  8.58 us (6%)
  other arithmetic  5.05 us (3%)
    ppermute x14, starting transfers between devices, turn(): return lax.ppermute(values, CYZ, pairs)  46 us
    all_to_all x3, waiting for transfers between devices, swap(): lax.all_to_all(values, CYZ, split_axis=0, concat_axis=0, tiled=True, axis...  37.4 us
    all_to_all x3, starting transfers between devices, swap(): lax.all_to_all(values, CYZ, split_axis=0, concat_axis=0, tiled=True, axis...  19 us
    ppermute x3, starting transfers between devices, per_device(): lax.ppermute(paired[d], 'x', [(i, (i + d) % nx) for i in range(nx)])  9.15 us
    pallas_call x1, Pallas kernels, per_device(): pl.pallas_call(functools.partial(early_kernel, ((side, x_plan[1][:-1]), (...  6.97 us
    unnamed x42, local copies, waits for them, and re-layouts  6.49 us
    pallas_call x1, Pallas kernels, per_device(): pl.pallas_call(functools.partial(weight_kernel, (x_plan, y_plan)), out_sh...  5.77 us
    pallas_call x1, Pallas kernels, per_device(): pl.pallas_call(back_kernel, out_shape=(jax.ShapeDtypeStruct((blocks, tok,...  4.5 us
  transfers between devices with their start and end apart: 21, of which 6 were waited for; matrix products, arithmetic and copies ran while one was open for 3% of the time, Pallas kernels for 11%

profile of v6, /device:TPU:6, one launch (start us, length us, event | category | flops | bytes accessed | tf_op | source)
XLA Modules:
  0.0 154.4 jit_solution(17824626993948198623)
XLA Ops:
  2.7 10.3 %all-to-all-start = ((bf16[8,2,192,128]{3,2,1,0:T(8,128)(2,1)}), bf16[8,2,192,128]{3,2,1,0:T(8,128)(2,1)S(1)}, u32[]{:S(2)}, u32[]{:S(2)}) async-start(bf16[8,2,192,128]{3,2,1,0:T(8,128)(2,1)} %broadcast_in_dim.5), calls=%async_computation | async-start | bytes 1572864 | tf_op jit(solution)/shard_map/all_to_all | solution.py:195
  18.6 10.5 %all-to-all-done = bf16[8,2,192,128]{3,2,1,0:T(8,128)(2,1)S(1)} async-done(((bf16[8,2,192,128]{3,2,1,0:T(8,128)(2,1)}), bf16[8,2,192,128]{3,2,1,0:T(8,128)(2,1)S(1)}, u32[]{:S(2)}, u32[]{:S(2)}) %all-to-all-start) | async-done | bytes 786464 | tf_op jit(solution)/shard_map/all_to_all | solution.py:195
  29.2 5.4 %collective-permute-start.4 = (bf16[8,192,128]{2,1,0:T(8,128)(2,1)S(1)}, bf16[8,192,128]{2,1,0:T(8,128)(2,1)S(1)}, u32[]{:S(2)}, u32[]{:S(2)}) collective-permute-start(bf16[8,192,128]{2,1,0:T(8,128)(2,1)S(1)} %get-tuple-element.38.refs_7_.refs_8_), channel_id=1, source_target_pairs={{0,56},{8,0},{16,8},{24,16},{32,24},{40,32},{48,40},{56,48},{1,57}... | collective-permute-start | bytes 1179656 | tf_op jit(solution)/shard_map/ppermute | solution.py:201
  36.5 2.0 %collective-permute-start.11 = (bf16[8,192,128]{2,1,0:T(8,128)(2,1)S(1)}, bf16[8,192,128]{2,1,0:T(8,128)(2,1)S(1)}, u32[]{:S(2)}, u32[]{:S(2)}) collective-permute-start(bf16[8,192,128]{2,1,0:T(8,128)(2,1)S(1)} %get-tuple-element.38.refs_7_.refs_8_), channel_id=1, source_target_pairs={{0,8},{8,16},{16,24},{24,32},{32,40},{40,48},{48,56},{56,0},{1,9},... | collective-permute-start | bytes 1179656 | tf_op jit(solution)/shard_map/ppermute | solution.py:201
  38.6 5.0 %collective-permute-start.8 = (bf16[8,192,128]{2,1,0:T(8,128)(2,1)S(1)}, bf16[8,192,128]{2,1,0:T(8,128)(2,1)S(1)}, u32[]{:S(2)}, u32[]{:S(2)}) collective-permute-start(bf16[8,192,128]{2,1,0:T(8,128)(2,1)S(1)} %get-tuple-element.39.refs_0_), channel_id=1, source_target_pairs={{0,56},{8,0},{16,8},{24,16},{32,24},{40,32},{48,40},{56,48},{1,57}... | collective-permute-start | bytes 1179656 | tf_op jit(solution)/shard_map/ppermute | solution.py:201
  43.6 3.9 %collective-permute-start.5 = (bf16[8,192,128]{2,1,0:T(8,128)(2,1)S(1)}, bf16[8,192,128]{2,1,0:T(8,128)(2,1)S(1)}, u32[]{:S(2)}, u32[]{:S(2)}) collective-permute-start(bf16[8,192,128]{2,1,0:T(8,128)(2,1)S(1)} %collective-permute-done.4.refs_9_.refs_10_), channel_id=1, source_target_pairs={{0,56},{8,0},{16,8},{24,16},{32,24},{40,32},{48,40},{56,48},{1,57}... | collective-permute-start | bytes 1179656 | tf_op jit(solution)/shard_map/ppermute | solution.py:201
  51.6 5.1 %collective-permute-start.9 = (bf16[8,192,128]{2,1,0:T(8,128)(2,1)S(1)}, bf16[8,192,128]{2,1,0:T(8,128)(2,1)S(1)}, u32[]{:S(2)}, u32[]{:S(2)}) collective-permute-start(bf16[8,192,128]{2,1,0:T(8,128)(2,1)S(1)} %collective-permute-done.8.refs_2_), channel_id=1, source_target_pairs={{0,56},{8,0},{16,8},{24,16},{32,24},{40,32},{48,40},{56,48},{1,57}... | collective-permute-start | bytes 1179656 | tf_op jit(solution)/shard_map/ppermute | solution.py:201
  56.8 3.8 %collective-permute-start.6 = (bf16[8,192,128]{2,1,0:T(8,128)(2,1)S(1)}, bf16[8,192,128]{2,1,0:T(8,128)(2,1)S(1)}, u32[]{:S(2)}, u32[]{:S(2)}) collective-permute-start(bf16[8,192,128]{2,1,0:T(8,128)(2,1)S(1)} %collective-permute-done.5.refs_11_.refs_12_), channel_id=1, source_target_pairs={{0,56},{8,0},{16,8},{24,16},{32,24},{40,32},{48,40},{56,48},{1,57}... | collective-permute-start | bytes 1179656 | tf_op jit(solution)/shard_map/ppermute | solution.py:201
  60.6 2.1 %collective-permute-start.2 = (bf16[8,192,128]{2,1,0:T(8,128)(2,1)S(1)}, bf16[8,192,128]{2,1,0:T(8,128)(2,1)S(1)}, u32[]{:S(2)}, u32[]{:S(2)}) collective-permute-start(bf16[8,192,128]{2,1,0:T(8,128)(2,1)S(1)} %collective-permute-done.1.refs_3_), channel_id=1, source_target_pairs={{0,8},{8,16},{16,24},{24,32},{32,40},{40,48},{48,56},{56,0},{1,9},... | collective-permute-start | bytes 1179656 | tf_op jit(solution)/shard_map/ppermute | solution.py:201
  64.6 5.1 %collective-permute-start.10 = (bf16[8,192,128]{2,1,0:T(8,128)(2,1)S(1)}, bf16[8,192,128]{2,1,0:T(8,128)(2,1)S(1)}, u32[]{:S(2)}, u32[]{:S(2)}) collective-permute-start(bf16[8,192,128]{2,1,0:T(8,128)(2,1)S(1)} %collective-permute-done.9.refs_4_), channel_id=1, source_target_pairs={{0,56},{8,0},{16,8},{24,16},{32,24},{40,32},{48,40},{56,48},{1,57}... | collective-permute-start | bytes 1179656 | tf_op jit(solution)/shard_map/ppermute | solution.py:201
  69.8 3.8 %collective-permute-start.7 = (bf16[8,192,128]{2,1,0:T(8,128)(2,1)S(1)}, bf16[8,192,128]{2,1,0:T(8,128)(2,1)S(1)}, u32[]{:S(2)}, u32[]{:S(2)}) collective-permute-start(bf16[8,192,128]{2,1,0:T(8,128)(2,1)S(1)} %collective-permute-done.6.refs_13_.refs_14_), channel_id=1, source_target_pairs={{0,56},{8,0},{16,8},{24,16},{32,24},{40,32},{48,40},{56,48},{1,57}... | collective-permute-start | bytes 1179656 | tf_op jit(solution)/shard_map/ppermute | solution.py:201
  73.6 2.1 %collective-permute-start.3 = (bf16[8,192,128]{2,1,0:T(8,128)(2,1)S(1)}, bf16[8,192,128]{2,1,0:T(8,128)(2,1)S(1)}, u32[]{:S(2)}, u32[]{:S(2)}) collective-permute-start(bf16[8,192,128]{2,1,0:T(8,128)(2,1)S(1)} %collective-permute-done.2.refs_5_), channel_id=1, source_target_pairs={{0,8},{8,16},{16,24},{24,32},{32,40},{40,48},{48,56},{56,0},{1,9},... | collective-permute-start | bytes 1179656 | tf_op jit(solution)/shard_map/ppermute | solution.py:201
  77.2 7.0 %early.1 = (f32[192,512]{1,0:T(8,128)S(1)}, f32[192,512]{1,0:T(8,128)S(1)}, bf16[4,16,128,128]{3,2,1,0:T(8,128)(2,1)S(1)}, bf16[8,128,512]{2,1,0:T(8,128)(2,1)S(1)}, bf16[8,128,512]{2,1,0:T(8,128)(2,1)S(1)}) custom-call(s32[5,64]{1,0:T(8,128)S(1)} %pad_add_fusion.where, bf16[8,192,128]{2,1,0:T(8,128)(2,1)} %copy-done.5, bf16[8,192,128]{2,1,0:T(8,128)(2,1)} %copy-done.8, ...), custom_call_target="tpu_custom_call" | custom-call | tf_op jit(solution)/shard_map/early/pallas_call | solution.py:248
  84.5 4.5 %back.1 = (bf16[64,192,128]{2,1,0:T(8,128)(2,1)}, bf16[4,192,128]{2,1,0:T(8,128)(2,1)S(1)}, bf16[4,192,128]{2,1,0:T(8,128)(2,1)S(1)}) custom-call(s32[5,64]{1,0:T(8,128)S(1)} %pad_add_fusion.where, bf16[8,192,128]{2,1,0:T(8,128)(2,1)S(1)} %collective-permute-done.3.x_last.refs_7_, bf16[8,192,128]{2,1,0:T(8,128)(2,1)S(1)} %collective-permute-done.7.y_last.refs_15_, ...), custom_call_target="tpu_custom_call" | custom-call | tf_op jit(solution)/shard_map/back/pallas_call | solution.py:263
  89.0 5.2 %all-to-all-start.1 = ((bf16[8,8,192,128]{3,2,1,0:T(8,128)(2,1)}), bf16[8,8,192,128]{3,2,1,0:T(8,128)(2,1)}, u32[]{:S(2)}, u32[]{:S(2)}) async-start(bf16[8,8,192,128]{3,2,1,0:T(8,128)(2,1)} %bitcast.8), calls=%async_computation.1 | async-start | bytes 6291456 | tf_op jit(solution)/shard_map/all_to_all | solution.py:195
  94.2 5.8 %weights.1 = (bf16[4,2,4,2,128,128]{5,4,3,2,1,0:T(8,128)(2,1)S(1)}, bf16[4,2,4,2,128,128]{5,4,3,2,1,0:T(8,128)(2,1)S(1)}) custom-call(s32[5,64]{1,0:T(8,128)S(1)} %pad_add_fusion.where, bf16[8,192,128]{2,1,0:T(8,128)(2,1)} %copy-done.5, bf16[8,192,128]{2,1,0:T(8,128)(2,1)} %copy-done.8, bf16[8,192,128]{2,1,0:T(8,128)(2,1)} %copy-done.10, ...), custom_call_target="tpu_custom_call" | custom-call | tf_op jit(solution)/shard_map/weights/pallas_call | solution.py:280
  101.9 4.1 %collective-permute-done.14 = bf16[4,2,4,2,128,128]{5,4,3,2,1,0:T(8,128)(2,1)S(1)} collective-permute-done((bf16[4,2,4,2,128,128]{5,4,3,2,1,0:T(8,128)(2,1)S(1)}, bf16[4,2,4,2,128,128]{5,4,3,2,1,0:T(8,128)(2,1)S(1)}, u32[]{:S(2)}, u32[]{:S(2)}) %collective-permute-start.14) | collective-permute-done | bytes 2097184 | tf_op jit(solution)/shard_map/ppermute | solution.py:289
  108.7 2.4 %collective-permute-start.15 = (bf16[2,4,2,128,128]{4,3,2,1,0:T(8,128)(2,1)}, bf16[2,4,2,128,128]{4,3,2,1,0:T(8,128)(2,1)}, u32[]{:S(2)}, u32[]{:S(2)}) collective-permute-start(bf16[2,4,2,128,128]{4,3,2,1,0:T(8,128)(2,1)} %get-tuple-element.35), channel_id=1, source_target_pairs={{0,128},{128,256},{256,384},{384,0},{1,129},{129,257},{257,385},{3... | collective-permute-start | bytes 1572872 | tf_op jit(solution)/shard_map/ppermute | solution.py:292
  111.1 3.5 %collective-permute-start.17 = (bf16[2,4,2,128,128]{4,3,2,1,0:T(8,128)(2,1)S(1)}, bf16[2,4,2,128,128]{4,3,2,1,0:T(8,128)(2,1)}, u32[]{:S(2)}, u32[]{:S(2)}) collective-permute-start(bf16[2,4,2,128,128]{4,3,2,1,0:T(8,128)(2,1)S(1)} %get-tuple-element.36), channel_id=1, source_target_pairs={{0,384},{128,0},{256,128},{384,256},{1,385},{129,1},{257,129},{385... | collective-permute-start | bytes 1572872 | tf_op jit(solution)/shard_map/ppermute | solution.py:292
  114.6 3.3 %collective-permute-start.16 = (bf16[2,4,2,128,128]{4,3,2,1,0:T(8,128)(2,1)S(1)}, bf16[2,4,2,128,128]{4,3,2,1,0:T(8,128)(2,1)}, u32[]{:S(2)}, u32[]{:S(2)}) collective-permute-start(bf16[2,4,2,128,128]{4,3,2,1,0:T(8,128)(2,1)S(1)} %get-tuple-element.37), channel_id=1, source_target_pairs={{0,256},{128,384},{256,0},{384,128},{1,257},{129,385},{257,1},{385... | collective-permute-start | bytes 1572872 | tf_op jit(solution)/shard_map/ppermute | solution.py:292
  117.9 17.8 %all-to-all-done.1.parts = bf16[8,8,192,128]{3,2,1,0:T(8,128)(2,1)} async-done(((bf16[8,8,192,128]{3,2,1,0:T(8,128)(2,1)}), bf16[8,8,192,128]{3,2,1,0:T(8,128)(2,1)}, u32[]{:S(2)}, u32[]{:S(2)}) %all-to-all-start.1) | async-done | bytes 3145760 | tf_op jit(solution)/shard_map/all_to_all | solution.py:195
  135.8 2.7 %sums.1 = bf16[8,192,128]{2,1,0:T(8,128)(2,1)} custom-call(bf16[8,8,192,128]{3,2,1,0:T(8,128)(2,1)} %all-to-all-done.1.parts), custom_call_target="tpu_custom_call" | custom-call | tf_op jit(solution)/shard_map/sums/pallas_call | solution.py:296
  138.5 3.5 %all-to-all-start.2 = ((bf16[8,192,128]{2,1,0:T(8,128)(2,1)}), bf16[8,192,128]{2,1,0:T(8,128)(2,1)S(1)}, u32[]{:S(2)}, u32[]{:S(2)}) async-start(bf16[8,192,128]{2,1,0:T(8,128)(2,1)} %sums.1), calls=%async_computation.2 | async-start | bytes 786432 | tf_op jit(solution)/shard_map/all_to_all | solution.py:195
  144.7 9.0 %all-to-all-done.2 = bf16[8,192,128]{2,1,0:T(8,128)(2,1)S(1)} async-done(((bf16[8,192,128]{2,1,0:T(8,128)(2,1)}), bf16[8,192,128]{2,1,0:T(8,128)(2,1)S(1)}, u32[]{:S(2)}, u32[]{:S(2)}) %all-to-all-start.2) | async-done | bytes 393248 | tf_op jit(solution)/shard_map/all_to_all | solution.py:195
  (78 shorter events, 25.3 us)
Async XLA Ops:
  2.7 26.5 %all-to-all-start = ((bf16[8,2,192,128]{3,2,1,0:T(8,128)(2,1)}), bf16[8,2,192,128]{3,2,1,0:T(8,128)(2,1)S(1)}, u32[]{:S(2)}, u32[]{:S(2)}) async-start(bf16[8,2,192,128]{3,2,1,0:T(8,128)(2,1)} %broadcast_in_dim.5), calls=%async_computation | async-start | bytes 1572864 | tf_op jit(solution)/shard_map/all_to_all | solution.py:195
  29.2 46.5 %copy-start.4 = (bf16[8,192,128]{2,1,0:T(8,128)(2,1)}, bf16[8,192,128]{2,1,0:T(8,128)(2,1)S(1)}, u32[]{:S(2)}) copy-start(bf16[8,192,128]{2,1,0:T(8,128)(2,1)S(1)} %get-tuple-element.38.refs_7_.refs_8_) | copy-start | bytes 1179652
  29.2 46.5 %copy-start.5 = (bf16[8,192,128]{2,1,0:T(8,128)(2,1)}, bf16[8,192,128]{2,1,0:T(8,128)(2,1)S(1)}, u32[]{:S(2)}) copy-start(bf16[8,192,128]{2,1,0:T(8,128)(2,1)S(1)} %get-tuple-element.39.refs_0_) | copy-start | bytes 1179652
  29.2 14.4 %collective-permute-start.4 = (bf16[8,192,128]{2,1,0:T(8,128)(2,1)S(1)}, bf16[8,192,128]{2,1,0:T(8,128)(2,1)S(1)}, u32[]{:S(2)}, u32[]{:S(2)}) collective-permute-start(bf16[8,192,128]{2,1,0:T(8,128)(2,1)S(1)} %get-tuple-element.38.refs_7_.refs_8_), channel_id=1, source_target_pairs={{0,56},{8,0},{16,8},{24,16},{32,24},{40,32},{48,40},{56,48},{1,57}... | collective-permute-start | bytes 1179656 | tf_op jit(solution)/shard_map/ppermute | solution.py:201
  34.6 13.0 %collective-permute-start = (bf16[8,192,128]{2,1,0:T(8,128)(2,1)S(1)}, bf16[8,192,128]{2,1,0:T(8,128)(2,1)S(1)}, u32[]{:S(2)}, u32[]{:S(2)}) collective-permute-start(bf16[8,192,128]{2,1,0:T(8,128)(2,1)S(1)} %get-tuple-element.39.refs_0_), channel_id=1, source_target_pairs={{0,8},{8,16},{16,24},{24,32},{32,40},{40,48},{48,56},{56,0},{1,9},... | collective-permute-start | bytes 1179656 | tf_op jit(solution)/shard_map/ppermute | solution.py:201
  36.5 13.2 %collective-permute-start.11 = (bf16[8,192,128]{2,1,0:T(8,128)(2,1)S(1)}, bf16[8,192,128]{2,1,0:T(8,128)(2,1)S(1)}, u32[]{:S(2)}, u32[]{:S(2)}) collective-permute-start(bf16[8,192,128]{2,1,0:T(8,128)(2,1)S(1)} %get-tuple-element.38.refs_7_.refs_8_), channel_id=1, source_target_pairs={{0,8},{8,16},{16,24},{24,32},{32,40},{40,48},{48,56},{56,0},{1,9},... | collective-permute-start | bytes 1179656 | tf_op jit(solution)/shard_map/ppermute | solution.py:201
  38.6 13.1 %collective-permute-start.8 = (bf16[8,192,128]{2,1,0:T(8,128)(2,1)S(1)}, bf16[8,192,128]{2,1,0:T(8,128)(2,1)S(1)}, u32[]{:S(2)}, u32[]{:S(2)}) collective-permute-start(bf16[8,192,128]{2,1,0:T(8,128)(2,1)S(1)} %get-tuple-element.39.refs_0_), channel_id=1, source_target_pairs={{0,56},{8,0},{16,8},{24,16},{32,24},{40,32},{48,40},{56,48},{1,57}... | collective-permute-start | bytes 1179656 | tf_op jit(solution)/shard_map/ppermute | solution.py:201
  43.6 32.1 %copy-start.7 = (bf16[8,192,128]{2,1,0:T(8,128)(2,1)}, bf16[8,192,128]{2,1,0:T(8,128)(2,1)S(1)}, u32[]{:S(2)}) copy-start(bf16[8,192,128]{2,1,0:T(8,128)(2,1)S(1)} %collective-permute-done.4.refs_9_.refs_10_) | copy-start | bytes 1179652
  43.6 13.2 %collective-permute-start.5 = (bf16[8,192,128]{2,1,0:T(8,128)(2,1)S(1)}, bf16[8,192,128]{2,1,0:T(8,128)(2,1)S(1)}, u32[]{:S(2)}, u32[]{:S(2)}) collective-permute-start(bf16[8,192,128]{2,1,0:T(8,128)(2,1)S(1)} %collective-permute-done.4.refs_9_.refs_10_), channel_id=1, source_target_pairs={{0,56},{8,0},{16,8},{24,16},{32,24},{40,32},{48,40},{56,48},{1,57}... | collective-permute-start | bytes 1179656 | tf_op jit(solution)/shard_map/ppermute | solution.py:201
  47.6 13.0 %collective-permute-start.1 = (bf16[8,192,128]{2,1,0:T(8,128)(2,1)S(1)}, bf16[8,192,128]{2,1,0:T(8,128)(2,1)S(1)}, u32[]{:S(2)}, u32[]{:S(2)}) collective-permute-start(bf16[8,192,128]{2,1,0:T(8,128)(2,1)S(1)} %collective-permute-done.refs_1_), channel_id=1, source_target_pairs={{0,8},{8,16},{16,24},{24,32},{32,40},{40,48},{48,56},{56,0},{1,9},... | collective-permute-start | bytes 1179656 | tf_op jit(solution)/shard_map/ppermute | solution.py:201
  49.7 13.0 %collective-permute-start.12 = (bf16[8,192,128]{2,1,0:T(8,128)(2,1)S(1)}, bf16[8,192,128]{2,1,0:T(8,128)(2,1)S(1)}, u32[]{:S(2)}, u32[]{:S(2)}) collective-permute-start(bf16[8,192,128]{2,1,0:T(8,128)(2,1)S(1)} %collective-permute-done.11.refs_8_.refs_9_), channel_id=1, source_target_pairs={{0,8},{8,16},{16,24},{24,32},{32,40},{40,48},{48,56},{56,0},{1,9},... | collective-permute-start | bytes 1179656 | tf_op jit(solution)/shard_map/ppermute | solution.py:201
  51.6 13.0 %collective-permute-start.9 = (bf16[8,192,128]{2,1,0:T(8,128)(2,1)S(1)}, bf16[8,192,128]{2,1,0:T(8,128)(2,1)S(1)}, u32[]{:S(2)}, u32[]{:S(2)}) collective-permute-start(bf16[8,192,128]{2,1,0:T(8,128)(2,1)S(1)} %collective-permute-done.8.refs_2_), channel_id=1, source_target_pairs={{0,56},{8,0},{16,8},{24,16},{32,24},{40,32},{48,40},{56,48},{1,57}... | collective-permute-start | bytes 1179656 | tf_op jit(solution)/shard_map/ppermute | solution.py:201
  56.8 13.0 %collective-permute-start.6 = (bf16[8,192,128]{2,1,0:T(8,128)(2,1)S(1)}, bf16[8,192,128]{2,1,0:T(8,128)(2,1)S(1)}, u32[]{:S(2)}, u32[]{:S(2)}) collective-permute-start(bf16[8,192,128]{2,1,0:T(8,128)(2,1)S(1)} %collective-permute-done.5.refs_11_.refs_12_), channel_id=1, source_target_pairs={{0,56},{8,0},{16,8},{24,16},{32,24},{40,32},{48,40},{56,48},{1,57}... | collective-permute-start | bytes 1179656 | tf_op jit(solution)/shard_map/ppermute | solution.py:201
  60.6 13.0 %collective-permute-start.2 = (bf16[8,192,128]{2,1,0:T(8,128)(2,1)S(1)}, bf16[8,192,128]{2,1,0:T(8,128)(2,1)S(1)}, u32[]{:S(2)}, u32[]{:S(2)}) collective-permute-start(bf16[8,192,128]{2,1,0:T(8,128)(2,1)S(1)} %collective-permute-done.1.refs_3_), channel_id=1, source_target_pairs={{0,8},{8,16},{16,24},{24,32},{32,40},{40,48},{48,56},{56,0},{1,9},... | collective-permute-start | bytes 1179656 | tf_op jit(solution)/shard_map/ppermute | solution.py:201
  62.7 13.0 %collective-permute-start.13 = (bf16[8,192,128]{2,1,0:T(8,128)(2,1)S(1)}, bf16[8,192,128]{2,1,0:T(8,128)(2,1)S(1)}, u32[]{:S(2)}, u32[]{:S(2)}) collective-permute-start(bf16[8,192,128]{2,1,0:T(8,128)(2,1)S(1)} %collective-permute-done.12.refs_10_.refs_11_), channel_id=1, source_target_pairs={{0,8},{8,16},{16,24},{24,32},{32,40},{40,48},{48,56},{56,0},{1,9},... | collective-permute-start | bytes 1179656 | tf_op jit(solution)/shard_map/ppermute | solution.py:201
  64.6 11.1 %collective-permute-start.10 = (bf16[8,192,128]{2,1,0:T(8,128)(2,1)S(1)}, bf16[8,192,128]{2,1,0:T(8,128)(2,1)S(1)}, u32[]{:S(2)}, u32[]{:S(2)}) collective-permute-start(bf16[8,192,128]{2,1,0:T(8,128)(2,1)S(1)} %collective-permute-done.9.refs_4_), channel_id=1, source_target_pairs={{0,56},{8,0},{16,8},{24,16},{32,24},{40,32},{48,40},{56,48},{1,57}... | collective-permute-start | bytes 1179656 | tf_op jit(solution)/shard_map/ppermute | solution.py:201
  69.8 14.4 %collective-permute-start.7 = (bf16[8,192,128]{2,1,0:T(8,128)(2,1)S(1)}, bf16[8,192,128]{2,1,0:T(8,128)(2,1)S(1)}, u32[]{:S(2)}, u32[]{:S(2)}) collective-permute-start(bf16[8,192,128]{2,1,0:T(8,128)(2,1)S(1)} %collective-permute-done.6.refs_13_.refs_14_), channel_id=1, source_target_pairs={{0,56},{8,0},{16,8},{24,16},{32,24},{40,32},{48,40},{56,48},{1,57}... | collective-permute-start | bytes 1179656 | tf_op jit(solution)/shard_map/ppermute | solution.py:201
  73.6 10.9 %collective-permute-start.3 = (bf16[8,192,128]{2,1,0:T(8,128)(2,1)S(1)}, bf16[8,192,128]{2,1,0:T(8,128)(2,1)S(1)}, u32[]{:S(2)}, u32[]{:S(2)}) collective-permute-start(bf16[8,192,128]{2,1,0:T(8,128)(2,1)S(1)} %collective-permute-done.2.refs_5_), channel_id=1, source_target_pairs={{0,8},{8,16},{16,24},{24,32},{32,40},{40,48},{48,56},{56,0},{1,9},... | collective-permute-start | bytes 1179656 | tf_op jit(solution)/shard_map/ppermute | solution.py:201
  89.0 46.8 %all-to-all-start.1 = ((bf16[8,8,192,128]{3,2,1,0:T(8,128)(2,1)}), bf16[8,8,192,128]{3,2,1,0:T(8,128)(2,1)}, u32[]{:S(2)}, u32[]{:S(2)}) async-start(bf16[8,8,192,128]{3,2,1,0:T(8,128)(2,1)} %bitcast.8), calls=%async_computation.1 | async-start | bytes 6291456 | tf_op jit(solution)/shard_map/all_to_all | solution.py:195
  100.0 6.1 %collective-permute-start.14 = (bf16[4,2,4,2,128,128]{5,4,3,2,1,0:T(8,128)(2,1)S(1)}, bf16[4,2,4,2,128,128]{5,4,3,2,1,0:T(8,128)(2,1)S(1)}, u32[]{:S(2)}, u32[]{:S(2)}) collective-permute-start(bf16[4,2,4,2,128,128]{5,4,3,2,1,0:T(8,128)(2,1)S(1)} %get-tuple-element.32), channel_id=1, source_target_pairs={{0,64},{64,0},{1,65},{65,1},{2,66},{66,2},{3,67},{67,3},{4,68},{68... | collective-permute-start | bytes 6291464 | tf_op jit(solution)/shard_map/ppermute | solution.py:289
  108.7 33.2 %collective-permute-start.15 = (bf16[2,4,2,128,128]{4,3,2,1,0:T(8,128)(2,1)}, bf16[2,4,2,128,128]{4,3,2,1,0:T(8,128)(2,1)}, u32[]{:S(2)}, u32[]{:S(2)}) collective-permute-start(bf16[2,4,2,128,128]{4,3,2,1,0:T(8,128)(2,1)} %get-tuple-element.35), channel_id=1, source_target_pairs={{0,128},{128,256},{256,384},{384,0},{1,129},{129,257},{257,385},{3... | collective-permute-start | bytes 1572872 | tf_op jit(solution)/shard_map/ppermute | solution.py:292
  111.1 30.8 %collective-permute-start.17 = (bf16[2,4,2,128,128]{4,3,2,1,0:T(8,128)(2,1)S(1)}, bf16[2,4,2,128,128]{4,3,2,1,0:T(8,128)(2,1)}, u32[]{:S(2)}, u32[]{:S(2)}) collective-permute-start(bf16[2,4,2,128,128]{4,3,2,1,0:T(8,128)(2,1)S(1)} %get-tuple-element.36), channel_id=1, source_target_pairs={{0,384},{128,0},{256,128},{384,256},{1,385},{129,1},{257,129},{385... | collective-permute-start | bytes 1572872 | tf_op jit(solution)/shard_map/ppermute | solution.py:292
  114.6 27.4 %collective-permute-start.16 = (bf16[2,4,2,128,128]{4,3,2,1,0:T(8,128)(2,1)S(1)}, bf16[2,4,2,128,128]{4,3,2,1,0:T(8,128)(2,1)}, u32[]{:S(2)}, u32[]{:S(2)}) collective-permute-start(bf16[2,4,2,128,128]{4,3,2,1,0:T(8,128)(2,1)S(1)} %get-tuple-element.37), channel_id=1, source_target_pairs={{0,256},{128,384},{256,0},{384,128},{1,257},{129,385},{257,1},{385... | collective-permute-start | bytes 1572872 | tf_op jit(solution)/shard_map/ppermute | solution.py:292
  138.5 15.3 %all-to-all-start.2 = ((bf16[8,192,128]{2,1,0:T(8,128)(2,1)}), bf16[8,192,128]{2,1,0:T(8,128)(2,1)S(1)}, u32[]{:S(2)}, u32[]{:S(2)}) async-start(bf16[8,192,128]{2,1,0:T(8,128)(2,1)} %sums.1), calls=%async_computation.2 | async-start | bytes 786432 | tf_op jit(solution)/shard_map/all_to_all | solution.py:195
  (18 other events, 189.2 us)

commit v7 on v6

--- a/solution.py
+++ b/solution.py
@@ -96,7 +96,7 @@
 
 
 def back_kernel(where, x_last, y_last, hidden_most, grad_most, wi, li, lo, *refs):
-    placed, act, grad, total, rounded, out_sem = refs
+    placed, act_out, grad_out, total, rounded, act, grad, out_sem = refs
     rows, per_row, width, _ = wi.shape
     blocks, side = total.shape[0], x_last.shape[0]
     total[...] = jnp.zeros_like(total)
@@ -116,16 +116,23 @@
         at = slice(r * width, (r + 1) * width)
         act[r] = activated[:, at]
         grad[r] = grad_hidden[:, at]
+    stores = [
+        pltpu.make_async_copy(act, act_out, out_sem.at[SLABS]),
+        pltpu.make_async_copy(grad, grad_out, out_sem.at[SLABS + 1]),
+    ]
+    for copy in stores:
+        copy.start()
+    for r in range(rows):
+        at = slice(r * width, (r + 1) * width)
         terms = dot_nt(grad_hidden[:, at], wi[r].reshape(per_row * width, width))
         for k in range(per_row):
             c = where[0, r * per_row + k]
             total[c] = total[c] + terms[:, k * width : (k + 1) * width]
-    stores = []
     slab = blocks // SLABS
     for s in range(SLABS):
         at = pl.ds(s * slab, slab)
         rounded[at] = total[at].astype(BF16)
-        stores.append(pltpu.make_async_copy(rounded.at[at], placed.at[at], out_sem.at[s]))
+        stores.append(pltpu.make_async_copy(rounded.at[at], placed.at[s], out_sem.at[s]))
         stores[-1].start()
     for copy in stores:
         copy.wait()
@@ -134,8 +141,14 @@
 def weight_kernel(plans, where, *refs):
     (side, x_steps), (_, y_steps) = plans
     n_x, n_y = len(x_steps), len(y_steps)
-    act, grad, own, other, x, y, x_sem, y_sem = refs[n_x + n_y :]
-    loads = start_loads(where, list(zip(refs[:n_x], x_steps)), x, x_sem, side)
+    act_in, grad_in, own, other, x, y, act, grad, x_sem, y_sem, sem = refs[n_x + n_y :]
+    loads = [
+        pltpu.make_async_copy(act_in, act, sem.at[0]),
+        pltpu.make_async_copy(grad_in, grad, sem.at[1]),
+    ]
+    for copy in loads:
+        copy.start()
+    loads += start_loads(where, list(zip(refs[:n_x], x_steps)), x, x_sem, side)
     loads += start_loads(where, list(zip(refs[n_x : n_x + n_y], y_steps)), y, y_sem, side)
     for copy in loads:
         copy.wait()
@@ -154,17 +167,11 @@
                     out[away, 1, r, j] = dot_nn(act_t, y[where[1, at]]).astype(BF16)
 
 
-def sum_kernel(parts, out, here, sem):
-    loads = [
-        pltpu.make_async_copy(parts.at[:, n], here.at[n], sem.at[n]) for n in range(here.shape[0])
-    ]
-    for copy in loads:
-        copy.start()
-    for n, copy in enumerate(loads):
-        copy.wait()
-        kept = here[n, 0].astype(F32)
-        for s in range(1, here.shape[1]):
-            kept = kept + here[n, s].astype(F32)
+def sum_kernel(parts, out):
+    for n in range(parts.shape[1]):
+        kept = parts[0, n].astype(F32)
+        for s in range(1, parts.shape[0]):
+            kept = kept + parts[s, n].astype(F32)
         out[n] = kept.astype(BF16)
 
 
@@ -210,8 +217,8 @@
     lasts = jnp.where(cols // side == opposite, cols % side, side)
     where = jnp.concatenate([cols, here, lasts])
 
-    mine = jnp.stack([inputs, upstream])
-    unit = swap(jnp.broadcast_to(mine, (side, *mine.shape)), lines)
+    which = lax.broadcasted_iota(jnp.int32, (side, 2, tok, width), 1)
+    unit = swap(jnp.where(which == 0, inputs, upstream), lines)
     dense = jax.ShapeDtypeStruct((side + 1, width, rows * width), BF16)
     in_last, out_last = pl.pallas_call(
         last_kernel,
@@ -242,7 +249,7 @@
 
     gathered = pltpu.VMEM((blocks, tok, width), BF16)
     loaded = pltpu.SemaphoreType.DMA((side,))
-    values = jax.ShapeDtypeStruct((rows, tok, width), BF16)
+    values = pltpu.HBM((rows, tok, width), BF16)
     kept = pltpu.VMEM((tok, rows * width), F32)
     last = pltpu.VMEM((side, width, rows * width), BF16)
     hidden_most, grad_most, wi, li, lo = pl.pallas_call(
@@ -262,27 +269,36 @@
     )(where, *x_units[:-1], *y_units[:-1], *(in_hbm(v) for v in (w_in, w_out, in_last, out_last)))
     placed, act, grad = pl.pallas_call(
         back_kernel,
-        out_shape=(jax.ShapeDtypeStruct((blocks, tok, width), BF16), values, values),
+        out_shape=(pltpu.HBM((side, blocks // side, tok, width), BF16), values, values),
         in_specs=[smem] + [vmem] * 7,
-        out_specs=(anywhere, vmem, vmem),
         scratch_shapes=[
             pltpu.VMEM((blocks, tok, width), F32),
             pltpu.VMEM((blocks, tok, width), BF16),
-            pltpu.SemaphoreType.DMA((SLABS,)),
+            pltpu.VMEM((rows, tok, width), BF16),
+            pltpu.VMEM((rows, tok, width), BF16),
+            pltpu.SemaphoreType.DMA((SLABS + 2,)),
         ],
         compiler_params=params,
         name="back",
     )(where, x_units[-1], y_units[-1], hidden_most, grad_most, wi, li, lo)
 
-    on_ring = swap(placed.reshape(side, blocks // side, tok, width), rings)
+    on_ring = swap(placed, rings)
 
     half = jax.ShapeDtypeStruct((nx, 2, rows, each, width, width), BF16)
     own, other = pl.pallas_call(
         functools.partial(weight_kernel, (x_plan, y_plan)),
         out_shape=(half, half),
-        in_specs=[smem] + [anywhere] * (len(x_units) + len(y_units)) + [vmem, vmem],
+        in_specs=[smem] + [anywhere] * (len(x_units) + len(y_units) + 2),
         out_specs=(vmem, vmem),
-        scratch_shapes=[gathered, gathered, loaded, loaded],
+        scratch_shapes=[
+            gathered,
+            gathered,
+            pltpu.VMEM((rows, tok, width), BF16),
+            pltpu.VMEM((rows, tok, width), BF16),
+            loaded,
+            loaded,
+            pltpu.SemaphoreType.DMA((2,)),
+        ],
         compiler_params=params,
         name="weights",
     )(where, *x_units, *y_units, act, grad)
@@ -296,12 +312,11 @@
     on_line = pl.pallas_call(
         sum_kernel,
         out_shape=jax.ShapeDtypeStruct(on_ring.shape[1:], BF16),
-        in_specs=[anywhere],
+        in_specs=[vmem],
         out_specs=vmem,
-        scratch_shapes=[pltpu.VMEM((blocks // side, side, tok, width), BF16), loaded],
         compiler_params=params,
         name="sums",
-    )(in_hbm(on_ring))
+    )(pltpu.with_memory_space_constraint(on_ring, pltpu.VMEM))
     received = swap(on_line, lines)
     grad_inputs = jnp.sum(received.astype(F32), axis=0).astype(BF16)
     return grad_inputs, summed[0], summed[1]

time: 155 us -> 156 us (level)
  waiting for transfers between devices: 42 us -> 39.3 us
  other arithmetic: 5.05 us -> 6.7 us
    all_to_all x3, waiting for transfers between devices: 37.4 us -> 33 us  [swap(): lax.all_to_all(values, CYZ, split_axis=0, concat_axis=0, tiled=True, axis...]
    pallas_call x1, Pallas kernels: 4.5 us -> 6.9 us  [per_device(): pl.pallas_call(back_kernel, out_shape=(pltpu.HBM((side, blocks // side, t...]
    select_n x0 -> x1, other arithmetic: none -> 1.97 us  [per_device(): unit = swap(jnp.where(which == 0, inputs, upstream), lines)]
    ppermute x3, waiting for transfers between devices: 0.01 us -> 1.67 us  [per_device(): lax.ppermute(paired[d], 'x', [(i, (i + d) % nx) for i in range(nx)])]
    unnamed x42 -> x52, local copies, waits for them, and re-layouts: 6.49 us -> 8 us
  transfers between devices with their start and end apart: 21 -> 21, of which waited for: 6 -> 7; matrix products, arithmetic and copies ran while one was open for 3% -> 3% of each run, Pallas kernels for 11% -> 10%
where the time goes in v7:
time: 156 us; the launch traced here: 155 us
  starting transfers between devices  76 us (49%)
  waiting for transfers between devices  39.3 us (25%)
  Pallas kernels  22.8 us (15%)
  local copies, waits for them, and re-layouts  9.06 us (6%)
  other arithmetic  6.7 us (4%)
    ppermute x14, starting transfers between devices, turn(): return lax.ppermute(values, CYZ, pairs)  46 us
    all_to_all x3, waiting for transfers between devices, swap(): lax.all_to_all(values, CYZ, split_axis=0, concat_axis=0, tiled=True, axis...  33 us
    all_to_all x3, starting transfers between devices, swap(): lax.all_to_all(values, CYZ, split_axis=0, concat_axis=0, tiled=True, axis...  19 us
    ppermute x3, starting transfers between devices, per_device(): lax.ppermute(paired[d], 'x', [(i, (i + d) % nx) for i in range(nx)])  9.15 us
    unnamed x52, local copies, waits for them, and re-layouts  8 us
    pallas_call x1, Pallas kernels, per_device(): pl.pallas_call(functools.partial(early_kernel, ((side, x_plan[1][:-1]), (...  6.94 us
    pallas_call x1, Pallas kernels, per_device(): pl.pallas_call(back_kernel, out_shape=(pltpu.HBM((side, blocks // side, t...  6.9 us
    pallas_call x1, Pallas kernels, per_device(): pl.pallas_call(functools.partial(weight_kernel, (x_plan, y_plan)), out_sh...  6.27 us
  transfers between devices with their start and end apart: 21, of which 7 were waited for; matrix products, arithmetic and copies ran while one was open for 3% of the time, Pallas kernels for 10%

profile of v7, /device:TPU:6, one launch (start us, length us, event | category | flops | bytes accessed | tf_op | source)
XLA Modules:
  0.0 155.1 jit_solution(7735180194243379257)
XLA Ops:
  2.6 10.3 %all-to-all-start = ((bf16[8,2,192,128]{3,2,1,0:T(8,128)(2,1)}), bf16[8,2,192,128]{3,2,1,0:T(8,128)(2,1)S(1)}, u32[]{:S(2)}, u32[]{:S(2)}) async-start(bf16[8,2,192,128]{3,2,1,0:T(8,128)(2,1)} %broadcast_select_fusion), calls=%async_computation | async-start | bytes 1572864 | tf_op jit(solution)/shard_map/all_to_all | solution.py:202
  18.6 10.5 %all-to-all-done = bf16[8,2,192,128]{3,2,1,0:T(8,128)(2,1)S(1)} async-done(((bf16[8,2,192,128]{3,2,1,0:T(8,128)(2,1)}), bf16[8,2,192,128]{3,2,1,0:T(8,128)(2,1)S(1)}, u32[]{:S(2)}, u32[]{:S(2)}) %all-to-all-start) | async-done | bytes 786464 | tf_op jit(solution)/shard_map/all_to_all | solution.py:202
  29.2 5.4 %collective-permute-start.4 = (bf16[8,192,128]{2,1,0:T(8,128)(2,1)S(1)}, bf16[8,192,128]{2,1,0:T(8,128)(2,1)S(1)}, u32[]{:S(2)}, u32[]{:S(2)}) collective-permute-start(bf16[8,192,128]{2,1,0:T(8,128)(2,1)S(1)} %get-tuple-element.38.refs_7_.refs_8_), channel_id=1, source_target_pairs={{0,56},{8,0},{16,8},{24,16},{32,24},{40,32},{48,40},{56,48},{1,57}... | collective-permute-start | bytes 1179656 | tf_op jit(solution)/shard_map/ppermute | solution.py:208
  36.5 2.0 %collective-permute-start.11 = (bf16[8,192,128]{2,1,0:T(8,128)(2,1)S(1)}, bf16[8,192,128]{2,1,0:T(8,128)(2,1)S(1)}, u32[]{:S(2)}, u32[]{:S(2)}) collective-permute-start(bf16[8,192,128]{2,1,0:T(8,128)(2,1)S(1)} %get-tuple-element.38.refs_7_.refs_8_), channel_id=1, source_target_pairs={{0,8},{8,16},{16,24},{24,32},{32,40},{40,48},{48,56},{56,0},{1,9},... | collective-permute-start | bytes 1179656 | tf_op jit(solution)/shard_map/ppermute | solution.py:208
  38.5 5.0 %collective-permute-start.8 = (bf16[8,192,128]{2,1,0:T(8,128)(2,1)S(1)}, bf16[8,192,128]{2,1,0:T(8,128)(2,1)S(1)}, u32[]{:S(2)}, u32[]{:S(2)}) collective-permute-start(bf16[8,192,128]{2,1,0:T(8,128)(2,1)S(1)} %get-tuple-element.39.refs_0_), channel_id=1, source_target_pairs={{0,56},{8,0},{16,8},{24,16},{32,24},{40,32},{48,40},{56,48},{1,57}... | collective-permute-start | bytes 1179656 | tf_op jit(solution)/shard_map/ppermute | solution.py:208
  43.6 3.9 %collective-permute-start.5 = (bf16[8,192,128]{2,1,0:T(8,128)(2,1)S(1)}, bf16[8,192,128]{2,1,0:T(8,128)(2,1)S(1)}, u32[]{:S(2)}, u32[]{:S(2)}) collective-permute-start(bf16[8,192,128]{2,1,0:T(8,128)(2,1)S(1)} %collective-permute-done.4.refs_9_.refs_10_), channel_id=1, source_target_pairs={{0,56},{8,0},{16,8},{24,16},{32,24},{40,32},{48,40},{56,48},{1,57}... | collective-permute-start | bytes 1179656 | tf_op jit(solution)/shard_map/ppermute | solution.py:208
  51.6 5.1 %collective-permute-start.9 = (bf16[8,192,128]{2,1,0:T(8,128)(2,1)S(1)}, bf16[8,192,128]{2,1,0:T(8,128)(2,1)S(1)}, u32[]{:S(2)}, u32[]{:S(2)}) collective-permute-start(bf16[8,192,128]{2,1,0:T(8,128)(2,1)S(1)} %collective-permute-done.8.refs_2_), channel_id=1, source_target_pairs={{0,56},{8,0},{16,8},{24,16},{32,24},{40,32},{48,40},{56,48},{1,57}... | collective-permute-start | bytes 1179656 | tf_op jit(solution)/shard_map/ppermute | solution.py:208
  56.8 3.8 %collective-permute-start.6 = (bf16[8,192,128]{2,1,0:T(8,128)(2,1)S(1)}, bf16[8,192,128]{2,1,0:T(8,128)(2,1)S(1)}, u32[]{:S(2)}, u32[]{:S(2)}) collective-permute-start(bf16[8,192,128]{2,1,0:T(8,128)(2,1)S(1)} %collective-permute-done.5.refs_11_.refs_12_), channel_id=1, source_target_pairs={{0,56},{8,0},{16,8},{24,16},{32,24},{40,32},{48,40},{56,48},{1,57}... | collective-permute-start | bytes 1179656 | tf_op jit(solution)/shard_map/ppermute | solution.py:208
  60.5 2.1 %collective-permute-start.2 = (bf16[8,192,128]{2,1,0:T(8,128)(2,1)S(1)}, bf16[8,192,128]{2,1,0:T(8,128)(2,1)S(1)}, u32[]{:S(2)}, u32[]{:S(2)}) collective-permute-start(bf16[8,192,128]{2,1,0:T(8,128)(2,1)S(1)} %collective-permute-done.1.refs_3_), channel_id=1, source_target_pairs={{0,8},{8,16},{16,24},{24,32},{32,40},{40,48},{48,56},{56,0},{1,9},... | collective-permute-start | bytes 1179656 | tf_op jit(solution)/shard_map/ppermute | solution.py:208
  64.6 5.1 %collective-permute-start.10 = (bf16[8,192,128]{2,1,0:T(8,128)(2,1)S(1)}, bf16[8,192,128]{2,1,0:T(8,128)(2,1)S(1)}, u32[]{:S(2)}, u32[]{:S(2)}) collective-permute-start(bf16[8,192,128]{2,1,0:T(8,128)(2,1)S(1)} %collective-permute-done.9.refs_4_), channel_id=1, source_target_pairs={{0,56},{8,0},{16,8},{24,16},{32,24},{40,32},{48,40},{56,48},{1,57}... | collective-permute-start | bytes 1179656 | tf_op jit(solution)/shard_map/ppermute | solution.py:208
  69.8 3.8 %collective-permute-start.7 = (bf16[8,192,128]{2,1,0:T(8,128)(2,1)S(1)}, bf16[8,192,128]{2,1,0:T(8,128)(2,1)S(1)}, u32[]{:S(2)}, u32[]{:S(2)}) collective-permute-start(bf16[8,192,128]{2,1,0:T(8,128)(2,1)S(1)} %collective-permute-done.6.refs_13_.refs_14_), channel_id=1, source_target_pairs={{0,56},{8,0},{16,8},{24,16},{32,24},{40,32},{48,40},{56,48},{1,57}... | collective-permute-start | bytes 1179656 | tf_op jit(solution)/shard_map/ppermute | solution.py:208
  73.6 2.1 %collective-permute-start.3 = (bf16[8,192,128]{2,1,0:T(8,128)(2,1)S(1)}, bf16[8,192,128]{2,1,0:T(8,128)(2,1)S(1)}, u32[]{:S(2)}, u32[]{:S(2)}) collective-permute-start(bf16[8,192,128]{2,1,0:T(8,128)(2,1)S(1)} %collective-permute-done.2.refs_5_), channel_id=1, source_target_pairs={{0,8},{8,16},{16,24},{24,32},{32,40},{40,48},{48,56},{56,0},{1,9},... | collective-permute-start | bytes 1179656 | tf_op jit(solution)/shard_map/ppermute | solution.py:208
  77.2 6.9 %early.1 = (f32[192,512]{1,0:T(8,128)S(1)}, f32[192,512]{1,0:T(8,128)S(1)}, bf16[4,16,128,128]{3,2,1,0:T(8,128)(2,1)S(1)}, bf16[8,128,512]{2,1,0:T(8,128)(2,1)S(1)}, bf16[8,128,512]{2,1,0:T(8,128)(2,1)S(1)}) custom-call(s32[5,64]{1,0:T(8,128)S(1)} %pad_add_fusion.where, bf16[8,192,128]{2,1,0:T(8,128)(2,1)} %copy-done.10, bf16[8,192,128]{2,1,0:T(8,128)(2,1)} %copy-done.13, ...), custom_call_target="tpu_custom_call" | custom-call | tf_op jit(solution)/shard_map/early/pallas_call | solution.py:255
  84.4 6.9 %back.1 = (bf16[8,8,192,128]{3,2,1,0:T(8,128)(2,1)}, bf16[4,192,128]{2,1,0:T(8,128)(2,1)}, bf16[4,192,128]{2,1,0:T(8,128)(2,1)}) custom-call(s32[5,64]{1,0:T(8,128)S(1)} %pad_add_fusion.where, bf16[8,192,128]{2,1,0:T(8,128)(2,1)S(1)} %collective-permute-done.3.x_last.refs_7_, bf16[8,192,128]{2,1,0:T(8,128)(2,1)S(1)} %collective-permute-done.7.y_last.refs_15_, ...), custom_call_target="tpu_custom_call" | custom-call | tf_op jit(solution)/shard_map/back/pallas_call | solution.py:270
  91.4 5.2 %all-to-all-start.1 = ((bf16[8,8,192,128]{3,2,1,0:T(8,128)(2,1)}), bf16[8,8,192,128]{3,2,1,0:T(8,128)(2,1)S(1)}, u32[]{:S(2)}, u32[]{:S(2)}) async-start(bf16[8,8,192,128]{3,2,1,0:T(8,128)(2,1)} %get-tuple-element.28), calls=%async_computation.1 | async-start | bytes 6291456 | tf_op jit(solution)/shard_map/all_to_all | solution.py:202
  99.4 6.3 %weights.1 = (bf16[4,2,4,2,128,128]{5,4,3,2,1,0:T(8,128)(2,1)S(1)}, bf16[4,2,4,2,128,128]{5,4,3,2,1,0:T(8,128)(2,1)S(1)}) custom-call(s32[5,64]{1,0:T(8,128)S(1)} %pad_add_fusion.where, bf16[8,192,128]{2,1,0:T(8,128)(2,1)} %copy-done.10, bf16[8,192,128]{2,1,0:T(8,128)(2,1)} %copy-done.13, bf16[8,192,128]{2,1,0:T(8,128)(2,1)} %copy-done.15, ...), custom_call_target="tpu_custom_call" | custom-call | tf_op jit(solution)/shard_map/weights/pallas_call | solution.py:288
  107.6 4.1 %collective-permute-done.14 = bf16[4,2,4,2,128,128]{5,4,3,2,1,0:T(8,128)(2,1)S(1)} collective-permute-done((bf16[4,2,4,2,128,128]{5,4,3,2,1,0:T(8,128)(2,1)S(1)}, bf16[4,2,4,2,128,128]{5,4,3,2,1,0:T(8,128)(2,1)S(1)}, u32[]{:S(2)}, u32[]{:S(2)}) %collective-permute-start.14) | collective-permute-done | bytes 2097184 | tf_op jit(solution)/shard_map/ppermute | solution.py:305
  113.6 2.4 %collective-permute-start.15 = (bf16[2,4,2,128,128]{4,3,2,1,0:T(8,128)(2,1)}, bf16[2,4,2,128,128]{4,3,2,1,0:T(8,128)(2,1)}, u32[]{:S(2)}, u32[]{:S(2)}) collective-permute-start(bf16[2,4,2,128,128]{4,3,2,1,0:T(8,128)(2,1)} %get-tuple-element.35), channel_id=1, source_target_pairs={{0,128},{128,256},{256,384},{384,0},{1,129},{129,257},{257,385},{3... | collective-permute-start | bytes 1572872 | tf_op jit(solution)/shard_map/ppermute | solution.py:308
  116.0 3.5 %collective-permute-start.17 = (bf16[2,4,2,128,128]{4,3,2,1,0:T(8,128)(2,1)}, bf16[2,4,2,128,128]{4,3,2,1,0:T(8,128)(2,1)}, u32[]{:S(2)}, u32[]{:S(2)}) collective-permute-start(bf16[2,4,2,128,128]{4,3,2,1,0:T(8,128)(2,1)} %get-tuple-element.36), channel_id=1, source_target_pairs={{0,384},{128,0},{256,128},{384,256},{1,385},{129,1},{257,129},{385... | collective-permute-start | bytes 1572872 | tf_op jit(solution)/shard_map/ppermute | solution.py:308
  119.5 3.3 %collective-permute-start.16 = (bf16[2,4,2,128,128]{4,3,2,1,0:T(8,128)(2,1)}, bf16[2,4,2,128,128]{4,3,2,1,0:T(8,128)(2,1)}, u32[]{:S(2)}, u32[]{:S(2)}) collective-permute-start(bf16[2,4,2,128,128]{4,3,2,1,0:T(8,128)(2,1)} %get-tuple-element.37), channel_id=1, source_target_pairs={{0,256},{128,384},{256,0},{384,128},{1,257},{129,385},{257,1},{385... | collective-permute-start | bytes 1572872 | tf_op jit(solution)/shard_map/ppermute | solution.py:308
  122.8 15.3 %all-to-all-done.1.parts = bf16[8,8,192,128]{3,2,1,0:T(8,128)(2,1)S(1)} async-done(((bf16[8,8,192,128]{3,2,1,0:T(8,128)(2,1)}), bf16[8,8,192,128]{3,2,1,0:T(8,128)(2,1)S(1)}, u32[]{:S(2)}, u32[]{:S(2)}) %all-to-all-start.1) | async-done | bytes 3145760 | tf_op jit(solution)/shard_map/all_to_all | solution.py:202
  139.2 3.5 %all-to-all-start.2 = ((bf16[8,192,128]{2,1,0:T(8,128)(2,1)}), bf16[8,192,128]{2,1,0:T(8,128)(2,1)S(1)}, u32[]{:S(2)}, u32[]{:S(2)}) async-start(bf16[8,192,128]{2,1,0:T(8,128)(2,1)} %sums.1), calls=%async_computation.2 | async-start | bytes 786432 | tf_op jit(solution)/shard_map/all_to_all | solution.py:202
  144.3 2.1 %fusion.2 = bf16[2,4,2,128,128]{4,3,2,1,0:T(8,128)(2,1)S(1)} fusion(bf16[2,4,2,128,128]{4,3,2,1,0:T(8,128)(2,1)} %collective-permute-done.17, bf16[2,4,2,128,128]{4,3,2,1,0:T(8,128)(2,1)} %collective-permute-done.16, bf16[2,4,2,128,128]{4,3,2,1,0:T(8,128)(2,1)} %collective-permute-done.15, bf16[4,2,4,2,128,128]{5,4,3,2,1,0:T(8,128)(2,1)} %copy-done.11, ...), kind=kLoop, calls=%fused_computation.3 | loop fusion | flops 3145728 | bytes 3145728 | tf_op jit(solution)/shard_map/convert_element_type | solution.py:310
  147.3 7.2 %all-to-all-done.2 = bf16[8,192,128]{2,1,0:T(8,128)(2,1)S(1)} async-done(((bf16[8,192,128]{2,1,0:T(8,128)(2,1)}), bf16[8,192,128]{2,1,0:T(8,128)(2,1)S(1)}, u32[]{:S(2)}, u32[]{:S(2)}) %all-to-all-start.2) | async-done | bytes 393248 | tf_op jit(solution)/shard_map/all_to_all | solution.py:202
  (88 shorter events, 28.2 us)
Async XLA Ops:
  2.6 26.5 %all-to-all-start = ((bf16[8,2,192,128]{3,2,1,0:T(8,128)(2,1)}), bf16[8,2,192,128]{3,2,1,0:T(8,128)(2,1)S(1)}, u32[]{:S(2)}, u32[]{:S(2)}) async-start(bf16[8,2,192,128]{3,2,1,0:T(8,128)(2,1)} %broadcast_select_fusion), calls=%async_computation | async-start | bytes 1572864 | tf_op jit(solution)/shard_map/all_to_all | solution.py:202
  29.2 46.5 %copy-start.9 = (bf16[8,192,128]{2,1,0:T(8,128)(2,1)}, bf16[8,192,128]{2,1,0:T(8,128)(2,1)S(1)}, u32[]{:S(2)}) copy-start(bf16[8,192,128]{2,1,0:T(8,128)(2,1)S(1)} %get-tuple-element.38.refs_7_.refs_8_) | copy-start | bytes 1179652
  29.2 46.5 %copy-start.10 = (bf16[8,192,128]{2,1,0:T(8,128)(2,1)}, bf16[8,192,128]{2,1,0:T(8,128)(2,1)S(1)}, u32[]{:S(2)}) copy-start(bf16[8,192,128]{2,1,0:T(8,128)(2,1)S(1)} %get-tuple-element.39.refs_0_) | copy-start | bytes 1179652
  29.2 14.4 %collective-permute-start.4 = (bf16[8,192,128]{2,1,0:T(8,128)(2,1)S(1)}, bf16[8,192,128]{2,1,0:T(8,128)(2,1)S(1)}, u32[]{:S(2)}, u32[]{:S(2)}) collective-permute-start(bf16[8,192,128]{2,1,0:T(8,128)(2,1)S(1)} %get-tuple-element.38.refs_7_.refs_8_), channel_id=1, source_target_pairs={{0,56},{8,0},{16,8},{24,16},{32,24},{40,32},{48,40},{56,48},{1,57}... | collective-permute-start | bytes 1179656 | tf_op jit(solution)/shard_map/ppermute | solution.py:208
  34.6 13.0 %collective-permute-start = (bf16[8,192,128]{2,1,0:T(8,128)(2,1)S(1)}, bf16[8,192,128]{2,1,0:T(8,128)(2,1)S(1)}, u32[]{:S(2)}, u32[]{:S(2)}) collective-permute-start(bf16[8,192,128]{2,1,0:T(8,128)(2,1)S(1)} %get-tuple-element.39.refs_0_), channel_id=1, source_target_pairs={{0,8},{8,16},{16,24},{24,32},{32,40},{40,48},{48,56},{56,0},{1,9},... | collective-permute-start | bytes 1179656 | tf_op jit(solution)/shard_map/ppermute | solution.py:208
  36.5 13.2 %collective-permute-start.11 = (bf16[8,192,128]{2,1,0:T(8,128)(2,1)S(1)}, bf16[8,192,128]{2,1,0:T(8,128)(2,1)S(1)}, u32[]{:S(2)}, u32[]{:S(2)}) collective-permute-start(bf16[8,192,128]{2,1,0:T(8,128)(2,1)S(1)} %get-tuple-element.38.refs_7_.refs_8_), channel_id=1, source_target_pairs={{0,8},{8,16},{16,24},{24,32},{32,40},{40,48},{48,56},{56,0},{1,9},... | collective-permute-start | bytes 1179656 | tf_op jit(solution)/shard_map/ppermute | solution.py:208
  38.5 13.1 %collective-permute-start.8 = (bf16[8,192,128]{2,1,0:T(8,128)(2,1)S(1)}, bf16[8,192,128]{2,1,0:T(8,128)(2,1)S(1)}, u32[]{:S(2)}, u32[]{:S(2)}) collective-permute-start(bf16[8,192,128]{2,1,0:T(8,128)(2,1)S(1)} %get-tuple-element.39.refs_0_), channel_id=1, source_target_pairs={{0,56},{8,0},{16,8},{24,16},{32,24},{40,32},{48,40},{56,48},{1,57}... | collective-permute-start | bytes 1179656 | tf_op jit(solution)/shard_map/ppermute | solution.py:208
  43.6 32.1 %copy-start.12 = (bf16[8,192,128]{2,1,0:T(8,128)(2,1)}, bf16[8,192,128]{2,1,0:T(8,128)(2,1)S(1)}, u32[]{:S(2)}) copy-start(bf16[8,192,128]{2,1,0:T(8,128)(2,1)S(1)} %collective-permute-done.4.refs_9_.refs_10_) | copy-start | bytes 1179652
  43.6 13.2 %collective-permute-start.5 = (bf16[8,192,128]{2,1,0:T(8,128)(2,1)S(1)}, bf16[8,192,128]{2,1,0:T(8,128)(2,1)S(1)}, u32[]{:S(2)}, u32[]{:S(2)}) collective-permute-start(bf16[8,192,128]{2,1,0:T(8,128)(2,1)S(1)} %collective-permute-done.4.refs_9_.refs_10_), channel_id=1, source_target_pairs={{0,56},{8,0},{16,8},{24,16},{32,24},{40,32},{48,40},{56,48},{1,57}... | collective-permute-start | bytes 1179656 | tf_op jit(solution)/shard_map/ppermute | solution.py:208
  47.5 13.0 %collective-permute-start.1 = (bf16[8,192,128]{2,1,0:T(8,128)(2,1)S(1)}, bf16[8,192,128]{2,1,0:T(8,128)(2,1)S(1)}, u32[]{:S(2)}, u32[]{:S(2)}) collective-permute-start(bf16[8,192,128]{2,1,0:T(8,128)(2,1)S(1)} %collective-permute-done.refs_1_), channel_id=1, source_target_pairs={{0,8},{8,16},{16,24},{24,32},{32,40},{40,48},{48,56},{56,0},{1,9},... | collective-permute-start | bytes 1179656 | tf_op jit(solution)/shard_map/ppermute | solution.py:208
  49.7 13.0 %collective-permute-start.12 = (bf16[8,192,128]{2,1,0:T(8,128)(2,1)S(1)}, bf16[8,192,128]{2,1,0:T(8,128)(2,1)S(1)}, u32[]{:S(2)}, u32[]{:S(2)}) collective-permute-start(bf16[8,192,128]{2,1,0:T(8,128)(2,1)S(1)} %collective-permute-done.11.refs_8_.refs_9_), channel_id=1, source_target_pairs={{0,8},{8,16},{16,24},{24,32},{32,40},{40,48},{48,56},{56,0},{1,9},... | collective-permute-start | bytes 1179656 | tf_op jit(solution)/shard_map/ppermute | solution.py:208
  51.6 13.0 %collective-permute-start.9 = (bf16[8,192,128]{2,1,0:T(8,128)(2,1)S(1)}, bf16[8,192,128]{2,1,0:T(8,128)(2,1)S(1)}, u32[]{:S(2)}, u32[]{:S(2)}) collective-permute-start(bf16[8,192,128]{2,1,0:T(8,128)(2,1)S(1)} %collective-permute-done.8.refs_2_), channel_id=1, source_target_pairs={{0,56},{8,0},{16,8},{24,16},{32,24},{40,32},{48,40},{56,48},{1,57}... | collective-permute-start | bytes 1179656 | tf_op jit(solution)/shard_map/ppermute | solution.py:208
  56.8 13.0 %collective-permute-start.6 = (bf16[8,192,128]{2,1,0:T(8,128)(2,1)S(1)}, bf16[8,192,128]{2,1,0:T(8,128)(2,1)S(1)}, u32[]{:S(2)}, u32[]{:S(2)}) collective-permute-start(bf16[8,192,128]{2,1,0:T(8,128)(2,1)S(1)} %collective-permute-done.5.refs_11_.refs_12_), channel_id=1, source_target_pairs={{0,56},{8,0},{16,8},{24,16},{32,24},{40,32},{48,40},{56,48},{1,57}... | collective-permute-start | bytes 1179656 | tf_op jit(solution)/shard_map/ppermute | solution.py:208
  60.5 13.0 %collective-permute-start.2 = (bf16[8,192,128]{2,1,0:T(8,128)(2,1)S(1)}, bf16[8,192,128]{2,1,0:T(8,128)(2,1)S(1)}, u32[]{:S(2)}, u32[]{:S(2)}) collective-permute-start(bf16[8,192,128]{2,1,0:T(8,128)(2,1)S(1)} %collective-permute-done.1.refs_3_), channel_id=1, source_target_pairs={{0,8},{8,16},{16,24},{24,32},{32,40},{40,48},{48,56},{56,0},{1,9},... | collective-permute-start | bytes 1179656 | tf_op jit(solution)/shard_map/ppermute | solution.py:208
  62.7 13.0 %collective-permute-start.13 = (bf16[8,192,128]{2,1,0:T(8,128)(2,1)S(1)}, bf16[8,192,128]{2,1,0:T(8,128)(2,1)S(1)}, u32[]{:S(2)}, u32[]{:S(2)}) collective-permute-start(bf16[8,192,128]{2,1,0:T(8,128)(2,1)S(1)} %collective-permute-done.12.refs_10_.refs_11_), channel_id=1, source_target_pairs={{0,8},{8,16},{16,24},{24,32},{32,40},{40,48},{48,56},{56,0},{1,9},... | collective-permute-start | bytes 1179656 | tf_op jit(solution)/shard_map/ppermute | solution.py:208
  64.6 11.1 %collective-permute-start.10 = (bf16[8,192,128]{2,1,0:T(8,128)(2,1)S(1)}, bf16[8,192,128]{2,1,0:T(8,128)(2,1)S(1)}, u32[]{:S(2)}, u32[]{:S(2)}) collective-permute-start(bf16[8,192,128]{2,1,0:T(8,128)(2,1)S(1)} %collective-permute-done.9.refs_4_), channel_id=1, source_target_pairs={{0,56},{8,0},{16,8},{24,16},{32,24},{40,32},{48,40},{56,48},{1,57}... | collective-permute-start | bytes 1179656 | tf_op jit(solution)/shard_map/ppermute | solution.py:208
  69.8 14.4 %collective-permute-start.7 = (bf16[8,192,128]{2,1,0:T(8,128)(2,1)S(1)}, bf16[8,192,128]{2,1,0:T(8,128)(2,1)S(1)}, u32[]{:S(2)}, u32[]{:S(2)}) collective-permute-start(bf16[8,192,128]{2,1,0:T(8,128)(2,1)S(1)} %collective-permute-done.6.refs_13_.refs_14_), channel_id=1, source_target_pairs={{0,56},{8,0},{16,8},{24,16},{32,24},{40,32},{48,40},{56,48},{1,57}... | collective-permute-start | bytes 1179656 | tf_op jit(solution)/shard_map/ppermute | solution.py:208
  73.6 10.9 %collective-permute-start.3 = (bf16[8,192,128]{2,1,0:T(8,128)(2,1)S(1)}, bf16[8,192,128]{2,1,0:T(8,128)(2,1)S(1)}, u32[]{:S(2)}, u32[]{:S(2)}) collective-permute-start(bf16[8,192,128]{2,1,0:T(8,128)(2,1)S(1)} %collective-permute-done.2.refs_5_), channel_id=1, source_target_pairs={{0,8},{8,16},{16,24},{24,32},{32,40},{40,48},{48,56},{56,0},{1,9},... | collective-permute-start | bytes 1179656 | tf_op jit(solution)/shard_map/ppermute | solution.py:208
  91.4 46.7 %all-to-all-start.1 = ((bf16[8,8,192,128]{3,2,1,0:T(8,128)(2,1)}), bf16[8,8,192,128]{3,2,1,0:T(8,128)(2,1)S(1)}, u32[]{:S(2)}, u32[]{:S(2)}) async-start(bf16[8,8,192,128]{3,2,1,0:T(8,128)(2,1)} %get-tuple-element.28), calls=%async_computation.1 | async-start | bytes 6291456 | tf_op jit(solution)/shard_map/all_to_all | solution.py:202
  105.7 6.1 %collective-permute-start.14 = (bf16[4,2,4,2,128,128]{5,4,3,2,1,0:T(8,128)(2,1)S(1)}, bf16[4,2,4,2,128,128]{5,4,3,2,1,0:T(8,128)(2,1)S(1)}, u32[]{:S(2)}, u32[]{:S(2)}) collective-permute-start(bf16[4,2,4,2,128,128]{5,4,3,2,1,0:T(8,128)(2,1)S(1)} %get-tuple-element.32), channel_id=1, source_target_pairs={{0,64},{64,0},{1,65},{65,1},{2,66},{66,2},{3,67},{67,3},{4,68},{68... | collective-permute-start | bytes 6291464 | tf_op jit(solution)/shard_map/ppermute | solution.py:305
  113.6 29.1 %collective-permute-start.15 = (bf16[2,4,2,128,128]{4,3,2,1,0:T(8,128)(2,1)}, bf16[2,4,2,128,128]{4,3,2,1,0:T(8,128)(2,1)}, u32[]{:S(2)}, u32[]{:S(2)}) collective-permute-start(bf16[2,4,2,128,128]{4,3,2,1,0:T(8,128)(2,1)} %get-tuple-element.35), channel_id=1, source_target_pairs={{0,128},{128,256},{256,384},{384,0},{1,129},{129,257},{257,385},{3... | collective-permute-start | bytes 1572872 | tf_op jit(solution)/shard_map/ppermute | solution.py:308
  116.0 28.3 %collective-permute-start.17 = (bf16[2,4,2,128,128]{4,3,2,1,0:T(8,128)(2,1)}, bf16[2,4,2,128,128]{4,3,2,1,0:T(8,128)(2,1)}, u32[]{:S(2)}, u32[]{:S(2)}) collective-permute-start(bf16[2,4,2,128,128]{4,3,2,1,0:T(8,128)(2,1)} %get-tuple-element.36), channel_id=1, source_target_pairs={{0,384},{128,0},{256,128},{384,256},{1,385},{129,1},{257,129},{385... | collective-permute-start | bytes 1572872 | tf_op jit(solution)/shard_map/ppermute | solution.py:308
  119.5 24.9 %collective-permute-start.16 = (bf16[2,4,2,128,128]{4,3,2,1,0:T(8,128)(2,1)}, bf16[2,4,2,128,128]{4,3,2,1,0:T(8,128)(2,1)}, u32[]{:S(2)}, u32[]{:S(2)}) collective-permute-start(bf16[2,4,2,128,128]{4,3,2,1,0:T(8,128)(2,1)} %get-tuple-element.37), channel_id=1, source_target_pairs={{0,256},{128,384},{256,0},{384,128},{1,257},{129,385},{257,1},{385... | collective-permute-start | bytes 1572872 | tf_op jit(solution)/shard_map/ppermute | solution.py:308
  139.2 15.3 %all-to-all-start.2 = ((bf16[8,192,128]{2,1,0:T(8,128)(2,1)}), bf16[8,192,128]{2,1,0:T(8,128)(2,1)S(1)}, u32[]{:S(2)}, u32[]{:S(2)}) async-start(bf16[8,192,128]{2,1,0:T(8,128)(2,1)} %sums.1), calls=%async_computation.2 | async-start | bytes 786432 | tf_op jit(solution)/shard_map/all_to_all | solution.py:202
  (23 other events, 213.1 us)

commit v8 on v7

--- a/solution.py
+++ b/solution.py
@@ -217,8 +217,8 @@
     lasts = jnp.where(cols // side == opposite, cols % side, side)
     where = jnp.concatenate([cols, here, lasts])
 
-    which = lax.broadcasted_iota(jnp.int32, (side, 2, tok, width), 1)
-    unit = swap(jnp.where(which == 0, inputs, upstream), lines)
+    mine = jnp.stack([inputs, upstream])
+    unit = swap(jnp.broadcast_to(mine, (side, *mine.shape)), lines)
     dense = jax.ShapeDtypeStruct((side + 1, width, rows * width), BF16)
     in_last, out_last = pl.pallas_call(
         last_kernel,
@@ -255,6 +255,7 @@
     hidden_most, grad_most, wi, li, lo = pl.pallas_call(
         functools.partial(early_kernel, ((side, x_plan[1][:-1]), (side, y_plan[1][:-1]))),
         out_shape=(kept, kept, pltpu.VMEM(w_in.shape, BF16), last, last),
+        out_specs=(vmem,) * 5,
         in_specs=[smem] + [anywhere] * (len(x_units) + len(y_units) + 2),
         scratch_shapes=[
             pltpu.VMEM(w_out.shape, BF16),
@@ -271,6 +272,7 @@
         back_kernel,
         out_shape=(pltpu.HBM((side, blocks // side, tok, width), BF16), values, values),
         in_specs=[smem] + [vmem] * 7,
+        out_specs=(anywhere, anywhere, anywhere),
         scratch_shapes=[
             pltpu.VMEM((blocks, tok, width), F32),
             pltpu.VMEM((blocks, tok, width), BF16),

time: 156 us -> 154 us (0.987)
  Pallas kernels: 22.8 us -> 20.4 us
    pallas_call x1, Pallas kernels: 6.9 us -> 4.48 us  [per_device(): pl.pallas_call(back_kernel, out_shape=(pltpu.HBM((side, blocks // side, t...]
    select_n x1 -> x0, other arithmetic: 1.97 us -> none  [per_device(): unit = swap(jnp.where(which == 0, inputs, upstream), lines)]
where the time goes in v8:
time: 154 us; the launch traced here: 153 us
  starting transfers between devices  76 us (49%)
  waiting for transfers between devices  39.3 us (26%)
  Pallas kernels  20.4 us (13%)
  local copies, waits for them, and re-layouts  10.1 us (7%)
  other arithmetic  5.71 us (4%)
    ppermute x14, starting transfers between devices, turn(): return lax.ppermute(values, CYZ, pairs)  46 us
    all_to_all x3, waiting for transfers between devices, swap(): lax.all_to_all(values, CYZ, split_axis=0, concat_axis=0, tiled=True, axis...  32.9 us
    all_to_all x3, starting transfers between devices, swap(): lax.all_to_all(values, CYZ, split_axis=0, concat_axis=0, tiled=True, axis...  19 us
    ppermute x3, starting transfers between devices, per_device(): lax.ppermute(paired[d], 'x', [(i, (i + d) % nx) for i in range(nx)])  9.16 us
    unnamed x52, local copies, waits for them, and re-layouts  8 us
    pallas_call x1, Pallas kernels, per_device(): pl.pallas_call(functools.partial(early_kernel, ((side, x_plan[1][:-1]), (...  6.94 us
    pallas_call x1, Pallas kernels, per_device(): pl.pallas_call(functools.partial(weight_kernel, (x_plan, y_plan)), out_sh...  6.27 us
    pallas_call x1, Pallas kernels, per_device(): pl.pallas_call(back_kernel, out_shape=(pltpu.HBM((side, blocks // side, t...  4.48 us
  transfers between devices with their start and end apart: 21, of which 7 were waited for; matrix products, arithmetic and copies ran while one was open for 3% of the time, Pallas kernels for 10%

profile of v8, /device:TPU:6, one launch (start us, length us, event | category | flops | bytes accessed | tf_op | source)
XLA Modules:
  0.0 152.8 jit_solution(15874956050830417548)
XLA Ops:
  2.7 10.3 %all-to-all-start = ((bf16[8,2,192,128]{3,2,1,0:T(8,128)(2,1)}), bf16[8,2,192,128]{3,2,1,0:T(8,128)(2,1)S(1)}, u32[]{:S(2)}, u32[]{:S(2)}) async-start(bf16[8,2,192,128]{3,2,1,0:T(8,128)(2,1)} %broadcast_in_dim.5), calls=%async_computation | async-start | bytes 1572864 | tf_op jit(solution)/shard_map/all_to_all | solution.py:202
  18.6 10.5 %all-to-all-done = bf16[8,2,192,128]{3,2,1,0:T(8,128)(2,1)S(1)} async-done(((bf16[8,2,192,128]{3,2,1,0:T(8,128)(2,1)}), bf16[8,2,192,128]{3,2,1,0:T(8,128)(2,1)S(1)}, u32[]{:S(2)}, u32[]{:S(2)}) %all-to-all-start) | async-done | bytes 786464 | tf_op jit(solution)/shard_map/all_to_all | solution.py:202
  29.2 5.4 %collective-permute-start.4 = (bf16[8,192,128]{2,1,0:T(8,128)(2,1)S(1)}, bf16[8,192,128]{2,1,0:T(8,128)(2,1)S(1)}, u32[]{:S(2)}, u32[]{:S(2)}) collective-permute-start(bf16[8,192,128]{2,1,0:T(8,128)(2,1)S(1)} %get-tuple-element.38.refs_7_.refs_8_), channel_id=1, source_target_pairs={{0,56},{8,0},{16,8},{24,16},{32,24},{40,32},{48,40},{56,48},{1,57}... | collective-permute-start | bytes 1179656 | tf_op jit(solution)/shard_map/ppermute | solution.py:208
  36.5 2.0 %collective-permute-start.11 = (bf16[8,192,128]{2,1,0:T(8,128)(2,1)S(1)}, bf16[8,192,128]{2,1,0:T(8,128)(2,1)S(1)}, u32[]{:S(2)}, u32[]{:S(2)}) collective-permute-start(bf16[8,192,128]{2,1,0:T(8,128)(2,1)S(1)} %get-tuple-element.38.refs_7_.refs_8_), channel_id=1, source_target_pairs={{0,8},{8,16},{16,24},{24,32},{32,40},{40,48},{48,56},{56,0},{1,9},... | collective-permute-start | bytes 1179656 | tf_op jit(solution)/shard_map/ppermute | solution.py:208
  38.6 5.0 %collective-permute-start.8 = (bf16[8,192,128]{2,1,0:T(8,128)(2,1)S(1)}, bf16[8,192,128]{2,1,0:T(8,128)(2,1)S(1)}, u32[]{:S(2)}, u32[]{:S(2)}) collective-permute-start(bf16[8,192,128]{2,1,0:T(8,128)(2,1)S(1)} %get-tuple-element.39.refs_0_), channel_id=1, source_target_pairs={{0,56},{8,0},{16,8},{24,16},{32,24},{40,32},{48,40},{56,48},{1,57}... | collective-permute-start | bytes 1179656 | tf_op jit(solution)/shard_map/ppermute | solution.py:208
  43.6 3.9 %collective-permute-start.5 = (bf16[8,192,128]{2,1,0:T(8,128)(2,1)S(1)}, bf16[8,192,128]{2,1,0:T(8,128)(2,1)S(1)}, u32[]{:S(2)}, u32[]{:S(2)}) collective-permute-start(bf16[8,192,128]{2,1,0:T(8,128)(2,1)S(1)} %collective-permute-done.4.refs_9_.refs_10_), channel_id=1, source_target_pairs={{0,56},{8,0},{16,8},{24,16},{32,24},{40,32},{48,40},{56,48},{1,57}... | collective-permute-start | bytes 1179656 | tf_op jit(solution)/shard_map/ppermute | solution.py:208
  51.6 5.1 %collective-permute-start.9 = (bf16[8,192,128]{2,1,0:T(8,128)(2,1)S(1)}, bf16[8,192,128]{2,1,0:T(8,128)(2,1)S(1)}, u32[]{:S(2)}, u32[]{:S(2)}) collective-permute-start(bf16[8,192,128]{2,1,0:T(8,128)(2,1)S(1)} %collective-permute-done.8.refs_2_), channel_id=1, source_target_pairs={{0,56},{8,0},{16,8},{24,16},{32,24},{40,32},{48,40},{56,48},{1,57}... | collective-permute-start | bytes 1179656 | tf_op jit(solution)/shard_map/ppermute | solution.py:208
  56.8 3.8 %collective-permute-start.6 = (bf16[8,192,128]{2,1,0:T(8,128)(2,1)S(1)}, bf16[8,192,128]{2,1,0:T(8,128)(2,1)S(1)}, u32[]{:S(2)}, u32[]{:S(2)}) collective-permute-start(bf16[8,192,128]{2,1,0:T(8,128)(2,1)S(1)} %collective-permute-done.5.refs_11_.refs_12_), channel_id=1, source_target_pairs={{0,56},{8,0},{16,8},{24,16},{32,24},{40,32},{48,40},{56,48},{1,57}... | collective-permute-start | bytes 1179656 | tf_op jit(solution)/shard_map/ppermute | solution.py:208
  60.6 2.1 %collective-permute-start.2 = (bf16[8,192,128]{2,1,0:T(8,128)(2,1)S(1)}, bf16[8,192,128]{2,1,0:T(8,128)(2,1)S(1)}, u32[]{:S(2)}, u32[]{:S(2)}) collective-permute-start(bf16[8,192,128]{2,1,0:T(8,128)(2,1)S(1)} %collective-permute-done.1.refs_3_), channel_id=1, source_target_pairs={{0,8},{8,16},{16,24},{24,32},{32,40},{40,48},{48,56},{56,0},{1,9},... | collective-permute-start | bytes 1179656 | tf_op jit(solution)/shard_map/ppermute | solution.py:208
  64.6 5.1 %collective-permute-start.10 = (bf16[8,192,128]{2,1,0:T(8,128)(2,1)S(1)}, bf16[8,192,128]{2,1,0:T(8,128)(2,1)S(1)}, u32[]{:S(2)}, u32[]{:S(2)}) collective-permute-start(bf16[8,192,128]{2,1,0:T(8,128)(2,1)S(1)} %collective-permute-done.9.refs_4_), channel_id=1, source_target_pairs={{0,56},{8,0},{16,8},{24,16},{32,24},{40,32},{48,40},{56,48},{1,57}... | collective-permute-start | bytes 1179656 | tf_op jit(solution)/shard_map/ppermute | solution.py:208
  69.8 3.8 %collective-permute-start.7 = (bf16[8,192,128]{2,1,0:T(8,128)(2,1)S(1)}, bf16[8,192,128]{2,1,0:T(8,128)(2,1)S(1)}, u32[]{:S(2)}, u32[]{:S(2)}) collective-permute-start(bf16[8,192,128]{2,1,0:T(8,128)(2,1)S(1)} %collective-permute-done.6.refs_13_.refs_14_), channel_id=1, source_target_pairs={{0,56},{8,0},{16,8},{24,16},{32,24},{40,32},{48,40},{56,48},{1,57}... | collective-permute-start | bytes 1179656 | tf_op jit(solution)/shard_map/ppermute | solution.py:208
  73.6 2.1 %collective-permute-start.3 = (bf16[8,192,128]{2,1,0:T(8,128)(2,1)S(1)}, bf16[8,192,128]{2,1,0:T(8,128)(2,1)S(1)}, u32[]{:S(2)}, u32[]{:S(2)}) collective-permute-start(bf16[8,192,128]{2,1,0:T(8,128)(2,1)S(1)} %collective-permute-done.2.refs_5_), channel_id=1, source_target_pairs={{0,8},{8,16},{16,24},{24,32},{32,40},{40,48},{48,56},{56,0},{1,9},... | collective-permute-start | bytes 1179656 | tf_op jit(solution)/shard_map/ppermute | solution.py:208
  77.2 6.9 %early.1 = (f32[192,512]{1,0:T(8,128)S(1)}, f32[192,512]{1,0:T(8,128)S(1)}, bf16[4,16,128,128]{3,2,1,0:T(8,128)(2,1)S(1)}, bf16[8,128,512]{2,1,0:T(8,128)(2,1)S(1)}, bf16[8,128,512]{2,1,0:T(8,128)(2,1)S(1)}) custom-call(s32[5,64]{1,0:T(8,128)S(1)} %pad_add_fusion.where, bf16[8,192,128]{2,1,0:T(8,128)(2,1)} %copy-done.10, bf16[8,192,128]{2,1,0:T(8,128)(2,1)} %copy-done.13, ...), custom_call_target="tpu_custom_call" | custom-call | tf_op jit(solution)/shard_map/early/pallas_call | solution.py:255
  84.5 4.5 %back.1 = (bf16[8,8,192,128]{3,2,1,0:T(8,128)(2,1)}, bf16[4,192,128]{2,1,0:T(8,128)(2,1)}, bf16[4,192,128]{2,1,0:T(8,128)(2,1)}) custom-call(s32[5,64]{1,0:T(8,128)S(1)} %pad_add_fusion.where, bf16[8,192,128]{2,1,0:T(8,128)(2,1)S(1)} %collective-permute-done.3.x_last.refs_7_, bf16[8,192,128]{2,1,0:T(8,128)(2,1)S(1)} %collective-permute-done.7.y_last.refs_15_, ...), custom_call_target="tpu_custom_call" | custom-call | tf_op jit(solution)/shard_map/back/pallas_call | solution.py:271
  89.0 5.2 %all-to-all-start.1 = ((bf16[8,8,192,128]{3,2,1,0:T(8,128)(2,1)}), bf16[8,8,192,128]{3,2,1,0:T(8,128)(2,1)S(1)}, u32[]{:S(2)}, u32[]{:S(2)}) async-start(bf16[8,8,192,128]{3,2,1,0:T(8,128)(2,1)} %get-tuple-element.28), calls=%async_computation.1 | async-start | bytes 6291456 | tf_op jit(solution)/shard_map/all_to_all | solution.py:202
  97.0 6.3 %weights.1 = (bf16[4,2,4,2,128,128]{5,4,3,2,1,0:T(8,128)(2,1)S(1)}, bf16[4,2,4,2,128,128]{5,4,3,2,1,0:T(8,128)(2,1)S(1)}) custom-call(s32[5,64]{1,0:T(8,128)S(1)} %pad_add_fusion.where, bf16[8,192,128]{2,1,0:T(8,128)(2,1)} %copy-done.10, bf16[8,192,128]{2,1,0:T(8,128)(2,1)} %copy-done.13, bf16[8,192,128]{2,1,0:T(8,128)(2,1)} %copy-done.15, ...), custom_call_target="tpu_custom_call" | custom-call | tf_op jit(solution)/shard_map/weights/pallas_call | solution.py:290
  105.3 4.1 %collective-permute-done.14 = bf16[4,2,4,2,128,128]{5,4,3,2,1,0:T(8,128)(2,1)S(1)} collective-permute-done((bf16[4,2,4,2,128,128]{5,4,3,2,1,0:T(8,128)(2,1)S(1)}, bf16[4,2,4,2,128,128]{5,4,3,2,1,0:T(8,128)(2,1)S(1)}, u32[]{:S(2)}, u32[]{:S(2)}) %collective-permute-start.14) | collective-permute-done | bytes 2097184 | tf_op jit(solution)/shard_map/ppermute | solution.py:307
  111.2 2.4 %collective-permute-start.15 = (bf16[2,4,2,128,128]{4,3,2,1,0:T(8,128)(2,1)}, bf16[2,4,2,128,128]{4,3,2,1,0:T(8,128)(2,1)}, u32[]{:S(2)}, u32[]{:S(2)}) collective-permute-start(bf16[2,4,2,128,128]{4,3,2,1,0:T(8,128)(2,1)} %get-tuple-element.35), channel_id=1, source_target_pairs={{0,128},{128,256},{256,384},{384,0},{1,129},{129,257},{257,385},{3... | collective-permute-start | bytes 1572872 | tf_op jit(solution)/shard_map/ppermute | solution.py:310
  113.6 3.5 %collective-permute-start.17 = (bf16[2,4,2,128,128]{4,3,2,1,0:T(8,128)(2,1)}, bf16[2,4,2,128,128]{4,3,2,1,0:T(8,128)(2,1)}, u32[]{:S(2)}, u32[]{:S(2)}) collective-permute-start(bf16[2,4,2,128,128]{4,3,2,1,0:T(8,128)(2,1)} %get-tuple-element.36), channel_id=1, source_target_pairs={{0,384},{128,0},{256,128},{384,256},{1,385},{129,1},{257,129},{385... | collective-permute-start | bytes 1572872 | tf_op jit(solution)/shard_map/ppermute | solution.py:310
  117.1 3.3 %collective-permute-start.16 = (bf16[2,4,2,128,128]{4,3,2,1,0:T(8,128)(2,1)}, bf16[2,4,2,128,128]{4,3,2,1,0:T(8,128)(2,1)}, u32[]{:S(2)}, u32[]{:S(2)}) collective-permute-start(bf16[2,4,2,128,128]{4,3,2,1,0:T(8,128)(2,1)} %get-tuple-element.37), channel_id=1, source_target_pairs={{0,256},{128,384},{256,0},{384,128},{1,257},{129,385},{257,1},{385... | collective-permute-start | bytes 1572872 | tf_op jit(solution)/shard_map/ppermute | solution.py:310
  120.4 15.2 %all-to-all-done.1.parts = bf16[8,8,192,128]{3,2,1,0:T(8,128)(2,1)S(1)} async-done(((bf16[8,8,192,128]{3,2,1,0:T(8,128)(2,1)}), bf16[8,8,192,128]{3,2,1,0:T(8,128)(2,1)S(1)}, u32[]{:S(2)}, u32[]{:S(2)}) %all-to-all-start.1) | async-done | bytes 3145760 | tf_op jit(solution)/shard_map/all_to_all | solution.py:202
  136.8 3.5 %all-to-all-start.2 = ((bf16[8,192,128]{2,1,0:T(8,128)(2,1)}), bf16[8,192,128]{2,1,0:T(8,128)(2,1)S(1)}, u32[]{:S(2)}, u32[]{:S(2)}) async-start(bf16[8,192,128]{2,1,0:T(8,128)(2,1)} %sums.1), calls=%async_computation.2 | async-start | bytes 786432 | tf_op jit(solution)/shard_map/all_to_all | solution.py:202
  142.0 2.1 %fusion.2 = bf16[2,4,2,128,128]{4,3,2,1,0:T(8,128)(2,1)S(1)} fusion(bf16[2,4,2,128,128]{4,3,2,1,0:T(8,128)(2,1)} %collective-permute-done.17, bf16[2,4,2,128,128]{4,3,2,1,0:T(8,128)(2,1)} %collective-permute-done.16, bf16[2,4,2,128,128]{4,3,2,1,0:T(8,128)(2,1)} %collective-permute-done.15, bf16[4,2,4,2,128,128]{5,4,3,2,1,0:T(8,128)(2,1)} %copy-done.11, ...), kind=kLoop, calls=%fused_computation.3 | loop fusion | flops 3145728 | bytes 3145728 | tf_op jit(solution)/shard_map/convert_element_type | solution.py:312
  144.9 7.2 %all-to-all-done.2 = bf16[8,192,128]{2,1,0:T(8,128)(2,1)S(1)} async-done(((bf16[8,192,128]{2,1,0:T(8,128)(2,1)}), bf16[8,192,128]{2,1,0:T(8,128)(2,1)S(1)}, u32[]{:S(2)}, u32[]{:S(2)}) %all-to-all-start.2) | async-done | bytes 393248 | tf_op jit(solution)/shard_map/all_to_all | solution.py:202
  (88 shorter events, 28.2 us)
Async XLA Ops:
  2.7 26.5 %all-to-all-start = ((bf16[8,2,192,128]{3,2,1,0:T(8,128)(2,1)}), bf16[8,2,192,128]{3,2,1,0:T(8,128)(2,1)S(1)}, u32[]{:S(2)}, u32[]{:S(2)}) async-start(bf16[8,2,192,128]{3,2,1,0:T(8,128)(2,1)} %broadcast_in_dim.5), calls=%async_computation | async-start | bytes 1572864 | tf_op jit(solution)/shard_map/all_to_all | solution.py:202
  29.2 46.5 %copy-start.9 = (bf16[8,192,128]{2,1,0:T(8,128)(2,1)}, bf16[8,192,128]{2,1,0:T(8,128)(2,1)S(1)}, u32[]{:S(2)}) copy-start(bf16[8,192,128]{2,1,0:T(8,128)(2,1)S(1)} %get-tuple-element.38.refs_7_.refs_8_) | copy-start | bytes 1179652
  29.2 46.5 %copy-start.10 = (bf16[8,192,128]{2,1,0:T(8,128)(2,1)}, bf16[8,192,128]{2,1,0:T(8,128)(2,1)S(1)}, u32[]{:S(2)}) copy-start(bf16[8,192,128]{2,1,0:T(8,128)(2,1)S(1)} %get-tuple-element.39.refs_0_) | copy-start | bytes 1179652
  29.2 14.4 %collective-permute-start.4 = (bf16[8,192,128]{2,1,0:T(8,128)(2,1)S(1)}, bf16[8,192,128]{2,1,0:T(8,128)(2,1)S(1)}, u32[]{:S(2)}, u32[]{:S(2)}) collective-permute-start(bf16[8,192,128]{2,1,0:T(8,128)(2,1)S(1)} %get-tuple-element.38.refs_7_.refs_8_), channel_id=1, source_target_pairs={{0,56},{8,0},{16,8},{24,16},{32,24},{40,32},{48,40},{56,48},{1,57}... | collective-permute-start | bytes 1179656 | tf_op jit(solution)/shard_map/ppermute | solution.py:208
  34.6 13.0 %collective-permute-start = (bf16[8,192,128]{2,1,0:T(8,128)(2,1)S(1)}, bf16[8,192,128]{2,1,0:T(8,128)(2,1)S(1)}, u32[]{:S(2)}, u32[]{:S(2)}) collective-permute-start(bf16[8,192,128]{2,1,0:T(8,128)(2,1)S(1)} %get-tuple-element.39.refs_0_), channel_id=1, source_target_pairs={{0,8},{8,16},{16,24},{24,32},{32,40},{40,48},{48,56},{56,0},{1,9},... | collective-permute-start | bytes 1179656 | tf_op jit(solution)/shard_map/ppermute | solution.py:208
  36.5 13.2 %collective-permute-start.11 = (bf16[8,192,128]{2,1,0:T(8,128)(2,1)S(1)}, bf16[8,192,128]{2,1,0:T(8,128)(2,1)S(1)}, u32[]{:S(2)}, u32[]{:S(2)}) collective-permute-start(bf16[8,192,128]{2,1,0:T(8,128)(2,1)S(1)} %get-tuple-element.38.refs_7_.refs_8_), channel_id=1, source_target_pairs={{0,8},{8,16},{16,24},{24,32},{32,40},{40,48},{48,56},{56,0},{1,9},... | collective-permute-start | bytes 1179656 | tf_op jit(solution)/shard_map/ppermute | solution.py:208
  38.6 13.1 %collective-permute-start.8 = (bf16[8,192,128]{2,1,0:T(8,128)(2,1)S(1)}, bf16[8,192,128]{2,1,0:T(8,128)(2,1)S(1)}, u32[]{:S(2)}, u32[]{:S(2)}) collective-permute-start(bf16[8,192,128]{2,1,0:T(8,128)(2,1)S(1)} %get-tuple-element.39.refs_0_), channel_id=1, source_target_pairs={{0,56},{8,0},{16,8},{24,16},{32,24},{40,32},{48,40},{56,48},{1,57}... | collective-permute-start | bytes 1179656 | tf_op jit(solution)/shard_map/ppermute | solution.py:208
  43.6 32.1 %copy-start.12 = (bf16[8,192,128]{2,1,0:T(8,128)(2,1)}, bf16[8,192,128]{2,1,0:T(8,128)(2,1)S(1)}, u32[]{:S(2)}) copy-start(bf16[8,192,128]{2,1,0:T(8,128)(2,1)S(1)} %collective-permute-done.4.refs_9_.refs_10_) | copy-start | bytes 1179652
  43.6 13.2 %collective-permute-start.5 = (bf16[8,192,128]{2,1,0:T(8,128)(2,1)S(1)}, bf16[8,192,128]{2,1,0:T(8,128)(2,1)S(1)}, u32[]{:S(2)}, u32[]{:S(2)}) collective-permute-start(bf16[8,192,128]{2,1,0:T(8,128)(2,1)S(1)} %collective-permute-done.4.refs_9_.refs_10_), channel_id=1, source_target_pairs={{0,56},{8,0},{16,8},{24,16},{32,24},{40,32},{48,40},{56,48},{1,57}... | collective-permute-start | bytes 1179656 | tf_op jit(solution)/shard_map/ppermute | solution.py:208
  47.6 13.0 %collective-permute-start.1 = (bf16[8,192,128]{2,1,0:T(8,128)(2,1)S(1)}, bf16[8,192,128]{2,1,0:T(8,128)(2,1)S(1)}, u32[]{:S(2)}, u32[]{:S(2)}) collective-permute-start(bf16[8,192,128]{2,1,0:T(8,128)(2,1)S(1)} %collective-permute-done.refs_1_), channel_id=1, source_target_pairs={{0,8},{8,16},{16,24},{24,32},{32,40},{40,48},{48,56},{56,0},{1,9},... | collective-permute-start | bytes 1179656 | tf_op jit(solution)/shard_map/ppermute | solution.py:208
  49.7 13.0 %collective-permute-start.12 = (bf16[8,192,128]{2,1,0:T(8,128)(2,1)S(1)}, bf16[8,192,128]{2,1,0:T(8,128)(2,1)S(1)}, u32[]{:S(2)}, u32[]{:S(2)}) collective-permute-start(bf16[8,192,128]{2,1,0:T(8,128)(2,1)S(1)} %collective-permute-done.11.refs_8_.refs_9_), channel_id=1, source_target_pairs={{0,8},{8,16},{16,24},{24,32},{32,40},{40,48},{48,56},{56,0},{1,9},... | collective-permute-start | bytes 1179656 | tf_op jit(solution)/shard_map/ppermute | solution.py:208
  51.6 13.0 %collective-permute-start.9 = (bf16[8,192,128]{2,1,0:T(8,128)(2,1)S(1)}, bf16[8,192,128]{2,1,0:T(8,128)(2,1)S(1)}, u32[]{:S(2)}, u32[]{:S(2)}) collective-permute-start(bf16[8,192,128]{2,1,0:T(8,128)(2,1)S(1)} %collective-permute-done.8.refs_2_), channel_id=1, source_target_pairs={{0,56},{8,0},{16,8},{24,16},{32,24},{40,32},{48,40},{56,48},{1,57}... | collective-permute-start | bytes 1179656 | tf_op jit(solution)/shard_map/ppermute | solution.py:208
  56.8 13.0 %collective-permute-start.6 = (bf16[8,192,128]{2,1,0:T(8,128)(2,1)S(1)}, bf16[8,192,128]{2,1,0:T(8,128)(2,1)S(1)}, u32[]{:S(2)}, u32[]{:S(2)}) collective-permute-start(bf16[8,192,128]{2,1,0:T(8,128)(2,1)S(1)} %collective-permute-done.5.refs_11_.refs_12_), channel_id=1, source_target_pairs={{0,56},{8,0},{16,8},{24,16},{32,24},{40,32},{48,40},{56,48},{1,57}... | collective-permute-start | bytes 1179656 | tf_op jit(solution)/shard_map/ppermute | solution.py:208
  60.6 13.0 %collective-permute-start.2 = (bf16[8,192,128]{2,1,0:T(8,128)(2,1)S(1)}, bf16[8,192,128]{2,1,0:T(8,128)(2,1)S(1)}, u32[]{:S(2)}, u32[]{:S(2)}) collective-permute-start(bf16[8,192,128]{2,1,0:T(8,128)(2,1)S(1)} %collective-permute-done.1.refs_3_), channel_id=1, source_target_pairs={{0,8},{8,16},{16,24},{24,32},{32,40},{40,48},{48,56},{56,0},{1,9},... | collective-permute-start | bytes 1179656 | tf_op jit(solution)/shard_map/ppermute | solution.py:208
  62.7 13.0 %collective-permute-start.13 = (bf16[8,192,128]{2,1,0:T(8,128)(2,1)S(1)}, bf16[8,192,128]{2,1,0:T(8,128)(2,1)S(1)}, u32[]{:S(2)}, u32[]{:S(2)}) collective-permute-start(bf16[8,192,128]{2,1,0:T(8,128)(2,1)S(1)} %collective-permute-done.12.refs_10_.refs_11_), channel_id=1, source_target_pairs={{0,8},{8,16},{16,24},{24,32},{32,40},{40,48},{48,56},{56,0},{1,9},... | collective-permute-start | bytes 1179656 | tf_op jit(solution)/shard_map/ppermute | solution.py:208
  64.6 11.1 %collective-permute-start.10 = (bf16[8,192,128]{2,1,0:T(8,128)(2,1)S(1)}, bf16[8,192,128]{2,1,0:T(8,128)(2,1)S(1)}, u32[]{:S(2)}, u32[]{:S(2)}) collective-permute-start(bf16[8,192,128]{2,1,0:T(8,128)(2,1)S(1)} %collective-permute-done.9.refs_4_), channel_id=1, source_target_pairs={{0,56},{8,0},{16,8},{24,16},{32,24},{40,32},{48,40},{56,48},{1,57}... | collective-permute-start | bytes 1179656 | tf_op jit(solution)/shard_map/ppermute | solution.py:208
  69.8 14.4 %collective-permute-start.7 = (bf16[8,192,128]{2,1,0:T(8,128)(2,1)S(1)}, bf16[8,192,128]{2,1,0:T(8,128)(2,1)S(1)}, u32[]{:S(2)}, u32[]{:S(2)}) collective-permute-start(bf16[8,192,128]{2,1,0:T(8,128)(2,1)S(1)} %collective-permute-done.6.refs_13_.refs_14_), channel_id=1, source_target_pairs={{0,56},{8,0},{16,8},{24,16},{32,24},{40,32},{48,40},{56,48},{1,57}... | collective-permute-start | bytes 1179656 | tf_op jit(solution)/shard_map/ppermute | solution.py:208
  73.6 10.9 %collective-permute-start.3 = (bf16[8,192,128]{2,1,0:T(8,128)(2,1)S(1)}, bf16[8,192,128]{2,1,0:T(8,128)(2,1)S(1)}, u32[]{:S(2)}, u32[]{:S(2)}) collective-permute-start(bf16[8,192,128]{2,1,0:T(8,128)(2,1)S(1)} %collective-permute-done.2.refs_5_), channel_id=1, source_target_pairs={{0,8},{8,16},{16,24},{24,32},{32,40},{40,48},{48,56},{56,0},{1,9},... | collective-permute-start | bytes 1179656 | tf_op jit(solution)/shard_map/ppermute | solution.py:208
  89.0 46.7 %all-to-all-start.1 = ((bf16[8,8,192,128]{3,2,1,0:T(8,128)(2,1)}), bf16[8,8,192,128]{3,2,1,0:T(8,128)(2,1)S(1)}, u32[]{:S(2)}, u32[]{:S(2)}) async-start(bf16[8,8,192,128]{3,2,1,0:T(8,128)(2,1)} %get-tuple-element.28), calls=%async_computation.1 | async-start | bytes 6291456 | tf_op jit(solution)/shard_map/all_to_all | solution.py:202
  103.3 6.1 %collective-permute-start.14 = (bf16[4,2,4,2,128,128]{5,4,3,2,1,0:T(8,128)(2,1)S(1)}, bf16[4,2,4,2,128,128]{5,4,3,2,1,0:T(8,128)(2,1)S(1)}, u32[]{:S(2)}, u32[]{:S(2)}) collective-permute-start(bf16[4,2,4,2,128,128]{5,4,3,2,1,0:T(8,128)(2,1)S(1)} %get-tuple-element.32), channel_id=1, source_target_pairs={{0,64},{64,0},{1,65},{65,1},{2,66},{66,2},{3,67},{67,3},{4,68},{68... | collective-permute-start | bytes 6291464 | tf_op jit(solution)/shard_map/ppermute | solution.py:307
  111.2 29.1 %collective-permute-start.15 = (bf16[2,4,2,128,128]{4,3,2,1,0:T(8,128)(2,1)}, bf16[2,4,2,128,128]{4,3,2,1,0:T(8,128)(2,1)}, u32[]{:S(2)}, u32[]{:S(2)}) collective-permute-start(bf16[2,4,2,128,128]{4,3,2,1,0:T(8,128)(2,1)} %get-tuple-element.35), channel_id=1, source_target_pairs={{0,128},{128,256},{256,384},{384,0},{1,129},{129,257},{257,385},{3... | collective-permute-start | bytes 1572872 | tf_op jit(solution)/shard_map/ppermute | solution.py:310
  113.6 28.3 %collective-permute-start.17 = (bf16[2,4,2,128,128]{4,3,2,1,0:T(8,128)(2,1)}, bf16[2,4,2,128,128]{4,3,2,1,0:T(8,128)(2,1)}, u32[]{:S(2)}, u32[]{:S(2)}) collective-permute-start(bf16[2,4,2,128,128]{4,3,2,1,0:T(8,128)(2,1)} %get-tuple-element.36), channel_id=1, source_target_pairs={{0,384},{128,0},{256,128},{384,256},{1,385},{129,1},{257,129},{385... | collective-permute-start | bytes 1572872 | tf_op jit(solution)/shard_map/ppermute | solution.py:310
  117.1 24.9 %collective-permute-start.16 = (bf16[2,4,2,128,128]{4,3,2,1,0:T(8,128)(2,1)}, bf16[2,4,2,128,128]{4,3,2,1,0:T(8,128)(2,1)}, u32[]{:S(2)}, u32[]{:S(2)}) collective-permute-start(bf16[2,4,2,128,128]{4,3,2,1,0:T(8,128)(2,1)} %get-tuple-element.37), channel_id=1, source_target_pairs={{0,256},{128,384},{256,0},{384,128},{1,257},{129,385},{257,1},{385... | collective-permute-start | bytes 1572872 | tf_op jit(solution)/shard_map/ppermute | solution.py:310
  136.8 15.3 %all-to-all-start.2 = ((bf16[8,192,128]{2,1,0:T(8,128)(2,1)}), bf16[8,192,128]{2,1,0:T(8,128)(2,1)S(1)}, u32[]{:S(2)}, u32[]{:S(2)}) async-start(bf16[8,192,128]{2,1,0:T(8,128)(2,1)} %sums.1), calls=%async_computation.2 | async-start | bytes 786432 | tf_op jit(solution)/shard_map/all_to_all | solution.py:202
  (23 other events, 210.8 us)

commit v9 on v8

--- a/solution.py
+++ b/solution.py
@@ -26,6 +26,21 @@
 
 def dot_tn(a, b):
     return lax.dot_general(a, b, (((0,), (0,)), ((), ())), preferred_element_type=F32)
+
+
+def repeat_kernel(first, second, out, both, sem, out_sem):
+    loads = [
+        pltpu.make_async_copy(ref, both.at[n], sem.at[n]) for n, ref in enumerate((first, second))
+    ]
+    stores = [pltpu.make_async_copy(both, out.at[s], out_sem.at[s]) for s in range(out.shape[0])]
+    for copy in loads:
+        copy.start()
+    for copy in loads:
+        copy.wait()
+    for copy in stores:
+        copy.start()
+    for copy in stores:
+        copy.wait()
 
 
 def start_loads(where, units, into, sem, side):
@@ -217,8 +232,20 @@
     lasts = jnp.where(cols // side == opposite, cols % side, side)
     where = jnp.concatenate([cols, here, lasts])
 
-    mine = jnp.stack([inputs, upstream])
-    unit = swap(jnp.broadcast_to(mine, (side, *mine.shape)), lines)
+    mine = pl.pallas_call(
+        repeat_kernel,
+        out_shape=jax.ShapeDtypeStruct((side, 2, tok, width), BF16),
+        in_specs=[anywhere, anywhere],
+        out_specs=anywhere,
+        scratch_shapes=[
+            pltpu.VMEM((2, tok, width), BF16),
+            pltpu.SemaphoreType.DMA((2,)),
+            pltpu.SemaphoreType.DMA((side,)),
+        ],
+        compiler_params=params,
+        name="repeat",
+    )(in_hbm(inputs), in_hbm(upstream))
+    unit = swap(mine, lines)
     dense = jax.ShapeDtypeStruct((side + 1, width, rows * width), BF16)
     in_last, out_last = pl.pallas_call(
         last_kernel,
@@ -244,7 +271,7 @@
     y_units.append(turn(y_back, -1))
     x_steps.append(-(side // 2))
     y_steps.append(side // 2)
-    x_units, y_units = ([in_hbm(u) for u in us[:-1]] + us[-1:] for us in (x_units, y_units))
+    x_units, y_units = ([in_hbm(u) for u in us[:-3]] + us[-3:] for us in (x_units, y_units))
     x_plan, y_plan = (side, tuple(x_steps)), (side, tuple(y_steps))
 
     gathered = pltpu.VMEM((blocks, tok, width), BF16)

time: 154 us -> 153 us (level)
    all_to_all x3, waiting for transfers between devices: 32.9 us -> 25.7 us  [swap(): lax.all_to_all(values, CYZ, split_axis=0, concat_axis=0, tiled=True, axis...]
    ppermute x3, waiting for transfers between devices: 1.67 us -> 5.3 us  [per_device(): lax.ppermute(paired[d], 'x', [(i, (i + d) % nx) for i in range(nx)])]
    ppermute x14, waiting for transfers between devices: 0.51 us -> 3.66 us  [turn(): return lax.ppermute(values, CYZ, pairs)]
    unnamed x52 -> x60, local copies, waits for them, and re-layouts: 8 us -> 10.6 us
    pallas_call x0 -> x1, Pallas kernels: none -> 1.95 us  [per_device(): pl.pallas_call(repeat_kernel, out_shape=jax.ShapeDtypeStruct((side, 2, to...]
    pallas_call x1, Pallas kernels: 6.94 us -> 5.15 us  [per_device(): pl.pallas_call(functools.partial(early_kernel, ((side, x_plan[1][:-1]), (...]
  transfers between devices with their start and end apart: 21 -> 21, of which waited for: 7 -> 7; matrix products, arithmetic and copies ran while one was open for 3% -> 3% of each run, Pallas kernels for 10% -> 9%
where the time goes in v9:
time: 153 us; the launch traced here: 152 us
  starting transfers between devices  74.9 us (49%)
  waiting for transfers between devices  38.8 us (25%)
  Pallas kernels  20.2 us (13%)
  local copies, waits for them, and re-layouts  11.6 us (8%)
  other arithmetic  4.74 us (3%)
    ppermute x14, starting transfers between devices, turn(): return lax.ppermute(values, CYZ, pairs)  46 us
    all_to_all x3, waiting for transfers between devices, swap(): lax.all_to_all(values, CYZ, split_axis=0, concat_axis=0, tiled=True, axis...  25.7 us
    all_to_all x3, starting transfers between devices, swap(): lax.all_to_all(values, CYZ, split_axis=0, concat_axis=0, tiled=True, axis...  17.9 us
    unnamed x60, local copies, waits for them, and re-layouts  10.6 us
    ppermute x3, starting transfers between devices, per_device(): lax.ppermute(paired[d], 'x', [(i, (i + d) % nx) for i in range(nx)])  9.17 us
    pallas_call x1, Pallas kernels, per_device(): pl.pallas_call(functools.partial(weight_kernel, (x_plan, y_plan)), out_sh...  5.9 us
    ppermute x3, waiting for transfers between devices, per_device(): lax.ppermute(paired[d], 'x', [(i, (i + d) % nx) for i in range(nx)])  5.3 us
    pallas_call x1, Pallas kernels, per_device(): pl.pallas_call(functools.partial(early_kernel, ((side, x_plan[1][:-1]), (...  5.15 us
  transfers between devices with their start and end apart: 21, of which 7 were waited for; matrix products, arithmetic and copies ran while one was open for 3% of the time, Pallas kernels for 9%

profile of v9, /device:TPU:6, one launch (start us, length us, event | category | flops | bytes accessed | tf_op | source)
XLA Modules:
  0.0 151.6 jit_solution(6473749241803341838)
XLA Ops:
  2.6 10.3 %all-to-all-start = ((bf16[8,2,192,128]{3,2,1,0:T(8,128)(2,1)}), bf16[8,2,192,128]{3,2,1,0:T(8,128)(2,1)S(1)}, u32[]{:S(2)}, u32[]{:S(2)}) async-start(bf16[8,2,192,128]{3,2,1,0:T(8,128)(2,1)} %repeat.1), calls=%async_computation | async-start | bytes 1572864 | tf_op jit(solution)/shard_map/all_to_all | solution.py:217
  18.5 10.5 %all-to-all-done = bf16[8,2,192,128]{3,2,1,0:T(8,128)(2,1)S(1)} async-done(((bf16[8,2,192,128]{3,2,1,0:T(8,128)(2,1)}), bf16[8,2,192,128]{3,2,1,0:T(8,128)(2,1)S(1)}, u32[]{:S(2)}, u32[]{:S(2)}) %all-to-all-start) | async-done | bytes 786464 | tf_op jit(solution)/shard_map/all_to_all | solution.py:217
  29.2 5.4 %collective-permute-start.4 = (bf16[8,192,128]{2,1,0:T(8,128)(2,1)S(1)}, bf16[8,192,128]{2,1,0:T(8,128)(2,1)S(1)}, u32[]{:S(2)}, u32[]{:S(2)}) collective-permute-start(bf16[8,192,128]{2,1,0:T(8,128)(2,1)S(1)} %get-tuple-element.38.refs_7_.refs_8_), channel_id=1, source_target_pairs={{0,56},{8,0},{16,8},{24,16},{32,24},{40,32},{48,40},{56,48},{1,57}... | collective-permute-start | bytes 1179656 | tf_op jit(solution)/shard_map/ppermute | solution.py:223
  38.5 5.0 %collective-permute-start.8 = (bf16[8,192,128]{2,1,0:T(8,128)(2,1)S(1)}, bf16[8,192,128]{2,1,0:T(8,128)(2,1)S(1)}, u32[]{:S(2)}, u32[]{:S(2)}) collective-permute-start(bf16[8,192,128]{2,1,0:T(8,128)(2,1)S(1)} %get-tuple-element.39.refs_0_), channel_id=1, source_target_pairs={{0,56},{8,0},{16,8},{24,16},{32,24},{40,32},{48,40},{56,48},{1,57}... | collective-permute-start | bytes 1179656 | tf_op jit(solution)/shard_map/ppermute | solution.py:223
  43.6 3.9 %collective-permute-start.5 = (bf16[8,192,128]{2,1,0:T(8,128)(2,1)S(1)}, bf16[8,192,128]{2,1,0:T(8,128)(2,1)S(1)}, u32[]{:S(2)}, u32[]{:S(2)}) collective-permute-start(bf16[8,192,128]{2,1,0:T(8,128)(2,1)S(1)} %collective-permute-done.4.refs_9_.refs_10_), channel_id=1, source_target_pairs={{0,56},{8,0},{16,8},{24,16},{32,24},{40,32},{48,40},{56,48},{1,57}... | collective-permute-start | bytes 1179656 | tf_op jit(solution)/shard_map/ppermute | solution.py:223
  51.6 5.1 %collective-permute-start.9 = (bf16[8,192,128]{2,1,0:T(8,128)(2,1)S(1)}, bf16[8,192,128]{2,1,0:T(8,128)(2,1)S(1)}, u32[]{:S(2)}, u32[]{:S(2)}) collective-permute-start(bf16[8,192,128]{2,1,0:T(8,128)(2,1)S(1)} %collective-permute-done.8.refs_2_), channel_id=1, source_target_pairs={{0,56},{8,0},{16,8},{24,16},{32,24},{40,32},{48,40},{56,48},{1,57}... | collective-permute-start | bytes 1179656 | tf_op jit(solution)/shard_map/ppermute | solution.py:223
  56.8 3.8 %collective-permute-start.6 = (bf16[8,192,128]{2,1,0:T(8,128)(2,1)S(1)}, bf16[8,192,128]{2,1,0:T(8,128)(2,1)S(1)}, u32[]{:S(2)}, u32[]{:S(2)}) collective-permute-start(bf16[8,192,128]{2,1,0:T(8,128)(2,1)S(1)} %collective-permute-done.5.refs_11_.refs_12_), channel_id=1, source_target_pairs={{0,56},{8,0},{16,8},{24,16},{32,24},{40,32},{48,40},{56,48},{1,57}... | collective-permute-start | bytes 1179656 | tf_op jit(solution)/shard_map/ppermute | solution.py:223
  60.5 2.1 %collective-permute-start.2 = (bf16[8,192,128]{2,1,0:T(8,128)(2,1)S(1)}, bf16[8,192,128]{2,1,0:T(8,128)(2,1)S(1)}, u32[]{:S(2)}, u32[]{:S(2)}) collective-permute-start(bf16[8,192,128]{2,1,0:T(8,128)(2,1)S(1)} %collective-permute-done.1.refs_3_), channel_id=1, source_target_pairs={{0,8},{8,16},{16,24},{24,32},{32,40},{40,48},{48,56},{56,0},{1,9},... | collective-permute-start | bytes 1179656 | tf_op jit(solution)/shard_map/ppermute | solution.py:223
  64.6 5.1 %collective-permute-start.10 = (bf16[8,192,128]{2,1,0:T(8,128)(2,1)S(1)}, bf16[8,192,128]{2,1,0:T(8,128)(2,1)S(1)}, u32[]{:S(2)}, u32[]{:S(2)}) collective-permute-start(bf16[8,192,128]{2,1,0:T(8,128)(2,1)S(1)} %collective-permute-done.9.refs_4_), channel_id=1, source_target_pairs={{0,56},{8,0},{16,8},{24,16},{32,24},{40,32},{48,40},{56,48},{1,57}... | collective-permute-start | bytes 1179656 | tf_op jit(solution)/shard_map/ppermute | solution.py:223
  69.8 3.8 %collective-permute-start.7 = (bf16[8,192,128]{2,1,0:T(8,128)(2,1)S(1)}, bf16[8,192,128]{2,1,0:T(8,128)(2,1)S(1)}, u32[]{:S(2)}, u32[]{:S(2)}) collective-permute-start(bf16[8,192,128]{2,1,0:T(8,128)(2,1)S(1)} %collective-permute-done.6.refs_13_.refs_14_), channel_id=1, source_target_pairs={{0,56},{8,0},{16,8},{24,16},{32,24},{40,32},{48,40},{56,48},{1,57}... | collective-permute-start | bytes 1179656 | tf_op jit(solution)/shard_map/ppermute | solution.py:223
  75.8 5.1 %early.1 = (f32[192,512]{1,0:T(8,128)S(1)}, f32[192,512]{1,0:T(8,128)S(1)}, bf16[4,16,128,128]{3,2,1,0:T(8,128)(2,1)S(1)}, bf16[8,128,512]{2,1,0:T(8,128)(2,1)S(1)}, bf16[8,128,512]{2,1,0:T(8,128)(2,1)S(1)}) custom-call(s32[5,64]{1,0:T(8,128)S(1)} %pad_add_fusion.where, bf16[8,192,128]{2,1,0:T(8,128)(2,1)} %copy-done.18, bf16[8,192,128]{2,1,0:T(8,128)(2,1)} %copy-done.21, ...), custom_call_target="tpu_custom_call" | custom-call | tf_op jit(solution)/shard_map/early/pallas_call | solution.py:282
  81.0 3.4 %collective-permute-done.3.x_last.refs_7_ = bf16[8,192,128]{2,1,0:T(8,128)(2,1)S(1)} collective-permute-done((bf16[8,192,128]{2,1,0:T(8,128)(2,1)S(1)}, bf16[8,192,128]{2,1,0:T(8,128)(2,1)S(1)}, u32[]{:S(2)}, u32[]{:S(2)}) %collective-permute-start.3) | collective-permute-done | bytes 393248 | tf_op jit(solution)/shard_map/ppermute | solution.py:223
  84.4 4.5 %back.1 = (bf16[8,8,192,128]{3,2,1,0:T(8,128)(2,1)}, bf16[4,192,128]{2,1,0:T(8,128)(2,1)}, bf16[4,192,128]{2,1,0:T(8,128)(2,1)}) custom-call(s32[5,64]{1,0:T(8,128)S(1)} %pad_add_fusion.where, bf16[8,192,128]{2,1,0:T(8,128)(2,1)S(1)} %collective-permute-done.3.x_last.refs_7_, bf16[8,192,128]{2,1,0:T(8,128)(2,1)S(1)} %collective-permute-done.7.y_last.refs_15_, ...), custom_call_target="tpu_custom_call" | custom-call | tf_op jit(solution)/shard_map/back/pallas_call | solution.py:298
  88.9 4.1 %all-to-all-start.1 = ((bf16[8,8,192,128]{3,2,1,0:T(8,128)(2,1)}), bf16[8,8,192,128]{3,2,1,0:T(8,128)(2,1)S(1)}, u32[]{:S(2)}, u32[]{:S(2)}) async-start(bf16[8,8,192,128]{3,2,1,0:T(8,128)(2,1)} %get-tuple-element.28), calls=%async_computation.1 | async-start | bytes 6291456 | tf_op jit(solution)/shard_map/all_to_all | solution.py:217
  99.9 5.9 %weights.1 = (bf16[4,2,4,2,128,128]{5,4,3,2,1,0:T(8,128)(2,1)S(1)}, bf16[4,2,4,2,128,128]{5,4,3,2,1,0:T(8,128)(2,1)S(1)}) custom-call(s32[5,64]{1,0:T(8,128)S(1)} %pad_add_fusion.where, bf16[8,192,128]{2,1,0:T(8,128)(2,1)} %copy-done.18, bf16[8,192,128]{2,1,0:T(8,128)(2,1)} %copy-done.21, bf16[8,192,128]{2,1,0:T(8,128)(2,1)} %copy-done.23, ...), custom_call_target="tpu_custom_call" | custom-call | tf_op jit(solution)/shard_map/weights/pallas_call | solution.py:317
  107.7 4.1 %collective-permute-done.14 = bf16[4,2,4,2,128,128]{5,4,3,2,1,0:T(8,128)(2,1)S(1)} collective-permute-done((bf16[4,2,4,2,128,128]{5,4,3,2,1,0:T(8,128)(2,1)S(1)}, bf16[4,2,4,2,128,128]{5,4,3,2,1,0:T(8,128)(2,1)S(1)}, u32[]{:S(2)}, u32[]{:S(2)}) %collective-permute-start.14) | collective-permute-done | bytes 2097184 | tf_op jit(solution)/shard_map/ppermute | solution.py:334
  113.7 2.4 %collective-permute-start.15 = (bf16[2,4,2,128,128]{4,3,2,1,0:T(8,128)(2,1)}, bf16[2,4,2,128,128]{4,3,2,1,0:T(8,128)(2,1)}, u32[]{:S(2)}, u32[]{:S(2)}) collective-permute-start(bf16[2,4,2,128,128]{4,3,2,1,0:T(8,128)(2,1)} %get-tuple-element.35), channel_id=1, source_target_pairs={{0,128},{128,256},{256,384},{384,0},{1,129},{129,257},{257,385},{3... | collective-permute-start | bytes 1572872 | tf_op jit(solution)/shard_map/ppermute | solution.py:337
  116.1 3.5 %collective-permute-start.17 = (bf16[2,4,2,128,128]{4,3,2,1,0:T(8,128)(2,1)}, bf16[2,4,2,128,128]{4,3,2,1,0:T(8,128)(2,1)}, u32[]{:S(2)}, u32[]{:S(2)}) collective-permute-start(bf16[2,4,2,128,128]{4,3,2,1,0:T(8,128)(2,1)} %get-tuple-element.36), channel_id=1, source_target_pairs={{0,384},{128,0},{256,128},{384,256},{1,385},{129,1},{257,129},{385... | collective-permute-start | bytes 1572872 | tf_op jit(solution)/shard_map/ppermute | solution.py:337
  119.5 3.3 %collective-permute-start.16 = (bf16[2,4,2,128,128]{4,3,2,1,0:T(8,128)(2,1)}, bf16[2,4,2,128,128]{4,3,2,1,0:T(8,128)(2,1)}, u32[]{:S(2)}, u32[]{:S(2)}) collective-permute-start(bf16[2,4,2,128,128]{4,3,2,1,0:T(8,128)(2,1)} %get-tuple-element.37), channel_id=1, source_target_pairs={{0,256},{128,384},{256,0},{384,128},{1,257},{129,385},{257,1},{385... | collective-permute-start | bytes 1572872 | tf_op jit(solution)/shard_map/ppermute | solution.py:337
  122.9 11.6 %all-to-all-done.1.parts = bf16[8,8,192,128]{3,2,1,0:T(8,128)(2,1)S(1)} async-done(((bf16[8,8,192,128]{3,2,1,0:T(8,128)(2,1)}), bf16[8,8,192,128]{3,2,1,0:T(8,128)(2,1)S(1)}, u32[]{:S(2)}, u32[]{:S(2)}) %all-to-all-start.1) | async-done | bytes 3145760 | tf_op jit(solution)/shard_map/all_to_all | solution.py:217
  135.6 3.5 %all-to-all-start.2 = ((bf16[8,192,128]{2,1,0:T(8,128)(2,1)}), bf16[8,192,128]{2,1,0:T(8,128)(2,1)S(1)}, u32[]{:S(2)}, u32[]{:S(2)}) async-start(bf16[8,192,128]{2,1,0:T(8,128)(2,1)} %sums.1), calls=%async_computation.2 | async-start | bytes 786432 | tf_op jit(solution)/shard_map/all_to_all | solution.py:217
  139.1 5.3 %collective-permute-done.17 = bf16[2,4,2,128,128]{4,3,2,1,0:T(8,128)(2,1)} collective-permute-done((bf16[2,4,2,128,128]{4,3,2,1,0:T(8,128)(2,1)}, bf16[2,4,2,128,128]{4,3,2,1,0:T(8,128)(2,1)}, u32[]{:S(2)}, u32[]{:S(2)}) %collective-permute-start.17) | collective-permute-done | bytes 524320 | tf_op jit(solution)/shard_map/ppermute | solution.py:337
  144.4 2.1 %fusion.2 = bf16[2,4,2,128,128]{4,3,2,1,0:T(8,128)(2,1)S(1)} fusion(bf16[2,4,2,128,128]{4,3,2,1,0:T(8,128)(2,1)} %collective-permute-done.17, bf16[2,4,2,128,128]{4,3,2,1,0:T(8,128)(2,1)} %collective-permute-done.16, bf16[2,4,2,128,128]{4,3,2,1,0:T(8,128)(2,1)} %collective-permute-done.15, bf16[4,2,4,2,128,128]{5,4,3,2,1,0:T(8,128)(2,1)} %copy-done.19, ...), kind=kLoop, calls=%fused_computation.3 | loop fusion | flops 3145728 | bytes 3145728 | tf_op jit(solution)/shard_map/convert_element_type | solution.py:339
  147.4 3.5 %all-to-all-done.2 = bf16[8,192,128]{2,1,0:T(8,128)(2,1)S(1)} async-done(((bf16[8,192,128]{2,1,0:T(8,128)(2,1)}), bf16[8,192,128]{2,1,0:T(8,128)(2,1)S(1)}, u32[]{:S(2)}, u32[]{:S(2)}) %all-to-all-start.2) | async-done | bytes 393248 | tf_op jit(solution)/shard_map/all_to_all | solution.py:217
  (95 shorter events, 32.9 us)
Async XLA Ops:
  2.6 26.5 %all-to-all-start = ((bf16[8,2,192,128]{3,2,1,0:T(8,128)(2,1)}), bf16[8,2,192,128]{3,2,1,0:T(8,128)(2,1)S(1)}, u32[]{:S(2)}, u32[]{:S(2)}) async-start(bf16[8,2,192,128]{3,2,1,0:T(8,128)(2,1)} %repeat.1), calls=%async_computation | async-start | bytes 1572864 | tf_op jit(solution)/shard_map/all_to_all | solution.py:217
  29.2 46.5 %copy-start.17 = (bf16[8,192,128]{2,1,0:T(8,128)(2,1)}, bf16[8,192,128]{2,1,0:T(8,128)(2,1)S(1)}, u32[]{:S(2)}) copy-start(bf16[8,192,128]{2,1,0:T(8,128)(2,1)S(1)} %get-tuple-element.38.refs_7_.refs_8_) | copy-start | bytes 1179652
  29.2 46.5 %copy-start.18 = (bf16[8,192,128]{2,1,0:T(8,128)(2,1)}, bf16[8,192,128]{2,1,0:T(8,128)(2,1)S(1)}, u32[]{:S(2)}) copy-start(bf16[8,192,128]{2,1,0:T(8,128)(2,1)S(1)} %get-tuple-element.39.refs_0_) | copy-start | bytes 1179652
  29.2 14.4 %collective-permute-start.4 = (bf16[8,192,128]{2,1,0:T(8,128)(2,1)S(1)}, bf16[8,192,128]{2,1,0:T(8,128)(2,1)S(1)}, u32[]{:S(2)}, u32[]{:S(2)}) collective-permute-start(bf16[8,192,128]{2,1,0:T(8,128)(2,1)S(1)} %get-tuple-element.38.refs_7_.refs_8_), channel_id=1, source_target_pairs={{0,56},{8,0},{16,8},{24,16},{32,24},{40,32},{48,40},{56,48},{1,57}... | collective-permute-start | bytes 1179656 | tf_op jit(solution)/shard_map/ppermute | solution.py:223
  34.6 13.0 %collective-permute-start = (bf16[8,192,128]{2,1,0:T(8,128)(2,1)S(1)}, bf16[8,192,128]{2,1,0:T(8,128)(2,1)S(1)}, u32[]{:S(2)}, u32[]{:S(2)}) collective-permute-start(bf16[8,192,128]{2,1,0:T(8,128)(2,1)S(1)} %get-tuple-element.39.refs_0_), channel_id=1, source_target_pairs={{0,8},{8,16},{16,24},{24,32},{32,40},{40,48},{48,56},{56,0},{1,9},... | collective-permute-start | bytes 1179656 | tf_op jit(solution)/shard_map/ppermute | solution.py:223
  36.5 13.2 %collective-permute-start.11 = (bf16[8,192,128]{2,1,0:T(8,128)(2,1)S(1)}, bf16[8,192,128]{2,1,0:T(8,128)(2,1)S(1)}, u32[]{:S(2)}, u32[]{:S(2)}) collective-permute-start(bf16[8,192,128]{2,1,0:T(8,128)(2,1)S(1)} %get-tuple-element.38.refs_7_.refs_8_), channel_id=1, source_target_pairs={{0,8},{8,16},{16,24},{24,32},{32,40},{40,48},{48,56},{56,0},{1,9},... | collective-permute-start | bytes 1179656 | tf_op jit(solution)/shard_map/ppermute | solution.py:223
  38.5 13.1 %collective-permute-start.8 = (bf16[8,192,128]{2,1,0:T(8,128)(2,1)S(1)}, bf16[8,192,128]{2,1,0:T(8,128)(2,1)S(1)}, u32[]{:S(2)}, u32[]{:S(2)}) collective-permute-start(bf16[8,192,128]{2,1,0:T(8,128)(2,1)S(1)} %get-tuple-element.39.refs_0_), channel_id=1, source_target_pairs={{0,56},{8,0},{16,8},{24,16},{32,24},{40,32},{48,40},{56,48},{1,57}... | collective-permute-start | bytes 1179656 | tf_op jit(solution)/shard_map/ppermute | solution.py:223
  43.6 32.1 %copy-start.20 = (bf16[8,192,128]{2,1,0:T(8,128)(2,1)}, bf16[8,192,128]{2,1,0:T(8,128)(2,1)S(1)}, u32[]{:S(2)}) copy-start(bf16[8,192,128]{2,1,0:T(8,128)(2,1)S(1)} %collective-permute-done.4.refs_9_.refs_10_) | copy-start | bytes 1179652
  43.6 13.2 %collective-permute-start.5 = (bf16[8,192,128]{2,1,0:T(8,128)(2,1)S(1)}, bf16[8,192,128]{2,1,0:T(8,128)(2,1)S(1)}, u32[]{:S(2)}, u32[]{:S(2)}) collective-permute-start(bf16[8,192,128]{2,1,0:T(8,128)(2,1)S(1)} %collective-permute-done.4.refs_9_.refs_10_), channel_id=1, source_target_pairs={{0,56},{8,0},{16,8},{24,16},{32,24},{40,32},{48,40},{56,48},{1,57}... | collective-permute-start | bytes 1179656 | tf_op jit(solution)/shard_map/ppermute | solution.py:223
  47.5 13.0 %collective-permute-start.1 = (bf16[8,192,128]{2,1,0:T(8,128)(2,1)S(1)}, bf16[8,192,128]{2,1,0:T(8,128)(2,1)S(1)}, u32[]{:S(2)}, u32[]{:S(2)}) collective-permute-start(bf16[8,192,128]{2,1,0:T(8,128)(2,1)S(1)} %collective-permute-done.refs_1_), channel_id=1, source_target_pairs={{0,8},{8,16},{16,24},{24,32},{32,40},{40,48},{48,56},{56,0},{1,9},... | collective-permute-start | bytes 1179656 | tf_op jit(solution)/shard_map/ppermute | solution.py:223
  49.7 13.0 %collective-permute-start.12 = (bf16[8,192,128]{2,1,0:T(8,128)(2,1)S(1)}, bf16[8,192,128]{2,1,0:T(8,128)(2,1)S(1)}, u32[]{:S(2)}, u32[]{:S(2)}) collective-permute-start(bf16[8,192,128]{2,1,0:T(8,128)(2,1)S(1)} %collective-permute-done.11.refs_8_.refs_9_), channel_id=1, source_target_pairs={{0,8},{8,16},{16,24},{24,32},{32,40},{40,48},{48,56},{56,0},{1,9},... | collective-permute-start | bytes 1179656 | tf_op jit(solution)/shard_map/ppermute | solution.py:223
  51.6 13.0 %collective-permute-start.9 = (bf16[8,192,128]{2,1,0:T(8,128)(2,1)S(1)}, bf16[8,192,128]{2,1,0:T(8,128)(2,1)S(1)}, u32[]{:S(2)}, u32[]{:S(2)}) collective-permute-start(bf16[8,192,128]{2,1,0:T(8,128)(2,1)S(1)} %collective-permute-done.8.refs_2_), channel_id=1, source_target_pairs={{0,56},{8,0},{16,8},{24,16},{32,24},{40,32},{48,40},{56,48},{1,57}... | collective-permute-start | bytes 1179656 | tf_op jit(solution)/shard_map/ppermute | solution.py:223
  56.8 13.0 %collective-permute-start.6 = (bf16[8,192,128]{2,1,0:T(8,128)(2,1)S(1)}, bf16[8,192,128]{2,1,0:T(8,128)(2,1)S(1)}, u32[]{:S(2)}, u32[]{:S(2)}) collective-permute-start(bf16[8,192,128]{2,1,0:T(8,128)(2,1)S(1)} %collective-permute-done.5.refs_11_.refs_12_), channel_id=1, source_target_pairs={{0,56},{8,0},{16,8},{24,16},{32,24},{40,32},{48,40},{56,48},{1,57}... | collective-permute-start | bytes 1179656 | tf_op jit(solution)/shard_map/ppermute | solution.py:223
  60.5 13.0 %collective-permute-start.2 = (bf16[8,192,128]{2,1,0:T(8,128)(2,1)S(1)}, bf16[8,192,128]{2,1,0:T(8,128)(2,1)S(1)}, u32[]{:S(2)}, u32[]{:S(2)}) collective-permute-start(bf16[8,192,128]{2,1,0:T(8,128)(2,1)S(1)} %collective-permute-done.1.refs_3_), channel_id=1, source_target_pairs={{0,8},{8,16},{16,24},{24,32},{32,40},{40,48},{48,56},{56,0},{1,9},... | collective-permute-start | bytes 1179656 | tf_op jit(solution)/shard_map/ppermute | solution.py:223
  62.7 13.0 %collective-permute-start.13 = (bf16[8,192,128]{2,1,0:T(8,128)(2,1)S(1)}, bf16[8,192,128]{2,1,0:T(8,128)(2,1)S(1)}, u32[]{:S(2)}, u32[]{:S(2)}) collective-permute-start(bf16[8,192,128]{2,1,0:T(8,128)(2,1)S(1)} %collective-permute-done.12.refs_10_.refs_11_), channel_id=1, source_target_pairs={{0,8},{8,16},{16,24},{24,32},{32,40},{40,48},{48,56},{56,0},{1,9},... | collective-permute-start | bytes 1179656 | tf_op jit(solution)/shard_map/ppermute | solution.py:223
  64.6 11.1 %collective-permute-start.10 = (bf16[8,192,128]{2,1,0:T(8,128)(2,1)S(1)}, bf16[8,192,128]{2,1,0:T(8,128)(2,1)S(1)}, u32[]{:S(2)}, u32[]{:S(2)}) collective-permute-start(bf16[8,192,128]{2,1,0:T(8,128)(2,1)S(1)} %collective-permute-done.9.refs_4_), channel_id=1, source_target_pairs={{0,56},{8,0},{16,8},{24,16},{32,24},{40,32},{48,40},{56,48},{1,57}... | collective-permute-start | bytes 1179656 | tf_op jit(solution)/shard_map/ppermute | solution.py:223
  69.8 11.2 %collective-permute-start.7 = (bf16[8,192,128]{2,1,0:T(8,128)(2,1)S(1)}, bf16[8,192,128]{2,1,0:T(8,128)(2,1)S(1)}, u32[]{:S(2)}, u32[]{:S(2)}) collective-permute-start(bf16[8,192,128]{2,1,0:T(8,128)(2,1)S(1)} %collective-permute-done.6.refs_13_.refs_14_), channel_id=1, source_target_pairs={{0,56},{8,0},{16,8},{24,16},{32,24},{40,32},{48,40},{56,48},{1,57}... | collective-permute-start | bytes 1179656 | tf_op jit(solution)/shard_map/ppermute | solution.py:223
  73.5 10.9 %collective-permute-start.3 = (bf16[8,192,128]{2,1,0:T(8,128)(2,1)S(1)}, bf16[8,192,128]{2,1,0:T(8,128)(2,1)S(1)}, u32[]{:S(2)}, u32[]{:S(2)}) collective-permute-start(bf16[8,192,128]{2,1,0:T(8,128)(2,1)S(1)} %collective-permute-done.2.refs_5_), channel_id=1, source_target_pairs={{0,8},{8,16},{16,24},{24,32},{32,40},{40,48},{48,56},{56,0},{1,9},... | collective-permute-start | bytes 1179656 | tf_op jit(solution)/shard_map/ppermute | solution.py:223
  88.9 45.6 %all-to-all-start.1 = ((bf16[8,8,192,128]{3,2,1,0:T(8,128)(2,1)}), bf16[8,8,192,128]{3,2,1,0:T(8,128)(2,1)S(1)}, u32[]{:S(2)}, u32[]{:S(2)}) async-start(bf16[8,8,192,128]{3,2,1,0:T(8,128)(2,1)} %get-tuple-element.28), calls=%async_computation.1 | async-start | bytes 6291456 | tf_op jit(solution)/shard_map/all_to_all | solution.py:217
  105.8 6.1 %collective-permute-start.14 = (bf16[4,2,4,2,128,128]{5,4,3,2,1,0:T(8,128)(2,1)S(1)}, bf16[4,2,4,2,128,128]{5,4,3,2,1,0:T(8,128)(2,1)S(1)}, u32[]{:S(2)}, u32[]{:S(2)}) collective-permute-start(bf16[4,2,4,2,128,128]{5,4,3,2,1,0:T(8,128)(2,1)S(1)} %get-tuple-element.32), channel_id=1, source_target_pairs={{0,64},{64,0},{1,65},{65,1},{2,66},{66,2},{3,67},{67,3},{4,68},{68... | collective-permute-start | bytes 6291464 | tf_op jit(solution)/shard_map/ppermute | solution.py:334
  113.7 25.4 %collective-permute-start.15 = (bf16[2,4,2,128,128]{4,3,2,1,0:T(8,128)(2,1)}, bf16[2,4,2,128,128]{4,3,2,1,0:T(8,128)(2,1)}, u32[]{:S(2)}, u32[]{:S(2)}) collective-permute-start(bf16[2,4,2,128,128]{4,3,2,1,0:T(8,128)(2,1)} %get-tuple-element.35), channel_id=1, source_target_pairs={{0,128},{128,256},{256,384},{384,0},{1,129},{129,257},{257,385},{3... | collective-permute-start | bytes 1572872 | tf_op jit(solution)/shard_map/ppermute | solution.py:337
  116.1 28.3 %collective-permute-start.17 = (bf16[2,4,2,128,128]{4,3,2,1,0:T(8,128)(2,1)}, bf16[2,4,2,128,128]{4,3,2,1,0:T(8,128)(2,1)}, u32[]{:S(2)}, u32[]{:S(2)}) collective-permute-start(bf16[2,4,2,128,128]{4,3,2,1,0:T(8,128)(2,1)} %get-tuple-element.36), channel_id=1, source_target_pairs={{0,384},{128,0},{256,128},{384,256},{1,385},{129,1},{257,129},{385... | collective-permute-start | bytes 1572872 | tf_op jit(solution)/shard_map/ppermute | solution.py:337
  119.5 24.9 %collective-permute-start.16 = (bf16[2,4,2,128,128]{4,3,2,1,0:T(8,128)(2,1)}, bf16[2,4,2,128,128]{4,3,2,1,0:T(8,128)(2,1)}, u32[]{:S(2)}, u32[]{:S(2)}) collective-permute-start(bf16[2,4,2,128,128]{4,3,2,1,0:T(8,128)(2,1)} %get-tuple-element.37), channel_id=1, source_target_pairs={{0,256},{128,384},{256,0},{384,128},{1,257},{129,385},{257,1},{385... | collective-permute-start | bytes 1572872 | tf_op jit(solution)/shard_map/ppermute | solution.py:337
  135.6 15.3 %all-to-all-start.2 = ((bf16[8,192,128]{2,1,0:T(8,128)(2,1)}), bf16[8,192,128]{2,1,0:T(8,128)(2,1)S(1)}, u32[]{:S(2)}, u32[]{:S(2)}) async-start(bf16[8,192,128]{2,1,0:T(8,128)(2,1)} %sums.1), calls=%async_computation.2 | async-start | bytes 786432 | tf_op jit(solution)/shard_map/all_to_all | solution.py:217
  (27 other events, 224.8 us)

commit v10 on v8

--- a/solution.py
+++ b/solution.py
@@ -42,57 +42,45 @@
     return jnp.concatenate([blocks[where[line, r * per_row + k]] for k in range(per_row)], axis=1)
 
 
-def last_kernel(where, w_in, w_out, in_last, out_last):
-    rows, per_row, width, _ = w_in.shape
-    in_last[...] = jnp.zeros_like(in_last)
-    out_last[...] = jnp.zeros_like(out_last)
-    for r in range(rows):
-        at = slice(r * width, (r + 1) * width)
-        for k in range(per_row):
-            in_last[where[3, r * per_row + k], :, at] = w_in[r, k]
-            out_last[where[4, r * per_row + k], :, at] = w_out[r, k].T
-
-
 def early_kernel(plans, where, *refs):
     (side, x_steps), (_, y_steps) = plans
     n_x, n_y = len(x_steps), len(y_steps)
     x_units = list(zip(refs[:n_x], x_steps))
     y_units = list(zip(refs[n_x : n_x + n_y], y_steps))
-    w_in, w_out, in_last, out_last = refs[n_x + n_y : n_x + n_y + 4]
-    hidden, grad_act, wi, li, lo, wo, x, y, x_sem, y_sem, w_sem = refs[n_x + n_y + 4 :]
+    w_in, w_out = refs[n_x + n_y : n_x + n_y + 2]
+    hidden, grad_act, wi, in_last, out_last, wo, x, y, x_sem, y_sem, w_sem = refs[n_x + n_y + 2 :]
     rows, per_row, width, _ = w_in.shape
     load_in = pltpu.make_async_copy(w_in, wi, w_sem.at[0])
     load_out = pltpu.make_async_copy(w_out, wo, w_sem.at[1])
     load_in.start()
+    load_out.start()
     x_loads = start_loads(where, x_units, x, x_sem, side)
-    load_out.start()
     y_loads = start_loads(where, y_units, y, y_sem, side)
-    lasts = [
-        pltpu.make_async_copy(ref.at[pl.ds(0, side)], into, w_sem.at[2 + n])
-        for n, (ref, into) in enumerate(((in_last, li), (out_last, lo)))
-    ]
-    for copy in lasts:
-        copy.start()
+    in_last[...] = jnp.zeros_like(in_last)
+    out_last[...] = jnp.zeros_like(out_last)
     places = x.shape[0] // side
     opposite = pl.ds(lax.rem(where[2, 1] + places // 2, places) * side, side)
     x[opposite] = jnp.zeros((side, *x.shape[1:]), BF16)
     y[opposite] = jnp.zeros((side, *y.shape[1:]), BF16)
     load_in.wait()
+    load_out.wait()
+    for r in range(rows):
+        at = slice(r * width, (r + 1) * width)
+        for k in range(per_row):
+            in_last[where[3, r * per_row + k], :, at] = wi[r, k]
+            out_last[where[4, r * per_row + k], :, at] = wo[r, k].T
     for copy in x_loads:
         copy.wait()
     for r in range(rows):
         x_row = row_of(x, where, 0, r, per_row)
         at = slice(r * width, (r + 1) * width)
         hidden[:, at] = dot_nn(x_row, wi[r].reshape(per_row * width, width))
-    load_out.wait()
     for copy in y_loads:
         copy.wait()
     for r in range(rows):
         w_row = jnp.concatenate([wo[r, k] for k in range(per_row)], axis=1)
         at = slice(r * width, (r + 1) * width)
         grad_act[:, at] = dot_nt(row_of(y, where, 1, r, per_row), w_row)
-    for copy in lasts:
-        copy.wait()
 
 
 def back_kernel(where, x_last, y_last, hidden_most, grad_most, wi, li, lo, *refs):
@@ -102,8 +90,8 @@
     total[...] = jnp.zeros_like(total)
     x_unit = jnp.concatenate([x_last[n] for n in range(side)], axis=1)
     y_unit = jnp.concatenate([y_last[n] for n in range(side)], axis=1)
-    hidden = hidden_most[...] + dot_nn(x_unit, li[...].reshape(side * width, rows * width))
-    grad_act = grad_most[...] + dot_nn(y_unit, lo[...].reshape(side * width, rows * width))
+    hidden = hidden_most[...] + dot_nn(x_unit, li[:side].reshape(side * width, rows * width))
+    grad_act = grad_most[...] + dot_nn(y_unit, lo[:side].reshape(side * width, rows * width))
     square = hidden * hidden
     tanh = jnp.tanh(GELU_SCALE * hidden * (1.0 + GELU_CUBE * square))
     half = 0.5 * (1.0 + tanh)
@@ -219,16 +207,6 @@
 
     mine = jnp.stack([inputs, upstream])
     unit = swap(jnp.broadcast_to(mine, (side, *mine.shape)), lines)
-    dense = jax.ShapeDtypeStruct((side + 1, width, rows * width), BF16)
-    in_last, out_last = pl.pallas_call(
-        last_kernel,
-        out_shape=(dense, dense),
-        in_specs=[smem, vmem, vmem],
-        out_specs=(vmem, vmem),
-        compiler_params=params,
-        name="last",
-    )(where, w_in, w_out)
-    unit, in_last, out_last = lax.optimization_barrier((unit, in_last, out_last))
     x_units, y_units = [unit[:, 0]], [unit[:, 1]]
     x_steps, y_steps = [0], [0]
     x_ahead = x_back = x_units[0]
@@ -244,30 +222,30 @@
     y_units.append(turn(y_back, -1))
     x_steps.append(-(side // 2))
     y_steps.append(side // 2)
-    x_units, y_units = ([in_hbm(u) for u in us[:-1]] + us[-1:] for us in (x_units, y_units))
+    x_units, y_units = ([in_hbm(u) for u in us[:-3]] + us[-3:] for us in (x_units, y_units))
     x_plan, y_plan = (side, tuple(x_steps)), (side, tuple(y_steps))
 
     gathered = pltpu.VMEM((blocks, tok, width), BF16)
     loaded = pltpu.SemaphoreType.DMA((side,))
     values = pltpu.HBM((rows, tok, width), BF16)
     kept = pltpu.VMEM((tok, rows * width), F32)
-    last = pltpu.VMEM((side, width, rows * width), BF16)
+    last = pltpu.VMEM((side + 1, width, rows * width), BF16)
     hidden_most, grad_most, wi, li, lo = pl.pallas_call(
         functools.partial(early_kernel, ((side, x_plan[1][:-1]), (side, y_plan[1][:-1]))),
         out_shape=(kept, kept, pltpu.VMEM(w_in.shape, BF16), last, last),
         out_specs=(vmem,) * 5,
-        in_specs=[smem] + [anywhere] * (len(x_units) + len(y_units) + 2),
+        in_specs=[smem] + [anywhere] * (len(x_units) + len(y_units)),
         scratch_shapes=[
             pltpu.VMEM(w_out.shape, BF16),
             gathered,
             gathered,
             loaded,
             loaded,
-            pltpu.SemaphoreType.DMA((4,)),
+            pltpu.SemaphoreType.DMA((2,)),
         ],
         compiler_params=params,
         name="early",
-    )(where, *x_units[:-1], *y_units[:-1], *(in_hbm(v) for v in (w_in, w_out, in_last, out_last)))
+    )(where, *x_units[:-1], *y_units[:-1], in_hbm(w_in), in_hbm(w_out))
     placed, act, grad = pl.pallas_call(
         back_kernel,
         out_shape=(pltpu.HBM((side, blocks // side, tok, width), BF16), values, values),
@@ -303,7 +281,7 @@
         ],
         compiler_params=params,
         name="weights",
-    )(where, *x_units, *y_units, act, grad)
+    )(where, *(in_hbm(v) for v in (*x_units, *y_units)), act, grad)
     swapped = lax.ppermute(other, "c", [(0, 1), (1, 0)])
     paired = [(own[d].astype(F32) + swapped[d].astype(F32)).astype(BF16) for d in range(nx)]
     spread = [

time: 154 us -> 152 us (0.987)
  blocking collectives: 0 us -> 26.2 us
  starting transfers between devices: 76 us -> 64.7 us
  local copies, waits for them, and re-layouts: 10.1 us -> 1.29 us
  waiting for transfers between devices: 39.3 us -> 33.7 us
  Pallas kernels: 20.4 us -> 18 us
    all_to_all x0 -> x1, blocking collectives: none -> 26.2 us  [swap(): lax.all_to_all(values, CYZ, split_axis=0, concat_axis=0, tiled=True, axis...]
    all_to_all x3 -> x2, starting transfers between devices: 19 us -> 7.68 us  [swap(): lax.all_to_all(values, CYZ, split_axis=0, concat_axis=0, tiled=True, axis...]
    unnamed x52 -> x38, local copies, waits for them, and re-layouts: 8 us -> 0.08 us
    all_to_all x3 -> x2, waiting for transfers between devices: 32.9 us -> 26.7 us  [swap(): lax.all_to_all(values, CYZ, split_axis=0, concat_axis=0, tiled=True, axis...]
    ppermute x14, waiting for transfers between devices: 0.51 us -> 2.83 us  [turn(): return lax.ppermute(values, CYZ, pairs)]
    ppermute x3, waiting for transfers between devices: 1.67 us -> 0.01 us  [per_device(): lax.ppermute(paired[d], 'x', [(i, (i + d) % nx) for i in range(nx)])]
    pallas_call x1 -> x0, Pallas kernels: 1.58 us -> none  [per_device(): pl.pallas_call(last_kernel, out_shape=(dense, dense), in_specs=[smem, vme...]
  transfers between devices with their start and end apart: 21 -> 20, of which waited for: 7 -> 5; matrix products, arithmetic and copies ran while one was open for 3% -> 3% of each run, Pallas kernels for 10% -> 9%
where the time goes in v10:
time: 152 us; the launch traced here: 151 us
  starting transfers between devices  64.7 us (43%)
  waiting for transfers between devices  33.7 us (22%)
  blocking collectives  26.2 us (17%)
  Pallas kernels  18 us (12%)
  other arithmetic  5.61 us (4%)
    ppermute x14, starting transfers between devices, turn(): return lax.ppermute(values, CYZ, pairs)  46 us
    all_to_all x2, waiting for transfers between devices, swap(): lax.all_to_all(values, CYZ, split_axis=0, concat_axis=0, tiled=True, axis...  26.7 us
    all_to_all x1, blocking collectives, swap(): lax.all_to_all(values, CYZ, split_axis=0, concat_axis=0, tiled=True, axis...  26.2 us
    ppermute x3, starting transfers between devices, per_device(): lax.ppermute(paired[d], 'x', [(i, (i + d) % nx) for i in range(nx)])  9.15 us
    all_to_all x2, starting transfers between devices, swap(): lax.all_to_all(values, CYZ, split_axis=0, concat_axis=0, tiled=True, axis...  7.68 us
    pallas_call x1, Pallas kernels, per_device(): pl.pallas_call(functools.partial(weight_kernel, (x_plan, y_plan)), out_sh...  6.46 us
    pallas_call x1, Pallas kernels, per_device(): pl.pallas_call(functools.partial(early_kernel, ((side, x_plan[1][:-1]), (...  5.88 us
    pallas_call x1, Pallas kernels, per_device(): pl.pallas_call(back_kernel, out_shape=(pltpu.HBM((side, blocks // side, t...  4.49 us
  transfers between devices with their start and end apart: 20, of which 5 were waited for; matrix products, arithmetic and copies ran while one was open for 3% of the time, Pallas kernels for 9%

profile of v10, /device:TPU:6, one launch (start us, length us, event | category | flops | bytes accessed | tf_op | source)
XLA Modules:
  0.0 150.7 jit_solution(6434672429901871390)
XLA Ops:
  1.7 26.2 %all_to_all.15 = bf16[8,2,192,128]{3,2,1,0:T(8,128)(2,1)S(1)} all-to-all(bf16[8,2,192,128]{3,2,1,0:T(8,128)(2,1)S(1)} %broadcast_in_dim.5), channel_id=1, replica_groups={{0,1,2,3,4,5,6,7},{8,9,10,11,12,13,14,15},{16,17,18,19,20,21,22,23},{24..., dimensions={0} | all-to-all | bytes 1572864 | tf_op jit(solution)/shard_map/all_to_all | solution.py:190
  27.9 5.4 %collective-permute-start.4 = (bf16[8,192,128]{2,1,0:T(8,128)(2,1)S(1)}, bf16[8,192,128]{2,1,0:T(8,128)(2,1)S(1)}, u32[]{:S(2)}, u32[]{:S(2)}) collective-permute-start(bf16[8,192,128]{2,1,0:T(8,128)(2,1)S(1)} %get-tuple-element.28.refs_7_.refs_8_), channel_id=1, source_target_pairs={{0,56},{8,0},{16,8},{24,16},{32,24},{40,32},{48,40},{56,48},{1,57}... | collective-permute-start | bytes 1179656 | tf_op jit(solution)/shard_map/ppermute | solution.py:196
  35.3 2.0 %collective-permute-start.11 = (bf16[8,192,128]{2,1,0:T(8,128)(2,1)S(1)}, bf16[8,192,128]{2,1,0:T(8,128)(2,1)S(1)}, u32[]{:S(2)}, u32[]{:S(2)}) collective-permute-start(bf16[8,192,128]{2,1,0:T(8,128)(2,1)S(1)} %get-tuple-element.28.refs_7_.refs_8_), channel_id=1, source_target_pairs={{0,8},{8,16},{16,24},{24,32},{32,40},{40,48},{48,56},{56,0},{1,9},... | collective-permute-start | bytes 1179656 | tf_op jit(solution)/shard_map/ppermute | solution.py:196
  37.3 5.0 %collective-permute-start.8 = (bf16[8,192,128]{2,1,0:T(8,128)(2,1)S(1)}, bf16[8,192,128]{2,1,0:T(8,128)(2,1)S(1)}, u32[]{:S(2)}, u32[]{:S(2)}) collective-permute-start(bf16[8,192,128]{2,1,0:T(8,128)(2,1)S(1)} %get-tuple-element.29.refs_0_), channel_id=1, source_target_pairs={{0,56},{8,0},{16,8},{24,16},{32,24},{40,32},{48,40},{56,48},{1,57}... | collective-permute-start | bytes 1179656 | tf_op jit(solution)/shard_map/ppermute | solution.py:196
  42.3 3.9 %collective-permute-start.5 = (bf16[8,192,128]{2,1,0:T(8,128)(2,1)S(1)}, bf16[8,192,128]{2,1,0:T(8,128)(2,1)S(1)}, u32[]{:S(2)}, u32[]{:S(2)}) collective-permute-start(bf16[8,192,128]{2,1,0:T(8,128)(2,1)S(1)} %collective-permute-done.4.refs_9_.refs_10_), channel_id=1, source_target_pairs={{0,56},{8,0},{16,8},{24,16},{32,24},{40,32},{48,40},{56,48},{1,57}... | collective-permute-start | bytes 1179656 | tf_op jit(solution)/shard_map/ppermute | solution.py:196
  50.4 5.1 %collective-permute-start.9 = (bf16[8,192,128]{2,1,0:T(8,128)(2,1)S(1)}, bf16[8,192,128]{2,1,0:T(8,128)(2,1)}, u32[]{:S(2)}, u32[]{:S(2)}) collective-permute-start(bf16[8,192,128]{2,1,0:T(8,128)(2,1)S(1)} %collective-permute-done.8.refs_2_), channel_id=1, source_target_pairs={{0,56},{8,0},{16,8},{24,16},{32,24},{40,32},{48,40},{56,48},{1,57}... | collective-permute-start | bytes 1179656 | tf_op jit(solution)/shard_map/ppermute | solution.py:196
  55.5 3.8 %collective-permute-start.6 = (bf16[8,192,128]{2,1,0:T(8,128)(2,1)S(1)}, bf16[8,192,128]{2,1,0:T(8,128)(2,1)S(1)}, u32[]{:S(2)}, u32[]{:S(2)}) collective-permute-start(bf16[8,192,128]{2,1,0:T(8,128)(2,1)S(1)} %collective-permute-done.5.refs_11_.refs_12_), channel_id=1, source_target_pairs={{0,56},{8,0},{16,8},{24,16},{32,24},{40,32},{48,40},{56,48},{1,57}... | collective-permute-start | bytes 1179656 | tf_op jit(solution)/shard_map/ppermute | solution.py:196
  59.3 2.1 %collective-permute-start.2 = (bf16[8,192,128]{2,1,0:T(8,128)(2,1)}, bf16[8,192,128]{2,1,0:T(8,128)(2,1)S(1)}, u32[]{:S(2)}, u32[]{:S(2)}) collective-permute-start(bf16[8,192,128]{2,1,0:T(8,128)(2,1)} %collective-permute-done.1.refs_3_), channel_id=1, source_target_pairs={{0,8},{8,16},{16,24},{24,32},{32,40},{40,48},{48,56},{56,0},{1,9},... | collective-permute-start | bytes 1179656 | tf_op jit(solution)/shard_map/ppermute | solution.py:196
  63.5 5.1 %collective-permute-start.10 = (bf16[8,192,128]{2,1,0:T(8,128)(2,1)}, bf16[8,192,128]{2,1,0:T(8,128)(2,1)S(1)}, u32[]{:S(2)}, u32[]{:S(2)}) collective-permute-start(bf16[8,192,128]{2,1,0:T(8,128)(2,1)} %collective-permute-done.9.refs_4_), channel_id=1, source_target_pairs={{0,56},{8,0},{16,8},{24,16},{32,24},{40,32},{48,40},{56,48},{1,57}... | collective-permute-start | bytes 1179656 | tf_op jit(solution)/shard_map/ppermute | solution.py:196
  68.7 3.8 %collective-permute-start.7 = (bf16[8,192,128]{2,1,0:T(8,128)(2,1)S(1)}, bf16[8,192,128]{2,1,0:T(8,128)(2,1)S(1)}, u32[]{:S(2)}, u32[]{:S(2)}) collective-permute-start(bf16[8,192,128]{2,1,0:T(8,128)(2,1)S(1)} %collective-permute-done.6.refs_13_.refs_14_), channel_id=1, source_target_pairs={{0,56},{8,0},{16,8},{24,16},{32,24},{40,32},{48,40},{56,48},{1,57}... | collective-permute-start | bytes 1179656 | tf_op jit(solution)/shard_map/ppermute | solution.py:196
  72.5 2.1 %collective-permute-start.3 = (bf16[8,192,128]{2,1,0:T(8,128)(2,1)S(1)}, bf16[8,192,128]{2,1,0:T(8,128)(2,1)S(1)}, u32[]{:S(2)}, u32[]{:S(2)}) collective-permute-start(bf16[8,192,128]{2,1,0:T(8,128)(2,1)S(1)} %collective-permute-done.2.refs_5_), channel_id=1, source_target_pairs={{0,8},{8,16},{16,24},{24,32},{32,40},{40,48},{48,56},{56,0},{1,9},... | collective-permute-start | bytes 1179656 | tf_op jit(solution)/shard_map/ppermute | solution.py:196
  74.8 5.9 %early.1 = (f32[192,512]{1,0:T(8,128)S(1)}, f32[192,512]{1,0:T(8,128)S(1)}, bf16[4,16,128,128]{3,2,1,0:T(8,128)(2,1)S(1)}, bf16[9,128,512]{2,1,0:T(8,128)(2,1)S(1)}, bf16[9,128,512]{2,1,0:T(8,128)(2,1)S(1)}) custom-call(s32[5,64]{1,0:T(8,128)S(1)} %pad_add_fusion.where, bf16[8,192,128]{2,1,0:T(8,128)(2,1)} %copy-done.10, bf16[8,192,128]{2,1,0:T(8,128)(2,1)} %copy-done.13, ...), custom_call_target="tpu_custom_call" | custom-call | tf_op jit(solution)/shard_map/early/pallas_call | solution.py:233
  80.8 2.6 %collective-permute-done.3.x_last.refs_7_ = bf16[8,192,128]{2,1,0:T(8,128)(2,1)S(1)} collective-permute-done((bf16[8,192,128]{2,1,0:T(8,128)(2,1)S(1)}, bf16[8,192,128]{2,1,0:T(8,128)(2,1)S(1)}, u32[]{:S(2)}, u32[]{:S(2)}) %collective-permute-start.3) | collective-permute-done | bytes 393248 | tf_op jit(solution)/shard_map/ppermute | solution.py:196
  83.4 4.5 %back.1 = (bf16[8,8,192,128]{3,2,1,0:T(8,128)(2,1)}, bf16[4,192,128]{2,1,0:T(8,128)(2,1)}, bf16[4,192,128]{2,1,0:T(8,128)(2,1)}) custom-call(s32[5,64]{1,0:T(8,128)S(1)} %pad_add_fusion.where, bf16[8,192,128]{2,1,0:T(8,128)(2,1)S(1)} %collective-permute-done.3.x_last.refs_7_, bf16[8,192,128]{2,1,0:T(8,128)(2,1)S(1)} %collective-permute-done.7.y_last.refs_15_, ...), custom_call_target="tpu_custom_call" | custom-call | tf_op jit(solution)/shard_map/back/pallas_call | solution.py:249
  87.9 4.2 %all-to-all-start.1 = ((bf16[8,8,192,128]{3,2,1,0:T(8,128)(2,1)}), bf16[8,8,192,128]{3,2,1,0:T(8,128)(2,1)S(1)}, u32[]{:S(2)}, u32[]{:S(2)}) async-start(bf16[8,8,192,128]{3,2,1,0:T(8,128)(2,1)} %get-tuple-element.18), calls=%async_computation.1 | async-start | bytes 6291456 | tf_op jit(solution)/shard_map/all_to_all | solution.py:190
  92.1 6.5 %weights.1 = (bf16[4,2,4,2,128,128]{5,4,3,2,1,0:T(8,128)(2,1)S(1)}, bf16[4,2,4,2,128,128]{5,4,3,2,1,0:T(8,128)(2,1)S(1)}) custom-call(s32[5,64]{1,0:T(8,128)S(1)} %pad_add_fusion.where, bf16[8,192,128]{2,1,0:T(8,128)(2,1)} %copy-done.10, bf16[8,192,128]{2,1,0:T(8,128)(2,1)} %copy-done.13, bf16[8,192,128]{2,1,0:T(8,128)(2,1)} %copy-done.15, ...), custom_call_target="tpu_custom_call" | custom-call | tf_op jit(solution)/shard_map/weights/pallas_call | solution.py:268
  100.6 4.1 %collective-permute-done.14 = bf16[4,2,4,2,128,128]{5,4,3,2,1,0:T(8,128)(2,1)S(1)} collective-permute-done((bf16[4,2,4,2,128,128]{5,4,3,2,1,0:T(8,128)(2,1)S(1)}, bf16[4,2,4,2,128,128]{5,4,3,2,1,0:T(8,128)(2,1)S(1)}, u32[]{:S(2)}, u32[]{:S(2)}) %collective-permute-start.14) | collective-permute-done | bytes 2097184 | tf_op jit(solution)/shard_map/ppermute | solution.py:285
  106.6 2.4 %collective-permute-start.15 = (bf16[2,4,2,128,128]{4,3,2,1,0:T(8,128)(2,1)}, bf16[2,4,2,128,128]{4,3,2,1,0:T(8,128)(2,1)}, u32[]{:S(2)}, u32[]{:S(2)}) collective-permute-start(bf16[2,4,2,128,128]{4,3,2,1,0:T(8,128)(2,1)} %get-tuple-element.25), channel_id=1, source_target_pairs={{0,128},{128,256},{256,384},{384,0},{1,129},{129,257},{257,385},{3... | collective-permute-start | bytes 1572872 | tf_op jit(solution)/shard_map/ppermute | solution.py:288
  108.9 3.5 %collective-permute-start.17 = (bf16[2,4,2,128,128]{4,3,2,1,0:T(8,128)(2,1)}, bf16[2,4,2,128,128]{4,3,2,1,0:T(8,128)(2,1)}, u32[]{:S(2)}, u32[]{:S(2)}) collective-permute-start(bf16[2,4,2,128,128]{4,3,2,1,0:T(8,128)(2,1)} %get-tuple-element.26), channel_id=1, source_target_pairs={{0,384},{128,0},{256,128},{384,256},{1,385},{129,1},{257,129},{385... | collective-permute-start | bytes 1572872 | tf_op jit(solution)/shard_map/ppermute | solution.py:288
  112.4 3.3 %collective-permute-start.16 = (bf16[2,4,2,128,128]{4,3,2,1,0:T(8,128)(2,1)}, bf16[2,4,2,128,128]{4,3,2,1,0:T(8,128)(2,1)}, u32[]{:S(2)}, u32[]{:S(2)}) collective-permute-start(bf16[2,4,2,128,128]{4,3,2,1,0:T(8,128)(2,1)} %get-tuple-element.27), channel_id=1, source_target_pairs={{0,256},{128,384},{256,0},{384,128},{1,257},{129,385},{257,1},{385... | collective-permute-start | bytes 1572872 | tf_op jit(solution)/shard_map/ppermute | solution.py:288
  115.7 17.9 %all-to-all-done.1.parts = bf16[8,8,192,128]{3,2,1,0:T(8,128)(2,1)S(1)} async-done(((bf16[8,8,192,128]{3,2,1,0:T(8,128)(2,1)}), bf16[8,8,192,128]{3,2,1,0:T(8,128)(2,1)S(1)}, u32[]{:S(2)}, u32[]{:S(2)}) %all-to-all-start.1) | async-done | bytes 3145760 | tf_op jit(solution)/shard_map/all_to_all | solution.py:190
  134.7 3.5 %all-to-all-start.2 = ((bf16[8,192,128]{2,1,0:T(8,128)(2,1)}), bf16[8,192,128]{2,1,0:T(8,128)(2,1)S(1)}, u32[]{:S(2)}, u32[]{:S(2)}) async-start(bf16[8,192,128]{2,1,0:T(8,128)(2,1)} %sums.1), calls=%async_computation.2 | async-start | bytes 786432 | tf_op jit(solution)/shard_map/all_to_all | solution.py:190
  138.2 2.1 %fusion.2 = bf16[2,4,2,128,128]{4,3,2,1,0:T(8,128)(2,1)S(1)} fusion(bf16[2,4,2,128,128]{4,3,2,1,0:T(8,128)(2,1)} %collective-permute-done.17, bf16[2,4,2,128,128]{4,3,2,1,0:T(8,128)(2,1)} %collective-permute-done.16, bf16[2,4,2,128,128]{4,3,2,1,0:T(8,128)(2,1)} %collective-permute-done.15, bf16[4,2,4,2,128,128]{5,4,3,2,1,0:T(8,128)(2,1)} %copy-done.11, ...), kind=kLoop, calls=%fused_computation.3 | loop fusion | flops 3145728 | bytes 3145728 | tf_op jit(solution)/shard_map/convert_element_type | solution.py:290
  141.2 8.8 %all-to-all-done.2 = bf16[8,192,128]{2,1,0:T(8,128)(2,1)S(1)} async-done(((bf16[8,192,128]{2,1,0:T(8,128)(2,1)}), bf16[8,192,128]{2,1,0:T(8,128)(2,1)S(1)}, u32[]{:S(2)}, u32[]{:S(2)}) %all-to-all-start.2) | async-done | bytes 393248 | tf_op jit(solution)/shard_map/all_to_all | solution.py:190
  (72 shorter events, 15.7 us)
Async XLA Ops:
  0.6 60.8 %copy-start.17 = (s32[4,16]{1,0:T(4,128)S(1)}, s32[4,16]{1,0:T(4,128)}, u32[]{:S(2)}) copy-start(s32[4,16]{1,0:T(4,128)} %param.9) | copy-start | bytes 772
  0.6 60.9 %copy-start.18 = (s32[4,16]{1,0:T(4,128)S(1)}, s32[4,16]{1,0:T(4,128)}, u32[]{:S(2)}) copy-start(s32[4,16]{1,0:T(4,128)} %param.11) | copy-start | bytes 772
  27.9 46.8 %copy-start.9 = (bf16[8,192,128]{2,1,0:T(8,128)(2,1)}, bf16[8,192,128]{2,1,0:T(8,128)(2,1)S(1)}, u32[]{:S(2)}) copy-start(bf16[8,192,128]{2,1,0:T(8,128)(2,1)S(1)} %get-tuple-element.28.refs_7_.refs_8_) | copy-start | bytes 1179652
  27.9 46.8 %copy-start.10 = (bf16[8,192,128]{2,1,0:T(8,128)(2,1)}, bf16[8,192,128]{2,1,0:T(8,128)(2,1)S(1)}, u32[]{:S(2)}) copy-start(bf16[8,192,128]{2,1,0:T(8,128)(2,1)S(1)} %get-tuple-element.29.refs_0_) | copy-start | bytes 1179652
  27.9 14.4 %collective-permute-start.4 = (bf16[8,192,128]{2,1,0:T(8,128)(2,1)S(1)}, bf16[8,192,128]{2,1,0:T(8,128)(2,1)S(1)}, u32[]{:S(2)}, u32[]{:S(2)}) collective-permute-start(bf16[8,192,128]{2,1,0:T(8,128)(2,1)S(1)} %get-tuple-element.28.refs_7_.refs_8_), channel_id=1, source_target_pairs={{0,56},{8,0},{16,8},{24,16},{32,24},{40,32},{48,40},{56,48},{1,57}... | collective-permute-start | bytes 1179656 | tf_op jit(solution)/shard_map/ppermute | solution.py:196
  33.3 13.0 %collective-permute-start = (bf16[8,192,128]{2,1,0:T(8,128)(2,1)S(1)}, bf16[8,192,128]{2,1,0:T(8,128)(2,1)S(1)}, u32[]{:S(2)}, u32[]{:S(2)}) collective-permute-start(bf16[8,192,128]{2,1,0:T(8,128)(2,1)S(1)} %get-tuple-element.29.refs_0_), channel_id=1, source_target_pairs={{0,8},{8,16},{16,24},{24,32},{32,40},{40,48},{48,56},{56,0},{1,9},... | collective-permute-start | bytes 1179656 | tf_op jit(solution)/shard_map/ppermute | solution.py:196
  35.3 13.2 %collective-permute-start.11 = (bf16[8,192,128]{2,1,0:T(8,128)(2,1)S(1)}, bf16[8,192,128]{2,1,0:T(8,128)(2,1)S(1)}, u32[]{:S(2)}, u32[]{:S(2)}) collective-permute-start(bf16[8,192,128]{2,1,0:T(8,128)(2,1)S(1)} %get-tuple-element.28.refs_7_.refs_8_), channel_id=1, source_target_pairs={{0,8},{8,16},{16,24},{24,32},{32,40},{40,48},{48,56},{56,0},{1,9},... | collective-permute-start | bytes 1179656 | tf_op jit(solution)/shard_map/ppermute | solution.py:196
  37.3 13.1 %collective-permute-start.8 = (bf16[8,192,128]{2,1,0:T(8,128)(2,1)S(1)}, bf16[8,192,128]{2,1,0:T(8,128)(2,1)S(1)}, u32[]{:S(2)}, u32[]{:S(2)}) collective-permute-start(bf16[8,192,128]{2,1,0:T(8,128)(2,1)S(1)} %get-tuple-element.29.refs_0_), channel_id=1, source_target_pairs={{0,56},{8,0},{16,8},{24,16},{32,24},{40,32},{48,40},{56,48},{1,57}... | collective-permute-start | bytes 1179656 | tf_op jit(solution)/shard_map/ppermute | solution.py:196
  42.3 13.2 %collective-permute-start.5 = (bf16[8,192,128]{2,1,0:T(8,128)(2,1)S(1)}, bf16[8,192,128]{2,1,0:T(8,128)(2,1)S(1)}, u32[]{:S(2)}, u32[]{:S(2)}) collective-permute-start(bf16[8,192,128]{2,1,0:T(8,128)(2,1)S(1)} %collective-permute-done.4.refs_9_.refs_10_), channel_id=1, source_target_pairs={{0,56},{8,0},{16,8},{24,16},{32,24},{40,32},{48,40},{56,48},{1,57}... | collective-permute-start | bytes 1179656 | tf_op jit(solution)/shard_map/ppermute | solution.py:196
  46.3 13.0 %collective-permute-start.1 = (bf16[8,192,128]{2,1,0:T(8,128)(2,1)S(1)}, bf16[8,192,128]{2,1,0:T(8,128)(2,1)}, u32[]{:S(2)}, u32[]{:S(2)}) collective-permute-start(bf16[8,192,128]{2,1,0:T(8,128)(2,1)S(1)} %collective-permute-done.refs_1_), channel_id=1, source_target_pairs={{0,8},{8,16},{16,24},{24,32},{32,40},{40,48},{48,56},{56,0},{1,9},... | collective-permute-start | bytes 1179656 | tf_op jit(solution)/shard_map/ppermute | solution.py:196
  48.4 13.2 %collective-permute-start.12 = (bf16[8,192,128]{2,1,0:T(8,128)(2,1)S(1)}, bf16[8,192,128]{2,1,0:T(8,128)(2,1)}, u32[]{:S(2)}, u32[]{:S(2)}) collective-permute-start(bf16[8,192,128]{2,1,0:T(8,128)(2,1)S(1)} %collective-permute-done.11.refs_8_.refs_9_), channel_id=1, source_target_pairs={{0,8},{8,16},{16,24},{24,32},{32,40},{40,48},{48,56},{56,0},{1,9},... | collective-permute-start | bytes 1179656 | tf_op jit(solution)/shard_map/ppermute | solution.py:196
  50.4 13.2 %collective-permute-start.9 = (bf16[8,192,128]{2,1,0:T(8,128)(2,1)S(1)}, bf16[8,192,128]{2,1,0:T(8,128)(2,1)}, u32[]{:S(2)}, u32[]{:S(2)}) collective-permute-start(bf16[8,192,128]{2,1,0:T(8,128)(2,1)S(1)} %collective-permute-done.8.refs_2_), channel_id=1, source_target_pairs={{0,56},{8,0},{16,8},{24,16},{32,24},{40,32},{48,40},{56,48},{1,57}... | collective-permute-start | bytes 1179656 | tf_op jit(solution)/shard_map/ppermute | solution.py:196
  55.5 13.2 %collective-permute-start.6 = (bf16[8,192,128]{2,1,0:T(8,128)(2,1)S(1)}, bf16[8,192,128]{2,1,0:T(8,128)(2,1)S(1)}, u32[]{:S(2)}, u32[]{:S(2)}) collective-permute-start(bf16[8,192,128]{2,1,0:T(8,128)(2,1)S(1)} %collective-permute-done.5.refs_11_.refs_12_), channel_id=1, source_target_pairs={{0,56},{8,0},{16,8},{24,16},{32,24},{40,32},{48,40},{56,48},{1,57}... | collective-permute-start | bytes 1179656 | tf_op jit(solution)/shard_map/ppermute | solution.py:196
  59.3 13.2 %collective-permute-start.2 = (bf16[8,192,128]{2,1,0:T(8,128)(2,1)}, bf16[8,192,128]{2,1,0:T(8,128)(2,1)S(1)}, u32[]{:S(2)}, u32[]{:S(2)}) collective-permute-start(bf16[8,192,128]{2,1,0:T(8,128)(2,1)} %collective-permute-done.1.refs_3_), channel_id=1, source_target_pairs={{0,8},{8,16},{16,24},{24,32},{32,40},{40,48},{48,56},{56,0},{1,9},... | collective-permute-start | bytes 1179656 | tf_op jit(solution)/shard_map/ppermute | solution.py:196
  61.6 13.1 %collective-permute-start.13 = (bf16[8,192,128]{2,1,0:T(8,128)(2,1)}, bf16[8,192,128]{2,1,0:T(8,128)(2,1)S(1)}, u32[]{:S(2)}, u32[]{:S(2)}) collective-permute-start(bf16[8,192,128]{2,1,0:T(8,128)(2,1)} %collective-permute-done.12.refs_10_.refs_11_), channel_id=1, source_target_pairs={{0,8},{8,16},{16,24},{24,32},{32,40},{40,48},{48,56},{56,0},{1,9},... | collective-permute-start | bytes 1179656 | tf_op jit(solution)/shard_map/ppermute | solution.py:196
  63.5 11.2 %collective-permute-start.10 = (bf16[8,192,128]{2,1,0:T(8,128)(2,1)}, bf16[8,192,128]{2,1,0:T(8,128)(2,1)S(1)}, u32[]{:S(2)}, u32[]{:S(2)}) collective-permute-start(bf16[8,192,128]{2,1,0:T(8,128)(2,1)} %collective-permute-done.9.refs_4_), channel_id=1, source_target_pairs={{0,56},{8,0},{16,8},{24,16},{32,24},{40,32},{48,40},{56,48},{1,57}... | collective-permute-start | bytes 1179656 | tf_op jit(solution)/shard_map/ppermute | solution.py:196
  68.7 12.0 %collective-permute-start.7 = (bf16[8,192,128]{2,1,0:T(8,128)(2,1)S(1)}, bf16[8,192,128]{2,1,0:T(8,128)(2,1)S(1)}, u32[]{:S(2)}, u32[]{:S(2)}) collective-permute-start(bf16[8,192,128]{2,1,0:T(8,128)(2,1)S(1)} %collective-permute-done.6.refs_13_.refs_14_), channel_id=1, source_target_pairs={{0,56},{8,0},{16,8},{24,16},{32,24},{40,32},{48,40},{56,48},{1,57}... | collective-permute-start | bytes 1179656 | tf_op jit(solution)/shard_map/ppermute | solution.py:196
  72.5 10.9 %collective-permute-start.3 = (bf16[8,192,128]{2,1,0:T(8,128)(2,1)S(1)}, bf16[8,192,128]{2,1,0:T(8,128)(2,1)S(1)}, u32[]{:S(2)}, u32[]{:S(2)}) collective-permute-start(bf16[8,192,128]{2,1,0:T(8,128)(2,1)S(1)} %collective-permute-done.2.refs_5_), channel_id=1, source_target_pairs={{0,8},{8,16},{16,24},{24,32},{32,40},{40,48},{48,56},{56,0},{1,9},... | collective-permute-start | bytes 1179656 | tf_op jit(solution)/shard_map/ppermute | solution.py:196
  87.9 45.7 %all-to-all-start.1 = ((bf16[8,8,192,128]{3,2,1,0:T(8,128)(2,1)}), bf16[8,8,192,128]{3,2,1,0:T(8,128)(2,1)S(1)}, u32[]{:S(2)}, u32[]{:S(2)}) async-start(bf16[8,8,192,128]{3,2,1,0:T(8,128)(2,1)} %get-tuple-element.18), calls=%async_computation.1 | async-start | bytes 6291456 | tf_op jit(solution)/shard_map/all_to_all | solution.py:190
  98.6 6.1 %collective-permute-start.14 = (bf16[4,2,4,2,128,128]{5,4,3,2,1,0:T(8,128)(2,1)S(1)}, bf16[4,2,4,2,128,128]{5,4,3,2,1,0:T(8,128)(2,1)S(1)}, u32[]{:S(2)}, u32[]{:S(2)}) collective-permute-start(bf16[4,2,4,2,128,128]{5,4,3,2,1,0:T(8,128)(2,1)S(1)} %get-tuple-element.22), channel_id=1, source_target_pairs={{0,64},{64,0},{1,65},{65,1},{2,66},{66,2},{3,67},{67,3},{4,68},{68... | collective-permute-start | bytes 6291464 | tf_op jit(solution)/shard_map/ppermute | solution.py:285
  106.6 31.7 %collective-permute-start.15 = (bf16[2,4,2,128,128]{4,3,2,1,0:T(8,128)(2,1)}, bf16[2,4,2,128,128]{4,3,2,1,0:T(8,128)(2,1)}, u32[]{:S(2)}, u32[]{:S(2)}) collective-permute-start(bf16[2,4,2,128,128]{4,3,2,1,0:T(8,128)(2,1)} %get-tuple-element.25), channel_id=1, source_target_pairs={{0,128},{128,256},{256,384},{384,0},{1,129},{129,257},{257,385},{3... | collective-permute-start | bytes 1572872 | tf_op jit(solution)/shard_map/ppermute | solution.py:288
  108.9 29.3 %collective-permute-start.17 = (bf16[2,4,2,128,128]{4,3,2,1,0:T(8,128)(2,1)}, bf16[2,4,2,128,128]{4,3,2,1,0:T(8,128)(2,1)}, u32[]{:S(2)}, u32[]{:S(2)}) collective-permute-start(bf16[2,4,2,128,128]{4,3,2,1,0:T(8,128)(2,1)} %get-tuple-element.26), channel_id=1, source_target_pairs={{0,384},{128,0},{256,128},{384,256},{1,385},{129,1},{257,129},{385... | collective-permute-start | bytes 1572872 | tf_op jit(solution)/shard_map/ppermute | solution.py:288
  112.4 25.8 %collective-permute-start.16 = (bf16[2,4,2,128,128]{4,3,2,1,0:T(8,128)(2,1)}, bf16[2,4,2,128,128]{4,3,2,1,0:T(8,128)(2,1)}, u32[]{:S(2)}, u32[]{:S(2)}) collective-permute-start(bf16[2,4,2,128,128]{4,3,2,1,0:T(8,128)(2,1)} %get-tuple-element.27), channel_id=1, source_target_pairs={{0,256},{128,384},{256,0},{384,128},{1,257},{129,385},{257,1},{385... | collective-permute-start | bytes 1572872 | tf_op jit(solution)/shard_map/ppermute | solution.py:288
  134.7 15.3 %all-to-all-start.2 = ((bf16[8,192,128]{2,1,0:T(8,128)(2,1)}), bf16[8,192,128]{2,1,0:T(8,128)(2,1)S(1)}, u32[]{:S(2)}, u32[]{:S(2)}) async-start(bf16[8,192,128]{2,1,0:T(8,128)(2,1)} %sums.1), calls=%async_computation.2 | async-start | bytes 786432 | tf_op jit(solution)/shard_map/all_to_all | solution.py:190
  (15 other events, 192.8 us)

commit v11 on v10

--- a/solution.py
+++ b/solution.py
@@ -48,7 +48,7 @@
     x_units = list(zip(refs[:n_x], x_steps))
     y_units = list(zip(refs[n_x : n_x + n_y], y_steps))
     w_in, w_out = refs[n_x + n_y : n_x + n_y + 2]
-    hidden, grad_act, wi, in_last, out_last, wo, x, y, x_sem, y_sem, w_sem = refs[n_x + n_y + 2 :]
+    hidden, grad_act, wi, in_last, out_last, total, wo, x, y, x_sem, y_sem, w_sem = refs[n_x + n_y + 2 :]
     rows, per_row, width, _ = w_in.shape
     load_in = pltpu.make_async_copy(w_in, wi, w_sem.at[0])
     load_out = pltpu.make_async_copy(w_out, wo, w_sem.at[1])
@@ -56,6 +56,7 @@
     load_out.start()
     x_loads = start_loads(where, x_units, x, x_sem, side)
     y_loads = start_loads(where, y_units, y, y_sem, side)
+    total[...] = jnp.zeros_like(total)
     in_last[...] = jnp.zeros_like(in_last)
     out_last[...] = jnp.zeros_like(out_last)
     places = x.shape[0] // side
@@ -83,11 +84,10 @@
         grad_act[:, at] = dot_nt(row_of(y, where, 1, r, per_row), w_row)
 
 
-def back_kernel(where, x_last, y_last, hidden_most, grad_most, wi, li, lo, *refs):
+def back_kernel(where, x_last, y_last, hidden_most, grad_most, wi, li, lo, zeros, *refs):
     placed, act_out, grad_out, total, rounded, act, grad, out_sem = refs
     rows, per_row, width, _ = wi.shape
     blocks, side = total.shape[0], x_last.shape[0]
-    total[...] = jnp.zeros_like(total)
     x_unit = jnp.concatenate([x_last[n] for n in range(side)], axis=1)
     y_unit = jnp.concatenate([y_last[n] for n in range(side)], axis=1)
     hidden = hidden_most[...] + dot_nn(x_unit, li[:side].reshape(side * width, rows * width))
@@ -230,10 +230,11 @@
     values = pltpu.HBM((rows, tok, width), BF16)
     kept = pltpu.VMEM((tok, rows * width), F32)
     last = pltpu.VMEM((side + 1, width, rows * width), BF16)
-    hidden_most, grad_most, wi, li, lo = pl.pallas_call(
+    sums = pltpu.VMEM((blocks, tok, width), F32)
+    hidden_most, grad_most, wi, li, lo, zeros = pl.pallas_call(
         functools.partial(early_kernel, ((side, x_plan[1][:-1]), (side, y_plan[1][:-1]))),
-        out_shape=(kept, kept, pltpu.VMEM(w_in.shape, BF16), last, last),
-        out_specs=(vmem,) * 5,
+        out_shape=(kept, kept, pltpu.VMEM(w_in.shape, BF16), last, last, sums),
+        out_specs=(vmem,) * 6,
         in_specs=[smem] + [anywhere] * (len(x_units) + len(y_units)),
         scratch_shapes=[
             pltpu.VMEM(w_out.shape, BF16),
@@ -246,13 +247,13 @@
         compiler_params=params,
         name="early",
     )(where, *x_units[:-1], *y_units[:-1], in_hbm(w_in), in_hbm(w_out))
-    placed, act, grad = pl.pallas_call(
+    placed, act, grad, _ = pl.pallas_call(
         back_kernel,
-        out_shape=(pltpu.HBM((side, blocks // side, tok, width), BF16), values, values),
-        in_specs=[smem] + [vmem] * 7,
-        out_specs=(anywhere, anywhere, anywhere),
+        out_shape=(pltpu.HBM((side, blocks // side, tok, width), BF16), values, values, sums),
+        in_specs=[smem] + [vmem] * 8,
+        out_specs=(anywhere, anywhere, anywhere, vmem),
+        input_output_aliases={8: 3},
         scratch_shapes=[
-            pltpu.VMEM((blocks, tok, width), F32),
             pltpu.VMEM((blocks, tok, width), BF16),
             pltpu.VMEM((rows, tok, width), BF16),
             pltpu.VMEM((rows, tok, width), BF16),
@@ -260,7 +261,7 @@
         ],
         compiler_params=params,
         name="back",
-    )(where, x_units[-1], y_units[-1], hidden_most, grad_most, wi, li, lo)
+    )(where, x_units[-1], y_units[-1], hidden_most, grad_most, wi, li, lo, zeros)
 
     on_ring = swap(placed, rings)
 

time: 152 us -> 151 us (level)
  no operation moved by 1% of the time
where the time goes in v11:
time: 151 us; the launch traced here: 150 us
  starting transfers between devices  64.7 us (43%)
  waiting for transfers between devices  33.7 us (22%)
  blocking collectives  26.2 us (17%)
  Pallas kernels  17.5 us (12%)
  other arithmetic  5.61 us (4%)
    ppermute x14, starting transfers between devices, turn(): return lax.ppermute(values, CYZ, pairs)  46 us
    all_to_all x2, waiting for transfers between devices, swap(): lax.all_to_all(values, CYZ, split_axis=0, concat_axis=0, tiled=True, axis...  26.7 us
    all_to_all x1, blocking collectives, swap(): lax.all_to_all(values, CYZ, split_axis=0, concat_axis=0, tiled=True, axis...  26.2 us
    ppermute x3, starting transfers between devices, per_device(): lax.ppermute(paired[d], 'x', [(i, (i + d) % nx) for i in range(nx)])  9.16 us
    all_to_all x2, starting transfers between devices, swap(): lax.all_to_all(values, CYZ, split_axis=0, concat_axis=0, tiled=True, axis...  7.68 us
    pallas_call x1, Pallas kernels, per_device(): pl.pallas_call(functools.partial(weight_kernel, (x_plan, y_plan)), out_sh...  6.46 us
    pallas_call x1, Pallas kernels, per_device(): pl.pallas_call(functools.partial(early_kernel, ((side, x_plan[1][:-1]), (...  5.88 us
    ppermute x1, waiting for transfers between devices, per_device(): swapped = lax.ppermute(other, 'c', [(0, 1), (1, 0)])  4.13 us
  transfers between devices with their start and end apart: 20, of which 5 were waited for; matrix products, arithmetic and copies ran while one was open for 3% of the time, Pallas kernels for 9%

profile of v11, /device:TPU:6, one launch (start us, length us, event | category | flops | bytes accessed | tf_op | source)
XLA Modules:
  0.0 150.3 jit_solution(1110125448681642685)
XLA Ops:
  1.7 26.2 %all_to_all.15 = bf16[8,2,192,128]{3,2,1,0:T(8,128)(2,1)S(1)} all-to-all(bf16[8,2,192,128]{3,2,1,0:T(8,128)(2,1)S(1)} %broadcast_in_dim.5), channel_id=1, replica_groups={{0,1,2,3,4,5,6,7},{8,9,10,11,12,13,14,15},{16,17,18,19,20,21,22,23},{24..., dimensions={0} | all-to-all | bytes 1572864 | tf_op jit(solution)/shard_map/all_to_all | solution.py:190
  27.9 5.4 %collective-permute-start.4 = (bf16[8,192,128]{2,1,0:T(8,128)(2,1)S(1)}, bf16[8,192,128]{2,1,0:T(8,128)(2,1)S(1)}, u32[]{:S(2)}, u32[]{:S(2)}) collective-permute-start(bf16[8,192,128]{2,1,0:T(8,128)(2,1)S(1)} %get-tuple-element.30.refs_7_.refs_8_), channel_id=1, source_target_pairs={{0,56},{8,0},{16,8},{24,16},{32,24},{40,32},{48,40},{56,48},{1,57}... | collective-permute-start | bytes 1179656 | tf_op jit(solution)/shard_map/ppermute | solution.py:196
  35.3 2.0 %collective-permute-start.11 = (bf16[8,192,128]{2,1,0:T(8,128)(2,1)S(1)}, bf16[8,192,128]{2,1,0:T(8,128)(2,1)S(1)}, u32[]{:S(2)}, u32[]{:S(2)}) collective-permute-start(bf16[8,192,128]{2,1,0:T(8,128)(2,1)S(1)} %get-tuple-element.30.refs_7_.refs_8_), channel_id=1, source_target_pairs={{0,8},{8,16},{16,24},{24,32},{32,40},{40,48},{48,56},{56,0},{1,9},... | collective-permute-start | bytes 1179656 | tf_op jit(solution)/shard_map/ppermute | solution.py:196
  37.3 5.0 %collective-permute-start.8 = (bf16[8,192,128]{2,1,0:T(8,128)(2,1)S(1)}, bf16[8,192,128]{2,1,0:T(8,128)(2,1)S(1)}, u32[]{:S(2)}, u32[]{:S(2)}) collective-permute-start(bf16[8,192,128]{2,1,0:T(8,128)(2,1)S(1)} %get-tuple-element.31.refs_0_), channel_id=1, source_target_pairs={{0,56},{8,0},{16,8},{24,16},{32,24},{40,32},{48,40},{56,48},{1,57}... | collective-permute-start | bytes 1179656 | tf_op jit(solution)/shard_map/ppermute | solution.py:196
  42.3 3.9 %collective-permute-start.5 = (bf16[8,192,128]{2,1,0:T(8,128)(2,1)S(1)}, bf16[8,192,128]{2,1,0:T(8,128)(2,1)S(1)}, u32[]{:S(2)}, u32[]{:S(2)}) collective-permute-start(bf16[8,192,128]{2,1,0:T(8,128)(2,1)S(1)} %collective-permute-done.4.refs_9_.refs_10_), channel_id=1, source_target_pairs={{0,56},{8,0},{16,8},{24,16},{32,24},{40,32},{48,40},{56,48},{1,57}... | collective-permute-start | bytes 1179656 | tf_op jit(solution)/shard_map/ppermute | solution.py:196
  50.4 5.1 %collective-permute-start.9 = (bf16[8,192,128]{2,1,0:T(8,128)(2,1)S(1)}, bf16[8,192,128]{2,1,0:T(8,128)(2,1)}, u32[]{:S(2)}, u32[]{:S(2)}) collective-permute-start(bf16[8,192,128]{2,1,0:T(8,128)(2,1)S(1)} %collective-permute-done.8.refs_2_), channel_id=1, source_target_pairs={{0,56},{8,0},{16,8},{24,16},{32,24},{40,32},{48,40},{56,48},{1,57}... | collective-permute-start | bytes 1179656 | tf_op jit(solution)/shard_map/ppermute | solution.py:196
  55.5 3.8 %collective-permute-start.6 = (bf16[8,192,128]{2,1,0:T(8,128)(2,1)S(1)}, bf16[8,192,128]{2,1,0:T(8,128)(2,1)S(1)}, u32[]{:S(2)}, u32[]{:S(2)}) collective-permute-start(bf16[8,192,128]{2,1,0:T(8,128)(2,1)S(1)} %collective-permute-done.5.refs_11_.refs_12_), channel_id=1, source_target_pairs={{0,56},{8,0},{16,8},{24,16},{32,24},{40,32},{48,40},{56,48},{1,57}... | collective-permute-start | bytes 1179656 | tf_op jit(solution)/shard_map/ppermute | solution.py:196
  59.3 2.1 %collective-permute-start.2 = (bf16[8,192,128]{2,1,0:T(8,128)(2,1)}, bf16[8,192,128]{2,1,0:T(8,128)(2,1)S(1)}, u32[]{:S(2)}, u32[]{:S(2)}) collective-permute-start(bf16[8,192,128]{2,1,0:T(8,128)(2,1)} %collective-permute-done.1.refs_3_), channel_id=1, source_target_pairs={{0,8},{8,16},{16,24},{24,32},{32,40},{40,48},{48,56},{56,0},{1,9},... | collective-permute-start | bytes 1179656 | tf_op jit(solution)/shard_map/ppermute | solution.py:196
  63.5 5.1 %collective-permute-start.10 = (bf16[8,192,128]{2,1,0:T(8,128)(2,1)}, bf16[8,192,128]{2,1,0:T(8,128)(2,1)S(1)}, u32[]{:S(2)}, u32[]{:S(2)}) collective-permute-start(bf16[8,192,128]{2,1,0:T(8,128)(2,1)} %collective-permute-done.9.refs_4_), channel_id=1, source_target_pairs={{0,56},{8,0},{16,8},{24,16},{32,24},{40,32},{48,40},{56,48},{1,57}... | collective-permute-start | bytes 1179656 | tf_op jit(solution)/shard_map/ppermute | solution.py:196
  68.7 3.8 %collective-permute-start.7 = (bf16[8,192,128]{2,1,0:T(8,128)(2,1)S(1)}, bf16[8,192,128]{2,1,0:T(8,128)(2,1)S(1)}, u32[]{:S(2)}, u32[]{:S(2)}) collective-permute-start(bf16[8,192,128]{2,1,0:T(8,128)(2,1)S(1)} %collective-permute-done.6.refs_13_.refs_14_), channel_id=1, source_target_pairs={{0,56},{8,0},{16,8},{24,16},{32,24},{40,32},{48,40},{56,48},{1,57}... | collective-permute-start | bytes 1179656 | tf_op jit(solution)/shard_map/ppermute | solution.py:196
  72.5 2.1 %collective-permute-start.3 = (bf16[8,192,128]{2,1,0:T(8,128)(2,1)S(1)}, bf16[8,192,128]{2,1,0:T(8,128)(2,1)S(1)}, u32[]{:S(2)}, u32[]{:S(2)}) collective-permute-start(bf16[8,192,128]{2,1,0:T(8,128)(2,1)S(1)} %collective-permute-done.2.refs_5_), channel_id=1, source_target_pairs={{0,8},{8,16},{16,24},{24,32},{32,40},{40,48},{48,56},{56,0},{1,9},... | collective-permute-start | bytes 1179656 | tf_op jit(solution)/shard_map/ppermute | solution.py:196
  74.8 5.9 %early.1 = (f32[192,512]{1,0:T(8,128)S(1)}, f32[192,512]{1,0:T(8,128)S(1)}, bf16[4,16,128,128]{3,2,1,0:T(8,128)(2,1)S(1)}, bf16[9,128,512]{2,1,0:T(8,128)(2,1)S(...) custom-call(s32[5,64]{1,0:T(8,128)S(1)} %pad_add_fusion.where, bf16[8,192,128]{2,1,0:T(8,128)(2,1)} %copy-done.10, ...), custom_call_target="tpu_custom_call" | custom-call | tf_op jit(solution)/shard_map/early/pallas_call | solution.py:234
  80.8 2.6 %collective-permute-done.3.x_last.refs_7_ = bf16[8,192,128]{2,1,0:T(8,128)(2,1)S(1)} collective-permute-done((bf16[8,192,128]{2,1,0:T(8,128)(2,1)S(1)}, bf16[8,192,128]{2,1,0:T(8,128)(2,1)S(1)}, u32[]{:S(2)}, u32[]{:S(2)}) %collective-permute-start.3) | collective-permute-done | bytes 393248 | tf_op jit(solution)/shard_map/ppermute | solution.py:196
  83.4 4.1 %back.1 = (bf16[8,8,192,128]{3,2,1,0:T(8,128)(2,1)}, bf16[4,192,128]{2,1,0:T(8,128)(2,1)}, bf16[4,192,128]{2,1,0:T(8,128)(2,1)}, f32[64,192,128]{2,1,0:T(8,128)S(1)}) custom-call(s32[5,64]{1,0:T(8,128)S(1)} %pad_add_fusion.where, bf16[8,192,128]{2,1,0:T(8,128)(2,1)S(1)} %collective-permute-done.3.x_last.refs_7_, ...), custom_call_target="tpu_custom_call", output_to_operand_aliasing={{3}: (8, {})} | custom-call | tf_op jit(solution)/shard_map/back/pallas_call | solution.py:250
  87.5 4.2 %all-to-all-start.1 = ((bf16[8,8,192,128]{3,2,1,0:T(8,128)(2,1)}), bf16[8,8,192,128]{3,2,1,0:T(8,128)(2,1)S(1)}, u32[]{:S(2)}, u32[]{:S(2)}) async-start(bf16[8,8,192,128]{3,2,1,0:T(8,128)(2,1)} %get-tuple-element.20), calls=%async_computation.1 | async-start | bytes 6291456 | tf_op jit(solution)/shard_map/all_to_all | solution.py:190
  91.7 6.5 %weights.1 = (bf16[4,2,4,2,128,128]{5,4,3,2,1,0:T(8,128)(2,1)S(1)}, bf16[4,2,4,2,128,128]{5,4,3,2,1,0:T(8,128)(2,1)S(1)}) custom-call(s32[5,64]{1,0:T(8,128)S(1)} %pad_add_fusion.where, bf16[8,192,128]{2,1,0:T(8,128)(2,1)} %copy-done.10, bf16[8,192,128]{2,1,0:T(8,128)(2,1)} %copy-done.13, bf16[8,192,128]{2,1,0:T(8,128)(2,1)} %copy-done.15, ...), custom_call_target="tpu_custom_call" | custom-call | tf_op jit(solution)/shard_map/weights/pallas_call | solution.py:269
  100.1 4.1 %collective-permute-done.14 = bf16[4,2,4,2,128,128]{5,4,3,2,1,0:T(8,128)(2,1)S(1)} collective-permute-done((bf16[4,2,4,2,128,128]{5,4,3,2,1,0:T(8,128)(2,1)S(1)}, bf16[4,2,4,2,128,128]{5,4,3,2,1,0:T(8,128)(2,1)S(1)}, u32[]{:S(2)}, u32[]{:S(2)}) %collective-permute-start.14) | collective-permute-done | bytes 2097184 | tf_op jit(solution)/shard_map/ppermute | solution.py:286
  106.1 2.4 %collective-permute-start.15 = (bf16[2,4,2,128,128]{4,3,2,1,0:T(8,128)(2,1)}, bf16[2,4,2,128,128]{4,3,2,1,0:T(8,128)(2,1)}, u32[]{:S(2)}, u32[]{:S(2)}) collective-permute-start(bf16[2,4,2,128,128]{4,3,2,1,0:T(8,128)(2,1)} %get-tuple-element.27), channel_id=1, source_target_pairs={{0,128},{128,256},{256,384},{384,0},{1,129},{129,257},{257,385},{3... | collective-permute-start | bytes 1572872 | tf_op jit(solution)/shard_map/ppermute | solution.py:289
  108.5 3.5 %collective-permute-start.17 = (bf16[2,4,2,128,128]{4,3,2,1,0:T(8,128)(2,1)}, bf16[2,4,2,128,128]{4,3,2,1,0:T(8,128)(2,1)}, u32[]{:S(2)}, u32[]{:S(2)}) collective-permute-start(bf16[2,4,2,128,128]{4,3,2,1,0:T(8,128)(2,1)} %get-tuple-element.28), channel_id=1, source_target_pairs={{0,384},{128,0},{256,128},{384,256},{1,385},{129,1},{257,129},{385... | collective-permute-start | bytes 1572872 | tf_op jit(solution)/shard_map/ppermute | solution.py:289
  112.0 3.3 %collective-permute-start.16 = (bf16[2,4,2,128,128]{4,3,2,1,0:T(8,128)(2,1)}, bf16[2,4,2,128,128]{4,3,2,1,0:T(8,128)(2,1)}, u32[]{:S(2)}, u32[]{:S(2)}) collective-permute-start(bf16[2,4,2,128,128]{4,3,2,1,0:T(8,128)(2,1)} %get-tuple-element.29), channel_id=1, source_target_pairs={{0,256},{128,384},{256,0},{384,128},{1,257},{129,385},{257,1},{385... | collective-permute-start | bytes 1572872 | tf_op jit(solution)/shard_map/ppermute | solution.py:289
  115.3 17.9 %all-to-all-done.1.parts = bf16[8,8,192,128]{3,2,1,0:T(8,128)(2,1)S(1)} async-done(((bf16[8,8,192,128]{3,2,1,0:T(8,128)(2,1)}), bf16[8,8,192,128]{3,2,1,0:T(8,128)(2,1)S(1)}, u32[]{:S(2)}, u32[]{:S(2)}) %all-to-all-start.1) | async-done | bytes 3145760 | tf_op jit(solution)/shard_map/all_to_all | solution.py:190
  134.3 3.5 %all-to-all-start.2 = ((bf16[8,192,128]{2,1,0:T(8,128)(2,1)}), bf16[8,192,128]{2,1,0:T(8,128)(2,1)S(1)}, u32[]{:S(2)}, u32[]{:S(2)}) async-start(bf16[8,192,128]{2,1,0:T(8,128)(2,1)} %sums.1), calls=%async_computation.2 | async-start | bytes 786432 | tf_op jit(solution)/shard_map/all_to_all | solution.py:190
  137.8 2.1 %fusion.2 = bf16[2,4,2,128,128]{4,3,2,1,0:T(8,128)(2,1)S(1)} fusion(bf16[2,4,2,128,128]{4,3,2,1,0:T(8,128)(2,1)} %collective-permute-done.17, bf16[2,4,2,128,128]{4,3,2,1,0:T(8,128)(2,1)} %collective-permute-done.16, bf16[2,4,2,128,128]{4,3,2,1,0:T(8,128)(2,1)} %collective-permute-done.15, bf16[4,2,4,2,128,128]{5,4,3,2,1,0:T(8,128)(2,1)} %copy-done.11, ...), kind=kLoop, calls=%fused_computation.3 | loop fusion | flops 3145728 | bytes 3145728 | tf_op jit(solution)/shard_map/convert_element_type | solution.py:291
  140.8 8.8 %all-to-all-done.2 = bf16[8,192,128]{2,1,0:T(8,128)(2,1)S(1)} async-done(((bf16[8,192,128]{2,1,0:T(8,128)(2,1)}), bf16[8,192,128]{2,1,0:T(8,128)(2,1)S(1)}, u32[]{:S(2)}, u32[]{:S(2)}) %all-to-all-start.2) | async-done | bytes 393248 | tf_op jit(solution)/shard_map/all_to_all | solution.py:190
  (72 shorter events, 15.7 us)
Async XLA Ops:
  0.6 60.8 %copy-start.17 = (s32[4,16]{1,0:T(4,128)S(1)}, s32[4,16]{1,0:T(4,128)}, u32[]{:S(2)}) copy-start(s32[4,16]{1,0:T(4,128)} %param.9) | copy-start | bytes 772
  0.6 60.9 %copy-start.18 = (s32[4,16]{1,0:T(4,128)S(1)}, s32[4,16]{1,0:T(4,128)}, u32[]{:S(2)}) copy-start(s32[4,16]{1,0:T(4,128)} %param.11) | copy-start | bytes 772
  27.9 46.8 %copy-start.9 = (bf16[8,192,128]{2,1,0:T(8,128)(2,1)}, bf16[8,192,128]{2,1,0:T(8,128)(2,1)S(1)}, u32[]{:S(2)}) copy-start(bf16[8,192,128]{2,1,0:T(8,128)(2,1)S(1)} %get-tuple-element.30.refs_7_.refs_8_) | copy-start | bytes 1179652
  27.9 46.8 %copy-start.10 = (bf16[8,192,128]{2,1,0:T(8,128)(2,1)}, bf16[8,192,128]{2,1,0:T(8,128)(2,1)S(1)}, u32[]{:S(2)}) copy-start(bf16[8,192,128]{2,1,0:T(8,128)(2,1)S(1)} %get-tuple-element.31.refs_0_) | copy-start | bytes 1179652
  27.9 14.4 %collective-permute-start.4 = (bf16[8,192,128]{2,1,0:T(8,128)(2,1)S(1)}, bf16[8,192,128]{2,1,0:T(8,128)(2,1)S(1)}, u32[]{:S(2)}, u32[]{:S(2)}) collective-permute-start(bf16[8,192,128]{2,1,0:T(8,128)(2,1)S(1)} %get-tuple-element.30.refs_7_.refs_8_), channel_id=1, source_target_pairs={{0,56},{8,0},{16,8},{24,16},{32,24},{40,32},{48,40},{56,48},{1,57}... | collective-permute-start | bytes 1179656 | tf_op jit(solution)/shard_map/ppermute | solution.py:196
  33.3 13.0 %collective-permute-start = (bf16[8,192,128]{2,1,0:T(8,128)(2,1)S(1)}, bf16[8,192,128]{2,1,0:T(8,128)(2,1)S(1)}, u32[]{:S(2)}, u32[]{:S(2)}) collective-permute-start(bf16[8,192,128]{2,1,0:T(8,128)(2,1)S(1)} %get-tuple-element.31.refs_0_), channel_id=1, source_target_pairs={{0,8},{8,16},{16,24},{24,32},{32,40},{40,48},{48,56},{56,0},{1,9},... | collective-permute-start | bytes 1179656 | tf_op jit(solution)/shard_map/ppermute | solution.py:196
  35.3 13.2 %collective-permute-start.11 = (bf16[8,192,128]{2,1,0:T(8,128)(2,1)S(1)}, bf16[8,192,128]{2,1,0:T(8,128)(2,1)S(1)}, u32[]{:S(2)}, u32[]{:S(2)}) collective-permute-start(bf16[8,192,128]{2,1,0:T(8,128)(2,1)S(1)} %get-tuple-element.30.refs_7_.refs_8_), channel_id=1, source_target_pairs={{0,8},{8,16},{16,24},{24,32},{32,40},{40,48},{48,56},{56,0},{1,9},... | collective-permute-start | bytes 1179656 | tf_op jit(solution)/shard_map/ppermute | solution.py:196
  37.3 13.1 %collective-permute-start.8 = (bf16[8,192,128]{2,1,0:T(8,128)(2,1)S(1)}, bf16[8,192,128]{2,1,0:T(8,128)(2,1)S(1)}, u32[]{:S(2)}, u32[]{:S(2)}) collective-permute-start(bf16[8,192,128]{2,1,0:T(8,128)(2,1)S(1)} %get-tuple-element.31.refs_0_), channel_id=1, source_target_pairs={{0,56},{8,0},{16,8},{24,16},{32,24},{40,32},{48,40},{56,48},{1,57}... | collective-permute-start | bytes 1179656 | tf_op jit(solution)/shard_map/ppermute | solution.py:196
  42.3 13.2 %collective-permute-start.5 = (bf16[8,192,128]{2,1,0:T(8,128)(2,1)S(1)}, bf16[8,192,128]{2,1,0:T(8,128)(2,1)S(1)}, u32[]{:S(2)}, u32[]{:S(2)}) collective-permute-start(bf16[8,192,128]{2,1,0:T(8,128)(2,1)S(1)} %collective-permute-done.4.refs_9_.refs_10_), channel_id=1, source_target_pairs={{0,56},{8,0},{16,8},{24,16},{32,24},{40,32},{48,40},{56,48},{1,57}... | collective-permute-start | bytes 1179656 | tf_op jit(solution)/shard_map/ppermute | solution.py:196
  46.3 13.0 %collective-permute-start.1 = (bf16[8,192,128]{2,1,0:T(8,128)(2,1)S(1)}, bf16[8,192,128]{2,1,0:T(8,128)(2,1)}, u32[]{:S(2)}, u32[]{:S(2)}) collective-permute-start(bf16[8,192,128]{2,1,0:T(8,128)(2,1)S(1)} %collective-permute-done.refs_1_), channel_id=1, source_target_pairs={{0,8},{8,16},{16,24},{24,32},{32,40},{40,48},{48,56},{56,0},{1,9},... | collective-permute-start | bytes 1179656 | tf_op jit(solution)/shard_map/ppermute | solution.py:196
  48.4 13.2 %collective-permute-start.12 = (bf16[8,192,128]{2,1,0:T(8,128)(2,1)S(1)}, bf16[8,192,128]{2,1,0:T(8,128)(2,1)}, u32[]{:S(2)}, u32[]{:S(2)}) collective-permute-start(bf16[8,192,128]{2,1,0:T(8,128)(2,1)S(1)} %collective-permute-done.11.refs_8_.refs_9_), channel_id=1, source_target_pairs={{0,8},{8,16},{16,24},{24,32},{32,40},{40,48},{48,56},{56,0},{1,9},... | collective-permute-start | bytes 1179656 | tf_op jit(solution)/shard_map/ppermute | solution.py:196
  50.4 13.2 %collective-permute-start.9 = (bf16[8,192,128]{2,1,0:T(8,128)(2,1)S(1)}, bf16[8,192,128]{2,1,0:T(8,128)(2,1)}, u32[]{:S(2)}, u32[]{:S(2)}) collective-permute-start(bf16[8,192,128]{2,1,0:T(8,128)(2,1)S(1)} %collective-permute-done.8.refs_2_), channel_id=1, source_target_pairs={{0,56},{8,0},{16,8},{24,16},{32,24},{40,32},{48,40},{56,48},{1,57}... | collective-permute-start | bytes 1179656 | tf_op jit(solution)/shard_map/ppermute | solution.py:196
  55.5 13.2 %collective-permute-start.6 = (bf16[8,192,128]{2,1,0:T(8,128)(2,1)S(1)}, bf16[8,192,128]{2,1,0:T(8,128)(2,1)S(1)}, u32[]{:S(2)}, u32[]{:S(2)}) collective-permute-start(bf16[8,192,128]{2,1,0:T(8,128)(2,1)S(1)} %collective-permute-done.5.refs_11_.refs_12_), channel_id=1, source_target_pairs={{0,56},{8,0},{16,8},{24,16},{32,24},{40,32},{48,40},{56,48},{1,57}... | collective-permute-start | bytes 1179656 | tf_op jit(solution)/shard_map/ppermute | solution.py:196
  59.3 13.2 %collective-permute-start.2 = (bf16[8,192,128]{2,1,0:T(8,128)(2,1)}, bf16[8,192,128]{2,1,0:T(8,128)(2,1)S(1)}, u32[]{:S(2)}, u32[]{:S(2)}) collective-permute-start(bf16[8,192,128]{2,1,0:T(8,128)(2,1)} %collective-permute-done.1.refs_3_), channel_id=1, source_target_pairs={{0,8},{8,16},{16,24},{24,32},{32,40},{40,48},{48,56},{56,0},{1,9},... | collective-permute-start | bytes 1179656 | tf_op jit(solution)/shard_map/ppermute | solution.py:196
  61.6 13.1 %collective-permute-start.13 = (bf16[8,192,128]{2,1,0:T(8,128)(2,1)}, bf16[8,192,128]{2,1,0:T(8,128)(2,1)S(1)}, u32[]{:S(2)}, u32[]{:S(2)}) collective-permute-start(bf16[8,192,128]{2,1,0:T(8,128)(2,1)} %collective-permute-done.12.refs_10_.refs_11_), channel_id=1, source_target_pairs={{0,8},{8,16},{16,24},{24,32},{32,40},{40,48},{48,56},{56,0},{1,9},... | collective-permute-start | bytes 1179656 | tf_op jit(solution)/shard_map/ppermute | solution.py:196
  63.5 11.2 %collective-permute-start.10 = (bf16[8,192,128]{2,1,0:T(8,128)(2,1)}, bf16[8,192,128]{2,1,0:T(8,128)(2,1)S(1)}, u32[]{:S(2)}, u32[]{:S(2)}) collective-permute-start(bf16[8,192,128]{2,1,0:T(8,128)(2,1)} %collective-permute-done.9.refs_4_), channel_id=1, source_target_pairs={{0,56},{8,0},{16,8},{24,16},{32,24},{40,32},{48,40},{56,48},{1,57}... | collective-permute-start | bytes 1179656 | tf_op jit(solution)/shard_map/ppermute | solution.py:196
  68.7 12.0 %collective-permute-start.7 = (bf16[8,192,128]{2,1,0:T(8,128)(2,1)S(1)}, bf16[8,192,128]{2,1,0:T(8,128)(2,1)S(1)}, u32[]{:S(2)}, u32[]{:S(2)}) collective-permute-start(bf16[8,192,128]{2,1,0:T(8,128)(2,1)S(1)} %collective-permute-done.6.refs_13_.refs_14_), channel_id=1, source_target_pairs={{0,56},{8,0},{16,8},{24,16},{32,24},{40,32},{48,40},{56,48},{1,57}... | collective-permute-start | bytes 1179656 | tf_op jit(solution)/shard_map/ppermute | solution.py:196
  72.5 10.9 %collective-permute-start.3 = (bf16[8,192,128]{2,1,0:T(8,128)(2,1)S(1)}, bf16[8,192,128]{2,1,0:T(8,128)(2,1)S(1)}, u32[]{:S(2)}, u32[]{:S(2)}) collective-permute-start(bf16[8,192,128]{2,1,0:T(8,128)(2,1)S(1)} %collective-permute-done.2.refs_5_), channel_id=1, source_target_pairs={{0,8},{8,16},{16,24},{24,32},{32,40},{40,48},{48,56},{56,0},{1,9},... | collective-permute-start | bytes 1179656 | tf_op jit(solution)/shard_map/ppermute | solution.py:196
  87.5 45.7 %all-to-all-start.1 = ((bf16[8,8,192,128]{3,2,1,0:T(8,128)(2,1)}), bf16[8,8,192,128]{3,2,1,0:T(8,128)(2,1)S(1)}, u32[]{:S(2)}, u32[]{:S(2)}) async-start(bf16[8,8,192,128]{3,2,1,0:T(8,128)(2,1)} %get-tuple-element.20), calls=%async_computation.1 | async-start | bytes 6291456 | tf_op jit(solution)/shard_map/all_to_all | solution.py:190
  98.2 6.1 %collective-permute-start.14 = (bf16[4,2,4,2,128,128]{5,4,3,2,1,0:T(8,128)(2,1)S(1)}, bf16[4,2,4,2,128,128]{5,4,3,2,1,0:T(8,128)(2,1)S(1)}, u32[]{:S(2)}, u32[]{:S(2)}) collective-permute-start(bf16[4,2,4,2,128,128]{5,4,3,2,1,0:T(8,128)(2,1)S(1)} %get-tuple-element.24), channel_id=1, source_target_pairs={{0,64},{64,0},{1,65},{65,1},{2,66},{66,2},{3,67},{67,3},{4,68},{68... | collective-permute-start | bytes 6291464 | tf_op jit(solution)/shard_map/ppermute | solution.py:286
  106.1 31.7 %collective-permute-start.15 = (bf16[2,4,2,128,128]{4,3,2,1,0:T(8,128)(2,1)}, bf16[2,4,2,128,128]{4,3,2,1,0:T(8,128)(2,1)}, u32[]{:S(2)}, u32[]{:S(2)}) collective-permute-start(bf16[2,4,2,128,128]{4,3,2,1,0:T(8,128)(2,1)} %get-tuple-element.27), channel_id=1, source_target_pairs={{0,128},{128,256},{256,384},{384,0},{1,129},{129,257},{257,385},{3... | collective-permute-start | bytes 1572872 | tf_op jit(solution)/shard_map/ppermute | solution.py:289
  108.5 29.3 %collective-permute-start.17 = (bf16[2,4,2,128,128]{4,3,2,1,0:T(8,128)(2,1)}, bf16[2,4,2,128,128]{4,3,2,1,0:T(8,128)(2,1)}, u32[]{:S(2)}, u32[]{:S(2)}) collective-permute-start(bf16[2,4,2,128,128]{4,3,2,1,0:T(8,128)(2,1)} %get-tuple-element.28), channel_id=1, source_target_pairs={{0,384},{128,0},{256,128},{384,256},{1,385},{129,1},{257,129},{385... | collective-permute-start | bytes 1572872 | tf_op jit(solution)/shard_map/ppermute | solution.py:289
  112.0 25.8 %collective-permute-start.16 = (bf16[2,4,2,128,128]{4,3,2,1,0:T(8,128)(2,1)}, bf16[2,4,2,128,128]{4,3,2,1,0:T(8,128)(2,1)}, u32[]{:S(2)}, u32[]{:S(2)}) collective-permute-start(bf16[2,4,2,128,128]{4,3,2,1,0:T(8,128)(2,1)} %get-tuple-element.29), channel_id=1, source_target_pairs={{0,256},{128,384},{256,0},{384,128},{1,257},{129,385},{257,1},{385... | collective-permute-start | bytes 1572872 | tf_op jit(solution)/shard_map/ppermute | solution.py:289
  134.3 15.3 %all-to-all-start.2 = ((bf16[8,192,128]{2,1,0:T(8,128)(2,1)}), bf16[8,192,128]{2,1,0:T(8,128)(2,1)S(1)}, u32[]{:S(2)}, u32[]{:S(2)}) async-start(bf16[8,192,128]{2,1,0:T(8,128)(2,1)} %sums.1), calls=%async_computation.2 | async-start | bytes 786432 | tf_op jit(solution)/shard_map/all_to_all | solution.py:190
  (15 other events, 191.9 us)

commit v12 on v11

--- a/solution.py
+++ b/solution.py
@@ -155,12 +155,17 @@
                     out[away, 1, r, j] = dot_nn(act_t, y[where[1, at]]).astype(BF16)
 
 
-def sum_kernel(parts, out):
+def sum_kernel(parts, out, sums, sem):
+    copies = []
     for n in range(parts.shape[1]):
         kept = parts[0, n].astype(F32)
         for s in range(1, parts.shape[0]):
             kept = kept + parts[s, n].astype(F32)
-        out[n] = kept.astype(BF16)
+        sums[n] = kept.astype(BF16)
+        copies.append(pltpu.make_async_copy(sums.at[n], out.at[n], sem.at[n]))
+        copies[-1].start()
+    for copy in copies:
+        copy.wait()
 
 
 def lines_and_rings(ny, nz):
@@ -292,9 +297,10 @@
 
     on_line = pl.pallas_call(
         sum_kernel,
-        out_shape=jax.ShapeDtypeStruct(on_ring.shape[1:], BF16),
+        out_shape=pltpu.HBM((blocks // side, tok, width), BF16),
         in_specs=[vmem],
-        out_specs=vmem,
+        out_specs=anywhere,
+        scratch_shapes=[pltpu.VMEM((blocks // side, tok, width), BF16), loaded],
         compiler_params=params,
         name="sums",
     )(pltpu.with_memory_space_constraint(on_ring, pltpu.VMEM))

time: 151 us -> 151 us (level)
  no operation moved by 1% of the time
where the time goes in v12:
time: 151 us; the launch traced here: 150 us
  starting transfers between devices  64.7 us (43%)
  waiting for transfers between devices  33.6 us (22%)
  blocking collectives  26.2 us (17%)
  Pallas kernels  17.5 us (12%)
  other arithmetic  5.61 us (4%)
    ppermute x14, starting transfers between devices, turn(): return lax.ppermute(values, CYZ, pairs)  46 us
    all_to_all x2, waiting for transfers between devices, swap(): lax.all_to_all(values, CYZ, split_axis=0, concat_axis=0, tiled=True, axis...  26.7 us
    all_to_all x1, blocking collectives, swap(): lax.all_to_all(values, CYZ, split_axis=0, concat_axis=0, tiled=True, axis...  26.2 us
    ppermute x3, starting transfers between devices, per_device(): lax.ppermute(paired[d], 'x', [(i, (i + d) % nx) for i in range(nx)])  9.16 us
    all_to_all x2, starting transfers between devices, swap(): lax.all_to_all(values, CYZ, split_axis=0, concat_axis=0, tiled=True, axis...  7.69 us
    pallas_call x1, Pallas kernels, per_device(): pl.pallas_call(functools.partial(weight_kernel, (x_plan, y_plan)), out_sh...  6.46 us
    pallas_call x1, Pallas kernels, per_device(): pl.pallas_call(functools.partial(early_kernel, ((side, x_plan[1][:-1]), (...  5.88 us
    ppermute x1, waiting for transfers between devices, per_device(): swapped = lax.ppermute(other, 'c', [(0, 1), (1, 0)])  4.13 us
  transfers between devices with their start and end apart: 20, of which 5 were waited for; matrix products, arithmetic and copies ran while one was open for 3% of the time, Pallas kernels for 9%

profile of v12, /device:TPU:6, one launch (start us, length us, event | category | flops | bytes accessed | tf_op | source)
XLA Modules:
  0.0 150.2 jit_solution(10786768946676365476)
XLA Ops:
  1.7 26.2 %all_to_all.15 = bf16[8,2,192,128]{3,2,1,0:T(8,128)(2,1)S(1)} all-to-all(bf16[8,2,192,128]{3,2,1,0:T(8,128)(2,1)S(1)} %broadcast_in_dim.5), channel_id=1, replica_groups={{0,1,2,3,4,5,6,7},{8,9,10,11,12,13,14,15},{16,17,18,19,20,21,22,23},{24..., dimensions={0} | all-to-all | bytes 1572864 | tf_op jit(solution)/shard_map/all_to_all | solution.py:195
  27.9 5.4 %collective-permute-start.4 = (bf16[8,192,128]{2,1,0:T(8,128)(2,1)S(1)}, bf16[8,192,128]{2,1,0:T(8,128)(2,1)S(1)}, u32[]{:S(2)}, u32[]{:S(2)}) collective-permute-start(bf16[8,192,128]{2,1,0:T(8,128)(2,1)S(1)} %get-tuple-element.30.refs_7_.refs_8_), channel_id=1, source_target_pairs={{0,56},{8,0},{16,8},{24,16},{32,24},{40,32},{48,40},{56,48},{1,57}... | collective-permute-start | bytes 1179656 | tf_op jit(solution)/shard_map/ppermute | solution.py:201
  35.3 2.0 %collective-permute-start.11 = (bf16[8,192,128]{2,1,0:T(8,128)(2,1)S(1)}, bf16[8,192,128]{2,1,0:T(8,128)(2,1)S(1)}, u32[]{:S(2)}, u32[]{:S(2)}) collective-permute-start(bf16[8,192,128]{2,1,0:T(8,128)(2,1)S(1)} %get-tuple-element.30.refs_7_.refs_8_), channel_id=1, source_target_pairs={{0,8},{8,16},{16,24},{24,32},{32,40},{40,48},{48,56},{56,0},{1,9},... | collective-permute-start | bytes 1179656 | tf_op jit(solution)/shard_map/ppermute | solution.py:201
  37.3 5.0 %collective-permute-start.8 = (bf16[8,192,128]{2,1,0:T(8,128)(2,1)S(1)}, bf16[8,192,128]{2,1,0:T(8,128)(2,1)S(1)}, u32[]{:S(2)}, u32[]{:S(2)}) collective-permute-start(bf16[8,192,128]{2,1,0:T(8,128)(2,1)S(1)} %get-tuple-element.31.refs_0_), channel_id=1, source_target_pairs={{0,56},{8,0},{16,8},{24,16},{32,24},{40,32},{48,40},{56,48},{1,57}... | collective-permute-start | bytes 1179656 | tf_op jit(solution)/shard_map/ppermute | solution.py:201
  42.3 3.9 %collective-permute-start.5 = (bf16[8,192,128]{2,1,0:T(8,128)(2,1)S(1)}, bf16[8,192,128]{2,1,0:T(8,128)(2,1)S(1)}, u32[]{:S(2)}, u32[]{:S(2)}) collective-permute-start(bf16[8,192,128]{2,1,0:T(8,128)(2,1)S(1)} %collective-permute-done.4.refs_9_.refs_10_), channel_id=1, source_target_pairs={{0,56},{8,0},{16,8},{24,16},{32,24},{40,32},{48,40},{56,48},{1,57}... | collective-permute-start | bytes 1179656 | tf_op jit(solution)/shard_map/ppermute | solution.py:201
  50.4 5.1 %collective-permute-start.9 = (bf16[8,192,128]{2,1,0:T(8,128)(2,1)S(1)}, bf16[8,192,128]{2,1,0:T(8,128)(2,1)}, u32[]{:S(2)}, u32[]{:S(2)}) collective-permute-start(bf16[8,192,128]{2,1,0:T(8,128)(2,1)S(1)} %collective-permute-done.8.refs_2_), channel_id=1, source_target_pairs={{0,56},{8,0},{16,8},{24,16},{32,24},{40,32},{48,40},{56,48},{1,57}... | collective-permute-start | bytes 1179656 | tf_op jit(solution)/shard_map/ppermute | solution.py:201
  55.5 3.8 %collective-permute-start.6 = (bf16[8,192,128]{2,1,0:T(8,128)(2,1)S(1)}, bf16[8,192,128]{2,1,0:T(8,128)(2,1)S(1)}, u32[]{:S(2)}, u32[]{:S(2)}) collective-permute-start(bf16[8,192,128]{2,1,0:T(8,128)(2,1)S(1)} %collective-permute-done.5.refs_11_.refs_12_), channel_id=1, source_target_pairs={{0,56},{8,0},{16,8},{24,16},{32,24},{40,32},{48,40},{56,48},{1,57}... | collective-permute-start | bytes 1179656 | tf_op jit(solution)/shard_map/ppermute | solution.py:201
  59.3 2.1 %collective-permute-start.2 = (bf16[8,192,128]{2,1,0:T(8,128)(2,1)}, bf16[8,192,128]{2,1,0:T(8,128)(2,1)S(1)}, u32[]{:S(2)}, u32[]{:S(2)}) collective-permute-start(bf16[8,192,128]{2,1,0:T(8,128)(2,1)} %collective-permute-done.1.refs_3_), channel_id=1, source_target_pairs={{0,8},{8,16},{16,24},{24,32},{32,40},{40,48},{48,56},{56,0},{1,9},... | collective-permute-start | bytes 1179656 | tf_op jit(solution)/shard_map/ppermute | solution.py:201
  63.5 5.1 %collective-permute-start.10 = (bf16[8,192,128]{2,1,0:T(8,128)(2,1)}, bf16[8,192,128]{2,1,0:T(8,128)(2,1)S(1)}, u32[]{:S(2)}, u32[]{:S(2)}) collective-permute-start(bf16[8,192,128]{2,1,0:T(8,128)(2,1)} %collective-permute-done.9.refs_4_), channel_id=1, source_target_pairs={{0,56},{8,0},{16,8},{24,16},{32,24},{40,32},{48,40},{56,48},{1,57}... | collective-permute-start | bytes 1179656 | tf_op jit(solution)/shard_map/ppermute | solution.py:201
  68.7 3.8 %collective-permute-start.7 = (bf16[8,192,128]{2,1,0:T(8,128)(2,1)S(1)}, bf16[8,192,128]{2,1,0:T(8,128)(2,1)S(1)}, u32[]{:S(2)}, u32[]{:S(2)}) collective-permute-start(bf16[8,192,128]{2,1,0:T(8,128)(2,1)S(1)} %collective-permute-done.6.refs_13_.refs_14_), channel_id=1, source_target_pairs={{0,56},{8,0},{16,8},{24,16},{32,24},{40,32},{48,40},{56,48},{1,57}... | collective-permute-start | bytes 1179656 | tf_op jit(solution)/shard_map/ppermute | solution.py:201
  72.5 2.1 %collective-permute-start.3 = (bf16[8,192,128]{2,1,0:T(8,128)(2,1)S(1)}, bf16[8,192,128]{2,1,0:T(8,128)(2,1)S(1)}, u32[]{:S(2)}, u32[]{:S(2)}) collective-permute-start(bf16[8,192,128]{2,1,0:T(8,128)(2,1)S(1)} %collective-permute-done.2.refs_5_), channel_id=1, source_target_pairs={{0,8},{8,16},{16,24},{24,32},{32,40},{40,48},{48,56},{56,0},{1,9},... | collective-permute-start | bytes 1179656 | tf_op jit(solution)/shard_map/ppermute | solution.py:201
  74.8 5.9 %early.1 = (f32[192,512]{1,0:T(8,128)S(1)}, f32[192,512]{1,0:T(8,128)S(1)}, bf16[4,16,128,128]{3,2,1,0:T(8,128)(2,1)S(1)}, bf16[9,128,512]{2,1,0:T(8,128)(2,1)S(...) custom-call(s32[5,64]{1,0:T(8,128)S(1)} %pad_add_fusion.where, bf16[8,192,128]{2,1,0:T(8,128)(2,1)} %copy-done.10, ...), custom_call_target="tpu_custom_call" | custom-call | tf_op jit(solution)/shard_map/early/pallas_call | solution.py:239
  80.8 2.6 %collective-permute-done.3.x_last.refs_7_ = bf16[8,192,128]{2,1,0:T(8,128)(2,1)S(1)} collective-permute-done((bf16[8,192,128]{2,1,0:T(8,128)(2,1)S(1)}, bf16[8,192,128]{2,1,0:T(8,128)(2,1)S(1)}, u32[]{:S(2)}, u32[]{:S(2)}) %collective-permute-start.3) | collective-permute-done | bytes 393248 | tf_op jit(solution)/shard_map/ppermute | solution.py:201
  83.4 4.1 %back.1 = (bf16[8,8,192,128]{3,2,1,0:T(8,128)(2,1)}, bf16[4,192,128]{2,1,0:T(8,128)(2,1)}, bf16[4,192,128]{2,1,0:T(8,128)(2,1)}, f32[64,192,128]{2,1,0:T(8,128)S(1)}) custom-call(s32[5,64]{1,0:T(8,128)S(1)} %pad_add_fusion.where, bf16[8,192,128]{2,1,0:T(8,128)(2,1)S(1)} %collective-permute-done.3.x_last.refs_7_, ...), custom_call_target="tpu_custom_call", output_to_operand_aliasing={{3}: (8, {})} | custom-call | tf_op jit(solution)/shard_map/back/pallas_call | solution.py:255
  87.5 4.2 %all-to-all-start.1 = ((bf16[8,8,192,128]{3,2,1,0:T(8,128)(2,1)}), bf16[8,8,192,128]{3,2,1,0:T(8,128)(2,1)S(1)}, u32[]{:S(2)}, u32[]{:S(2)}) async-start(bf16[8,8,192,128]{3,2,1,0:T(8,128)(2,1)} %get-tuple-element.20), calls=%async_computation.1 | async-start | bytes 6291456 | tf_op jit(solution)/shard_map/all_to_all | solution.py:195
  91.7 6.5 %weights.1 = (bf16[4,2,4,2,128,128]{5,4,3,2,1,0:T(8,128)(2,1)S(1)}, bf16[4,2,4,2,128,128]{5,4,3,2,1,0:T(8,128)(2,1)S(1)}) custom-call(s32[5,64]{1,0:T(8,128)S(1)} %pad_add_fusion.where, bf16[8,192,128]{2,1,0:T(8,128)(2,1)} %copy-done.10, bf16[8,192,128]{2,1,0:T(8,128)(2,1)} %copy-done.13, bf16[8,192,128]{2,1,0:T(8,128)(2,1)} %copy-done.15, ...), custom_call_target="tpu_custom_call" | custom-call | tf_op jit(solution)/shard_map/weights/pallas_call | solution.py:274
  100.1 4.1 %collective-permute-done.14 = bf16[4,2,4,2,128,128]{5,4,3,2,1,0:T(8,128)(2,1)S(1)} collective-permute-done((bf16[4,2,4,2,128,128]{5,4,3,2,1,0:T(8,128)(2,1)S(1)}, bf16[4,2,4,2,128,128]{5,4,3,2,1,0:T(8,128)(2,1)S(1)}, u32[]{:S(2)}, u32[]{:S(2)}) %collective-permute-start.14) | collective-permute-done | bytes 2097184 | tf_op jit(solution)/shard_map/ppermute | solution.py:291
  106.1 2.4 %collective-permute-start.15 = (bf16[2,4,2,128,128]{4,3,2,1,0:T(8,128)(2,1)}, bf16[2,4,2,128,128]{4,3,2,1,0:T(8,128)(2,1)}, u32[]{:S(2)}, u32[]{:S(2)}) collective-permute-start(bf16[2,4,2,128,128]{4,3,2,1,0:T(8,128)(2,1)} %get-tuple-element.27), channel_id=1, source_target_pairs={{0,128},{128,256},{256,384},{384,0},{1,129},{129,257},{257,385},{3... | collective-permute-start | bytes 1572872 | tf_op jit(solution)/shard_map/ppermute | solution.py:294
  108.5 3.5 %collective-permute-start.17 = (bf16[2,4,2,128,128]{4,3,2,1,0:T(8,128)(2,1)}, bf16[2,4,2,128,128]{4,3,2,1,0:T(8,128)(2,1)}, u32[]{:S(2)}, u32[]{:S(2)}) collective-permute-start(bf16[2,4,2,128,128]{4,3,2,1,0:T(8,128)(2,1)} %get-tuple-element.28), channel_id=1, source_target_pairs={{0,384},{128,0},{256,128},{384,256},{1,385},{129,1},{257,129},{385... | collective-permute-start | bytes 1572872 | tf_op jit(solution)/shard_map/ppermute | solution.py:294
  112.0 3.3 %collective-permute-start.16 = (bf16[2,4,2,128,128]{4,3,2,1,0:T(8,128)(2,1)}, bf16[2,4,2,128,128]{4,3,2,1,0:T(8,128)(2,1)}, u32[]{:S(2)}, u32[]{:S(2)}) collective-permute-start(bf16[2,4,2,128,128]{4,3,2,1,0:T(8,128)(2,1)} %get-tuple-element.29), channel_id=1, source_target_pairs={{0,256},{128,384},{256,0},{384,128},{1,257},{129,385},{257,1},{385... | collective-permute-start | bytes 1572872 | tf_op jit(solution)/shard_map/ppermute | solution.py:294
  115.3 17.9 %all-to-all-done.1.parts = bf16[8,8,192,128]{3,2,1,0:T(8,128)(2,1)S(1)} async-done(((bf16[8,8,192,128]{3,2,1,0:T(8,128)(2,1)}), bf16[8,8,192,128]{3,2,1,0:T(8,128)(2,1)S(1)}, u32[]{:S(2)}, u32[]{:S(2)}) %all-to-all-start.1) | async-done | bytes 3145760 | tf_op jit(solution)/shard_map/all_to_all | solution.py:195
  134.3 3.5 %all-to-all-start.2 = ((bf16[8,192,128]{2,1,0:T(8,128)(2,1)}), bf16[8,192,128]{2,1,0:T(8,128)(2,1)S(1)}, u32[]{:S(2)}, u32[]{:S(2)}) async-start(bf16[8,192,128]{2,1,0:T(8,128)(2,1)} %sums.1), calls=%async_computation.2 | async-start | bytes 786432 | tf_op jit(solution)/shard_map/all_to_all | solution.py:195
  137.8 2.1 %fusion.2 = bf16[2,4,2,128,128]{4,3,2,1,0:T(8,128)(2,1)S(1)} fusion(bf16[2,4,2,128,128]{4,3,2,1,0:T(8,128)(2,1)} %collective-permute-done.17, bf16[2,4,2,128,128]{4,3,2,1,0:T(8,128)(2,1)} %collective-permute-done.16, bf16[2,4,2,128,128]{4,3,2,1,0:T(8,128)(2,1)} %collective-permute-done.15, bf16[4,2,4,2,128,128]{5,4,3,2,1,0:T(8,128)(2,1)} %copy-done.11, ...), kind=kLoop, calls=%fused_computation.3 | loop fusion | flops 3145728 | bytes 3145728 | tf_op jit(solution)/shard_map/convert_element_type | solution.py:296
  140.7 8.8 %all-to-all-done.2 = bf16[8,192,128]{2,1,0:T(8,128)(2,1)S(1)} async-done(((bf16[8,192,128]{2,1,0:T(8,128)(2,1)}), bf16[8,192,128]{2,1,0:T(8,128)(2,1)S(1)}, u32[]{:S(2)}, u32[]{:S(2)}) %all-to-all-start.2) | async-done | bytes 393248 | tf_op jit(solution)/shard_map/all_to_all | solution.py:195
  (72 shorter events, 15.7 us)
Async XLA Ops:
  0.6 60.8 %copy-start.17 = (s32[4,16]{1,0:T(4,128)S(1)}, s32[4,16]{1,0:T(4,128)}, u32[]{:S(2)}) copy-start(s32[4,16]{1,0:T(4,128)} %param.9) | copy-start | bytes 772
  0.6 60.9 %copy-start.18 = (s32[4,16]{1,0:T(4,128)S(1)}, s32[4,16]{1,0:T(4,128)}, u32[]{:S(2)}) copy-start(s32[4,16]{1,0:T(4,128)} %param.11) | copy-start | bytes 772
  27.9 46.8 %copy-start.9 = (bf16[8,192,128]{2,1,0:T(8,128)(2,1)}, bf16[8,192,128]{2,1,0:T(8,128)(2,1)S(1)}, u32[]{:S(2)}) copy-start(bf16[8,192,128]{2,1,0:T(8,128)(2,1)S(1)} %get-tuple-element.30.refs_7_.refs_8_) | copy-start | bytes 1179652
  27.9 46.8 %copy-start.10 = (bf16[8,192,128]{2,1,0:T(8,128)(2,1)}, bf16[8,192,128]{2,1,0:T(8,128)(2,1)S(1)}, u32[]{:S(2)}) copy-start(bf16[8,192,128]{2,1,0:T(8,128)(2,1)S(1)} %get-tuple-element.31.refs_0_) | copy-start | bytes 1179652
  27.9 14.4 %collective-permute-start.4 = (bf16[8,192,128]{2,1,0:T(8,128)(2,1)S(1)}, bf16[8,192,128]{2,1,0:T(8,128)(2,1)S(1)}, u32[]{:S(2)}, u32[]{:S(2)}) collective-permute-start(bf16[8,192,128]{2,1,0:T(8,128)(2,1)S(1)} %get-tuple-element.30.refs_7_.refs_8_), channel_id=1, source_target_pairs={{0,56},{8,0},{16,8},{24,16},{32,24},{40,32},{48,40},{56,48},{1,57}... | collective-permute-start | bytes 1179656 | tf_op jit(solution)/shard_map/ppermute | solution.py:201
  33.3 13.0 %collective-permute-start = (bf16[8,192,128]{2,1,0:T(8,128)(2,1)S(1)}, bf16[8,192,128]{2,1,0:T(8,128)(2,1)S(1)}, u32[]{:S(2)}, u32[]{:S(2)}) collective-permute-start(bf16[8,192,128]{2,1,0:T(8,128)(2,1)S(1)} %get-tuple-element.31.refs_0_), channel_id=1, source_target_pairs={{0,8},{8,16},{16,24},{24,32},{32,40},{40,48},{48,56},{56,0},{1,9},... | collective-permute-start | bytes 1179656 | tf_op jit(solution)/shard_map/ppermute | solution.py:201
  35.3 13.2 %collective-permute-start.11 = (bf16[8,192,128]{2,1,0:T(8,128)(2,1)S(1)}, bf16[8,192,128]{2,1,0:T(8,128)(2,1)S(1)}, u32[]{:S(2)}, u32[]{:S(2)}) collective-permute-start(bf16[8,192,128]{2,1,0:T(8,128)(2,1)S(1)} %get-tuple-element.30.refs_7_.refs_8_), channel_id=1, source_target_pairs={{0,8},{8,16},{16,24},{24,32},{32,40},{40,48},{48,56},{56,0},{1,9},... | collective-permute-start | bytes 1179656 | tf_op jit(solution)/shard_map/ppermute | solution.py:201
  37.3 13.1 %collective-permute-start.8 = (bf16[8,192,128]{2,1,0:T(8,128)(2,1)S(1)}, bf16[8,192,128]{2,1,0:T(8,128)(2,1)S(1)}, u32[]{:S(2)}, u32[]{:S(2)}) collective-permute-start(bf16[8,192,128]{2,1,0:T(8,128)(2,1)S(1)} %get-tuple-element.31.refs_0_), channel_id=1, source_target_pairs={{0,56},{8,0},{16,8},{24,16},{32,24},{40,32},{48,40},{56,48},{1,57}... | collective-permute-start | bytes 1179656 | tf_op jit(solution)/shard_map/ppermute | solution.py:201
  42.3 13.2 %collective-permute-start.5 = (bf16[8,192,128]{2,1,0:T(8,128)(2,1)S(1)}, bf16[8,192,128]{2,1,0:T(8,128)(2,1)S(1)}, u32[]{:S(2)}, u32[]{:S(2)}) collective-permute-start(bf16[8,192,128]{2,1,0:T(8,128)(2,1)S(1)} %collective-permute-done.4.refs_9_.refs_10_), channel_id=1, source_target_pairs={{0,56},{8,0},{16,8},{24,16},{32,24},{40,32},{48,40},{56,48},{1,57}... | collective-permute-start | bytes 1179656 | tf_op jit(solution)/shard_map/ppermute | solution.py:201
  46.3 13.0 %collective-permute-start.1 = (bf16[8,192,128]{2,1,0:T(8,128)(2,1)S(1)}, bf16[8,192,128]{2,1,0:T(8,128)(2,1)}, u32[]{:S(2)}, u32[]{:S(2)}) collective-permute-start(bf16[8,192,128]{2,1,0:T(8,128)(2,1)S(1)} %collective-permute-done.refs_1_), channel_id=1, source_target_pairs={{0,8},{8,16},{16,24},{24,32},{32,40},{40,48},{48,56},{56,0},{1,9},... | collective-permute-start | bytes 1179656 | tf_op jit(solution)/shard_map/ppermute | solution.py:201
  48.4 13.2 %collective-permute-start.12 = (bf16[8,192,128]{2,1,0:T(8,128)(2,1)S(1)}, bf16[8,192,128]{2,1,0:T(8,128)(2,1)}, u32[]{:S(2)}, u32[]{:S(2)}) collective-permute-start(bf16[8,192,128]{2,1,0:T(8,128)(2,1)S(1)} %collective-permute-done.11.refs_8_.refs_9_), channel_id=1, source_target_pairs={{0,8},{8,16},{16,24},{24,32},{32,40},{40,48},{48,56},{56,0},{1,9},... | collective-permute-start | bytes 1179656 | tf_op jit(solution)/shard_map/ppermute | solution.py:201
  50.4 13.2 %collective-permute-start.9 = (bf16[8,192,128]{2,1,0:T(8,128)(2,1)S(1)}, bf16[8,192,128]{2,1,0:T(8,128)(2,1)}, u32[]{:S(2)}, u32[]{:S(2)}) collective-permute-start(bf16[8,192,128]{2,1,0:T(8,128)(2,1)S(1)} %collective-permute-done.8.refs_2_), channel_id=1, source_target_pairs={{0,56},{8,0},{16,8},{24,16},{32,24},{40,32},{48,40},{56,48},{1,57}... | collective-permute-start | bytes 1179656 | tf_op jit(solution)/shard_map/ppermute | solution.py:201
  55.5 13.2 %collective-permute-start.6 = (bf16[8,192,128]{2,1,0:T(8,128)(2,1)S(1)}, bf16[8,192,128]{2,1,0:T(8,128)(2,1)S(1)}, u32[]{:S(2)}, u32[]{:S(2)}) collective-permute-start(bf16[8,192,128]{2,1,0:T(8,128)(2,1)S(1)} %collective-permute-done.5.refs_11_.refs_12_), channel_id=1, source_target_pairs={{0,56},{8,0},{16,8},{24,16},{32,24},{40,32},{48,40},{56,48},{1,57}... | collective-permute-start | bytes 1179656 | tf_op jit(solution)/shard_map/ppermute | solution.py:201
  59.3 13.2 %collective-permute-start.2 = (bf16[8,192,128]{2,1,0:T(8,128)(2,1)}, bf16[8,192,128]{2,1,0:T(8,128)(2,1)S(1)}, u32[]{:S(2)}, u32[]{:S(2)}) collective-permute-start(bf16[8,192,128]{2,1,0:T(8,128)(2,1)} %collective-permute-done.1.refs_3_), channel_id=1, source_target_pairs={{0,8},{8,16},{16,24},{24,32},{32,40},{40,48},{48,56},{56,0},{1,9},... | collective-permute-start | bytes 1179656 | tf_op jit(solution)/shard_map/ppermute | solution.py:201
  61.6 13.1 %collective-permute-start.13 = (bf16[8,192,128]{2,1,0:T(8,128)(2,1)}, bf16[8,192,128]{2,1,0:T(8,128)(2,1)S(1)}, u32[]{:S(2)}, u32[]{:S(2)}) collective-permute-start(bf16[8,192,128]{2,1,0:T(8,128)(2,1)} %collective-permute-done.12.refs_10_.refs_11_), channel_id=1, source_target_pairs={{0,8},{8,16},{16,24},{24,32},{32,40},{40,48},{48,56},{56,0},{1,9},... | collective-permute-start | bytes 1179656 | tf_op jit(solution)/shard_map/ppermute | solution.py:201
  63.5 11.2 %collective-permute-start.10 = (bf16[8,192,128]{2,1,0:T(8,128)(2,1)}, bf16[8,192,128]{2,1,0:T(8,128)(2,1)S(1)}, u32[]{:S(2)}, u32[]{:S(2)}) collective-permute-start(bf16[8,192,128]{2,1,0:T(8,128)(2,1)} %collective-permute-done.9.refs_4_), channel_id=1, source_target_pairs={{0,56},{8,0},{16,8},{24,16},{32,24},{40,32},{48,40},{56,48},{1,57}... | collective-permute-start | bytes 1179656 | tf_op jit(solution)/shard_map/ppermute | solution.py:201
  68.7 12.0 %collective-permute-start.7 = (bf16[8,192,128]{2,1,0:T(8,128)(2,1)S(1)}, bf16[8,192,128]{2,1,0:T(8,128)(2,1)S(1)}, u32[]{:S(2)}, u32[]{:S(2)}) collective-permute-start(bf16[8,192,128]{2,1,0:T(8,128)(2,1)S(1)} %collective-permute-done.6.refs_13_.refs_14_), channel_id=1, source_target_pairs={{0,56},{8,0},{16,8},{24,16},{32,24},{40,32},{48,40},{56,48},{1,57}... | collective-permute-start | bytes 1179656 | tf_op jit(solution)/shard_map/ppermute | solution.py:201
  72.5 10.9 %collective-permute-start.3 = (bf16[8,192,128]{2,1,0:T(8,128)(2,1)S(1)}, bf16[8,192,128]{2,1,0:T(8,128)(2,1)S(1)}, u32[]{:S(2)}, u32[]{:S(2)}) collective-permute-start(bf16[8,192,128]{2,1,0:T(8,128)(2,1)S(1)} %collective-permute-done.2.refs_5_), channel_id=1, source_target_pairs={{0,8},{8,16},{16,24},{24,32},{32,40},{40,48},{48,56},{56,0},{1,9},... | collective-permute-start | bytes 1179656 | tf_op jit(solution)/shard_map/ppermute | solution.py:201
  87.5 45.7 %all-to-all-start.1 = ((bf16[8,8,192,128]{3,2,1,0:T(8,128)(2,1)}), bf16[8,8,192,128]{3,2,1,0:T(8,128)(2,1)S(1)}, u32[]{:S(2)}, u32[]{:S(2)}) async-start(bf16[8,8,192,128]{3,2,1,0:T(8,128)(2,1)} %get-tuple-element.20), calls=%async_computation.1 | async-start | bytes 6291456 | tf_op jit(solution)/shard_map/all_to_all | solution.py:195
  98.2 6.1 %collective-permute-start.14 = (bf16[4,2,4,2,128,128]{5,4,3,2,1,0:T(8,128)(2,1)S(1)}, bf16[4,2,4,2,128,128]{5,4,3,2,1,0:T(8,128)(2,1)S(1)}, u32[]{:S(2)}, u32[]{:S(2)}) collective-permute-start(bf16[4,2,4,2,128,128]{5,4,3,2,1,0:T(8,128)(2,1)S(1)} %get-tuple-element.24), channel_id=1, source_target_pairs={{0,64},{64,0},{1,65},{65,1},{2,66},{66,2},{3,67},{67,3},{4,68},{68... | collective-permute-start | bytes 6291464 | tf_op jit(solution)/shard_map/ppermute | solution.py:291
  106.1 31.6 %collective-permute-start.15 = (bf16[2,4,2,128,128]{4,3,2,1,0:T(8,128)(2,1)}, bf16[2,4,2,128,128]{4,3,2,1,0:T(8,128)(2,1)}, u32[]{:S(2)}, u32[]{:S(2)}) collective-permute-start(bf16[2,4,2,128,128]{4,3,2,1,0:T(8,128)(2,1)} %get-tuple-element.27), channel_id=1, source_target_pairs={{0,128},{128,256},{256,384},{384,0},{1,129},{129,257},{257,385},{3... | collective-permute-start | bytes 1572872 | tf_op jit(solution)/shard_map/ppermute | solution.py:294
  108.5 29.2 %collective-permute-start.17 = (bf16[2,4,2,128,128]{4,3,2,1,0:T(8,128)(2,1)}, bf16[2,4,2,128,128]{4,3,2,1,0:T(8,128)(2,1)}, u32[]{:S(2)}, u32[]{:S(2)}) collective-permute-start(bf16[2,4,2,128,128]{4,3,2,1,0:T(8,128)(2,1)} %get-tuple-element.28), channel_id=1, source_target_pairs={{0,384},{128,0},{256,128},{384,256},{1,385},{129,1},{257,129},{385... | collective-permute-start | bytes 1572872 | tf_op jit(solution)/shard_map/ppermute | solution.py:294
  112.0 25.8 %collective-permute-start.16 = (bf16[2,4,2,128,128]{4,3,2,1,0:T(8,128)(2,1)}, bf16[2,4,2,128,128]{4,3,2,1,0:T(8,128)(2,1)}, u32[]{:S(2)}, u32[]{:S(2)}) collective-permute-start(bf16[2,4,2,128,128]{4,3,2,1,0:T(8,128)(2,1)} %get-tuple-element.29), channel_id=1, source_target_pairs={{0,256},{128,384},{256,0},{384,128},{1,257},{129,385},{257,1},{385... | collective-permute-start | bytes 1572872 | tf_op jit(solution)/shard_map/ppermute | solution.py:294
  134.3 15.3 %all-to-all-start.2 = ((bf16[8,192,128]{2,1,0:T(8,128)(2,1)}), bf16[8,192,128]{2,1,0:T(8,128)(2,1)S(1)}, u32[]{:S(2)}, u32[]{:S(2)}) async-start(bf16[8,192,128]{2,1,0:T(8,128)(2,1)} %sums.1), calls=%async_computation.2 | async-start | bytes 786432 | tf_op jit(solution)/shard_map/all_to_all | solution.py:195
  (15 other events, 191.9 us)
